TPU v7x, 32 devices: a whole 2x2x4 slice. The times are simulated.
32 devices in a mesh: row: 8 (over z, core), col: 4 (over y, x).
Axes of the slice: x: 2, y: 2, z: 4, core: 2. Of those that a mesh axis runs over, the one named last changes fastest.
Arguments:
- hidden_in: bfloat16 [16384, 1024], P(('row', 'col')), may hold values from -7.2 to 7.2
- out_cotangent: bfloat16 [16384, 1024], P(('row', 'col')), may hold values from -6 to 6
- query_weight: bfloat16 [1024, 1024], P(('row', 'col')), may hold values from -0.046875 to 0.046875
- key_weight: bfloat16 [1024, 1024], P(('row', 'col')), may hold values from -0.1875 to 0.1875
- value_weight: bfloat16 [1024, 1024], P(('row', 'col')), may hold values from -0.1875 to 0.1875
- output_weight: bfloat16 [1024, 1024], P(('row', 'col')), may hold values from -0.75 to 0.75
- attn_gain: bfloat16 [1024], P(('row', 'col')), may hold values from 0.5 to 1.5
- relative_table: bfloat16 [512], P(('row', 'col')), may hold values from -3.1875 to 3.1875
- horiz_table: bfloat16 [512], P(('row', 'col')), may hold values from -3.1875 to 3.1875
- vert_table: bfloat16 [512], P(('row', 'col')), may hold values from -3.1875 to 3.1875
- ffn_gain: bfloat16 [1024], P(('row', 'col')), may hold values from 0.5 to 1.5
- gate_weight: bfloat16 [1024, 2816], P(('row', 'col')), may hold values from -0.1875 to 0.1875
- up_weight: bfloat16 [1024, 2816], P(('row', 'col')), may hold values from -0.1875 to 0.1875
- down_weight: bfloat16 [2816, 1024], P(('row', 'col')), may hold values from -0.109375 to 0.109375
- key_keep: int32 [16384], replicated, may hold values from 0 to 1, as said below
- halo_rows: int32 [32, 4, 128], replicated, may hold values from 0 to 511, as said below
- relative_bucket: int32 [16384, 1024], P(('row', 'col')), may hold values from 0 to 31
- horiz_bucket: int32 [16384, 1024], P(('row', 'col')), may hold values from 0 to 31
- vert_bucket: int32 [16384, 1024], P(('row', 'col')), may hold values from 0 to 31
Outputs:
- layer_out: bfloat16 [16384, 1024], P(('row', 'col'))
- input_grad: bfloat16 [16384, 1024], P(('row', 'col'))
- query_grad: float32 [1024, 1024], P(('row', 'col'))
- key_grad: float32 [1024, 1024], P(('row', 'col'))
- value_grad: float32 [1024, 1024], P(('row', 'col'))
- output_grad: float32 [1024, 1024], P(('row', 'col'))
- attn_gain_grad: float32 [1024], P(('row', 'col'))
- relative_grad: float32 [512], P(('row', 'col'))
- horiz_grad: float32 [512], P(('row', 'col'))
- vert_grad: float32 [512], P(('row', 'col'))
- ffn_gain_grad: float32 [1024], P(('row', 'col'))
- gate_grad: float32 [1024, 2816], P(('row', 'col'))
- up_grad: float32 [1024, 2816], P(('row', 'col'))
- down_grad: float32 [2816, 1024], P(('row', 'col'))
- residual_rms: float32 [3], replicated
Inputs may be any that keep to these rules, and one draw needn't show every extreme that they name: `key_keep`: the first token of every region is kept; about a quarter of the other tokens are kept. `halo_rows`: each list holds 128 distinct rows of its region, counted from the region's first row; direction 0 is lent to the region above, 1 below, 2 to the left, 3 to the right.
All inputs are finite; a program needn't handle non-finite values.
Results may differ from a plain program's by a relative error of at most 0.015.
The roundings to bfloat16 on the way count: a program that leaves them out, or rounds other values in their place, can miss the bound.
Values may be sent and summed in bfloat16 or wider, within the bound.
No kernel may reach another device: no remote copies, remote signals or barrier semaphores. Data moves between devices by JAX's collectives and lax.ppermute only.
A program may use at most 320 MiB of HBM per device.

v0:
```python
import jax
import jax.numpy as jnp
from jax import lax
from jax.sharding import PartitionSpec as P

D = 1024
HEADS = 16
HEAD_DIM = 64
BUCKETS = 32


EPS = 1e-06
masked_score = -1e30
piece_rows = 64


def extended(block, sides, width):
    for axis, dim in sides:
        count = lax.axis_size(axis)
        forward = [(i, i + 1) for i in range(count - 1)]
        backward = [(target, source) for source, target in forward]
        low = lax.ppermute(
            lax.slice_in_dim(block, block.shape[dim] - width, None, axis=dim), axis, forward
        )
        high = lax.ppermute(lax.slice_in_dim(block, 0, width, axis=dim), axis, backward)
        block = jnp.concatenate([low, block, high], axis=dim)
    return block


def norm_rows(values, gain_row):
    return values * lax.rsqrt(jnp.mean(values * values, -1, keepdims=True) + EPS) * gain_row


def bucket_onehot(rel_rows, hor_rows, ver_rows):
    bucket_ids = jnp.arange(BUCKETS, dtype=jnp.int32)
    return jnp.concatenate(
        [
            rel_rows[:, :, None] == bucket_ids,
            hor_rows[:, :, None] == bucket_ids,
            ver_rows[:, :, None] == bucket_ids,
        ],
        -1,
    ).astype(jnp.bfloat16)


def layout_bias(rel_rows, hor_rows, ver_rows, table_all):
    row_total = rel_rows.shape[0]
    step_rows = min(piece_rows, row_total)
    pieces = []
    for offset in range(0, row_total, step_rows):
        onehot = bucket_onehot(
            rel_rows[offset : offset + step_rows],
            hor_rows[offset : offset + step_rows],
            ver_rows[offset : offset + step_rows],
        )
        pieces.append(
            jnp.einsum("qkb,bh->hqk", onehot, table_all, preferred_element_type=jnp.float32)
        )
    return jnp.concatenate(pieces, 1)


def layout_grad(rel_rows, hor_rows, ver_rows, grad_scores):
    row_total = rel_rows.shape[0]
    step_rows = min(piece_rows, row_total)
    table_sum = jnp.zeros((3 * BUCKETS, HEADS), jnp.float32)
    for offset in range(0, row_total, step_rows):
        onehot = bucket_onehot(
            rel_rows[offset : offset + step_rows],
            hor_rows[offset : offset + step_rows],
            ver_rows[offset : offset + step_rows],
        )
        table_sum = table_sum + jnp.einsum(
            "qkb,hqk->bh",
            onehot,
            grad_scores[:, offset : offset + step_rows],
            preferred_element_type=jnp.float32,
        )
    return table_sum


def block_scores(query_block, key_heads, rel_rows, hor_rows, ver_rows, key_mask, table_all):
    scores = jnp.einsum("qhd,khd->hqk", query_block, key_heads, preferred_element_type=jnp.float32)
    scores = scores + layout_bias(rel_rows, hor_rows, ver_rows, table_all)
    return jnp.where(key_mask[None, None, :] > 0, scores, masked_score)


def gated(gate_val, up_val):
    return jax.nn.gelu(gate_val, approximate=True) * up_val


def on_device(
    hidden_in,
    out_cotangent,
    query_weight,
    key_weight,
    value_weight,
    output_weight,
    attn_gain,
    relative_table,
    horiz_table,
    vert_table,
    ffn_gain,
    gate_weight,
    up_weight,
    down_weight,
    key_keep,
    halo_rows,
    relative_bucket,
    horiz_bucket,
    vert_bucket,
):
    tokens = hidden_in.shape[0]
    all_parts = (
        lax.all_gather(query_weight, ("row", "col"), axis=0, tiled=True),
        lax.all_gather(key_weight, ("row", "col"), axis=0, tiled=True),
        lax.all_gather(value_weight, ("row", "col"), axis=0, tiled=True),
        lax.all_gather(output_weight, ("row", "col"), axis=0, tiled=True),
        lax.all_gather(attn_gain, ("row", "col"), axis=0, tiled=True),
        lax.all_gather(relative_table, ("row", "col"), axis=0, tiled=True),
        lax.all_gather(horiz_table, ("row", "col"), axis=0, tiled=True),
        lax.all_gather(vert_table, ("row", "col"), axis=0, tiled=True),
        lax.all_gather(ffn_gain, ("row", "col"), axis=0, tiled=True),
        lax.all_gather(gate_weight, ("row", "col"), axis=0, tiled=True),
        lax.all_gather(up_weight, ("row", "col"), axis=0, tiled=True),
        lax.all_gather(down_weight, ("row", "col"), axis=0, tiled=True),
    )
    attn_parts = all_parts[:8]
    ffn_parts = all_parts[8:]
    w_query, w_key, w_value, w_output, gain_attn, table_rel, table_hor, table_ver = attn_parts
    table_all = jnp.concatenate(
        [
            table_rel.reshape(BUCKETS, HEADS),
            table_hor.reshape(BUCKETS, HEADS),
            table_ver.reshape(BUCKETS, HEADS),
        ],
        0,
    )
    gain_one = gain_attn.astype(jnp.float32)
    x_input = hidden_in.astype(jnp.float32)
    normed_one = norm_rows(x_input, gain_one).astype(jnp.bfloat16)
    queries = jnp.dot(normed_one, w_query, preferred_element_type=jnp.float32).astype(jnp.bfloat16)
    key_rows = jnp.dot(normed_one, w_key, preferred_element_type=jnp.float32).astype(jnp.bfloat16)
    value_rows = jnp.dot(normed_one, w_value, preferred_element_type=jnp.float32).astype(
        jnp.bfloat16
    )
    pair_rows = jnp.concatenate([key_rows, value_rows], 1)
    row_index = lax.axis_index("row")
    col_index = lax.axis_index("col")
    row_count = lax.axis_size("row")
    col_count = lax.axis_size("col")
    region = row_index * col_count + col_index
    own_lists = lax.dynamic_index_in_dim(halo_rows, region, 0, keepdims=False)
    rim_rows = pair_rows[own_lists]
    row_padded = extended(rim_rows[0:2], (("row", 0),), 1)
    col_padded = extended(rim_rows[2:4], (("col", 0),), 1)
    pair_all = jnp.concatenate(
        [pair_rows, row_padded[0], row_padded[3], col_padded[0], col_padded[3]], 0
    )
    key_heads = pair_all[:, :D].reshape(-1, HEADS, HEAD_DIM)
    value_heads = pair_all[:, D:].reshape(-1, HEADS, HEAD_DIM)
    neighbours = jnp.stack([region - col_count, region + col_count, region - 1, region + 1])
    present = jnp.stack(
        [row_index > 0, row_index < row_count - 1, col_index > 0, col_index < col_count - 1]
    ).astype(jnp.int32)
    list_ids = jnp.array([1, 0, 3, 2], dtype=jnp.int32)
    clipped = jnp.clip(neighbours, 0, row_count * col_count - 1)
    their_lists = halo_rows[clipped, list_ids]
    halo_keep = key_keep[clipped[:, None] * tokens + their_lists] * present[:, None]
    own_keep = lax.dynamic_slice_in_dim(key_keep, region * tokens, tokens)
    key_mask = jnp.concatenate([own_keep, halo_keep.reshape(-1)])
    block_rows = min(512, tokens)
    num_blocks = tokens // block_rows
    query_blocks = queries.reshape(num_blocks, block_rows, HEADS, HEAD_DIM)
    rel_blocks = relative_bucket.reshape(num_blocks, block_rows, -1)
    hor_blocks = horiz_bucket.reshape(num_blocks, block_rows, -1)
    ver_blocks = vert_bucket.reshape(num_blocks, block_rows, -1)

    def forward_block(pieces):
        query_block, rel_rows, hor_rows, ver_rows = pieces
        scores = block_scores(
            query_block, key_heads, rel_rows, hor_rows, ver_rows, key_mask, table_all
        )
        row_max = jnp.max(scores, -1, keepdims=True)
        exp_scores = jnp.exp(scores - row_max)
        exp_total = jnp.sum(exp_scores, -1, keepdims=True)
        attn_probs = (exp_scores / exp_total).astype(jnp.bfloat16)
        head_mix = jnp.einsum(
            "hqk,khd->qhd", attn_probs, value_heads, preferred_element_type=jnp.float32
        )
        return (head_mix, row_max + jnp.log(exp_total))

    head_mix, log_total = lax.map(forward_block, (query_blocks, rel_blocks, hor_blocks, ver_blocks))
    attended = head_mix.reshape(tokens, D).astype(jnp.bfloat16)
    attn_branch = jnp.dot(attended, w_output, preferred_element_type=jnp.float32)
    x_middle = x_input + attn_branch
    gain_ffn, w_gate, w_up, w_down = ffn_parts
    gain_two = gain_ffn.astype(jnp.float32)
    normed_two = norm_rows(x_middle, gain_two).astype(jnp.bfloat16)
    gate_pre = jnp.dot(normed_two, w_gate, preferred_element_type=jnp.float32)
    up_pre = jnp.dot(normed_two, w_up, preferred_element_type=jnp.float32)
    activated = gated(gate_pre, up_pre).astype(jnp.bfloat16)
    ffn_branch = jnp.dot(activated, w_down, preferred_element_type=jnp.float32)
    x_final = x_middle + ffn_branch
    layer_out = x_final.astype(jnp.bfloat16)
    keep_float = own_keep.astype(jnp.float32)
    stat_sums = lax.psum(
        (
            jnp.sum(keep_float * jnp.sum(x_input * x_input, -1)),
            jnp.sum(keep_float * jnp.sum(x_middle * x_middle, -1)),
            jnp.sum(keep_float * jnp.sum(x_final * x_final, -1)),
            jnp.sum(keep_float),
        ),
        ("row", "col"),
    )
    residual_rms = jnp.sqrt(
        jnp.stack([stat_sums[0], stat_sums[1], stat_sums[2]]) / (stat_sums[3] * D)
    )
    down_part = jnp.einsum(
        "tf,td->fd", activated, out_cotangent, preferred_element_type=jnp.float32
    )
    grad_act = jnp.einsum("td,fd->tf", out_cotangent, w_down, preferred_element_type=jnp.float32)
    gated_out, gated_pull = jax.vjp(gated, gate_pre, up_pre)
    grad_gate_f, grad_up_f = gated_pull(grad_act)
    grad_gate = grad_gate_f.astype(jnp.bfloat16)
    grad_up = grad_up_f.astype(jnp.bfloat16)
    gate_part = jnp.einsum("td,tf->df", normed_two, grad_gate, preferred_element_type=jnp.float32)
    up_part = jnp.einsum("td,tf->df", normed_two, grad_up, preferred_element_type=jnp.float32)
    grad_normed_two = jnp.einsum(
        "tf,df->td", grad_gate, w_gate, preferred_element_type=jnp.float32
    ) + jnp.einsum("tf,df->td", grad_up, w_up, preferred_element_type=jnp.float32)
    norm_out, second_pull = jax.vjp(norm_rows, x_middle, gain_two)
    grad_middle_local, ffn_gain_part = second_pull(grad_normed_two)
    grad_middle = out_cotangent.astype(jnp.float32) + grad_middle_local
    grad_attn = grad_middle.astype(jnp.bfloat16)
    output_part = jnp.einsum("td,te->de", attended, grad_attn, preferred_element_type=jnp.float32)
    grad_attended = jnp.einsum(
        "te,de->td", grad_attn, w_output, preferred_element_type=jnp.float32
    ).astype(jnp.bfloat16)
    grad_blocks = grad_attended.reshape(num_blocks, block_rows, HEADS, HEAD_DIM)

    def backward_block(carry, pieces):
        grad_key_sum, grad_value_sum, grad_table = carry
        query_block, grad_block, lse_block, rel_rows, hor_rows, ver_rows = pieces
        scores = block_scores(
            query_block, key_heads, rel_rows, hor_rows, ver_rows, key_mask, table_all
        )
        attn_probs = jnp.exp(scores - lse_block)
        grad_probs = jnp.einsum(
            "qhd,khd->hqk", grad_block, value_heads, preferred_element_type=jnp.float32
        )
        row_inner = jnp.sum(attn_probs * grad_probs, -1, keepdims=True)
        grad_scores = (attn_probs * (grad_probs - row_inner)).astype(jnp.bfloat16)
        grad_query = jnp.einsum(
            "hqk,khd->qhd", grad_scores, key_heads, preferred_element_type=jnp.float32
        )
        grad_key_sum = grad_key_sum + jnp.einsum(
            "hqk,qhd->khd", grad_scores, query_block, preferred_element_type=jnp.float32
        )
        grad_value_sum = grad_value_sum + jnp.einsum(
            "hqk,qhd->khd",
            attn_probs.astype(jnp.bfloat16),
            grad_block,
            preferred_element_type=jnp.float32,
        )
        grad_table = grad_table + layout_grad(rel_rows, hor_rows, ver_rows, grad_scores)
        return ((grad_key_sum, grad_value_sum, grad_table), grad_query)

    key_total = pair_all.shape[0]
    start_carry = (
        jnp.zeros((key_total, HEADS, HEAD_DIM), jnp.float32),
        jnp.zeros((key_total, HEADS, HEAD_DIM), jnp.float32),
        jnp.zeros((3 * BUCKETS, HEADS), jnp.float32),
    )
    (grad_key_sum, grad_value_sum, grad_table), grad_query = lax.scan(
        backward_block,
        start_carry,
        (query_blocks, grad_blocks, log_total, rel_blocks, hor_blocks, ver_blocks),
    )
    grad_pairs = jnp.concatenate(
        [grad_key_sum.reshape(key_total, D), grad_value_sum.reshape(key_total, D)], 1
    )
    halo_grads = grad_pairs[tokens:].reshape(4, -1, 2 * D)
    row_back = extended(halo_grads[0:2].astype(jnp.bfloat16), (("row", 0),), 1).astype(jnp.float32)
    col_back = extended(halo_grads[2:4].astype(jnp.bfloat16), (("col", 0),), 1).astype(jnp.float32)
    returned = jnp.stack([row_back[0], row_back[3], col_back[0], col_back[3]])
    own_grads = grad_pairs[:tokens].at[own_lists.reshape(-1)].add(returned.reshape(-1, 2 * D))
    grad_key_rows = own_grads[:, :D].astype(jnp.bfloat16)
    grad_value_rows = own_grads[:, D:].astype(jnp.bfloat16)
    grad_query_rows = grad_query.reshape(tokens, D).astype(jnp.bfloat16)
    query_part = jnp.einsum(
        "td,te->de", normed_one, grad_query_rows, preferred_element_type=jnp.float32
    )
    key_part = jnp.einsum(
        "td,te->de", normed_one, grad_key_rows, preferred_element_type=jnp.float32
    )
    value_part = jnp.einsum(
        "td,te->de", normed_one, grad_value_rows, preferred_element_type=jnp.float32
    )
    grad_normed_one = (
        jnp.einsum("te,de->td", grad_query_rows, w_query, preferred_element_type=jnp.float32)
        + jnp.einsum("te,de->td", grad_key_rows, w_key, preferred_element_type=jnp.float32)
        + jnp.einsum("te,de->td", grad_value_rows, w_value, preferred_element_type=jnp.float32)
    )
    first_out, first_pull = jax.vjp(norm_rows, x_input, gain_one)
    grad_input_local, attn_gain_part = first_pull(grad_normed_one)
    input_grad = (grad_middle + grad_input_local).astype(jnp.bfloat16)
    rel_part = grad_table[0:BUCKETS].reshape(-1)
    hor_part = grad_table[BUCKETS : 2 * BUCKETS].reshape(-1)
    ver_part = grad_table[2 * BUCKETS : 3 * BUCKETS].reshape(-1)
    grad_shards = (
        lax.psum_scatter(query_part, ("row", "col"), scatter_dimension=0, tiled=True),
        lax.psum_scatter(key_part, ("row", "col"), scatter_dimension=0, tiled=True),
        lax.psum_scatter(value_part, ("row", "col"), scatter_dimension=0, tiled=True),
        lax.psum_scatter(output_part, ("row", "col"), scatter_dimension=0, tiled=True),
        lax.psum_scatter(attn_gain_part, ("row", "col"), scatter_dimension=0, tiled=True),
        lax.psum_scatter(rel_part, ("row", "col"), scatter_dimension=0, tiled=True),
        lax.psum_scatter(hor_part, ("row", "col"), scatter_dimension=0, tiled=True),
        lax.psum_scatter(ver_part, ("row", "col"), scatter_dimension=0, tiled=True),
        lax.psum_scatter(ffn_gain_part, ("row", "col"), scatter_dimension=0, tiled=True),
        lax.psum_scatter(gate_part, ("row", "col"), scatter_dimension=0, tiled=True),
        lax.psum_scatter(up_part, ("row", "col"), scatter_dimension=0, tiled=True),
        lax.psum_scatter(down_part, ("row", "col"), scatter_dimension=0, tiled=True),
    )
    return (
        layer_out,
        input_grad,
        grad_shards[0],
        grad_shards[1],
        grad_shards[2],
        grad_shards[3],
        grad_shards[4],
        grad_shards[5],
        grad_shards[6],
        grad_shards[7],
        grad_shards[8],
        grad_shards[9],
        grad_shards[10],
        grad_shards[11],
        residual_rms,
    )


def solution(mesh):
    placed = (
        P(("row", "col"), None),
        P(("row", "col"), None),
        P(("row", "col"), None),
        P(("row", "col"), None),
        P(("row", "col"), None),
        P(("row", "col"), None),
        P(("row", "col")),
        P(("row", "col")),
        P(("row", "col")),
        P(("row", "col")),
        P(("row", "col")),
        P(("row", "col"), None),
        P(("row", "col"), None),
        P(("row", "col"), None),
        P(),
        P(),
        P(("row", "col"), None),
        P(("row", "col"), None),
        P(("row", "col"), None),
    )
    return jax.shard_map(
        on_device,
        mesh=mesh,
        in_specs=placed,
        out_specs=(
            P(("row", "col"), None),
            P(("row", "col"), None),
            P(("row", "col"), None),
            P(("row", "col"), None),
            P(("row", "col"), None),
            P(("row", "col"), None),
            P(("row", "col")),
            P(("row", "col")),
            P(("row", "col")),
            P(("row", "col")),
            P(("row", "col")),
            P(("row", "col"), None),
            P(("row", "col"), None),
            P(("row", "col"), None),
            P(),
        ),
        check_vma=False,
    )
```

profile of v0, /device:TPU:0, one launch (start us, length us, event | category | flops | bytes accessed | tf_op | source)
XLA Modules:
  0.0 1901.5 jit_solution(14135164211824539317)
XLA Ops:
  16.2 42.1 %all-reduce.11 = (bf16[1024]{0:T(1024)(128)(2,1)S(1)}, bf16[512]{0:T(512)(128)(2,1)S(1)}, bf16[512]{0:T(512)(128)(2,1)S(1)}, bf16[512]{0:T(512)(128)(2,1)S(1)}, bf16[1024]{0:T(1024)(128)(2,1)S(1)}) all-reduce(bf16[1024]{0:T(1024)(128)(2,1)S(1)} %dynamic-update-slice, ...), channel_id=1, replica_groups=mesh['row'=8,'col'=4] {'row','col'}, use_global_device_ids=true, to_apply=%add | all-reduce | flops 3584 | bytes 14336
  76.9 10.0 pad_add_fusion
  94.2 9.9 pad_add_fusion.1
  117.4 9.9 pad_add_fusion.2
  131.9 9.9 pad_add_fusion.3
  155.1 9.9 pad_add_fusion.4
  169.5 9.9 pad_add_fusion.5
  192.5 9.9 pad_add_fusion.6
  206.9 9.9 pad_add_fusion.7
  224.3 6.7 copy_dynamic-update-slice_fusion.6
  244.1 4.8 copy_dynamic-update-slice_fusion.2
  278.7 5.1 collective-permute-start.2
  296.8 19.8 %collective-permute-done.3 = bf16[1,128,2048]{2,1,0:T(8,128)(2,1)S(1)} collective-permute-done((bf16[1,128,2048]{2,1,0:T(8,128)(2,1)}, bf16[1,128,2048]{2,1,0:T(8,128)(2,1)S(1)}, u32[]{:S(2)}, u32[]{:S(2)}) %collective-permute-start.3) | collective-permute-done | bytes 524320 | tf_op jit(solution)/shard_map/ppermute | solution.py:25
  327.0 24.3 %fusion.123 = (f32[16,512]{1,0:T(8,128)S(1)}, f32[16,512,1024]{2,1,0:T(8,128)}) fusion(f32[16,512,1024]{2,1,0:T(8,128)} %copy_dynamic-update-slice_fusion, bf16[512,16,64]{0,2,1:T(8,128)(2,1)} %bitcast.189, bf16[1024,16,64]{0,2,1:T(8,128)(2,1)S(1)} %bitcast.184, pred[1024]{0:T(1024)(128)(4,1)S(1)} %add_compare_fusion), kind=kOutput, calls=%fused_computation.209 | convolution fusion | flops 1098899456 | bytes 70288384 | tf_op jit(solution)/shard_map/while/body/eval_jaxpr/qhd,khd->hqk/dot_general | solution.py:82
  351.3 14.5 fusion
  365.8 14.4 fusion.40
  384.9 8.6 fusion.132
  393.5 8.6 fusion.133
  402.1 60.5 %all-gather.20.cloned.1.call-done = bf16[2816,1024]{1,0:T(8,128)(2,1)} async-done(((bf16[88,1024]{1,0:T(8,128)(2,1)}), bf16[2816,1024]{1,0:T(8,128)(2,1)}) %all-gather.20.cloned.1.call-update) | async-done | bytes 5767184 | tf_op jit(solution)/shard_map/all_gather | solution.py:125
  462.6 13.3 multiply_convert_fusion.1
  475.8 7.6 fusion.134
  494.1 24.0 %multiply_reduce_fusion = (f32[16,512]{1,0:T(8,128)S(1)}, f32[16,512,1024]{2,1,0:T(8,128)}) fusion(f32[16,512,1024]{2,1,0:T(8,128)} %get-tuple-element.177, f32[16,512]{1,0:T(8,128)S(1)} %log_add_fusion, bf16[512,16,64]{0,2,1:T(8,128)(2,1)} %bitcast.193, bf16[1024,16,64]{0,2,1:T(8,128)(2,1)S(1)} %bitcast.192), kind=kOutput, calls=%fused_computation.5 | convolution fusion | flops 1098899456 | bytes 70320128 | tf_op jit(solution)/shard_map/while/body/eval_jaxpr/qhd,khd->hqk/dot_general | solution.py:248
  518.1 28.3 %multiply_convert_fusion = bf16[16,512,1024]{2,1,0:T(8,128)(2,1)} fusion(f32[16,512,1024]{2,1,0:T(8,128)} %get-tuple-element.183, f32[16,512,1024]{2,1,0:T(8,128)} %get-tuple-element.177, f32[16,512]{1,0:T(8,128)S(1)} %get-tuple-element.182, f32[16,512]{1,0:T(8,128)S(1)} %log_add_fusion), kind=kLoop, calls=%fused_computation.4 | loop fusion | flops 33554432 | bytes 83951616 | tf_op jit(solution)/shard_map/while/body/eval_jaxpr/convert_element_type | solution.py:252
  546.5 11.9 convolution_convert_fusion
  570.4 10.8 fusion.136
  581.1 5.6 copy.106
  586.8 15.4 fusion.2
  602.2 5.4 copy.107
  625.3 13.0 collective-permute-done.7
  642.6 13.0 scatter_fusion
  666.2 7.7 fusion.137
  674.0 7.7 fusion.138
  683.0 7.8 fusion.139
  690.9 10.6 fusion.116
  701.5 6.2 fusion.83
  712.2 6.4 fusion.77
  718.6 6.6 fusion.74
  725.3 6.1 fusion.71
  731.4 6.1 fusion.68
  737.6 6.4 fusion.65
  751.9 7.0 multiply_reduce_fusion.1
  765.2 63.1 %all-reduce.10 = (f32[1024]{0:T(1024)S(1)}, f32[512]{0:T(512)S(1)}, f32[512]{0:T(512)S(1)}, f32[512]{0:T(512)S(1)}, f32[1024]{0:T(1024)S(1)}, /*index=5*/f32[1]{0:T(128)}, f32[1]{0:T(128)}, f32[1]{0:T(128)}, f32[]{:T(128)}) all-reduce(f32[1024]{0:T(1024)S(1)} %get-tuple-element.80, ...), channel_id=6, replica_groups=mesh['row'=8,'col'=4] {'row','col'}, use_global_device_ids=true, to_apply=%region_13.14.clone | all-reduce | flops 3588 | bytes 28704
  837.4 17.8 reduce-scatter.14.cloned.1.call-done
  855.2 142.2 %reduce-scatter.10.cloned.1.call-done = f32[32,1024]{1,0:T(8,128)} async-done(((f32[1024,1024]{1,0:T(8,128)}), f32[32,1024]{1,0:T(8,128)}) %reduce-scatter.10.cloned.1.call-update) | async-done | bytes 131088 | tf_op jit(solution)/shard_map/reduce_scatter | solution.py:312
  997.4 142.9 %reduce-scatter.12.cloned.1.call-done = f32[32,1024]{1,0:T(8,128)} async-done(((f32[1024,1024]{1,0:T(8,128)}), f32[32,1024]{1,0:T(8,128)}) %reduce-scatter.12.cloned.1.call-update) | async-done | bytes 131088 | tf_op jit(solution)/shard_map/reduce_scatter | solution.py:313
  1140.2 249.2 %reduce-scatter.16.cloned.1.call-done = f32[32,2816]{1,0:T(8,128)} async-done(((f32[1024,2816]{1,0:T(8,128)}), f32[32,2816]{1,0:T(8,128)}) %reduce-scatter.16.cloned.1.call-update) | async-done | bytes 360464 | tf_op jit(solution)/shard_map/reduce_scatter | solution.py:320
  1389.4 252.7 %reduce-scatter.18.cloned.1.call-done = f32[32,2816]{1,0:T(8,128)} async-done(((f32[1024,2816]{1,0:T(8,128)}), f32[32,2816]{1,0:T(8,128)}) %reduce-scatter.18.cloned.1.call-update) | async-done | bytes 360464 | tf_op jit(solution)/shard_map/reduce_scatter | solution.py:321
  1642.1 252.6 %reduce-scatter.20.cloned.1.call-done = f32[88,1024]{1,0:T(8,128)} async-done(((f32[2816,1024]{1,0:T(8,128)}), f32[88,1024]{1,0:T(8,128)}) %reduce-scatter.20.cloned.1.call-update) | async-done | bytes 360464 | tf_op jit(solution)/shard_map/reduce_scatter | solution.py:322
  (320 shorter events, 249.7 us)
Async XLA Ops:
  7.2 59.2 %copy-start.34 = (s32[512,1024]{1,0:T(8,128)S(1)}, s32[512,1024]{1,0:T(8,128)}, u32[]{:S(2)}) copy-start(s32[512,1024]{1,0:T(8,128)} %param.37) | copy-start | bytes 6291460
  7.2 253.7 %all-gather.10.cloned.1.call-start = ((), (), s32[]{:S(2)}) async-start(), calls=%async_computation.8 | async-start | bytes 2162688 | tf_op jit(solution)/shard_map/all_gather | solution.py:116
  7.9 256.8 %all-gather.8.cloned.1.call-start = ((), (), s32[]{:S(2)}) async-start(), calls=%async_computation.7 | async-start | bytes 2162688 | tf_op jit(solution)/shard_map/all_gather | solution.py:115
  8.7 276.4 %all-gather.12.cloned.1.call-start = ((), (), s32[]{:S(2)}) async-start(), calls=%async_computation.9 | async-start | bytes 2162688 | tf_op jit(solution)/shard_map/all_gather | solution.py:114
  9.4 370.8 %all-gather.14.cloned.1.call-start = ((), (), s32[]{:S(2)}) async-start(), calls=%async_computation.10 | async-start | bytes 2162688 | tf_op jit(solution)/shard_map/all_gather | solution.py:117
  10.0 374.9 %all-gather.16.cloned.1.call-start = ((), (), s32[]{:S(2)}) async-start(), calls=%async_computation.11 | async-start | bytes 5947392 | tf_op jit(solution)/shard_map/all_gather | solution.py:123
  10.6 383.0 %all-gather.18.cloned.1.call-start = ((), (), s32[]{:S(2)}) async-start(), calls=%async_computation.12 | async-start | bytes 5947392 | tf_op jit(solution)/shard_map/all_gather | solution.py:124
  11.1 451.4 %all-gather.20.cloned.1.call-start = ((), (), s32[]{:S(2)}) async-start(), calls=%async_computation.13 | async-start | bytes 5947392 | tf_op jit(solution)/shard_map/all_gather | solution.py:125
  11.9 825.5 %reduce-scatter.8.cloned.1.call-start = ((), (), s32[]{:S(2)}) async-start(), calls=%async_computation.14 | async-start | bytes 4325376 | tf_op jit(solution)/shard_map/reduce_scatter | solution.py:311
  58.3 226.8 %copy-start.50 = (f32[1024]{0:T(1024)}, f32[1024]{0:T(1024)S(1)}, u32[]{:S(2)}) copy-start(f32[1024]{0:T(1024)S(1)} %convert_element_type.145) | copy-start | bytes 12292
  59.8 225.2 %copy-start.56 = (f32[512]{0:T(512)}, f32[512]{0:T(512)S(1)}, u32[]{:S(2)}) copy-start(f32[512]{0:T(512)S(1)} %fusion.101) | copy-start | bytes 6148
  253.3 7.6 copy-start.24
  275.9 13.6 collective-permute-start
  277.4 12.9 collective-permute-start.1
  278.7 16.2 collective-permute-start.2
  283.8 32.9 %collective-permute-start.3 = (bf16[1,128,2048]{2,1,0:T(8,128)(2,1)}, bf16[1,128,2048]{2,1,0:T(8,128)(2,1)S(1)}, u32[]{:S(2)}, u32[]{:S(2)}) collective-permute-start(bf16[1,128,2048]{2,1,0:T(8,128)(2,1)} %get-tuple-element.166), channel_id=1, source_target_pairs={{1,0},{2,1},{3,2},{5,4},{6,5},{7,6},{9,8},{10,9},{11,10},{13,12},{... | collective-permute-start | bytes 1572872 | tf_op jit(solution)/shard_map/ppermute | solution.py:25
  327.0 24.3 %copy-start.11 = (bf16[1024,1024]{0,1:T(8,128)(2,1)}, bf16[1024,1024]{0,1:T(8,128)(2,1)S(1)}, u32[]{:S(2)}) copy-start(bf16[1024,1024]{0,1:T(8,128)(2,1)S(1)} %copy.93) | copy-start | bytes 6291460
  351.3 14.5 copy-start.27
  383.5 104.0 %copy-start.52 = (f32[512]{0:T(512)}, f32[512]{0:T(512)S(1)}, u32[]{:S(2)}) copy-start(f32[512]{0:T(512)S(1)} %get-tuple-element.178) | copy-start | bytes 6148
  383.5 104.0 %copy-start.16 = (f32[512,1024]{1,0:T(8,128)}, f32[512,1024]{1,0:T(8,128)S(1)}, u32[]{:S(2)}) copy-start(f32[512,1024]{1,0:T(8,128)S(1)} %get-tuple-element.179) | copy-start | bytes 6291460
  475.8 7.6 copy-start.63
  475.8 7.6 copy-start.62
  475.8 7.6 copy-start.60
  518.1 28.4 %copy-start.12 = (bf16[1024,1024]{0,1:T(8,128)(2,1)S(1)}, bf16[1024,1024]{0,1:T(8,128)(2,1)}, u32[]{:S(2)}) copy-start(bf16[1024,1024]{0,1:T(8,128)(2,1)} %copy-done.11) | copy-start | bytes 6291460
  546.5 12.0 copy-start.51
  546.5 12.0 copy-start.57
  563.1 292.1 %reduce-scatter.14.cloned.1.call-start = ((), (), s32[]{:S(2)}) async-start(), calls=%async_computation.17 | async-start | bytes 4325376 | tf_op jit(solution)/shard_map/reduce_scatter | solution.py:314
  569.2 428.2 %reduce-scatter.10.cloned.1.call-start = ((), (), s32[]{:S(2)}) async-start(), calls=%async_computation.15 | async-start | bytes 4325376 | tf_op jit(solution)/shard_map/reduce_scatter | solution.py:312
  611.7 11.0 copy-start.9
  611.7 11.0 copy-start.10
  612.0 26.3 %collective-permute-start.7 = (bf16[1,128,2048]{2,1,0:T(8,128)(2,1)S(1)}, bf16[1,128,2048]{2,1,0:T(8,128)(2,1)S(1)}, u32[]{:S(2)}, u32[]{:S(2)}) collective-permute-start(bf16[1,128,2048]{2,1,0:T(8,128)(2,1)S(1)} %get-tuple-element.129), channel_id=1, source_target_pairs={{1,0},{2,1},{3,2},{5,4},{6,5},{7,6},{9,8},{10,9},{11,10},{13,12},{... | collective-permute-start | bytes 1572872 | tf_op jit(solution)/shard_map/ppermute | solution.py:25
  613.6 26.5 %collective-permute-start.6 = (bf16[1,128,2048]{2,1,0:T(8,128)(2,1)S(1)}, bf16[1,128,2048]{2,1,0:T(8,128)(2,1)S(1)}, u32[]{:S(2)}, u32[]{:S(2)}) collective-permute-start(bf16[1,128,2048]{2,1,0:T(8,128)(2,1)S(1)} %get-tuple-element.130), channel_id=1, source_target_pairs={{0,1},{1,2},{2,3},{4,5},{5,6},{6,7},{8,9},{9,10},{10,11},{12,13},{... | collective-permute-start | bytes 1572872 | tf_op jit(solution)/shard_map/ppermute | solution.py:22
  618.4 21.8 %collective-permute-start.5 = (bf16[1,128,2048]{2,1,0:T(8,128)(2,1)S(1)}, bf16[1,128,2048]{2,1,0:T(8,128)(2,1)S(1)}, u32[]{:S(2)}, u32[]{:S(2)}) collective-permute-start(bf16[1,128,2048]{2,1,0:T(8,128)(2,1)S(1)} %get-tuple-element.131), channel_id=1, source_target_pairs={{4,0},{8,4},{12,8},{16,12},{20,16},{24,20},{28,24},{5,1},{9,5},{13... | collective-permute-start | bytes 1572872 | tf_op jit(solution)/shard_map/ppermute | solution.py:25
  619.7 20.5 %collective-permute-start.4 = (bf16[1,128,2048]{2,1,0:T(8,128)(2,1)S(1)}, bf16[1,128,2048]{2,1,0:T(8,128)(2,1)S(1)}, u32[]{:S(2)}, u32[]{:S(2)}) collective-permute-start(bf16[1,128,2048]{2,1,0:T(8,128)(2,1)S(1)} %get-tuple-element.128), channel_id=1, source_target_pairs={{0,4},{4,8},{8,12},{12,16},{16,20},{20,24},{24,28},{1,5},{5,9},{9,... | collective-permute-start | bytes 1572872 | tf_op jit(solution)/shard_map/ppermute | solution.py:22
  661.6 478.6 %reduce-scatter.12.cloned.1.call-start = ((), (), s32[]{:S(2)}) async-start(), calls=%async_computation.16 | async-start | bytes 4325376 | tf_op jit(solution)/shard_map/reduce_scatter | solution.py:313
  665.0 724.4 %reduce-scatter.16.cloned.1.call-start = ((), (), s32[]{:S(2)}) async-start(), calls=%async_computation.18 | async-start | bytes 11894784 | tf_op jit(solution)/shard_map/reduce_scatter | solution.py:320
  674.0 968.2 %reduce-scatter.18.cloned.1.call-start = ((), (), s32[]{:S(2)}) async-start(), calls=%async_computation.19 | async-start | bytes 11894784 | tf_op jit(solution)/shard_map/reduce_scatter | solution.py:321
  681.8 1213.0 %reduce-scatter.20.cloned.1.call-start = ((), (), s32[]{:S(2)}) async-start(), calls=%async_computation.20 | async-start | bytes 11894784 | tf_op jit(solution)/shard_map/reduce_scatter | solution.py:322
  690.8 16.9 slice-start.8
  690.9 16.9 slice-start.9
  707.8 17.5 slice-start.6
  712.2 13.0 slice-start.7
  712.2 19.2 %slice-start.4 = ((s8[6291456]{0:T(1024)(128)(4,1)}), s8[4194304]{0:T(1024)(128)(4,1)S(1)}, s32[]{:S(2)}) async-start(s8[6291456]{0:T(1024)(128)(4,1)} %bitcast.178), calls=%async_computation.25 | async-start | bytes 8388608
  718.6 12.8 slice-start.5
  718.6 19.0 slice-start.2
  725.2 12.3 slice-start.3
  731.4 12.5 slice-start
  760.8 73.5 %copy-start.15 = (f32[512,1024]{1,0:T(8,128)S(1)}, f32[512,1024]{1,0:T(8,128)}, u32[]{:S(2)}) copy-start(f32[512,1024]{1,0:T(8,128)} %copy-done.13) | copy-start | bytes 6291460
  (49 other events, 190.1 us)
Sparse Core Ops, SparseCore 0:
  10.9 59.0 all-gather.9
  72.9 55.4 all-gather.7
  131.2 55.2 all-gather.11
  189.2 55.2 all-gather.13
  247.2 77.4 all-gather.15
  327.4 65.9 all-gather.17
  396.3 66.2 all-gather.19
  563.2 149.8 reduce-scatter.7
  716.0 139.1 reduce-scatter.13
  857.9 139.4 reduce-scatter.9
  1000.3 139.9 reduce-scatter.11
  1143.0 246.3 reduce-scatter.15
  1392.3 249.7 reduce-scatter.17
  1644.9 249.8 reduce-scatter.19
where the time goes:
time: 1910 us; the launch traced here: 1900 us
  waiting for transfers between devices  1160 us (61%)
  matrix products  293 us (15%)
  other arithmetic  196 us (10%)
  local copies, waits for them, and re-layouts  112 us (6%)
  blocking collectives  105 us (5%)
  starting transfers between devices  20 us (1%)
    reduce_scatter x1, waiting for transfers between devices, on_device(): lax.psum_scatter(up_part, ('row', 'col'), scatter_dimension=0, tiled=True)  253 us
    reduce_scatter x1, waiting for transfers between devices, on_device(): lax.psum_scatter(down_part, ('row', 'col'), scatter_dimension=0, tiled=True)  253 us
    reduce_scatter x1, waiting for transfers between devices, on_device(): lax.psum_scatter(gate_part, ('row', 'col'), scatter_dimension=0, tiled=True)  249 us
    reduce_scatter x1, waiting for transfers between devices, on_device(): lax.psum_scatter(value_part, ('row', 'col'), scatter_dimension=0, tiled=T...  143 us
    reduce_scatter x1, waiting for transfers between devices, on_device(): lax.psum_scatter(key_part, ('row', 'col'), scatter_dimension=0, tiled=True)  142 us
    unnamed x2, blocking collectives  105 us
    concatenate x8, other arithmetic, bucket_onehot(): jnp.concatenate([rel_rows[:, :, None] == bucket_ids, hor_rows[:, :, None]...  79.2 us
    all_gather x1, waiting for transfers between devices, on_device(): lax.all_gather(down_weight, ('row', 'col'), axis=0, tiled=True)  60.5 us
  transfers between devices with their start and end apart: 22, of which 11 were waited for; matrix products, arithmetic and copies ran while one was open for 26% of the time, Pallas kernels for 0%

commit v1 on v0

v1 whole, which is shorter than its diff:
```python
import functools

import jax
import jax.numpy as jnp
from jax import lax
from jax.experimental import pallas as pl
from jax.experimental.pallas import tpu as pltpu
from jax.sharding import PartitionSpec as P

D = 1024
HEADS = 16
HEAD_DIM = 64
BUCKETS = 32
TABLES = 3

EPS = 1e-06
masked_score = -1e30
FEW = 384
COLS = 128
ROWS = 64
GROUP = 4
WIDE = GROUP * HEAD_DIM
HIST_ROWS = 16
FF_TILE = 256
VMEM_LIMIT = 56 * 1024 * 1024
BF = jnp.bfloat16
F32 = jnp.float32


def shifted(block, axis):
    count = lax.axis_size(axis)
    forward = [(i, i + 1) for i in range(count - 1)]
    backward = [(target, source) for source, target in forward]
    return (
        lax.ppermute(block[1], axis, forward),
        lax.ppermute(block[0], axis, backward),
    )


def norm_rows(values, gain_row):
    return values * lax.rsqrt(jnp.mean(values * values, -1, keepdims=True) + EPS) * gain_row


def stages_of(kind):
    row_bits = [("row", bit) for bit in range(lax.axis_size("row").bit_length() - 1)]
    col_bits = [("col", bit) for bit in range(lax.axis_size("col").bit_length() - 1)]
    if kind == 0:
        return row_bits[:1] + col_bits + row_bits[1:]
    if kind == 1:
        return row_bits[:1] + col_bits[::-1] + row_bits[1:]
    return row_bits[:2] + col_bits + row_bits[2:]


def mask_of(stage):
    axis, bit = stage
    return (lax.axis_size("col") if axis == "row" else 1) << bit


def scatter_masks(kind):
    masks = [0]
    for stage in stages_of(kind)[::-1]:
        masks = masks + [mask ^ mask_of(stage) for mask in masks]
    return tuple(masks)


def gather_masks(kind):
    masks = [0]
    for stage in stages_of(kind)[:0:-1]:
        masks = masks + [mask ^ mask_of(stage) for mask in masks]
    return tuple(masks), mask_of(("row", 0))


def exchange(values, stage):
    axis, bit = stage
    pairs = [(i, i ^ (1 << bit)) for i in range(lax.axis_size(axis))]
    return lax.ppermute(values, axis, pairs)


def after(values, *earlier):
    return lax.optimization_barrier((values, earlier))[0]


class Gather:
    def __init__(self, shard, kind, both=False):
        self.held = shard[None]
        self.stages = stages_of(kind)[::-1] if both else stages_of(kind)[:0:-1]
        self.flight = None

    def send(self):
        if self.stages:
            self.flight = exchange(self.held, self.stages.pop(0))
        return self.held

    def land(self, *done):
        if self.flight is not None:
            if done:
                self.flight = after(self.flight, *done)
            self.held = jnp.concatenate([self.held, self.flight], 0)
            self.flight = None


class Scatter:
    def __init__(self, sent, kept, kind):
        self.stages = stages_of(kind)
        self.parts = [kept]
        self.sent = sent

    def land(self, flight):
        self.parts.append(flight)
        half = flight.shape[0] // 2
        self.sent = None
        if self.stages:
            self.sent = sum(part[half : 2 * half].astype(F32) for part in self.parts).astype(BF)

    def total(self):
        return sum(part[0].astype(F32) for part in self.parts)


class Summing:
    def __init__(self, values):
        self.stages = stages_of(0)
        self.sent = values

    def land(self, flight):
        self.value = self.sent + flight
        self.sent = self.value if self.stages else None


class Rounds:
    def __init__(self):
        self.chains = []
        self.flights = []

    def land(self, *done):
        for chains, flight in self.flights:
            if done:
                flight = after(flight, *done)
            at = 0
            for chain in chains:
                width = chain.sent.shape[-1]
                chain.land(flight[..., at : at + width])
                at += width
        self.flights = []
        self.chains = [chain for chain in self.chains if chain.sent is not None]

    def send(self):
        groups = {}
        for chain in self.chains:
            alone = id(chain) if chain.sent.shape[0] > 4 else 0
            alike = (chain.stages.pop(0), chain.sent.shape[:-1], alone)
            groups.setdefault(alike, []).append(chain)
        sent = []
        for (stage, *_), chains in groups.items():
            values = [chain.sent for chain in chains]
            values = jnp.concatenate(values, -1) if len(values) > 1 else values[0]
            self.flights.append((chains, exchange(values, stage)))
            sent.append(values)
        return sent

    def turn(self, *done):
        self.land(*done)
        return self.send()


def dot_nn(left, right):
    return lax.dot_general(left, right, (((1,), (0,)), ((), ())), preferred_element_type=F32)


def dot_nt(left, right):
    return lax.dot_general(left, right, (((1,), (1,)), ((), ())), preferred_element_type=F32)


def dot_tn(left, right):
    return lax.dot_general(left, right, (((0,), (0,)), ((), ())), preferred_element_type=F32)


LANE_GATHER = lax.GatherDimensionNumbers(
    offset_dims=(),
    collapsed_slice_dims=(1,),
    start_index_map=(1,),
    operand_batching_dims=(0,),
    start_indices_batching_dims=(0,),
)


def lane_gather(rows, index):
    return lax.gather(
        rows,
        index[:, :, None],
        LANE_GATHER,
        (1, 1),
        mode=lax.GatherScatterMode.PROMISE_IN_BOUNDS,
    )


def lanes_of(group):
    if isinstance(group, int):
        return pl.ds(group * WIDE, WIDE)
    return pl.ds(pl.multiple_of(group * WIDE, WIDE), WIDE)


def held_type(height):
    return BF if height % 16 == 0 else F32


def reordered(low, high, masks, device):
    place = [0] * len(masks)
    for at, mask in enumerate(masks):
        place[mask] = at
    index = jnp.array(place, jnp.int32)[jnp.array(masks, jnp.int32) ^ device]
    both = jnp.concatenate([low, high], 0)[index]
    return both[: len(masks) // 2], both[len(masks) // 2 :]


def placed(owner, height):
    start = owner * height
    if isinstance(start, int):
        return pl.ds(start, height)
    if height % 8 == 0:
        start = pl.multiple_of(start, height & -height)
    return pl.ds(start, height)


def join_pieces(own_ref, other_ref, joined_ref, device, masks, core_mask):
    height = own_ref.shape[1]
    for p, mask in enumerate(masks):
        joined_ref[placed(device ^ mask, height), :] = own_ref[p].astype(joined_ref.dtype)
        joined_ref[placed(device ^ mask ^ core_mask, height), :] = other_ref[p].astype(
            joined_ref.dtype
        )


def part_pieces(joined_ref, sent_ref, kept_ref, device, masks, at=0):
    half, height = kept_ref.shape[:2]
    lanes = slice(at, at + joined_ref.shape[1])
    for p, mask in enumerate(masks):
        target_ref = kept_ref if p < half else sent_ref
        target_ref[p % half, :, lanes] = joined_ref[placed(device ^ mask, height), :].astype(BF)


def head_masks():
    lane = lax.broadcasted_iota(jnp.int32, (1, WIDE), 1) >> 6
    return [(lane == h).astype(F32).astype(BF) for h in range(GROUP)]


def stack_heads(block, masks):
    return jnp.concatenate([block * mask for mask in masks], 0)


def unpack_codes(codes_ref, split_ref, keys):
    code = codes_ref[:keys, :]
    split_ref[0, :keys, :] = code & 31
    split_ref[1, :keys, :] = (code >> 5) & 31
    split_ref[2, :keys, :] = code >> 10


def bias_of(split_ref, table_ref, head, keys):
    spread = [
        jnp.broadcast_to(table_ref[pl.ds(t * HEADS + head, 1), :], (keys, COLS))
        for t in range(TABLES)
    ]
    found = [lane_gather(spread[t], split_ref[t, :keys, :]) for t in range(TABLES)]
    return found[0] + found[1] + found[2]


def bias_kernel(codes_ref, table_ref, bias_ref, split_ref, *, first_head):
    unpack_codes(codes_ref, split_ref, FEW)

    @pl.loop(0, bias_ref.shape[0])
    def _(head):
        bias_ref[head] = bias_of(split_ref, table_ref, first_head + head, FEW)


def layout_bias(codes, table_lanes, first_head):
    tokens = codes.shape[1]
    return pl.pallas_call(
        functools.partial(bias_kernel, first_head=first_head),
        grid=(tokens // COLS,),
        in_specs=[
            pl.BlockSpec((FEW, COLS), lambda i: (0, i)),
            pl.BlockSpec(table_lanes.shape, lambda i: (0, 0)),
        ],
        out_specs=pl.BlockSpec((HEADS // 2, FEW, COLS), lambda i: (0, 0, i)),
        out_shape=jax.ShapeDtypeStruct((HEADS // 2, FEW, tokens), F32),
        scratch_shapes=[pltpu.VMEM((TABLES, FEW, COLS), jnp.int32)],
        compiler_params=pltpu.CompilerParams(vmem_limit_bytes=VMEM_LIMIT),
        cost_estimate=pl.CostEstimate(
            flops=16_000_000_000, bytes_accessed=7_000_000, transcendentals=0
        ),
        name="layout_bias",
    )(codes, table_lanes)


def each_group(run, groups, short):
    if short:
        for group in range(groups):
            run(group)
    else:
        lax.fori_loop(0, groups, lambda group, carry: (run(group), carry)[1], 0)


def own_blocks(turned):
    return jnp.concatenate(
        [
            turned[h * HEAD_DIM : (h + 1) * HEAD_DIM, h * COLS : (h + 1) * COLS]
            for h in range(GROUP)
        ],
        0,
    )


def attend_kernel(
    count_ref,
    normed_ref,
    picked_ref,
    wq_ref,
    wk_ref,
    wv_ref,
    wo_ref,
    codes_ref,
    table_ref,
    low_bias_ref,
    high_bias_ref,
    x_ref,
    gain_ref,
    q_ref,
    k_ref,
    v_ref,
    mixed_ref,
    lse_ref,
    prob_ref,
    mid_ref,
    normed_two_ref,
    split_ref,
    turned_ref,
    attended_ref,
):
    step = pl.program_id(0)
    few = count_ref[0] <= FEW
    total_keys = picked_ref.shape[0]

    def project(rows):
        picked = picked_ref[rows, :]
        k_ref[rows, :] = dot_nn(picked, wk_ref[...]).astype(BF)
        values = dot_nn(picked, wv_ref[...]).astype(BF)
        v_ref[rows, :] = values
        turned_ref[:, rows] = values.T

    @pl.when(step == 0)
    def _():
        q_ref[...] = dot_nn(normed_ref[...], wq_ref[...]).astype(BF)

    @pl.when(jnp.logical_and(step == 0, few))
    def _():
        project(pl.ds(0, FEW))

    @pl.when(jnp.logical_and(step == 0, jnp.logical_not(few)))
    def _():
        @pl.loop(0, total_keys // 256)
        def _(block):
            project(pl.ds(pl.multiple_of(block * 256, 256), 256))

    here = pl.ds(pl.multiple_of(step * COLS, COLS), COLS)
    masks = head_masks()

    def attend(keys, short):
        def run(group):
            lanes = lanes_of(group)
            queries = stack_heads(q_ref[here, lanes], masks)
            scores = dot_nt(k_ref[0:keys, lanes], queries)
            pieces = []
            for h in range(GROUP):
                head = group * GROUP + h
                if short:
                    half = HEADS // 2
                    bias = low_bias_ref[head] if head < half else high_bias_ref[head - half]
                else:
                    bias = bias_of(split_ref, table_ref, head, keys)
                score = scores[:, h * COLS : (h + 1) * COLS] + bias
                top = jnp.max(score, 0, keepdims=True)
                grown = jnp.exp(score - top)
                total = jnp.sum(grown, 0, keepdims=True)
                prob = grown * (1.0 / total)
                if short:
                    prob_ref[head] = prob
                lse_ref[pl.ds(head, 1), :] = top + jnp.log(total)
                pieces.append(prob.astype(BF))
            mixed = dot_nn(turned_ref[lanes, 0:keys], jnp.concatenate(pieces, 1))
            mixed_ref[lanes, here] = own_blocks(mixed).astype(BF)

        if not short:
            unpack_codes(codes_ref, split_ref, keys)
        each_group(run, HEADS // GROUP, short)

    pl.when(few)(lambda: attend(FEW, True))
    pl.when(jnp.logical_not(few))(lambda: attend(total_keys, False))

    @pl.when(step == pl.num_programs(0) - 1)
    def _():
        gain = gain_ref[0:1, :]
        attended_ref[...] = mixed_ref[...].T

        @pl.loop(0, x_ref.shape[0] // 256)
        def _(block):
            rows = pl.ds(pl.multiple_of(block * 256, 256), 256)
            middle = x_ref[rows, :].astype(F32) + dot_nn(attended_ref[rows, :], wo_ref[...])
            mid_ref[rows, :] = middle
            normed_two_ref[rows, :] = norm_rows(middle, gain).astype(BF)


def attention_forward(count, normed, picked, weights, codes, table_lanes, bias, x_block, gain_two):
    tokens = normed.shape[0]
    keys = picked.shape[0]
    full = lambda shape: pl.BlockSpec(shape, lambda i, c: (0, 0))
    weight = lambda at: pl.BlockSpec((D, D), lambda i, c: (0, at), pipeline_mode=pl.Buffered(1))
    across = lambda height: pl.BlockSpec((height, COLS), lambda i, c: (0, i))
    headed = pl.BlockSpec((HEADS, FEW, COLS), lambda i, c: (0, 0, i))
    shape = jax.ShapeDtypeStruct
    return pl.pallas_call(
        attend_kernel,
        grid_spec=pltpu.PrefetchScalarGridSpec(
            num_scalar_prefetch=1,
            grid=(tokens // COLS,),
            in_specs=[
                full((tokens, D)),
                full((keys, D)),
                weight(0),
                weight(1),
                weight(2),
                weight(3),
                across(keys),
                full(table_lanes.shape),
                pl.BlockSpec((HEADS // 2, FEW, COLS), lambda i, c: (0, 0, i)),
                pl.BlockSpec((HEADS // 2, FEW, COLS), lambda i, c: (0, 0, i)),
                full((tokens, D)),
                full((8, D)),
            ],
            out_specs=[
                full((tokens, D)),
                full((keys, D)),
                full((keys, D)),
                full((D, tokens)),
                across(HEADS),
                headed,
                full((tokens, D)),
                full((tokens, D)),
            ],
            scratch_shapes=[
                pltpu.VMEM((TABLES, keys, COLS), jnp.int32),
                pltpu.VMEM((D, keys), BF),
                pltpu.VMEM((tokens, D), BF),
            ],
        ),
        out_shape=[
            shape((tokens, D), BF),
            shape((keys, D), BF),
            shape((keys, D), BF),
            shape((D, tokens), BF),
            shape((HEADS, tokens), F32),
            shape((HEADS, FEW, tokens), F32),
            shape((tokens, D), F32),
            shape((tokens, D), BF),
        ],
        compiler_params=pltpu.CompilerParams(vmem_limit_bytes=VMEM_LIMIT),
        cost_estimate=pl.CostEstimate(
            flops=20_000_000_000, bytes_accessed=50_000_000, transcendentals=3_000_000
        ),
        name="attention_forward",
    )(count, normed, picked, weights, weights, weights, weights, codes, table_lanes, *bias, x_block, gain_two)


def ffn_kernel(
    scalar_ref,
    normed_ref,
    out_cot_ref,
    mid_ref,
    gain_ref,
    gate_own_ref,
    gate_other_ref,
    up_own_ref,
    up_other_ref,
    down_own_ref,
    down_other_ref,
    gate_sent_ref,
    gate_kept_ref,
    up_sent_ref,
    up_kept_ref,
    down_sent_ref,
    down_kept_ref,
    layer_ref,
    middle_grad_ref,
    attn_grad_ref,
    gain_grad_ref,
    stat_ref,
    turned_ref,
    branch_ref,
    back_ref,
    down_all_ref,
    gate_ref,
    up_ref,
    gate_grad_ref,
    up_grad_ref,
    down_ref,
    *,
    gather_order,
    scatter_order,
):
    step = pl.program_id(0)
    device = scalar_ref[1]
    down_device = device if down_kept_ref.shape[1] % 8 == 0 else 0

    @pl.when(step == 0)
    def _():
        turned_ref[...] = normed_ref[...].T
        join_pieces(down_own_ref, down_other_ref, down_all_ref, down_device, *gather_order[2])

    join_pieces(gate_own_ref, gate_other_ref, gate_ref, device, *gather_order[0])
    join_pieces(up_own_ref, up_other_ref, up_ref, device, *gather_order[1])
    here = pl.ds(pl.multiple_of(step * FF_TILE, FF_TILE), FF_TILE)
    down_ref[...] = down_all_ref[here, :].astype(BF)

    normed = normed_ref[...]
    gate_weight = gate_ref[...].astype(BF)
    up_weight = up_ref[...].astype(BF)
    gate = dot_nn(normed, gate_weight)
    up = dot_nn(normed, up_weight)
    grad_act = dot_nt(out_cot_ref[...], down_ref[...])
    scale = 0.7978845608028654
    square = gate * gate
    bent = jnp.tanh(scale * (gate + 0.044715 * (square * gate)))
    half = 0.5 * (1.0 + bent)
    curved = gate * half
    slope = half + 0.5 * gate * (1.0 - bent * bent) * (scale * (1.0 + 0.134145 * square))
    activated = (curved * up).astype(BF)
    grad_gate = (grad_act * up * slope).astype(BF)
    grad_up = (grad_act * curved).astype(BF)
    branch = dot_nn(activated, down_ref[...])
    back = dot_nt(grad_gate, gate_weight) + dot_nt(grad_up, up_weight)

    @pl.when(step == 0)
    def _():
        branch_ref[...] = branch
        back_ref[...] = back

    @pl.when(step > 0)
    def _():
        branch_ref[...] += branch
        back_ref[...] += back

    gate_grad_ref[...] = dot_nn(turned_ref[...], grad_gate).astype(gate_grad_ref.dtype)
    part_pieces(gate_grad_ref, gate_sent_ref, gate_kept_ref, device, scatter_order[0])
    up_grad_ref[...] = dot_nn(turned_ref[...], grad_up).astype(up_grad_ref.dtype)
    part_pieces(up_grad_ref, up_sent_ref, up_kept_ref, device, scatter_order[1])
    down_all_ref[here, :] = dot_tn(activated, out_cot_ref[...])

    @pl.when(step == pl.num_programs(0) - 1)
    def _():
        part_pieces(
            down_all_ref, down_sent_ref, down_kept_ref, down_device, scatter_order[2]
        )
        gain = gain_ref[0:1, :]
        gain_grad_ref[...] = jnp.zeros_like(gain_grad_ref)
        lane = lax.broadcasted_iota(jnp.int32, (ROWS, 128), 1)

        @pl.loop(0, mid_ref.shape[0] // ROWS)
        def _(block):
            rows = pl.ds(pl.multiple_of(block * ROWS, ROWS), ROWS)
            middle = mid_ref[rows, :]
            final = middle + branch_ref[rows, :]
            layer_ref[rows, :] = final.astype(BF)
            mid_sum = jnp.sum(middle * middle, -1, keepdims=True)
            final_sum = jnp.sum(final * final, -1, keepdims=True)
            stat_ref[rows, :] = jnp.where(lane == 0, mid_sum, final_sum)
            inverse = lax.rsqrt(mid_sum * (1.0 / D) + EPS)
            unit = middle * inverse
            grad_normed = back_ref[rows, :]
            weighted = grad_normed * gain
            inner = jnp.mean(weighted * unit, -1, keepdims=True)
            grad_middle = out_cot_ref[rows, :].astype(F32) + inverse * (weighted - unit * inner)
            middle_grad_ref[rows, :] = grad_middle
            attn_grad_ref[rows, :] = grad_middle.astype(BF)
            gain_grad_ref[0:1, :] += jnp.sum(grad_normed * unit, 0, keepdims=True)


def feed_forward(scalars, normed_two, out_cot, middle, gain_two, gate, up, down):
    tokens = normed_two.shape[0]
    ff = gate[0].shape[2]
    half, rows = gate[0].shape[:2]
    down_rows = down[0].shape[1]
    once = pl.Buffered(1)
    full = lambda shape: pl.BlockSpec(shape, lambda i, c: (0,) * len(shape), pipeline_mode=once)
    tile = pl.BlockSpec((half, rows, FF_TILE), lambda i, c: (0, 0, i))
    shape = jax.ShapeDtypeStruct
    kernel = functools.partial(
        ffn_kernel,
        gather_order=[gather_masks(kind) for kind in range(3)],
        scatter_order=[scatter_masks(kind) for kind in range(3)],
    )
    return pl.pallas_call(
        kernel,
        grid_spec=pltpu.PrefetchScalarGridSpec(
            num_scalar_prefetch=1,
            grid=(ff // FF_TILE,),
            in_specs=[
                full((tokens, D)),
                full((tokens, D)),
                full((tokens, D)),
                full((8, D)),
                tile,
                tile,
                tile,
                tile,
                full((half, down_rows, D)),
                full((half, down_rows, D)),
            ],
            out_specs=[
                tile,
                tile,
                tile,
                tile,
                full((half, down_rows, D)),
                full((half, down_rows, D)),
                full((tokens, D)),
                full((tokens, D)),
                full((tokens, D)),
                full((8, D)),
                full((tokens, 128)),
            ],
            scratch_shapes=[
                pltpu.VMEM((D, tokens), BF),
                pltpu.VMEM((tokens, D), F32),
                pltpu.VMEM((tokens, D), F32),
                pltpu.VMEM((ff, D), F32),
                pltpu.VMEM((D, FF_TILE), held_type(rows)),
                pltpu.VMEM((D, FF_TILE), held_type(rows)),
                pltpu.VMEM((D, FF_TILE), held_type(rows)),
                pltpu.VMEM((D, FF_TILE), held_type(rows)),
                pltpu.VMEM((FF_TILE, D), BF),
            ],
        ),
        out_shape=[shape((half, rows, ff), BF)] * 4
        + [shape((half, down_rows, D), BF)] * 2
        + [
            shape((tokens, D), BF),
            shape((tokens, D), F32),
            shape((tokens, D), BF),
            shape((8, D), F32),
            shape((tokens, 128), F32),
        ],
        compiler_params=pltpu.CompilerParams(vmem_limit_bytes=VMEM_LIMIT),
        cost_estimate=pl.CostEstimate(
            flops=27_000_000_000, bytes_accessed=44_000_000, transcendentals=1_500_000
        ),
        name="feed_forward",
    )(scalars, normed_two, out_cot, middle, gain_two, *gate, *up, *down)


def add_histogram(split_ref, grad_ref, hist_ref, chosen_ref, keys):
    heads = grad_ref.shape[0]
    cols = split_ref.shape[2]
    bucket = lax.broadcasted_iota(jnp.int32, (BUCKETS, cols), 0)

    @pl.loop(0, keys // HIST_ROWS)
    def _(block):
        base = pl.multiple_of(block * HIST_ROWS, HIST_ROWS)
        grads = grad_ref[:, pl.ds(base, HIST_ROWS), :]
        grads = grads.reshape(heads * HIST_ROWS, cols)
        for row in range(HIST_ROWS):
            for t in range(TABLES):
                at = (row * TABLES + t) * BUCKETS
                match = split_ref[t, pl.ds(base + row, 1), :] == bucket
                chosen_ref[at : at + BUCKETS, :] = match.astype(F32).astype(BF)
        hist_ref[...] += dot_nt(chosen_ref[...], grads)


def take_histogram(hist_ref, out_ref):
    height, width = out_ref.shape
    own = lax.broadcasted_iota(jnp.int32, (height, width), 1) & (HIST_ROWS - 1)
    total = jnp.zeros((height, width), F32)
    for row in range(HIST_ROWS):
        piece = hist_ref[row * height : (row + 1) * height, :]
        total = total + jnp.where(own == row, piece, 0.0)
    out_ref[...] = total


def backward_kernel(
    count_ref,
    attn_grad_ref,
    wo_ref,
    q_ref,
    k_ref,
    v_ref,
    lse_ref,
    prob_ref,
    codes_ref,
    table_ref,
    normed_turned_ref,
    picked_turned_ref,
    mixed_ref,
    dq_ref,
    dk_ref,
    dv_ref,
    grad_ref,
    hist_out_ref,
    sent_ref,
    kept_ref,
    back_ref,
    split_ref,
    long_grad_ref,
    turned_ref,
    dq_turned_ref,
    dk_sum_ref,
    dv_sum_ref,
    hist_ref,
    chosen_ref,
    joined_ref,
    *,
    first_head,
    scatter_order,
):
    step = pl.program_id(0)
    few = count_ref[0] <= FEW
    total_keys = k_ref.shape[0]
    heads = q_ref.shape[1] // HEAD_DIM

    @pl.when(step == 0)
    def _():
        back_ref[...] = dot_nt(attn_grad_ref[...], wo_ref[...]).astype(BF)
        dk_sum_ref[...] = jnp.zeros_like(dk_sum_ref)
        dv_sum_ref[...] = jnp.zeros_like(dv_sum_ref)
        hist_ref[...] = jnp.zeros_like(hist_ref)

    @pl.when(jnp.logical_and(step == 0, few))
    def _():
        turned_ref[:, 0:FEW] = k_ref[0:FEW, :].T

    @pl.when(jnp.logical_and(step == 0, jnp.logical_not(few)))
    def _():
        turned_ref[...] = k_ref[...].T

    here = pl.ds(pl.multiple_of(step * COLS, COLS), COLS)
    masks = head_masks()

    def turn_back(keys, short):
        def run(group):
            lanes = lanes_of(group)
            queries = stack_heads(q_ref[here, lanes], masks)
            grads = stack_heads(back_ref[here, lanes], masks)
            prob_grads = dot_nt(v_ref[0:keys, lanes], grads)
            if not short:
                scores = dot_nt(k_ref[0:keys, lanes], queries)
            score_grads = []
            probs = []
            for h in range(GROUP):
                cols = slice(h * COLS, (h + 1) * COLS)
                local = group * GROUP + h
                if short:
                    prob = prob_ref[local]
                else:
                    head = first_head + local
                    bias = bias_of(split_ref, table_ref, head, keys)
                    prob = jnp.exp(scores[:, cols] + bias - lse_ref[pl.ds(head, 1), :])
                weighted = prob * prob_grads[:, cols]
                inner = jnp.sum(weighted, 0, keepdims=True)
                score_grad = (weighted - prob * inner).astype(BF)
                if short:
                    grad_ref[local] = score_grad
                else:
                    long_grad_ref[local] = score_grad
                score_grads.append(score_grad)
                probs.append(prob.astype(BF))
            score_grads = jnp.concatenate(score_grads, 1)
            probs = jnp.concatenate(probs, 1)
            dq_turned_ref[lanes, here] = own_blocks(
                dot_nn(turned_ref[lanes, 0:keys], score_grads)
            ).astype(BF)
            dk_sum_ref[0:keys, lanes] += dot_nn(score_grads, queries)
            dv_sum_ref[0:keys, lanes] += dot_nn(probs, grads)

        if not short:
            unpack_codes(codes_ref, split_ref, keys)
        each_group(run, heads // GROUP, short)
        if not short:
            add_histogram(split_ref, long_grad_ref, hist_ref, chosen_ref, keys)

    pl.when(few)(lambda: turn_back(FEW, True))
    pl.when(jnp.logical_not(few))(lambda: turn_back(total_keys, False))

    def leave(number, gradient):
        joined_ref[...] = gradient.astype(joined_ref.dtype)
        at = number * joined_ref.shape[1]
        part_pieces(joined_ref, sent_ref, kept_ref, count_ref[1], scatter_order, at)

    def finish(keys):
        leave(1, dot_nn(picked_turned_ref[:, 0:keys], dk_ref[0:keys, :]))
        leave(2, dot_nn(picked_turned_ref[:, 0:keys], dv_ref[0:keys, :]))

    @pl.when(step == pl.num_programs(0) - 1)
    def _():
        dk_ref[...] = dk_sum_ref[...].astype(BF)
        dv_ref[...] = dv_sum_ref[...].astype(BF)
        dq_ref[...] = dq_turned_ref[...].T
        leave(0, dot_nn(normed_turned_ref[...], dq_ref[...]))
        first = first_head * HEAD_DIM
        leave(3, dot_nn(mixed_ref[...], attn_grad_ref[:, first : first + heads * HEAD_DIM]))
        take_histogram(hist_ref, hist_out_ref)
        pl.when(few)(lambda: finish(FEW))
        pl.when(jnp.logical_not(few))(lambda: finish(total_keys))


def attention_backward(
    half,
    kind,
    count,
    attn_grad,
    weights,
    queries,
    keys,
    values,
    lse,
    probs,
    codes,
    table_lanes,
    normed_turned,
    picked_turned,
    mixed,
):
    tokens = queries.shape[0]
    device_count = lax.axis_size("row") * lax.axis_size("col")
    rows = D // device_count
    key_total = keys.shape[0]
    heads = HEADS // 2
    width = heads * HEAD_DIM
    full = lambda shape: pl.BlockSpec(shape, lambda i, c: (0, 0))
    side = lambda height: pl.BlockSpec((height, width), lambda i, c: (0, half))
    across = lambda height: pl.BlockSpec((height, COLS), lambda i, c: (0, i))
    shape = jax.ShapeDtypeStruct
    hist_shape = (TABLES * BUCKETS, heads * HIST_ROWS)
    return pl.pallas_call(
        functools.partial(
            backward_kernel,
            first_head=half * heads,
            scatter_order=scatter_masks(kind),
        ),
        grid_spec=pltpu.PrefetchScalarGridSpec(
            num_scalar_prefetch=1,
            grid=(tokens // COLS,),
            in_specs=[
                full((tokens, D)),
                pl.BlockSpec((width, D), lambda i, c: (half, 3)),
                side(tokens),
                side(key_total),
                side(key_total),
                across(HEADS),
                pl.BlockSpec((heads, FEW, COLS), lambda i, c: (half, 0, i)),
                across(key_total),
                full(table_lanes.shape),
                full((D, tokens)),
                full((D, key_total)),
                full((D, tokens)),
            ],
            out_specs=[
                full((tokens, width)),
                full((key_total, width)),
                full((key_total, width)),
                pl.BlockSpec((heads, FEW, COLS), lambda i, c: (0, 0, i)),
                full(hist_shape),
            ]
            + [
                pl.BlockSpec((device_count // 2, rows, 4 * width), lambda i, c: (0, 0, 0)),
            ]
            * 2,
            scratch_shapes=[
                pltpu.VMEM((tokens, width), BF),
                pltpu.VMEM((TABLES, key_total, COLS), jnp.int32),
                pltpu.VMEM((heads, key_total, COLS), BF),
                pltpu.VMEM((width, key_total), BF),
                pltpu.VMEM((width, tokens), BF),
                pltpu.VMEM((key_total, width), F32),
                pltpu.VMEM((key_total, width), F32),
                pltpu.VMEM((HIST_ROWS * hist_shape[0], hist_shape[1]), F32),
                pltpu.VMEM((HIST_ROWS * hist_shape[0], COLS), BF),
                pltpu.VMEM((D, width), held_type(rows)),
            ],
        ),
        out_shape=[
            shape((tokens, width), BF),
            shape((key_total, width), BF),
            shape((key_total, width), BF),
            shape((heads, FEW, tokens), BF),
            shape(hist_shape, F32),
        ]
        + [shape((device_count // 2, rows, 4 * width), BF)] * 2,
        compiler_params=pltpu.CompilerParams(vmem_limit_bytes=VMEM_LIMIT),
        cost_estimate=pl.CostEstimate(
            flops=15_000_000_000, bytes_accessed=30_000_000, transcendentals=0
        ),
        name="attention_backward",
    )(
        count,
        attn_grad,
        weights,
        queries,
        keys,
        values,
        lse,
        probs,
        codes,
        table_lanes,
        normed_turned,
        picked_turned,
        mixed,
    )


def histogram_kernel(
    count_ref, codes_ref, low_ref, high_ref, out_ref, split_ref, both_ref, hist_ref, chosen_ref
):
    out_ref[...] = jnp.zeros_like(out_ref)

    @pl.when(count_ref[0] <= FEW)
    def _():
        unpack_codes(codes_ref, split_ref, FEW)
        both_ref[: HEADS // 2] = low_ref[...]
        both_ref[HEADS // 2 :] = high_ref[...]
        hist_ref[...] = jnp.zeros_like(hist_ref)
        add_histogram(split_ref, both_ref, hist_ref, chosen_ref, FEW)
        take_histogram(hist_ref, out_ref)


def table_histogram(count, codes, low, high):
    tokens = codes.shape[1]
    hist_shape = (TABLES * BUCKETS, HEADS * HIST_ROWS)
    whole = lambda shape: pl.BlockSpec(shape, lambda i, c: (0,) * len(shape))
    return pl.pallas_call(
        histogram_kernel,
        grid_spec=pltpu.PrefetchScalarGridSpec(
            num_scalar_prefetch=1,
            grid=(1,),
            in_specs=[whole((FEW, tokens)), whole(low.shape), whole(high.shape)],
            out_specs=whole(hist_shape),
            scratch_shapes=[
                pltpu.VMEM((TABLES, FEW, tokens), jnp.int32),
                pltpu.VMEM((HEADS, FEW, tokens), BF),
                pltpu.VMEM((HIST_ROWS * hist_shape[0], hist_shape[1]), F32),
                pltpu.VMEM((HIST_ROWS * hist_shape[0], tokens), BF),
            ],
        ),
        out_shape=jax.ShapeDtypeStruct(hist_shape, F32),
        compiler_params=pltpu.CompilerParams(vmem_limit_bytes=VMEM_LIMIT),
        cost_estimate=pl.CostEstimate(
            flops=20_000_000_000, bytes_accessed=8_000_000, transcendentals=0
        ),
        name="table_histogram",
    )(count, codes, low, high)


def key_gradients_kernel(
    count_ref,
    dq_low_ref,
    dq_high_ref,
    dk_low_ref,
    dk_high_ref,
    dv_low_ref,
    dv_high_ref,
    wq_ref,
    wk_ref,
    wv_ref,
    pack_ref,
    x_ref,
    picked_ref,
    lent_ref,
    own_ref,
    gain_ref,
    both_ref,
):
    tokens = x_ref.shape[0]
    half = D // 2
    few = count_ref[0] <= FEW

    def unit(rows):
        rows = rows.astype(F32)
        return rows * lax.rsqrt(jnp.mean(rows * rows, -1, keepdims=True) + EPS)

    def product(low, high, weight_ref):
        return dot_nt(low, weight_ref[:, :half]) + dot_nt(high, weight_ref[:, half:])

    gain_ref[...] = jnp.zeros_like(gain_ref)
    own_ref[...] = product(dq_low_ref[...], dq_high_ref[...], wq_ref)

    @pl.loop(0, tokens // COLS)
    def _(block):
        rows = pl.ds(pl.multiple_of(block * COLS, COLS), COLS)
        gain_ref[0:1, :] += jnp.sum(own_ref[rows, :] * unit(x_ref[rows, :]), 0, keepdims=True)

    def spread(keys, step):
        @pl.loop(0, keys // step)
        def _(block):
            rows = pl.ds(pl.multiple_of(block * step, step), step)
            grads = product(dk_low_ref[rows, :], dk_high_ref[rows, :], wk_ref)
            grads = grads + product(dv_low_ref[rows, :], dv_high_ref[rows, :], wv_ref)
            gain_ref[0:1, :] += jnp.sum(grads * unit(picked_ref[rows, :]), 0, keepdims=True)
            high = grads.astype(BF)
            both_ref[0, rows, :] = high
            both_ref[1, rows, :] = (grads - high.astype(F32)).astype(BF)

        high = both_ref[0, 0:keys, :]
        chosen = pack_ref[0:tokens, 0:keys]
        own_ref[...] += dot_nn(chosen, high) + dot_nn(chosen, both_ref[1, 0:keys, :])
        lent_ref[...] = dot_nn(pack_ref[tokens:, 0:keys], high).astype(BF)

    pl.when(few)(lambda: spread(FEW, FEW))
    pl.when(jnp.logical_not(few))(lambda: spread(pack_ref.shape[1], COLS))


def key_gradients(count, low, high, weights, pack, x_block, picked_x):
    tokens = x_block.shape[0]
    keys = pack.shape[0]
    whole = lambda shape: pl.BlockSpec(shape, lambda i, c: (0, 0))
    weight = lambda at: pl.BlockSpec((D, D), lambda i, c: (0, at))
    shape = jax.ShapeDtypeStruct
    return pl.pallas_call(
        key_gradients_kernel,
        grid_spec=pltpu.PrefetchScalarGridSpec(
            num_scalar_prefetch=1,
            grid=(1,),
            in_specs=[
                whole((tokens, D // 2)),
                whole((tokens, D // 2)),
                whole((keys, D // 2)),
                whole((keys, D // 2)),
                whole((keys, D // 2)),
                whole((keys, D // 2)),
                weight(0),
                weight(1),
                weight(2),
                whole(pack.shape),
                whole((tokens, D)),
                whole((keys, D)),
            ],
            out_specs=[whole((keys - tokens, D)), whole((tokens, D)), whole((8, D))],
            scratch_shapes=[pltpu.VMEM((2, keys, D), BF)],
        ),
        out_shape=[
            shape((keys - tokens, D), BF),
            shape((tokens, D), F32),
            shape((8, D), F32),
        ],
        compiler_params=pltpu.CompilerParams(vmem_limit_bytes=VMEM_LIMIT),
        cost_estimate=pl.CostEstimate(
            flops=9_000_000_000, bytes_accessed=18_000_000, transcendentals=0
        ),
        name="key_gradients",
    )(count, low[0], high[0], low[1], high[1], low[2], high[2], weights, weights, weights, pack, x_block, picked_x)


def input_kernel(own_ref, owner_ref, returned_ref, x_ref, gain_ref, middle_ref, out_ref):
    grads = own_ref[...] + dot_nn(owner_ref[...], returned_ref[...])
    rows = x_ref[...].astype(F32)
    inverse = lax.rsqrt(jnp.mean(rows * rows, -1, keepdims=True) + EPS)
    unit = rows * inverse
    weighted = grads * gain_ref[0:1, :]
    inner = jnp.mean(weighted * unit, -1, keepdims=True)
    out_ref[...] = (middle_ref[...] + inverse * (weighted - unit * inner)).astype(BF)


def input_gradient(own, owner, returned, x_block, gain_one, grad_middle):
    tokens = own.shape[0]
    streamed = lambda width: pl.BlockSpec((COLS, width), lambda i: (i, 0))
    whole = lambda shape: pl.BlockSpec(shape, lambda i: (0, 0))
    return pl.pallas_call(
        input_kernel,
        grid=(tokens // COLS,),
        in_specs=[
            streamed(D),
            streamed(owner.shape[1]),
            whole(returned.shape),
            streamed(D),
            whole((8, D)),
            streamed(D),
        ],
        out_specs=streamed(D),
        out_shape=jax.ShapeDtypeStruct((tokens, D), BF),
        compiler_params=pltpu.CompilerParams(vmem_limit_bytes=VMEM_LIMIT),
        cost_estimate=pl.CostEstimate(
            flops=1_000_000_000, bytes_accessed=8_000_000, transcendentals=0
        ),
        name="input_gradient",
    )(own, owner, returned, x_block, gain_one, grad_middle)


def on_device(
    hidden_in,
    out_cotangent,
    query_weight,
    key_weight,
    value_weight,
    output_weight,
    attn_gain,
    relative_table,
    horiz_table,
    vert_table,
    ffn_gain,
    gate_weight,
    up_weight,
    down_weight,
    key_keep,
    halo_rows,
    relative_bucket,
    horiz_bucket,
    vert_bucket,
):
    tokens = hidden_in.shape[0]
    rows = gate_weight.shape[0]
    table_share = relative_table.shape[0]
    row_index = lax.axis_index("row")
    col_index = lax.axis_index("col")
    row_count = lax.axis_size("row")
    col_count = lax.axis_size("col")
    region = row_index * col_count + col_index
    device_count = row_count * col_count

    packed_weights = jnp.concatenate([query_weight, key_weight, value_weight, output_weight], 1)
    weights = lax.all_gather(packed_weights, ("row", "col"), axis=0, tiled=True)
    small = jnp.stack(
        [attn_gain, ffn_gain]
        + [jnp.pad(t, (0, rows - table_share)) for t in (relative_table, horiz_table, vert_table)],
        1,
    )
    small = jnp.pad(small, ((0, 0), (0, 128 - small.shape[1])))
    small, gate_weight, up_weight, down_weight = after(
        (small, gate_weight, up_weight, down_weight), packed_weights
    )
    small_gather = Gather(small, 0, True)
    ffn_gathers = [
        Gather(weight, kind) for kind, weight in enumerate((gate_weight, up_weight, down_weight))
    ]

    def turn(gathers, *done):
        for gather in gathers:
            gather.land(*done)
        return [gather.send() for gather in gathers]

    sent = turn([small_gather] + ffn_gathers)

    halo_rows, key_keep, x_early = after((halo_rows, key_keep, hidden_in), sent)
    own_lists = lax.dynamic_index_in_dim(halo_rows, region, 0, keepdims=False)
    rim = x_early[own_lists]
    sent = turn([small_gather], rim)
    rim = after(rim, sent)
    above, below = shifted(rim[0:2], "row")
    left, right = shifted(rim[2:4], "col")
    neighbours = jnp.stack([region - col_count, region + col_count, region - 1, region + 1])
    present = jnp.stack(
        [row_index > 0, row_index < row_count - 1, col_index > 0, col_index < col_count - 1]
    ).astype(jnp.int32)
    list_ids = jnp.array([1, 0, 3, 2], dtype=jnp.int32)
    clipped = jnp.clip(neighbours, 0, device_count - 1)
    their_lists = after(halo_rows, rim)[clipped, list_ids]
    halo_keep = key_keep[clipped[:, None] * tokens + their_lists] * present[:, None]
    own_keep = lax.dynamic_slice_in_dim(key_keep, region * tokens, tokens)
    key_mask = jnp.concatenate([own_keep, halo_keep.reshape(-1)])
    key_total = key_mask.shape[0]

    place = jnp.cumsum(key_mask) - 1
    count = place[-1:] + 1
    scalars = jnp.concatenate([count, region.reshape(1)])
    slots = jnp.arange(key_total, dtype=jnp.int32)
    pack = ((place[:, None] == slots) & (key_mask[:, None] > 0)).astype(BF)

    sent = turn([small_gather] + ffn_gathers, pack)
    packed_by, relative_bucket = after((pack, relative_bucket), sent)
    found = [
        lax.dot_general(
            packed_by, bucket.astype(BF), (((0,), (1,)), ((), ())), preferred_element_type=F32
        ).astype(jnp.int32)
        for bucket in (relative_bucket, horiz_bucket, vert_bucket)
    ]
    found_vert = jnp.where(slots[:, None] < count, found[2], BUCKETS)
    codes = found[0] + found[1] * BUCKETS + found_vert * (BUCKETS * BUCKETS)

    sent = turn([small_gather], codes)
    packed_by, above = after((pack, above), sent, codes)
    x_keys = jnp.concatenate([hidden_in, above, below, left, right], 0)
    picked_x = dot_nn(packed_by.T, x_keys).astype(BF)
    turn([small_gather], picked_x)
    while small_gather.flight is not None:
        turn([small_gather])
    sent = turn(ffn_gathers, small_gather.held)
    small_masks = [0]
    for stage in stages_of(0)[::-1]:
        small_masks = small_masks + [mask ^ mask_of(stage) for mask in small_masks]
    place_of = [0] * device_count
    for at, mask in enumerate(small_masks):
        place_of[mask] = at
    devices = jnp.arange(device_count, dtype=jnp.int32)
    small_all = small_gather.held[jnp.array(place_of, jnp.int32)[devices ^ region]]
    gain_attn, gain_ffn = [small_all[:, :, i].reshape(-1) for i in range(2)]
    table_rows = [
        small_all[:, :table_share, 2 + t].reshape(BUCKETS, HEADS).T for t in range(TABLES)
    ]
    table_lanes = jnp.pad(
        jnp.stack(table_rows).astype(F32), ((0, 0), (0, 0), (0, 128 - BUCKETS))
    )
    table_lanes = table_lanes.at[2, :, BUCKETS].set(masked_score).reshape(TABLES * HEADS, 128)
    gain_one = gain_attn.astype(F32)
    gain_two = jnp.broadcast_to(gain_ffn.astype(F32), (8, D))

    low_bias = layout_bias(after(codes, sent), table_lanes, 0)
    sent = turn(ffn_gathers, low_bias)
    high_bias = layout_bias(after(codes, sent, low_bias), table_lanes, HEADS // 2)
    x_input = hidden_in.astype(F32)
    normed_one = norm_rows(x_input, gain_one).astype(BF)
    picked = norm_rows(picked_x.astype(F32), gain_one).astype(BF)
    normed_turned = normed_one.T
    picked_turned = picked.T
    turn(ffn_gathers, high_bias, picked_turned, normed_turned)
    while any(gather.flight is not None for gather in ffn_gathers):
        turn(ffn_gathers)
    gathered = [gather.held for gather in ffn_gathers]
    ffn_weights = [(held, exchange(held, ("row", 0))) for held in gathered]
    normed_one = after(normed_one, gathered, normed_turned, picked_turned)
    queries, keys, values, mixed, lse, probs, x_middle, normed_two = attention_forward(
        scalars,
        normed_one,
        picked,
        weights,
        codes,
        table_lanes,
        (low_bias, high_bias),
        hidden_in,
        gain_two,
    )
    ffn_weights = [(own, after(other, normed_two)) for own, other in ffn_weights]
    uneven = down_weight.shape[0] % 8 != 0
    if uneven:
        order, core_mask = gather_masks(2)
        order = order + tuple(mask ^ core_mask for mask in order)
        ffn_weights[2] = reordered(*ffn_weights[2], order, region)
    (
        gate_sent,
        gate_kept,
        up_sent,
        up_kept,
        down_sent,
        down_kept,
        layer_out,
        grad_middle,
        grad_attn,
        ffn_gain_part,
        row_stats,
    ) = feed_forward(scalars, normed_two, out_cotangent, x_middle, gain_two, *ffn_weights)
    if uneven:
        down_kept, down_sent = reordered(down_kept, down_sent, scatter_masks(2), region)
    ffn_chains = [
        Scatter(gate_sent, gate_kept, 0),
        Scatter(up_sent, up_kept, 1),
        Scatter(down_sent, down_kept, 2),
    ]
    rounds = Rounds()
    rounds.chains += ffn_chains

    def backward(half, kind, grad_attn):
        return attention_backward(
            half,
            kind,
            scalars,
            grad_attn,
            weights,
            queries,
            keys,
            values,
            lse,
            probs,
            codes,
            table_lanes,
            normed_turned,
            picked_turned,
            mixed,
        )

    sent = rounds.send()
    low_half = backward(0, 2, after(grad_attn, sent))
    low_chain = Scatter(low_half[5], low_half[6], 2)
    rounds.land(low_half[0])
    rounds.chains.append(low_chain)
    sent = rounds.send()
    high_half = backward(1, 1, after(grad_attn, low_half[0], sent))
    high_chain = Scatter(high_half[5], high_half[6], 1)
    rounds.land(high_half[0])
    rounds.chains.append(high_chain)
    sent = rounds.send()
    short_hist = table_histogram(
        scalars, after(codes, high_half[0], sent), low_half[3], high_half[3]
    )
    sent = rounds.turn(short_hist)
    lent, own_grads, attn_gain_part = key_gradients(
        scalars,
        low_half[:3],
        high_half[:3],
        weights,
        after(pack, short_hist, sent),
        hidden_in,
        picked_x,
    )
    hist = short_hist + jnp.concatenate([low_half[4], high_half[4]], 1)
    grad_table = jnp.sum(hist.reshape(TABLES * BUCKETS, HEADS, HIST_ROWS), -1)
    keep_float = own_keep.astype(F32)
    stat_part = jnp.stack(
        [
            jnp.sum(keep_float * jnp.sum(x_input * x_input, -1)),
            jnp.sum(keep_float * row_stats[:, 0]),
            jnp.sum(keep_float * row_stats[:, 1]),
            jnp.sum(keep_float),
        ]
    )
    small_chain = Summing(
        jnp.concatenate(
            [
                jnp.pad(stat_part, (0, 124)),
                ffn_gain_part[0],
                attn_gain_part[0],
                grad_table.reshape(-1),
            ]
        ).reshape(-1, 128)
    )
    rounds.land(lent)
    lent = lent.reshape(4, -1, D)
    back_above, back_below = shifted(lent[0:2], "row")
    back_left, back_right = shifted(lent[2:4], "col")
    rounds.chains.append(small_chain)
    sent = rounds.send()
    returned = jnp.concatenate([back_above, back_below, back_left, back_right], 0)
    owner_lists = own_lists.reshape(-1)
    owner = (jnp.arange(tokens, dtype=jnp.int32)[:, None] == owner_lists).astype(BF)
    input_grad = input_gradient(
        own_grads,
        owner,
        after(returned, sent),
        hidden_in,
        jnp.broadcast_to(gain_one, (8, D)),
        grad_middle,
    )
    rounds.turn(input_grad)
    while rounds.chains:
        rounds.turn()

    summed = small_chain.value.reshape(-1)
    residual_rms = jnp.sqrt(summed[:3] / (summed[3] * D))
    own_part = lambda at, size: lax.dynamic_slice_in_dim(summed, at + region * size, size)
    ffn_gain_grad = own_part(128, rows)
    attn_gain_grad = own_part(128 + D, rows)
    table_at = 128 + 2 * D
    table_grads = [own_part(table_at + t * BUCKETS * HEADS, table_share) for t in range(TABLES)]
    gate_grad, up_grad, down_grad = [chain.total() for chain in ffn_chains]
    sides = [low_chain.total(), high_chain.total()]
    width = D // 2
    query_grad, key_grad, value_grad, output_grad = [
        jnp.concatenate([side[:, i * width : (i + 1) * width] for side in sides], 1)
        for i in range(4)
    ]
    return (
        layer_out,
        input_grad,
        query_grad,
        key_grad,
        value_grad,
        output_grad,
        attn_gain_grad,
        table_grads[0],
        table_grads[1],
        table_grads[2],
        ffn_gain_grad,
        gate_grad,
        up_grad,
        down_grad,
        residual_rms,
    )


def solution(mesh):
    split = P(("row", "col"), None)
    line = P(("row", "col"))
    return jax.shard_map(
        on_device,
        mesh=mesh,
        in_specs=(split,) * 6 + (line,) * 5 + (split,) * 3 + (P(), P()) + (split,) * 3,
        out_specs=(split,) * 6 + (line,) * 5 + (split,) * 3 + (P(),),
        check_vma=False,
    )
```

time: 1910 us -> 531 us (0.28)
  waiting for transfers between devices: 1160 us -> 66.5 us
  matrix products: 293 us -> 8.38 us
  Pallas kernels: 0 us -> 193 us
  other arithmetic: 196 us -> 87.3 us
  blocking collectives: 105 us -> 0 us
  starting transfers between devices: 20 us -> 89.4 us
  local copies, waits for them, and re-layouts: 112 us -> 63.7 us
    reduce_scatter x7 -> x0, waiting for transfers between devices: 1060 us -> none  [the longest x1 253 us: on_device(): lax.psum_scatter(up_part, ('row', 'col'), scatter_dimension=0, tiled=True)]
    dot_general x43 -> x4, matrix products: 293 us -> 8.38 us  [the longest x3 5.85 us: on_device(): lax.dot_general(packed_by, bucket.astype(BF), (((0,), (1,)), ((), ())), p...]
    pallas_call x0 -> x9, Pallas kernels: none -> 193 us  [the longest x1 51.2 us: feed_forward(): pl.pallas_call(kernel, grid_spec=pltpu.PrefetchScalarGridSpec(num_scalar_...]
    unnamed x2 -> x0, blocking collectives: 105 us -> none
    ppermute x8 -> x56, starting transfers between devices: 19.5 us -> 89.4 us  [the longest x48 75.1 us: exchange(): return lax.ppermute(values, axis, pairs)]
    concatenate x12 -> x22, other arithmetic: 84.5 us -> 23.3 us  [the longest x12 16.2 us: land(): self.held = jnp.concatenate([self.held, self.flight], 0)]
    all_gather x7 -> x1, waiting for transfers between devices: 60.5 us -> 0.01 us  [on_device(): weights = lax.all_gather(packed_weights, ('row', 'col'), axis=0, tiled=True)]
    eq x12 -> x0, other arithmetic: 34.6 us -> none  [the longest x4 12.1 us: bucket_onehot(): rel_rows[:, :, None] == bucket_ids]
  transfers between devices with their start and end apart: 22 -> 57, of which waited for: 11 -> 15; matrix products, arithmetic and copies ran while one was open for 26% -> 28% of each run, Pallas kernels for 0% -> 27%
where the time goes in v1:
time: 531 us; the launch traced here: 524 us
  Pallas kernels  193 us (36%)
  starting transfers between devices  89.4 us (17%)
  other arithmetic  87.3 us (16%)
  waiting for transfers between devices  66.5 us (13%)
  local copies, waits for them, and re-layouts  63.7 us (12%)
  between operations  16.4 us (3%)
  matrix products  8.38 us (2%)
    ppermute x48, starting transfers between devices, exchange(): return lax.ppermute(values, axis, pairs)  75.1 us
    ppermute x48, waiting for transfers between devices, exchange(): return lax.ppermute(values, axis, pairs)  66.4 us
    pallas_call x1, Pallas kernels, feed_forward(): pl.pallas_call(kernel, grid_spec=pltpu.PrefetchScalarGridSpec(num_scalar_...  51.2 us
    convert_element_type x19, other arithmetic, land(): sum((part[half:2 * half].astype(F32) for part in self.parts)).astype(BF)  40.7 us
    pallas_call x2, Pallas kernels, attention_backward(): pl.pallas_call(functools.partial(backward_kernel, first_head=half * heads...  39.8 us
    pallas_call x2, Pallas kernels, layout_bias(): pl.pallas_call(functools.partial(bias_kernel, first_head=first_head), gri...  34.8 us
    pallas_call x1, Pallas kernels, attention_forward(): pl.pallas_call(attend_kernel, grid_spec=pltpu.PrefetchScalarGridSpec(num_...  27.8 us
    unnamed x106, local copies, waits for them, and re-layouts  25.5 us
  transfers between devices with their start and end apart: 57, of which 15 were waited for; matrix products, arithmetic and copies ran while one was open for 28% of the time, Pallas kernels for 27%

profile of v1, /device:TPU:0, one launch (start us, length us, event | category | flops | bytes accessed | tf_op | source)
XLA Modules:
  0.0 524.1 jit_solution(7506567152830989220)
XLA Ops:
  13.5 4.1 collective-permute-start
  17.7 2.8 collective-permute-start.4
  20.7 2.4 constant_dynamic-update-slice_fusion.8
  34.0 3.1 gather_fusion.2
  44.3 3.4 collective-permute-start.9
  49.8 3.0 collective-permute-start.2
  64.3 3.2 multiply_add_fusion.codes_ref
  70.9 3.5 collective-permute-start.14
  74.6 2.5 fusion
  91.5 16.8 %collective-permute-done.12 = bf16[2,32,2816]{2,1,0:T(8,128)(2,1)} collective-permute-done((bf16[2,32,2816]{2,1,0:T(8,128)(2,1)}, bf16[2,32,2816]{2,1,0:T(8,128)(2,1)}, u32[]{:S(2)}, u32[]{:S(2)}) %collective-permute-start.12) | collective-permute-done | bytes 360480 | tf_op jit(solution)/shard_map/ppermute | solution.py:76
  114.7 17.4 %layout_bias.2.low_bias_ref = f32[8,384,512]{2,1,0:T(8,128)} custom-call(s32[1024,512]{1,0:T(8,128)} %multiply_add_fusion.codes_ref, f32[48,128]{1,0:T(8,128)} %bitcast.141), custom_call_target="tpu_custom_call" | custom-call | flops 16000000000 | bytes 7000000 | tf_op jit(solution)/shard_map/layout_bias/pallas_call | solution.py:276
  137.4 2.9 collective-permute-done.17
  150.0 17.4 %layout_bias.3.high_bias_ref = f32[8,384,512]{2,1,0:T(8,128)} custom-call(s32[1024,512]{1,0:T(8,128)} %multiply_add_fusion.codes_ref, f32[48,128]{1,0:T(8,128)} %bitcast.142), custom_call_target="tpu_custom_call" | custom-call | flops 16000000000 | bytes 7000000 | tf_op jit(solution)/shard_map/layout_bias/pallas_call | solution.py:276
  167.3 7.3 %collective-permute-done.20 = bf16[8,88,1024]{2,1,0:T(8,128)(2,1)S(1)} collective-permute-done((bf16[8,88,1024]{2,1,0:T(8,128)(2,1)}, bf16[8,88,1024]{2,1,0:T(8,128)(2,1)S(1)}, u32[]{:S(2)}, u32[]{:S(2)}) %collective-permute-start.20) | collective-permute-done | bytes 1441824 | tf_op jit(solution)/shard_map/ppermute | solution.py:76
  174.7 2.4 collective-permute-done.19
  180.6 2.4 collective-permute-start.23
  183.0 2.5 constant_dynamic-update-slice_fusion.25.up_own_ref
  185.6 2.6 constant_dynamic-update-slice_fusion.20.gate_own_ref
  194.4 27.8 %attention_forward.1 = (bf16[512,1024]{1,0:T(8,128)(2,1)}, bf16[1024,1024]{1,0:T(8,128)(2,1)}, bf16[1024,1024]{1,0:T(8,128)(2,1)}, bf16[1024,512]{1,0:T(8,128)(2...) custom-call(s32[2]{0:T(128)} %pad_add_fusion.1.count_ref.scalar_ref, ...), custom_call_target="tpu_custom_call" | custom-call | flops 20000000000 | bytes 50000000 | tf_op jit(solution)/shard_map/attention_forward/pallas_call | solution.py:419
  222.2 51.2 %feed_forward.1 = (bf16[16,32,2816]{2,1,0:T(8,128)(2,1)}, bf16[16,32,2816]{2,1,0:T(8,128)(2,1)}, bf16[16,32,2816]{2,1,0:T(8,128)(2,1)}, bf16[16,32,2816]{2,1,0:T...) custom-call(s32[2]{0:T(128)} %pad_add_fusion.1.count_ref.scalar_ref,, ...), custom_call_target="tpu_custom_call" | custom-call | flops 27000000512 | bytes 44000000 | tf_op jit(solution)/shard_map/feed_forward/pallas_call | solution.py:599
  275.7 2.6 copy.107.picked_turned_ref
  278.3 19.7 %attention_backward.2 = (bf16[512,512]{1,0:T(8,128)(2,1)}, bf16[1024,512]{1,0:T(8,128)(2,1)}, bf16[1024,512]{1,0:T(8,128)(2,1)}, bf16[8,384,512]{2,1,0:T(8,128)(...) custom-call(s32[2]{0:T(128)} %pad_add_fusion.1.count_ref.scalar_ref, ...), custom_call_target="tpu_custom_call" | custom-call | flops 15000000512 | bytes 30000000 | tf_op jit(solution)/shard_map/attention_backward/pallas_call | solution.py:839
  300.3 3.2 select_maximum_fusion
  307.8 3.0 add_convert_fusion.1
  312.7 2.8 add_convert_fusion.2
  315.6 20.0 %attention_backward.3 = (bf16[512,512]{1,0:T(8,128)(2,1)}, bf16[1024,512]{1,0:T(8,128)(2,1)}, bf16[1024,512]{1,0:T(8,128)(2,1)}, bf16[8,384,512]{2,1,0:T(8,128)(...) custom-call(s32[2]{0:T(128)} %pad_add_fusion.1.count_ref.scalar_ref, ...), custom_call_target="tpu_custom_call" | custom-call | flops 15000000512 | bytes 30000000 | tf_op jit(solution)/shard_map/attention_backward/pallas_call | solution.py:839
  335.7 2.9 add_convert_fusion.4
  339.7 4.9 collective-permute-done.28
  344.6 2.8 add_convert_fusion.5
  347.4 2.5 add_convert_fusion.6
  349.9 2.4 add_convert_fusion.7
  356.1 19.7 %table_histogram.1 = f32[96,256]{1,0:T(8,128)} custom-call(s32[2]{0:T(128)} %pad_add_fusion.1.count_ref.scalar_ref, s32[1024,512]{1,0:T(8,128)} %multiply_add_fusion.codes_ref, bf16[8,384,512]{2,1,0:T(8,128)(2,1)} %get-tuple-element.194.low_ref, bf16[8,384,512]{2,1,0:T(8,128)(2,1)} %get-tuple-element.195.high_ref), custom_call_target="tpu_custom_call" | custom-call | flops 20000000000 | bytes 8000000 | tf_op jit(solution)/shard_map/table_histogram/pallas_call | solution.py:935
  375.8 2.6 add_convert_fusion.9
  378.4 2.7 add_convert_fusion.3
  381.1 2.3 add_convert_fusion.10
  389.6 13.8 %key_gradients.1 = (bf16[512,1024]{1,0:T(8,128)(2,1)}, f32[512,1024]{1,0:T(8,128)}, f32[8,1024]{1,0:T(8,128)}) custom-call(s32[2]{0:T(128)} %pad_add_fusion.1.count_ref.scalar_ref, bf16[512,512]{1,0:T(8,128)(2,1)} %get-tuple-element.173.dq_low_ref, bf16[512,512]{1,0:T(8,128)(2,1)} %get-tuple-element.182.dq_high_ref, ...), custom_call_target="tpu_custom_call" | custom-call | flops 8999999488 | bytes 18000000 | tf_op jit(solution)/shard_map/key_gradients/pallas_call | solution.py:1022
  419.6 3.9 collective-permute-start.43
  423.5 9.1 %collective-permute-start.49 = (f32[29,128]{1,0:T(8,128)S(1)}, f32[29,128]{1,0:T(8,128)S(1)}, u32[]{:S(2)}, u32[]{:S(2)}) collective-permute-start(f32[29,128]{1,0:T(8,128)S(1)} %maximum_bitcast_fusion), channel_id=1, source_target_pairs={{0,4},{4,0},{8,12},{12,8},{16,20},{20,16},{24,28},{28,24},{1,5},{5... | collective-permute-start | bytes 44552 | tf_op jit(solution)/shard_map/ppermute | solution.py:76
  444.9 5.5 %input_gradient.1 = bf16[512,1024]{1,0:T(8,128)(2,1)} custom-call(f32[512,1024]{1,0:T(8,128)} %get-tuple-element.203.own_ref, bf16[512,512]{1,0:T(8,128)(2,1)} %fusion.13.owner_ref, bf16[512,1024]{1,0:T(8,128)(2,1)} %pad_maximum_fusion.3.returned_ref, bf16[512,1024]{1,0:T(8,128)(2,1)} %x_ref.5, f32[8,1024]{1,0:T(8,128)} %broadcast_in_dim.31.gain_ref, ...), custom_call_target="tpu_custom_call" | custom-call | flops 1000000000 | bytes 8000000 | tf_op jit(solution)/shard_map/input_gradient/pallas_call | solution.py:1071
  450.4 5.5 %collective-permute-start.50 = (f32[29,128]{1,0:T(8,128)S(1)}, f32[29,128]{1,0:T(8,128)S(1)}, u32[]{:S(2)}, u32[]{:S(2)}) collective-permute-start(f32[29,128]{1,0:T(8,128)S(1)} %fusion.41), channel_id=1, source_target_pairs={{0,1},{1,0},{2,3},{3,2},{4,5},{5,4},{6,7},{7,6},{8,9},{9,8},{10,11... | collective-permute-start | bytes 44552 | tf_op jit(solution)/shard_map/ppermute | solution.py:76
  457.7 8.7 %collective-permute-start.55 = (bf16[1,88,1024]{2,1,0:T(8,128)(2,1)}, bf16[1,88,1024]{2,1,0:T(8,128)(2,1)S(1)}, u32[]{:S(2)}, u32[]{:S(2)}) collective-permute-start(bf16[1,88,1024]{2,1,0:T(8,128)(2,1)} %add_convert_fusion.15), channel_id=1, source_target_pairs={{0,16},{4,20},{8,24},{12,28},{16,0},{20,4},{24,8},{28,12},{1,17},{... | collective-permute-start | bytes 540680 | tf_op jit(solution)/shard_map/ppermute | solution.py:76
  466.5 7.3 %collective-permute-start.52 = (f32[29,128]{1,0:T(8,128)S(1)}, f32[29,128]{1,0:T(8,128)S(1)}, u32[]{:S(2)}, u32[]{:S(2)}) collective-permute-start(f32[29,128]{1,0:T(8,128)S(1)} %add.523), channel_id=1, source_target_pairs={{0,8},{4,12},{8,0},{12,4},{16,24},{20,28},{24,16},{28,20},{1,9},{5... | collective-permute-start | bytes 44552 | tf_op jit(solution)/shard_map/ppermute | solution.py:76
  475.0 4.5 collective-permute-done.55
  481.8 2.8 collective-permute-start.45
  484.6 4.7 collective-permute-done.53
  492.3 2.5 add_bitcast_fusion.1
  497.9 6.5 %collective-permute-done.47 = bf16[2,32,2048]{2,1,0:T(8,128)(2,1)S(1)} collective-permute-done((bf16[2,32,2048]{2,1,0:T(8,128)(2,1)S(1)}, bf16[2,32,2048]{2,1,0:T(8,128)(2,1)S(1)}, u32[]{:S(2)}, u32[]{:S(2)}) %collective-permute-start.47) | collective-permute-done | bytes 262176 | tf_op jit(solution)/shard_map/ppermute | solution.py:76
  505.6 7.7 %collective-permute-done.48 = bf16[1,32,2048]{2,1,0:T(8,128)(2,1)S(1)} collective-permute-done((bf16[1,32,2048]{2,1,0:T(8,128)(2,1)S(1)}, bf16[1,32,2048]{2,1,0:T(8,128)(2,1)S(1)}, u32[]{:S(2)}, u32[]{:S(2)}) %collective-permute-start.48) | collective-permute-done | bytes 131104 | tf_op jit(solution)/shard_map/ppermute | solution.py:76
  (319 shorter events, 152.5 us)
Async XLA Ops:
  7.2 186.6 %all-gather.2.cloned.1.call-start = ((), (), s32[]{:S(2)}) async-start(), calls=%async_computation | async-start | bytes 8650752 | tf_op jit(solution)/shard_map/all_gather | solution.py:1124
  13.5 17.1 %collective-permute-start = (bf16[1,32,128]{1,2,0:T(8,128)(2,1)S(1)}, bf16[1,32,128]{1,2,0:T(8,128)(2,1)S(1)}, u32[]{:S(2)}, u32[]{:S(2)}) collective-permute-start(bf16[1,32,128]{1,2,0:T(8,128)(2,1)S(1)} %bitcast.133), channel_id=1, source_target_pairs={{0,16},{4,20},{8,24},{12,28},{16,0},{20,4},{24,8},{28,12},{1,17},{... | collective-permute-start | bytes 24584 | tf_op jit(solution)/shard_map/ppermute | solution.py:76
  17.6 26.7 %collective-permute-start.5 = (bf16[1,88,1024]{2,1,0:T(8,128)(2,1)}, bf16[1,88,1024]{2,1,0:T(8,128)(2,1)}, u32[]{:S(2)}, u32[]{:S(2)}) collective-permute-start(bf16[1,88,1024]{2,1,0:T(8,128)(2,1)} %bitcast.121), channel_id=1, source_target_pairs={{0,16},{4,20},{8,24},{12,28},{16,0},{20,4},{24,8},{28,12},{1,17},{... | collective-permute-start | bytes 540680 | tf_op jit(solution)/shard_map/ppermute | solution.py:76
  17.7 30.0 %collective-permute-start.4 = (bf16[1,32,2816]{2,1,0:T(8,128)(2,1)}, bf16[1,32,2816]{2,1,0:T(8,128)(2,1)}, u32[]{:S(2)}, u32[]{:S(2)}) collective-permute-start(bf16[1,32,2816]{2,1,0:T(8,128)(2,1)} %bitcast.125), channel_id=1, source_target_pairs={{0,16},{4,20},{8,24},{12,28},{16,0},{20,4},{24,8},{28,12},{1,17},{... | collective-permute-start | bytes 540680 | tf_op jit(solution)/shard_map/ppermute | solution.py:76
  20.5 29.3 %collective-permute-start.3 = (bf16[1,32,2816]{2,1,0:T(8,128)(2,1)}, bf16[1,32,2816]{2,1,0:T(8,128)(2,1)}, u32[]{:S(2)}, u32[]{:S(2)}) collective-permute-start(bf16[1,32,2816]{2,1,0:T(8,128)(2,1)} %bitcast.129), channel_id=1, source_target_pairs={{0,16},{4,20},{8,24},{12,28},{16,0},{20,4},{24,8},{28,12},{1,17},{... | collective-permute-start | bytes 540680 | tf_op jit(solution)/shard_map/ppermute | solution.py:76
  30.6 11.7 %collective-permute-start.1 = (bf16[2,32,128]{2,1,0:T(8,128)(2,1)S(1)}, bf16[2,32,128]{2,1,0:T(8,128)(2,1)S(1)}, u32[]{:S(2)}, u32[]{:S(2)}) collective-permute-start(bf16[2,32,128]{2,1,0:T(8,128)(2,1)S(1)} %pad_maximum_fusion.18), channel_id=1, source_target_pairs={{0,8},{4,12},{8,0},{12,4},{16,24},{20,28},{24,16},{28,20},{1,9},{5... | collective-permute-start | bytes 49160 | tf_op jit(solution)/shard_map/ppermute | solution.py:76
  38.5 31.3 %collective-permute-start.7 = (bf16[128,1024]{1,0:T(8,128)(2,1)S(1)}, bf16[128,1024]{1,0:T(8,128)(2,1)S(1)}, u32[]{:S(2)}, u32[]{:S(2)}) collective-permute-start(bf16[128,1024]{1,0:T(8,128)(2,1)S(1)} %get-tuple-element.238), channel_id=1, source_target_pairs={{0,4},{4,8},{8,12},{12,16},{16,20},{20,24},{24,28},{1,5},{5,9},{9,... | collective-permute-start | bytes 786440 | tf_op jit(solution)/shard_map/ppermute | solution.py:35
  42.3 28.6 %collective-permute-start.8 = (bf16[128,1024]{1,0:T(8,128)(2,1)S(1)}, bf16[128,1024]{1,0:T(8,128)(2,1)S(1)}, u32[]{:S(2)}, u32[]{:S(2)}) collective-permute-start(bf16[128,1024]{1,0:T(8,128)(2,1)S(1)} %get-tuple-element.237), channel_id=1, source_target_pairs={{4,0},{8,4},{12,8},{16,12},{20,16},{24,20},{28,24},{5,1},{9,5},{13... | collective-permute-start | bytes 786440 | tf_op jit(solution)/shard_map/ppermute | solution.py:36
  44.3 30.1 %collective-permute-start.9 = (bf16[128,1024]{1,0:T(8,128)(2,1)S(1)}, bf16[128,1024]{1,0:T(8,128)(2,1)S(1)}, u32[]{:S(2)}, u32[]{:S(2)}) collective-permute-start(bf16[128,1024]{1,0:T(8,128)(2,1)S(1)} %get-tuple-element.236), channel_id=1, source_target_pairs={{0,1},{1,2},{2,3},{4,5},{5,6},{6,7},{8,9},{9,10},{10,11},{12,13},{... | collective-permute-start | bytes 786440 | tf_op jit(solution)/shard_map/ppermute | solution.py:35
  47.7 26.8 %collective-permute-start.10 = (bf16[128,1024]{1,0:T(8,128)(2,1)S(1)}, bf16[128,1024]{1,0:T(8,128)(2,1)S(1)}, u32[]{:S(2)}, u32[]{:S(2)}) collective-permute-start(bf16[128,1024]{1,0:T(8,128)(2,1)S(1)} %get-tuple-element.235), channel_id=1, source_target_pairs={{1,0},{2,1},{3,2},{5,4},{6,5},{7,6},{9,8},{10,9},{11,10},{13,12},{... | collective-permute-start | bytes 786440 | tf_op jit(solution)/shard_map/ppermute | solution.py:36
  49.8 19.3 %collective-permute-start.2 = (bf16[4,32,128]{2,1,0:T(8,128)(2,1)S(1)}, bf16[4,32,128]{2,1,0:T(8,128)(2,1)S(1)}, u32[]{:S(2)}, u32[]{:S(2)}) collective-permute-start(bf16[4,32,128]{2,1,0:T(8,128)(2,1)S(1)} %pad_maximum_fusion.17), channel_id=1, source_target_pairs={{0,2},{1,3},{2,0},{3,1},{4,6},{5,7},{6,4},{7,5},{8,10},{9,11},{10,... | collective-permute-start | bytes 98312 | tf_op jit(solution)/shard_map/ppermute | solution.py:76
  69.1 22.4 %collective-permute-start.15 = (bf16[2,88,1024]{2,1,0:T(8,128)(2,1)}, bf16[2,88,1024]{2,1,0:T(8,128)(2,1)}, u32[]{:S(2)}, u32[]{:S(2)}) collective-permute-start(bf16[2,88,1024]{2,1,0:T(8,128)(2,1)} %pad_maximum_fusion.10), channel_id=1, source_target_pairs={{0,2},{1,3},{2,0},{3,1},{4,6},{5,7},{6,4},{7,5},{8,10},{9,11},{10,... | collective-permute-start | bytes 1081352 | tf_op jit(solution)/shard_map/ppermute | solution.py:76
  70.9 20.6 %collective-permute-start.14 = (bf16[2,32,2816]{2,1,0:T(8,128)(2,1)}, bf16[2,32,2816]{2,1,0:T(8,128)(2,1)}, u32[]{:S(2)}, u32[]{:S(2)}) collective-permute-start(bf16[2,32,2816]{2,1,0:T(8,128)(2,1)} %pad_maximum_fusion.9), channel_id=1, source_target_pairs={{0,8},{4,12},{8,0},{12,4},{16,24},{20,28},{24,16},{28,20},{1,9},{5... | collective-permute-start | bytes 1081352 | tf_op jit(solution)/shard_map/ppermute | solution.py:76
  74.4 33.9 %collective-permute-start.12 = (bf16[2,32,2816]{2,1,0:T(8,128)(2,1)}, bf16[2,32,2816]{2,1,0:T(8,128)(2,1)}, u32[]{:S(2)}, u32[]{:S(2)}) collective-permute-start(bf16[2,32,2816]{2,1,0:T(8,128)(2,1)} %pad_maximum_fusion.8), channel_id=1, source_target_pairs={{0,8},{4,12},{8,0},{12,4},{16,24},{20,28},{24,16},{28,20},{1,9},{5... | collective-permute-start | bytes 1081352 | tf_op jit(solution)/shard_map/ppermute | solution.py:76
  109.4 28.0 %collective-permute-start.18 = (bf16[4,88,1024]{2,1,0:T(8,128)(2,1)S(1)}, bf16[4,88,1024]{2,1,0:T(8,128)(2,1)S(1)}, u32[]{:S(2)}, u32[]{:S(2)}) collective-permute-start(bf16[4,88,1024]{2,1,0:T(8,128)(2,1)S(1)} %pad_maximum_fusion.6), channel_id=1, source_target_pairs={{0,1},{1,0},{2,3},{3,2},{4,5},{5,4},{6,7},{7,6},{8,9},{9,8},{10,11... | collective-permute-start | bytes 2162696 | tf_op jit(solution)/shard_map/ppermute | solution.py:76
  110.6 29.7 %collective-permute-start.17 = (bf16[4,32,2816]{2,1,0:T(8,128)(2,1)S(1)}, bf16[4,32,2816]{2,1,0:T(8,128)(2,1)S(1)}, u32[]{:S(2)}, u32[]{:S(2)}) collective-permute-start(bf16[4,32,2816]{2,1,0:T(8,128)(2,1)S(1)} %pad_maximum_fusion.5), channel_id=1, source_target_pairs={{0,1},{1,0},{2,3},{3,2},{4,5},{5,4},{6,7},{7,6},{8,9},{9,8},{10,11... | collective-permute-start | bytes 2162696 | tf_op jit(solution)/shard_map/ppermute | solution.py:76
  114.7 25.5 %collective-permute-start.13 = (bf16[4,32,2816]{2,1,0:T(8,128)(2,1)}, bf16[4,32,2816]{2,1,0:T(8,128)(2,1)S(1)}, u32[]{:S(2)}, u32[]{:S(2)}) collective-permute-start(bf16[4,32,2816]{2,1,0:T(8,128)(2,1)} %pad_maximum_fusion.4), channel_id=1, source_target_pairs={{0,2},{1,3},{2,0},{3,1},{4,6},{5,7},{6,4},{7,5},{8,10},{9,11},{10,... | collective-permute-start | bytes 2162696 | tf_op jit(solution)/shard_map/ppermute | solution.py:76
  142.6 32.1 %collective-permute-start.20 = (bf16[8,88,1024]{2,1,0:T(8,128)(2,1)}, bf16[8,88,1024]{2,1,0:T(8,128)(2,1)S(1)}, u32[]{:S(2)}, u32[]{:S(2)}) collective-permute-start(bf16[8,88,1024]{2,1,0:T(8,128)(2,1)} %pad_maximum_fusion.2), channel_id=1, source_target_pairs={{0,8},{4,12},{8,0},{12,4},{16,24},{20,28},{24,16},{28,20},{1,9},{5... | collective-permute-start | bytes 4325384 | tf_op jit(solution)/shard_map/ppermute | solution.py:76
  144.9 32.2 %collective-permute-start.19 = (bf16[8,32,2816]{2,1,0:T(8,128)(2,1)}, bf16[8,32,2816]{2,1,0:T(8,128)(2,1)}, u32[]{:S(2)}, u32[]{:S(2)}) collective-permute-start(bf16[8,32,2816]{2,1,0:T(8,128)(2,1)} %pad_maximum_fusion.1), channel_id=1, source_target_pairs={{0,2},{1,3},{2,0},{3,1},{4,6},{5,7},{6,4},{7,5},{8,10},{9,11},{10,... | collective-permute-start | bytes 4325384 | tf_op jit(solution)/shard_map/ppermute | solution.py:76
  147.1 32.2 %collective-permute-start.16 = (bf16[8,32,2816]{2,1,0:T(8,128)(2,1)}, bf16[8,32,2816]{2,1,0:T(8,128)(2,1)}, u32[]{:S(2)}, u32[]{:S(2)}) collective-permute-start(bf16[8,32,2816]{2,1,0:T(8,128)(2,1)} %pad_maximum_fusion), channel_id=1, source_target_pairs={{0,1},{1,0},{2,3},{3,2},{4,5},{5,4},{6,7},{7,6},{8,9},{9,8},{10,11... | collective-permute-start | bytes 4325384 | tf_op jit(solution)/shard_map/ppermute | solution.py:76
  180.6 41.6 %collective-permute-start.23 = (bf16[16,88,1024]{2,1,0:T(8,128)(2,1)}, bf16[16,88,1024]{2,1,0:T(8,128)(2,1)}, u32[]{:S(2)}, u32[]{:S(2)}) collective-permute-start(bf16[16,88,1024]{2,1,0:T(8,128)(2,1)} %constant_dynamic-update-slice_fusion.30.down_own_ref), channel_id=1, source_target_pairs={{0,4},{4,0},{8,12},{12,8},{16,20},{20,16},{24,28},{28,24},{1,5},{5... | collective-permute-start | bytes 8650760 | tf_op jit(solution)/shard_map/ppermute | solution.py:76
  185.5 36.6 %collective-permute-start.22 = (bf16[16,32,2816]{2,1,0:T(8,128)(2,1)}, bf16[16,32,2816]{2,1,0:T(8,128)(2,1)}, u32[]{:S(2)}, u32[]{:S(2)}) collective-permute-start(bf16[16,32,2816]{2,1,0:T(8,128)(2,1)} %constant_dynamic-update-slice_fusion.25.up_own_ref), channel_id=1, source_target_pairs={{0,4},{4,0},{8,12},{12,8},{16,20},{20,16},{24,28},{28,24},{1,5},{5... | collective-permute-start | bytes 8650760 | tf_op jit(solution)/shard_map/ppermute | solution.py:76
  188.1 34.1 %collective-permute-start.21 = (bf16[16,32,2816]{2,1,0:T(8,128)(2,1)}, bf16[16,32,2816]{2,1,0:T(8,128)(2,1)}, u32[]{:S(2)}, u32[]{:S(2)}) collective-permute-start(bf16[16,32,2816]{2,1,0:T(8,128)(2,1)} %constant_dynamic-update-slice_fusion.20.gate_own_ref), channel_id=1, source_target_pairs={{0,4},{4,0},{8,12},{12,8},{16,20},{20,16},{24,28},{28,24},{1,5},{5... | collective-permute-start | bytes 8650760 | tf_op jit(solution)/shard_map/ppermute | solution.py:76
  273.4 30.1 %collective-permute-start.26 = (bf16[16,88,1024]{2,1,0:T(8,128)(2,1)}, bf16[16,88,1024]{2,1,0:T(8,128)(2,1)}, u32[]{:S(2)}, u32[]{:S(2)}) collective-permute-start(bf16[16,88,1024]{2,1,0:T(8,128)(2,1)} %get-tuple-element.165), channel_id=1, source_target_pairs={{0,4},{4,0},{8,12},{12,8},{16,20},{20,16},{24,28},{28,24},{1,5},{5... | collective-permute-start | bytes 8650760 | tf_op jit(solution)/shard_map/ppermute | solution.py:76
  273.5 30.0 %collective-permute-start.25 = (bf16[16,32,2816]{2,1,0:T(8,128)(2,1)}, bf16[16,32,2816]{2,1,0:T(8,128)(2,1)}, u32[]{:S(2)}, u32[]{:S(2)}) collective-permute-start(bf16[16,32,2816]{2,1,0:T(8,128)(2,1)} %get-tuple-element.164), channel_id=1, source_target_pairs={{0,4},{4,0},{8,12},{12,8},{16,20},{20,16},{24,28},{28,24},{1,5},{5... | collective-permute-start | bytes 8650760 | tf_op jit(solution)/shard_map/ppermute | solution.py:76
  274.0 29.5 %collective-permute-start.24 = (bf16[16,32,2816]{2,1,0:T(8,128)(2,1)}, bf16[16,32,2816]{2,1,0:T(8,128)(2,1)}, u32[]{:S(2)}, u32[]{:S(2)}) collective-permute-start(bf16[16,32,2816]{2,1,0:T(8,128)(2,1)} %get-tuple-element.163), channel_id=1, source_target_pairs={{0,4},{4,0},{8,12},{12,8},{16,20},{20,16},{24,28},{28,24},{1,5},{5... | collective-permute-start | bytes 8650760 | tf_op jit(solution)/shard_map/ppermute | solution.py:76
  298.0 37.6 %collective-permute-start.30 = (bf16[16,32,2048]{2,1,0:T(8,128)(2,1)}, bf16[16,32,2048]{2,1,0:T(8,128)(2,1)}, u32[]{:S(2)}, u32[]{:S(2)}) collective-permute-start(bf16[16,32,2048]{2,1,0:T(8,128)(2,1)} %get-tuple-element.180), channel_id=1, source_target_pairs={{0,4},{4,0},{8,12},{12,8},{16,20},{20,16},{24,28},{28,24},{1,5},{5... | collective-permute-start | bytes 6291464 | tf_op jit(solution)/shard_map/ppermute | solution.py:76
  305.7 34.0 %collective-permute-start.29 = (bf16[8,88,1024]{2,1,0:T(8,128)(2,1)S(1)}, bf16[8,88,1024]{2,1,0:T(8,128)(2,1)}, u32[]{:S(2)}, u32[]{:S(2)}) collective-permute-start(bf16[8,88,1024]{2,1,0:T(8,128)(2,1)S(1)} %add_convert_fusion), channel_id=1, source_target_pairs={{0,8},{4,12},{8,0},{12,4},{16,24},{20,28},{24,16},{28,20},{1,9},{5... | collective-permute-start | bytes 4325384 | tf_op jit(solution)/shard_map/ppermute | solution.py:76
  310.7 33.9 %collective-permute-start.28 = (bf16[8,32,2816]{2,1,0:T(8,128)(2,1)}, bf16[8,32,2816]{2,1,0:T(8,128)(2,1)}, u32[]{:S(2)}, u32[]{:S(2)}) collective-permute-start(bf16[8,32,2816]{2,1,0:T(8,128)(2,1)} %add_convert_fusion.1), channel_id=1, source_target_pairs={{0,2},{1,3},{2,0},{3,1},{4,6},{5,7},{6,4},{7,5},{8,10},{9,11},{10,... | collective-permute-start | bytes 4325384 | tf_op jit(solution)/shard_map/ppermute | solution.py:76
  315.6 34.3 %collective-permute-start.27 = (bf16[8,32,2816]{2,1,0:T(8,128)(2,1)}, bf16[8,32,2816]{2,1,0:T(8,128)(2,1)}, u32[]{:S(2)}, u32[]{:S(2)}) collective-permute-start(bf16[8,32,2816]{2,1,0:T(8,128)(2,1)} %add_convert_fusion.2), channel_id=1, source_target_pairs={{0,1},{1,0},{2,3},{3,2},{4,5},{5,4},{6,7},{7,6},{8,9},{9,8},{10,11... | collective-permute-start | bytes 4325384 | tf_op jit(solution)/shard_map/ppermute | solution.py:76
  335.6 42.8 %collective-permute-start.35 = (bf16[16,32,2048]{2,1,0:T(8,128)(2,1)}, bf16[16,32,2048]{2,1,0:T(8,128)(2,1)}, u32[]{:S(2)}, u32[]{:S(2)}) collective-permute-start(bf16[16,32,2048]{2,1,0:T(8,128)(2,1)} %get-tuple-element.192), channel_id=1, source_target_pairs={{0,4},{4,0},{8,12},{12,8},{16,20},{20,16},{24,28},{28,24},{1,5},{5... | collective-permute-start | bytes 6291464 | tf_op jit(solution)/shard_map/ppermute | solution.py:76
  338.6 37.2 %collective-permute-start.34 = (bf16[8,32,2048]{2,1,0:T(8,128)(2,1)}, bf16[8,32,2048]{2,1,0:T(8,128)(2,1)}, u32[]{:S(2)}, u32[]{:S(2)}) collective-permute-start(bf16[8,32,2048]{2,1,0:T(8,128)(2,1)} %add_convert_fusion.4), channel_id=1, source_target_pairs={{0,8},{4,12},{8,0},{12,4},{16,24},{20,28},{24,16},{28,20},{1,9},{5... | collective-permute-start | bytes 3145736 | tf_op jit(solution)/shard_map/ppermute | solution.py:76
  352.3 28.8 %collective-permute-start.33 = (bf16[4,88,1024]{2,1,0:T(8,128)(2,1)}, bf16[4,88,1024]{2,1,0:T(8,128)(2,1)}, u32[]{:S(2)}, u32[]{:S(2)}) collective-permute-start(bf16[4,88,1024]{2,1,0:T(8,128)(2,1)} %add_convert_fusion.5), channel_id=1, source_target_pairs={{0,1},{1,0},{2,3},{3,2},{4,5},{5,4},{6,7},{7,6},{8,9},{9,8},{10,11... | collective-permute-start | bytes 2162696 | tf_op jit(solution)/shard_map/ppermute | solution.py:76
  352.3 31.1 %collective-permute-start.31 = (bf16[4,32,2816]{2,1,0:T(8,128)(2,1)}, bf16[4,32,2816]{2,1,0:T(8,128)(2,1)S(1)}, u32[]{:S(2)}, u32[]{:S(2)}) collective-permute-start(bf16[4,32,2816]{2,1,0:T(8,128)(2,1)} %add_convert_fusion.7), channel_id=1, source_target_pairs={{0,2},{1,3},{2,0},{3,1},{4,6},{5,7},{6,4},{7,5},{8,10},{9,11},{10,... | collective-permute-start | bytes 2162696 | tf_op jit(solution)/shard_map/ppermute | solution.py:76
  354.1 33.0 %collective-permute-start.32 = (bf16[4,32,2816]{2,1,0:T(8,128)(2,1)}, bf16[4,32,2816]{2,1,0:T(8,128)(2,1)S(1)}, u32[]{:S(2)}, u32[]{:S(2)}) collective-permute-start(bf16[4,32,2816]{2,1,0:T(8,128)(2,1)} %add_convert_fusion.6), channel_id=1, source_target_pairs={{0,1},{1,0},{2,3},{3,2},{4,5},{5,4},{6,7},{7,6},{8,9},{9,8},{10,11... | collective-permute-start | bytes 2162696 | tf_op jit(solution)/shard_map/ppermute | solution.py:76
  378.4 33.1 %collective-permute-start.42 = (bf16[4,32,2048]{2,1,0:T(8,128)(2,1)}, bf16[4,32,2048]{2,1,0:T(8,128)(2,1)S(1)}, u32[]{:S(2)}, u32[]{:S(2)}) collective-permute-start(bf16[4,32,2048]{2,1,0:T(8,128)(2,1)} %add_convert_fusion.9), channel_id=1, source_target_pairs={{0,1},{1,0},{2,3},{3,2},{4,5},{5,4},{6,7},{7,6},{8,9},{9,8},{10,11... | collective-permute-start | bytes 1572872 | tf_op jit(solution)/shard_map/ppermute | solution.py:76
  409.5 26.8 %collective-permute-start.41 = (bf16[2,88,1024]{2,1,0:T(8,128)(2,1)}, bf16[2,88,1024]{2,1,0:T(8,128)(2,1)S(1)}, u32[]{:S(2)}, u32[]{:S(2)}) collective-permute-start(bf16[2,88,1024]{2,1,0:T(8,128)(2,1)} %add_convert_fusion.10), channel_id=1, source_target_pairs={{0,2},{1,3},{2,0},{3,1},{4,6},{5,7},{6,4},{7,5},{8,10},{9,11},{10,... | collective-permute-start | bytes 1081352 | tf_op jit(solution)/shard_map/ppermute | solution.py:76
  411.2 27.1 %collective-permute-start.40 = (bf16[2,32,5632]{2,1,0:T(8,128)(2,1)}, bf16[2,32,5632]{2,1,0:T(8,128)(2,1)S(1)}, u32[]{:S(2)}, u32[]{:S(2)}) collective-permute-start(bf16[2,32,5632]{2,1,0:T(8,128)(2,1)} %pad_maximum_fusion.7), channel_id=1, source_target_pairs={{0,8},{4,12},{8,0},{12,4},{16,24},{20,28},{24,16},{28,20},{1,9},{5... | collective-permute-start | bytes 2162696 | tf_op jit(solution)/shard_map/ppermute | solution.py:76
  413.0 10.5 %collective-permute-start.38 = (bf16[128,1024]{1,0:T(8,128)(2,1)}, bf16[128,1024]{1,0:T(8,128)(2,1)S(1)}, u32[]{:S(2)}, u32[]{:S(2)}) collective-permute-start(bf16[128,1024]{1,0:T(8,128)(2,1)} %get-tuple-element.233), channel_id=1, source_target_pairs={{0,1},{1,2},{2,3},{4,5},{5,6},{6,7},{8,9},{9,10},{10,11},{12,13},{... | collective-permute-start | bytes 786440 | tf_op jit(solution)/shard_map/ppermute | solution.py:35
  414.9 17.6 %collective-permute-start.39 = (bf16[128,1024]{1,0:T(8,128)(2,1)}, bf16[128,1024]{1,0:T(8,128)(2,1)S(1)}, u32[]{:S(2)}, u32[]{:S(2)}) collective-permute-start(bf16[128,1024]{1,0:T(8,128)(2,1)} %get-tuple-element.232), channel_id=1, source_target_pairs={{1,0},{2,1},{3,2},{5,4},{6,5},{7,6},{9,8},{10,9},{11,10},{13,12},{... | collective-permute-start | bytes 786440 | tf_op jit(solution)/shard_map/ppermute | solution.py:36
  419.6 21.3 %collective-permute-start.43 = (bf16[8,32,2048]{2,1,0:T(8,128)(2,1)}, bf16[8,32,2048]{2,1,0:T(8,128)(2,1)S(1)}, u32[]{:S(2)}, u32[]{:S(2)}) collective-permute-start(bf16[8,32,2048]{2,1,0:T(8,128)(2,1)} %add_convert_fusion.3), channel_id=1, source_target_pairs={{0,2},{1,3},{2,0},{3,1},{4,6},{5,7},{6,4},{7,5},{8,10},{9,11},{10,... | collective-permute-start | bytes 3145736 | tf_op jit(solution)/shard_map/ppermute | solution.py:76
  423.5 26.9 %collective-permute-start.49 = (f32[29,128]{1,0:T(8,128)S(1)}, f32[29,128]{1,0:T(8,128)S(1)}, u32[]{:S(2)}, u32[]{:S(2)}) collective-permute-start(f32[29,128]{1,0:T(8,128)S(1)} %maximum_bitcast_fusion), channel_id=1, source_target_pairs={{0,4},{4,0},{8,12},{12,8},{16,20},{20,16},{24,28},{28,24},{1,5},{5... | collective-permute-start | bytes 44552 | tf_op jit(solution)/shard_map/ppermute | solution.py:76
  432.6 33.9 %collective-permute-start.44 = (bf16[2,32,2048]{2,1,0:T(8,128)(2,1)}, bf16[2,32,2048]{2,1,0:T(8,128)(2,1)}, u32[]{:S(2)}, u32[]{:S(2)}) collective-permute-start(bf16[2,32,2048]{2,1,0:T(8,128)(2,1)} %add_convert_fusion.14), channel_id=1, source_target_pairs={{0,2},{1,3},{2,0},{3,1},{4,6},{5,7},{6,4},{7,5},{8,10},{9,11},{10,... | collective-permute-start | bytes 786440 | tf_op jit(solution)/shard_map/ppermute | solution.py:76
  457.7 21.8 %collective-permute-start.55 = (bf16[1,88,1024]{2,1,0:T(8,128)(2,1)}, bf16[1,88,1024]{2,1,0:T(8,128)(2,1)S(1)}, u32[]{:S(2)}, u32[]{:S(2)}) collective-permute-start(bf16[1,88,1024]{2,1,0:T(8,128)(2,1)} %add_convert_fusion.15), channel_id=1, source_target_pairs={{0,16},{4,20},{8,24},{12,28},{16,0},{20,4},{24,8},{28,12},{1,17},{... | collective-permute-start | bytes 540680 | tf_op jit(solution)/shard_map/ppermute | solution.py:76
  466.4 25.8 %collective-permute-start.54 = (bf16[1,32,5632]{2,1,0:T(8,128)(2,1)}, bf16[1,32,5632]{2,1,0:T(8,128)(2,1)S(1)}, u32[]{:S(2)}, u32[]{:S(2)}) collective-permute-start(bf16[1,32,5632]{2,1,0:T(8,128)(2,1)} %pad_maximum_fusion.11), channel_id=1, source_target_pairs={{0,16},{4,20},{8,24},{12,28},{16,0},{20,4},{24,8},{28,12},{1,17},{... | collective-permute-start | bytes 1081352 | tf_op jit(solution)/shard_map/ppermute | solution.py:76
  466.5 28.3 %collective-permute-start.46 = (bf16[4,32,2048]{2,1,0:T(8,128)(2,1)}, bf16[4,32,2048]{2,1,0:T(8,128)(2,1)S(1)}, u32[]{:S(2)}, u32[]{:S(2)}) collective-permute-start(bf16[4,32,2048]{2,1,0:T(8,128)(2,1)} %add_convert_fusion.8), channel_id=1, source_target_pairs={{0,1},{1,0},{2,3},{3,2},{4,5},{5,4},{6,7},{7,6},{8,9},{9,8},{10,11... | collective-permute-start | bytes 1572872 | tf_op jit(solution)/shard_map/ppermute | solution.py:76
  466.5 13.0 %collective-permute-start.52 = (f32[29,128]{1,0:T(8,128)S(1)}, f32[29,128]{1,0:T(8,128)S(1)}, u32[]{:S(2)}, u32[]{:S(2)}) collective-permute-start(f32[29,128]{1,0:T(8,128)S(1)} %add.523), channel_id=1, source_target_pairs={{0,8},{4,12},{8,0},{12,4},{16,24},{20,28},{24,16},{28,20},{1,9},{5... | collective-permute-start | bytes 44552 | tf_op jit(solution)/shard_map/ppermute | solution.py:76
  481.8 15.0 %collective-permute-start.45 = (bf16[1,32,2048]{2,1,0:T(8,128)(2,1)S(1)}, bf16[1,32,2048]{2,1,0:T(8,128)(2,1)S(1)}, u32[]{:S(2)}, u32[]{:S(2)}) collective-permute-start(bf16[1,32,2048]{2,1,0:T(8,128)(2,1)S(1)} %add_convert_fusion.19), channel_id=1, source_target_pairs={{0,16},{4,20},{8,24},{12,28},{16,0},{20,4},{24,8},{28,12},{1,17},{... | collective-permute-start | bytes 393224 | tf_op jit(solution)/shard_map/ppermute | solution.py:76
  (50 other events, 616.6 us)
Sparse Core Ops, SparseCore 0:
  11.5 106.5 all-gather.1

commit v2 on v1

--- a/solution.py
+++ b/solution.py
@@ -48,7 +48,9 @@
         return row_bits[:1] + col_bits + row_bits[1:]
     if kind == 1:
         return row_bits[:1] + col_bits[::-1] + row_bits[1:]
-    return row_bits[:2] + col_bits + row_bits[2:]
+    if kind == 2:
+        return row_bits[:2] + col_bits + row_bits[2:]
+    return row_bits[:2] + col_bits[::-1] + row_bits[2:]
 
 
 def mask_of(stage):
@@ -114,16 +116,6 @@
 
     def total(self):
         return sum(part[0].astype(F32) for part in self.parts)
-
-
-class Summing:
-    def __init__(self, values):
-        self.stages = stages_of(0)
-        self.sent = values
-
-    def land(self, flight):
-        self.value = self.sent + flight
-        self.sent = self.value if self.stages else None
 
 
 class Rounds:
@@ -221,21 +213,24 @@
     return pl.ds(start, height)
 
 
-def join_pieces(own_ref, other_ref, joined_ref, device, masks, core_mask):
+def join_pieces(own_ref, other_ref, joined_ref, device, masks, core_mask, at=0):
     height = own_ref.shape[1]
+    lanes = slice(at, at + own_ref.shape[2])
     for p, mask in enumerate(masks):
-        joined_ref[placed(device ^ mask, height), :] = own_ref[p].astype(joined_ref.dtype)
-        joined_ref[placed(device ^ mask ^ core_mask, height), :] = other_ref[p].astype(
+        joined_ref[placed(device ^ mask, height), lanes] = own_ref[p].astype(joined_ref.dtype)
+        joined_ref[placed(device ^ mask ^ core_mask, height), lanes] = other_ref[p].astype(
             joined_ref.dtype
         )
 
 
-def part_pieces(joined_ref, sent_ref, kept_ref, device, masks, at=0):
-    half, height = kept_ref.shape[:2]
-    lanes = slice(at, at + joined_ref.shape[1])
+def part_pieces(joined_ref, sent_ref, kept_ref, device, masks, at=0, source=0):
+    half, height, width = kept_ref.shape
+    width = min(width, joined_ref.shape[1])
+    lanes = slice(at, at + width)
+    taken = slice(source, source + width)
     for p, mask in enumerate(masks):
         target_ref = kept_ref if p < half else sent_ref
-        target_ref[p % half, :, lanes] = joined_ref[placed(device ^ mask, height), :].astype(BF)
+        target_ref[p % half, :, lanes] = joined_ref[placed(device ^ mask, height), taken].astype(BF)
 
 
 def head_masks():
@@ -475,8 +470,7 @@
     out_cot_ref,
     mid_ref,
     gain_ref,
-    gate_own_ref,
-    gate_other_ref,
+    gate_ref,
     up_own_ref,
     up_other_ref,
     down_own_ref,
@@ -496,10 +490,8 @@
     branch_ref,
     back_ref,
     down_all_ref,
-    gate_ref,
-    up_ref,
-    gate_grad_ref,
-    up_grad_ref,
+    pair_ref,
+    pair_grad_ref,
     down_ref,
     *,
     gather_order,
@@ -514,16 +506,16 @@
         turned_ref[...] = normed_ref[...].T
         join_pieces(down_own_ref, down_other_ref, down_all_ref, down_device, *gather_order[2])
 
-    join_pieces(gate_own_ref, gate_other_ref, gate_ref, device, *gather_order[0])
-    join_pieces(up_own_ref, up_other_ref, up_ref, device, *gather_order[1])
+    pair_ref[:, :FF_TILE] = gate_ref[...].astype(pair_ref.dtype)
+    join_pieces(up_own_ref, up_other_ref, pair_ref, device, *gather_order[1], FF_TILE)
     here = pl.ds(pl.multiple_of(step * FF_TILE, FF_TILE), FF_TILE)
     down_ref[...] = down_all_ref[here, :].astype(BF)
 
     normed = normed_ref[...]
-    gate_weight = gate_ref[...].astype(BF)
-    up_weight = up_ref[...].astype(BF)
-    gate = dot_nn(normed, gate_weight)
-    up = dot_nn(normed, up_weight)
+    pair_weight = pair_ref[...].astype(BF)
+    both = dot_nn(normed, pair_weight)
+    gate = both[:, :FF_TILE]
+    up = both[:, FF_TILE:]
     grad_act = dot_nt(out_cot_ref[...], down_ref[...])
     scale = 0.7978845608028654
     square = gate * gate
@@ -534,8 +526,9 @@
     activated = (curved * up).astype(BF)
     grad_gate = (grad_act * up * slope).astype(BF)
     grad_up = (grad_act * curved).astype(BF)
+    grad_pair = jnp.concatenate([grad_gate, grad_up], 1)
     branch = dot_nn(activated, down_ref[...])
-    back = dot_nt(grad_gate, gate_weight) + dot_nt(grad_up, up_weight)
+    back = dot_nt(grad_pair, pair_weight)
 
     @pl.when(step == 0)
     def _():
@@ -547,10 +540,9 @@
         branch_ref[...] += branch
         back_ref[...] += back
 
-    gate_grad_ref[...] = dot_nn(turned_ref[...], grad_gate).astype(gate_grad_ref.dtype)
-    part_pieces(gate_grad_ref, gate_sent_ref, gate_kept_ref, device, scatter_order[0])
-    up_grad_ref[...] = dot_nn(turned_ref[...], grad_up).astype(up_grad_ref.dtype)
-    part_pieces(up_grad_ref, up_sent_ref, up_kept_ref, device, scatter_order[1])
+    pair_grad_ref[...] = dot_nn(turned_ref[...], grad_pair).astype(pair_grad_ref.dtype)
+    part_pieces(pair_grad_ref, gate_sent_ref, gate_kept_ref, device, scatter_order[0])
+    part_pieces(pair_grad_ref, up_sent_ref, up_kept_ref, device, scatter_order[1], 0, FF_TILE)
     down_all_ref[here, :] = dot_tn(activated, out_cot_ref[...])
 
     @pl.when(step == pl.num_programs(0) - 1)
@@ -582,10 +574,10 @@
             gain_grad_ref[0:1, :] += jnp.sum(grad_normed * unit, 0, keepdims=True)
 
 
-def feed_forward(scalars, normed_two, out_cot, middle, gain_two, gate, up, down):
+def feed_forward(scalars, normed_two, out_cot, middle, gain_two, weights, up, down):
     tokens = normed_two.shape[0]
-    ff = gate[0].shape[2]
-    half, rows = gate[0].shape[:2]
+    half, rows, ff = up[0].shape
+    gate_at = 4 * D // FF_TILE
     down_rows = down[0].shape[1]
     once = pl.Buffered(1)
     full = lambda shape: pl.BlockSpec(shape, lambda i, c: (0,) * len(shape), pipeline_mode=once)
@@ -593,7 +585,7 @@
     shape = jax.ShapeDtypeStruct
     kernel = functools.partial(
         ffn_kernel,
-        gather_order=[gather_masks(kind) for kind in range(3)],
+        gather_order=[None, gather_masks(1), gather_masks(3)],
         scatter_order=[scatter_masks(kind) for kind in range(3)],
     )
     return pl.pallas_call(
@@ -606,8 +598,7 @@
                 full((tokens, D)),
                 full((tokens, D)),
                 full((8, D)),
-                tile,
-                tile,
+                pl.BlockSpec((D, FF_TILE), lambda i, c: (0, gate_at + i)),
                 tile,
                 tile,
                 full((half, down_rows, D)),
@@ -631,10 +622,8 @@
                 pltpu.VMEM((tokens, D), F32),
                 pltpu.VMEM((tokens, D), F32),
                 pltpu.VMEM((ff, D), F32),
-                pltpu.VMEM((D, FF_TILE), held_type(rows)),
-                pltpu.VMEM((D, FF_TILE), held_type(rows)),
-                pltpu.VMEM((D, FF_TILE), held_type(rows)),
-                pltpu.VMEM((D, FF_TILE), held_type(rows)),
+                pltpu.VMEM((D, 2 * FF_TILE), held_type(rows)),
+                pltpu.VMEM((D, 2 * FF_TILE), held_type(rows)),
                 pltpu.VMEM((FF_TILE, D), BF),
             ],
         ),
@@ -652,7 +641,7 @@
             flops=27_000_000_000, bytes_accessed=44_000_000, transcendentals=1_500_000
         ),
         name="feed_forward",
-    )(scalars, normed_two, out_cot, middle, gain_two, *gate, *up, *down)
+    )(scalars, normed_two, out_cot, middle, gain_two, weights, *up, *down)
 
 
 def add_histogram(split_ref, grad_ref, hist_ref, chosen_ref, keys):
@@ -1120,7 +1109,9 @@
     region = row_index * col_count + col_index
     device_count = row_count * col_count
 
-    packed_weights = jnp.concatenate([query_weight, key_weight, value_weight, output_weight], 1)
+    packed_weights = jnp.concatenate(
+        [query_weight, key_weight, value_weight, output_weight, gate_weight], 1
+    )
     weights = lax.all_gather(packed_weights, ("row", "col"), axis=0, tiled=True)
     small = jnp.stack(
         [attn_gain, ffn_gain]
@@ -1128,13 +1119,9 @@
         1,
     )
     small = jnp.pad(small, ((0, 0), (0, 128 - small.shape[1])))
-    small, gate_weight, up_weight, down_weight = after(
-        (small, gate_weight, up_weight, down_weight), packed_weights
-    )
+    small, up_weight, down_weight = after((small, up_weight, down_weight), packed_weights)
     small_gather = Gather(small, 0, True)
-    ffn_gathers = [
-        Gather(weight, kind) for kind, weight in enumerate((gate_weight, up_weight, down_weight))
-    ]
+    ffn_gathers = [Gather(up_weight, 1), Gather(down_weight, 3)]
 
     def turn(gathers, *done):
         for gather in gathers:
@@ -1234,9 +1221,9 @@
     ffn_weights = [(own, after(other, normed_two)) for own, other in ffn_weights]
     uneven = down_weight.shape[0] % 8 != 0
     if uneven:
-        order, core_mask = gather_masks(2)
+        order, core_mask = gather_masks(3)
         order = order + tuple(mask ^ core_mask for mask in order)
-        ffn_weights[2] = reordered(*ffn_weights[2], order, region)
+        ffn_weights[1] = reordered(*ffn_weights[1], order, region)
     (
         gate_sent,
         gate_kept,
@@ -1249,7 +1236,9 @@
         grad_attn,
         ffn_gain_part,
         row_stats,
-    ) = feed_forward(scalars, normed_two, out_cotangent, x_middle, gain_two, *ffn_weights)
+    ) = feed_forward(
+        scalars, normed_two, out_cotangent, x_middle, gain_two, weights, *ffn_weights
+    )
     if uneven:
         down_kept, down_sent = reordered(down_kept, down_sent, scatter_masks(2), region)
     ffn_chains = [
@@ -1314,21 +1303,22 @@
             jnp.sum(keep_float),
         ]
     )
-    small_chain = Summing(
-        jnp.concatenate(
-            [
-                jnp.pad(stat_part, (0, 124)),
-                ffn_gain_part[0],
-                attn_gain_part[0],
-                grad_table.reshape(-1),
-            ]
-        ).reshape(-1, 128)
-    )
+    small_part = jnp.concatenate(
+        [
+            jnp.pad(stat_part, (0, 124)),
+            ffn_gain_part[0],
+            attn_gain_part[0],
+            grad_table.reshape(-1),
+        ]
+    ).reshape(-1, 128)
+    small_rows = small_part.shape[0]
+    small_part = jnp.pad(small_part, ((0, 128 - small_rows), (0, 0)))
+    small_parts = lax.all_gather(small_part, ("row", "col"), axis=0, tiled=True)
+    summed = jnp.sum(small_parts.reshape(device_count, 128, 128)[:, :small_rows], 0).reshape(-1)
     rounds.land(lent)
     lent = lent.reshape(4, -1, D)
     back_above, back_below = shifted(lent[0:2], "row")
     back_left, back_right = shifted(lent[2:4], "col")
-    rounds.chains.append(small_chain)
     sent = rounds.send()
     returned = jnp.concatenate([back_above, back_below, back_left, back_right], 0)
     owner_lists = own_lists.reshape(-1)
@@ -1345,7 +1335,6 @@
     while rounds.chains:
         rounds.turn()
 
-    summed = small_chain.value.reshape(-1)
     residual_rms = jnp.sqrt(summed[:3] / (summed[3] * D))
     own_part = lambda at, size: lax.dynamic_slice_in_dim(summed, at + region * size, size)
     ffn_gain_grad = own_part(128, rows)

time: 531 us -> 510 us (0.960)
  local copies, waits for them, and re-layouts: 63.7 us -> 52.7 us
  other arithmetic: 87.3 us -> 77.5 us
  waiting for transfers between devices: 66.5 us -> 71.9 us
    unnamed x106 -> x95, local copies, waits for them, and re-layouts: 25.5 us -> 17.1 us
    concatenate x12 -> x9, other arithmetic: 16.2 us -> 8.34 us  [land(): self.held = jnp.concatenate([self.held, self.flight], 0)]
    ppermute x48 -> x38, starting transfers between devices: 75.1 us -> 69.8 us  [exchange(): return lax.ppermute(values, axis, pairs)]
    ppermute x48 -> x38, waiting for transfers between devices: 66.4 us -> 67.7 us  [exchange(): return lax.ppermute(values, axis, pairs)]
  transfers between devices with their start and end apart: 57 -> 48, of which waited for: 15 -> 11; matrix products, arithmetic and copies ran while one was open for 28% -> 26% of each run, Pallas kernels for 27% -> 28%
where the time goes in v2:
time: 510 us; the launch traced here: 504 us
  Pallas kernels  193 us (38%)
  starting transfers between devices  84.7 us (17%)
  other arithmetic  77.5 us (15%)
  waiting for transfers between devices  71.9 us (14%)
  local copies, waits for them, and re-layouts  52.7 us (10%)
  between operations  16.4 us (3%)
  matrix products  8.37 us (2%)
    ppermute x38, starting transfers between devices, exchange(): return lax.ppermute(values, axis, pairs)  69.8 us
    ppermute x38, waiting for transfers between devices, exchange(): return lax.ppermute(values, axis, pairs)  67.7 us
    pallas_call x1, Pallas kernels, feed_forward(): pl.pallas_call(kernel, grid_spec=pltpu.PrefetchScalarGridSpec(num_scalar_...  51.5 us
    pallas_call x2, Pallas kernels, attention_backward(): pl.pallas_call(functools.partial(backward_kernel, first_head=half * heads...  39.8 us
    convert_element_type x19, other arithmetic, land(): sum((part[half:2 * half].astype(F32) for part in self.parts)).astype(BF)  39.6 us
    pallas_call x2, Pallas kernels, layout_bias(): pl.pallas_call(functools.partial(bias_kernel, first_head=first_head), gri...  34.6 us
    pallas_call x1, Pallas kernels, attention_forward(): pl.pallas_call(attend_kernel, grid_spec=pltpu.PrefetchScalarGridSpec(num_...  27.8 us
    pallas_call x1, Pallas kernels, table_histogram(): pl.pallas_call(histogram_kernel, grid_spec=pltpu.PrefetchScalarGridSpec(n...  19.8 us
  transfers between devices with their start and end apart: 48, of which 11 were waited for; matrix products, arithmetic and copies ran while one was open for 26% of the time, Pallas kernels for 28%

profile of v2, /device:TPU:0, one launch (start us, length us, event | category | flops | bytes accessed | tf_op | source)
XLA Modules:
  0.0 504.2 jit_solution(15944729674183329158)
XLA Ops:
  14.5 4.1 collective-permute-start
  18.7 2.8 collective-permute-start.3
  32.8 3.1 gather_fusion.2
  42.4 3.4 collective-permute-start.8
  47.9 3.6 collective-permute-start.2
  56.9 3.2 multiply_add_fusion.codes_ref
  63.6 3.5 collective-permute-start.11
  67.2 2.5 fusion
  69.7 11.7 %collective-permute-done.5 = bf16[8,32,128]{2,1,0:T(8,128)(2,1)S(1)} collective-permute-done((bf16[8,32,128]{2,1,0:T(8,128)(2,1)S(1)}, bf16[8,32,128]{2,1,0:T(8,128)(2,1)S(1)}, u32[]{:S(2)}, u32[]{:S(2)}) %collective-permute-start.5) | collective-permute-done | bytes 65568 | tf_op jit(solution)/shard_map/ppermute | solution.py:78
  98.4 17.3 %layout_bias.2.low_bias_ref = f32[8,384,512]{2,1,0:T(8,128)} custom-call(s32[1024,512]{1,0:T(8,128)} %multiply_add_fusion.codes_ref, f32[48,128]{1,0:T(8,128)} %bitcast.126), custom_call_target="tpu_custom_call" | custom-call | flops 16000000000 | bytes 7000000 | tf_op jit(solution)/shard_map/layout_bias/pallas_call | solution.py:271
  119.1 10.3 %collective-permute-done.15 = bf16[4,88,1024]{2,1,0:T(8,128)(2,1)S(1)} collective-permute-done((bf16[4,88,1024]{2,1,0:T(8,128)(2,1)S(1)}, bf16[4,88,1024]{2,1,0:T(8,128)(2,1)S(1)}, u32[]{:S(2)}, u32[]{:S(2)}) %collective-permute-start.15) | collective-permute-done | bytes 720928 | tf_op jit(solution)/shard_map/ppermute | solution.py:78
  130.8 2.2 pad_maximum_fusion.1
  133.0 3.7 collective-permute-start.16
  136.7 2.2 pad_maximum_fusion
  142.6 17.3 %layout_bias.3.high_bias_ref = f32[8,384,512]{2,1,0:T(8,128)} custom-call(s32[1024,512]{1,0:T(8,128)} %multiply_add_fusion.codes_ref, f32[48,128]{1,0:T(8,128)} %bitcast.127), custom_call_target="tpu_custom_call" | custom-call | flops 16000000000 | bytes 7000000 | tf_op jit(solution)/shard_map/layout_bias/pallas_call | solution.py:271
  159.9 21.0 %collective-permute-done.16 = bf16[8,88,1024]{2,1,0:T(8,128)(2,1)S(1)} collective-permute-done((bf16[8,88,1024]{2,1,0:T(8,128)(2,1)}, bf16[8,88,1024]{2,1,0:T(8,128)(2,1)S(1)}, u32[]{:S(2)}, u32[]{:S(2)}) %collective-permute-start.16) | collective-permute-done | bytes 1441824 | tf_op jit(solution)/shard_map/ppermute | solution.py:78
  182.2 2.6 constant_dynamic-update-slice_fusion.21.up_own_ref
  191.0 27.8 %attention_forward.1 = (bf16[512,1024]{1,0:T(8,128)(2,1)}, bf16[1024,1024]{1,0:T(8,128)(2,1)}, bf16[1024,1024]{1,0:T(8,128)(2,1)}, bf16[1024,512]{1,0:T(8,128)(2...) custom-call(s32[2]{0:T(128)} %pad_add_fusion.1.count_ref.scalar_ref, ...), custom_call_target="tpu_custom_call" | custom-call | flops 20000000000 | bytes 50000000 | tf_op jit(solution)/shard_map/attention_forward/pallas_call | solution.py:414
  218.8 51.5 %feed_forward.1 = (bf16[16,32,2816]{2,1,0:T(8,128)(2,1)}, bf16[16,32,2816]{2,1,0:T(8,128)(2,1)}, bf16[16,32,2816]{2,1,0:T(8,128)(2,1)}, bf16[16,32,2816]{2,1,0:T...) custom-call(s32[2]{0:T(128)} %pad_add_fusion.1.count_ref.scalar_ref,, ...), custom_call_target="tpu_custom_call" | custom-call | flops 27000000512 | bytes 44000000 | tf_op jit(solution)/shard_map/feed_forward/pallas_call | solution.py:591
  272.6 2.6 copy.147.picked_turned_ref
  275.2 19.7 %attention_backward.2 = (bf16[512,512]{1,0:T(8,128)(2,1)}, bf16[1024,512]{1,0:T(8,128)(2,1)}, bf16[1024,512]{1,0:T(8,128)(2,1)}, bf16[8,384,512]{2,1,0:T(8,128)(...) custom-call(s32[2]{0:T(128)} %pad_add_fusion.1.count_ref.scalar_ref, ...), custom_call_target="tpu_custom_call" | custom-call | flops 15000000512 | bytes 30000000 | tf_op jit(solution)/shard_map/attention_backward/pallas_call | solution.py:828
  297.2 2.7 select_maximum_fusion
  299.9 3.2 add_convert_fusion
  304.9 3.0 add_convert_fusion.1
  311.7 20.1 %attention_backward.3 = (bf16[512,512]{1,0:T(8,128)(2,1)}, bf16[1024,512]{1,0:T(8,128)(2,1)}, bf16[1024,512]{1,0:T(8,128)(2,1)}, bf16[8,384,512]{2,1,0:T(8,128)(...) custom-call(s32[2]{0:T(128)} %pad_add_fusion.1.count_ref.scalar_ref, ...), custom_call_target="tpu_custom_call" | custom-call | flops 15000000512 | bytes 30000000 | tf_op jit(solution)/shard_map/attention_backward/pallas_call | solution.py:828
  331.9 2.9 add_convert_fusion.4
  337.1 4.5 collective-permute-done.23
  341.5 2.8 add_convert_fusion.5
  344.4 2.4 add_convert_fusion.6
  346.8 2.5 add_convert_fusion.7
  352.9 19.8 %table_histogram.1 = f32[96,256]{1,0:T(8,128)} custom-call(s32[2]{0:T(128)} %pad_add_fusion.1.count_ref.scalar_ref, s32[1024,512]{1,0:T(8,128)} %multiply_add_fusion.codes_ref, bf16[8,384,512]{2,1,0:T(8,128)(2,1)} %get-tuple-element.181.low_ref, bf16[8,384,512]{2,1,0:T(8,128)(2,1)} %get-tuple-element.182.high_ref), custom_call_target="tpu_custom_call" | custom-call | flops 20000000000 | bytes 8000000 | tf_op jit(solution)/shard_map/table_histogram/pallas_call | solution.py:924
  372.7 2.6 add_convert_fusion.9
  375.7 2.6 add_convert_fusion.3
  381.4 2.7 collective-permute-done.27
  386.5 13.8 %key_gradients.1 = (bf16[512,1024]{1,0:T(8,128)(2,1)}, f32[512,1024]{1,0:T(8,128)}, f32[8,1024]{1,0:T(8,128)}) custom-call(s32[2]{0:T(128)} %pad_add_fusion.1.count_ref.scalar_ref, bf16[512,512]{1,0:T(8,128)(2,1)} %get-tuple-element.160.dq_low_ref, bf16[512,512]{1,0:T(8,128)(2,1)} %get-tuple-element.169.dq_high_ref, ...), custom_call_target="tpu_custom_call" | custom-call | flops 8999999488 | bytes 18000000 | tf_op jit(solution)/shard_map/key_gradients/pallas_call | solution.py:1011
  400.3 2.2 fusion.30
  409.7 2.3 collective-permute-start.33
  415.5 3.5 collective-permute-start.38
  419.1 3.2 collective-permute-start.39
  422.2 4.1 collective-permute-done.34
  430.6 3.3 collective-permute-start.45
  438.4 9.9 %collective-permute-start.41 = (bf16[4,32,2048]{2,1,0:T(8,128)(2,1)}, bf16[4,32,2048]{2,1,0:T(8,128)(2,1)S(1)}, u32[]{:S(2)}, u32[]{:S(2)}) collective-permute-start(bf16[4,32,2048]{2,1,0:T(8,128)(2,1)} %add_convert_fusion.8), channel_id=1, source_target_pairs={{0,1},{1,0},{2,3},{3,2},{4,5},{5,4},{6,7},{7,6},{8,9},{9,8},{10,11... | collective-permute-start | bytes 1572872 | tf_op jit(solution)/shard_map/ppermute | solution.py:78
  448.9 5.5 %input_gradient.1 = bf16[512,1024]{1,0:T(8,128)(2,1)} custom-call(f32[512,1024]{1,0:T(8,128)} %get-tuple-element.190.own_ref, bf16[512,512]{1,0:T(8,128)(2,1)} %fusion.13.owner_ref, bf16[512,1024]{1,0:T(8,128)(2,1)} %pad_maximum_fusion.2.returned_ref, bf16[512,1024]{1,0:T(8,128)(2,1)} %x_ref.5, f32[8,1024]{1,0:T(8,128)} %broadcast_in_dim.28.gain_ref, ...), custom_call_target="tpu_custom_call" | custom-call | flops 1000000000 | bytes 8000000 | tf_op jit(solution)/shard_map/input_gradient/pallas_call | solution.py:1060
  455.7 4.5 collective-permute-start.40
  462.4 2.6 add_bitcast_fusion.1
  466.0 6.5 %collective-permute-start.42 = (bf16[2,32,2048]{2,1,0:T(8,128)(2,1)S(1)}, bf16[2,32,2048]{2,1,0:T(8,128)(2,1)S(1)}, u32[]{:S(2)}, u32[]{:S(2)}) collective-permute-start(bf16[2,32,2048]{2,1,0:T(8,128)(2,1)S(1)} %add_convert_fusion.13), channel_id=1, source_target_pairs={{0,8},{4,12},{8,0},{12,4},{16,24},{20,28},{24,16},{28,20},{1,9},{5... | collective-permute-start | bytes 786440 | tf_op jit(solution)/shard_map/ppermute | solution.py:78
  473.8 5.3 %collective-permute-done.42 = bf16[2,32,2048]{2,1,0:T(8,128)(2,1)S(1)} collective-permute-done((bf16[2,32,2048]{2,1,0:T(8,128)(2,1)S(1)}, bf16[2,32,2048]{2,1,0:T(8,128)(2,1)S(1)}, u32[]{:S(2)}, u32[]{:S(2)}) %collective-permute-start.42) | collective-permute-done | bytes 262176 | tf_op jit(solution)/shard_map/ppermute | solution.py:78
  481.7 7.7 %collective-permute-done.43 = bf16[1,32,2048]{2,1,0:T(8,128)(2,1)S(1)} collective-permute-done((bf16[1,32,2048]{2,1,0:T(8,128)(2,1)S(1)}, bf16[1,32,2048]{2,1,0:T(8,128)(2,1)S(1)}, u32[]{:S(2)}, u32[]{:S(2)}) %collective-permute-start.43) | collective-permute-done | bytes 131104 | tf_op jit(solution)/shard_map/ppermute | solution.py:78
  (284 shorter events, 125.3 us)
Async XLA Ops:
  7.2 183.2 %all-gather.3.cloned.1.call-start = ((), (), s32[]{:S(2)}) async-start(), calls=%async_computation | async-start | bytes 14598144 | tf_op jit(solution)/shard_map/all_gather | solution.py:1115
  12.4 480.7 %all-gather.5.cloned.1.call-start = ((), (), s32[]{:S(2)}) async-start(), calls=%async_computation.1 | async-start | bytes 2162688 | tf_op jit(solution)/shard_map/all_gather | solution.py:1316
  14.5 15.0 %collective-permute-start = (bf16[1,32,128]{1,2,0:T(8,128)(2,1)S(1)}, bf16[1,32,128]{1,2,0:T(8,128)(2,1)S(1)}, u32[]{:S(2)}, u32[]{:S(2)}) collective-permute-start(bf16[1,32,128]{1,2,0:T(8,128)(2,1)S(1)} %bitcast.123), channel_id=1, source_target_pairs={{0,16},{4,20},{8,24},{12,28},{16,0},{20,4},{24,8},{28,12},{1,17},{... | collective-permute-start | bytes 24584 | tf_op jit(solution)/shard_map/ppermute | solution.py:78
  18.6 27.8 %collective-permute-start.4 = (bf16[1,88,1024]{2,1,0:T(8,128)(2,1)}, bf16[1,88,1024]{2,1,0:T(8,128)(2,1)S(1)}, u32[]{:S(2)}, u32[]{:S(2)}) collective-permute-start(bf16[1,88,1024]{2,1,0:T(8,128)(2,1)} %bitcast.115), channel_id=1, source_target_pairs={{0,16},{4,20},{8,24},{12,28},{16,0},{20,4},{24,8},{28,12},{1,17},{... | collective-permute-start | bytes 540680 | tf_op jit(solution)/shard_map/ppermute | solution.py:78
  18.7 29.2 %collective-permute-start.3 = (bf16[1,32,2816]{2,1,0:T(8,128)(2,1)}, bf16[1,32,2816]{2,1,0:T(8,128)(2,1)S(1)}, u32[]{:S(2)}, u32[]{:S(2)}) collective-permute-start(bf16[1,32,2816]{2,1,0:T(8,128)(2,1)} %bitcast.119), channel_id=1, source_target_pairs={{0,16},{4,20},{8,24},{12,28},{16,0},{20,4},{24,8},{28,12},{1,17},{... | collective-permute-start | bytes 540680 | tf_op jit(solution)/shard_map/ppermute | solution.py:78
  29.7 12.7 %collective-permute-start.1 = (bf16[2,32,128]{2,1,0:T(8,128)(2,1)S(1)}, bf16[2,32,128]{2,1,0:T(8,128)(2,1)S(1)}, u32[]{:S(2)}, u32[]{:S(2)}) collective-permute-start(bf16[2,32,128]{2,1,0:T(8,128)(2,1)S(1)} %pad_maximum_fusion.15), channel_id=1, source_target_pairs={{0,8},{4,12},{8,0},{12,4},{16,24},{20,28},{24,16},{28,20},{1,9},{5... | collective-permute-start | bytes 49160 | tf_op jit(solution)/shard_map/ppermute | solution.py:78
  37.3 25.0 %collective-permute-start.6 = (bf16[128,1024]{1,0:T(8,128)(2,1)S(1)}, bf16[128,1024]{1,0:T(8,128)(2,1)S(1)}, u32[]{:S(2)}, u32[]{:S(2)}) collective-permute-start(bf16[128,1024]{1,0:T(8,128)(2,1)S(1)} %get-tuple-element.224), channel_id=1, source_target_pairs={{0,4},{4,8},{8,12},{12,16},{16,20},{20,24},{24,28},{1,5},{5,9},{9,... | collective-permute-start | bytes 786440 | tf_op jit(solution)/shard_map/ppermute | solution.py:35
  38.7 24.8 %collective-permute-start.7 = (bf16[128,1024]{1,0:T(8,128)(2,1)S(1)}, bf16[128,1024]{1,0:T(8,128)(2,1)S(1)}, u32[]{:S(2)}, u32[]{:S(2)}) collective-permute-start(bf16[128,1024]{1,0:T(8,128)(2,1)S(1)} %get-tuple-element.223), channel_id=1, source_target_pairs={{4,0},{8,4},{12,8},{16,12},{20,16},{24,20},{28,24},{5,1},{9,5},{13... | collective-permute-start | bytes 786440 | tf_op jit(solution)/shard_map/ppermute | solution.py:36
  42.4 24.7 %collective-permute-start.8 = (bf16[128,1024]{1,0:T(8,128)(2,1)S(1)}, bf16[128,1024]{1,0:T(8,128)(2,1)S(1)}, u32[]{:S(2)}, u32[]{:S(2)}) collective-permute-start(bf16[128,1024]{1,0:T(8,128)(2,1)S(1)} %get-tuple-element.222), channel_id=1, source_target_pairs={{0,1},{1,2},{2,3},{4,5},{5,6},{6,7},{8,9},{9,10},{10,11},{12,13},{... | collective-permute-start | bytes 786440 | tf_op jit(solution)/shard_map/ppermute | solution.py:35
  46.4 20.7 %collective-permute-start.9 = (bf16[128,1024]{1,0:T(8,128)(2,1)S(1)}, bf16[128,1024]{1,0:T(8,128)(2,1)S(1)}, u32[]{:S(2)}, u32[]{:S(2)}) collective-permute-start(bf16[128,1024]{1,0:T(8,128)(2,1)S(1)} %get-tuple-element.221), channel_id=1, source_target_pairs={{1,0},{2,1},{3,2},{5,4},{6,5},{7,6},{9,8},{10,9},{11,10},{13,12},{... | collective-permute-start | bytes 786440 | tf_op jit(solution)/shard_map/ppermute | solution.py:36
  47.9 13.0 %collective-permute-start.2 = (bf16[4,32,128]{2,1,0:T(8,128)(2,1)S(1)}, bf16[4,32,128]{2,1,0:T(8,128)(2,1)S(1)}, u32[]{:S(2)}, u32[]{:S(2)}) collective-permute-start(bf16[4,32,128]{2,1,0:T(8,128)(2,1)S(1)} %pad_maximum_fusion.14), channel_id=1, source_target_pairs={{0,2},{1,3},{2,0},{3,1},{4,6},{5,7},{6,4},{7,5},{8,10},{9,11},{10,... | collective-permute-start | bytes 98312 | tf_op jit(solution)/shard_map/ppermute | solution.py:78
  60.9 33.2 %collective-permute-start.13 = (bf16[2,88,1024]{2,1,0:T(8,128)(2,1)}, bf16[2,88,1024]{2,1,0:T(8,128)(2,1)}, u32[]{:S(2)}, u32[]{:S(2)}) collective-permute-start(bf16[2,88,1024]{2,1,0:T(8,128)(2,1)} %pad_maximum_fusion.7), channel_id=1, source_target_pairs={{0,1},{1,0},{2,3},{3,2},{4,5},{5,4},{6,7},{7,6},{8,9},{9,8},{10,11... | collective-permute-start | bytes 1081352 | tf_op jit(solution)/shard_map/ppermute | solution.py:78
  62.3 19.2 %collective-permute-start.5 = (bf16[8,32,128]{2,1,0:T(8,128)(2,1)S(1)}, bf16[8,32,128]{2,1,0:T(8,128)(2,1)S(1)}, u32[]{:S(2)}, u32[]{:S(2)}) collective-permute-start(bf16[8,32,128]{2,1,0:T(8,128)(2,1)S(1)} %pad_maximum_fusion.13), channel_id=1, source_target_pairs={{0,1},{1,0},{2,3},{3,2},{4,5},{5,4},{6,7},{7,6},{8,9},{9,8},{10,11... | collective-permute-start | bytes 196616 | tf_op jit(solution)/shard_map/ppermute | solution.py:78
  63.6 30.5 %collective-permute-start.11 = (bf16[2,32,2816]{2,1,0:T(8,128)(2,1)}, bf16[2,32,2816]{2,1,0:T(8,128)(2,1)}, u32[]{:S(2)}, u32[]{:S(2)}) collective-permute-start(bf16[2,32,2816]{2,1,0:T(8,128)(2,1)} %pad_maximum_fusion.6), channel_id=1, source_target_pairs={{0,8},{4,12},{8,0},{12,4},{16,24},{20,28},{24,16},{28,20},{1,9},{5... | collective-permute-start | bytes 1081352 | tf_op jit(solution)/shard_map/ppermute | solution.py:78
  82.1 1.3 collective-permute-start.10
  95.3 34.2 %collective-permute-start.15 = (bf16[4,88,1024]{2,1,0:T(8,128)(2,1)S(1)}, bf16[4,88,1024]{2,1,0:T(8,128)(2,1)S(1)}, u32[]{:S(2)}, u32[]{:S(2)}) collective-permute-start(bf16[4,88,1024]{2,1,0:T(8,128)(2,1)S(1)} %pad_maximum_fusion.4), channel_id=1, source_target_pairs={{0,2},{1,3},{2,0},{3,1},{4,6},{5,7},{6,4},{7,5},{8,10},{9,11},{10,... | collective-permute-start | bytes 2162696 | tf_op jit(solution)/shard_map/ppermute | solution.py:78
  96.6 34.2 %collective-permute-start.12 = (bf16[4,32,2816]{2,1,0:T(8,128)(2,1)S(1)}, bf16[4,32,2816]{2,1,0:T(8,128)(2,1)S(1)}, u32[]{:S(2)}, u32[]{:S(2)}) collective-permute-start(bf16[4,32,2816]{2,1,0:T(8,128)(2,1)S(1)} %pad_maximum_fusion.3), channel_id=1, source_target_pairs={{0,1},{1,0},{2,3},{3,2},{4,5},{5,4},{6,7},{7,6},{8,9},{9,8},{10,11... | collective-permute-start | bytes 2162696 | tf_op jit(solution)/shard_map/ppermute | solution.py:78
  133.0 47.9 %collective-permute-start.16 = (bf16[8,88,1024]{2,1,0:T(8,128)(2,1)}, bf16[8,88,1024]{2,1,0:T(8,128)(2,1)S(1)}, u32[]{:S(2)}, u32[]{:S(2)}) collective-permute-start(bf16[8,88,1024]{2,1,0:T(8,128)(2,1)} %pad_maximum_fusion.1), channel_id=1, source_target_pairs={{0,8},{4,12},{8,0},{12,4},{16,24},{20,28},{24,16},{28,20},{1,9},{5... | collective-permute-start | bytes 4325384 | tf_op jit(solution)/shard_map/ppermute | solution.py:78
  138.9 42.0 %collective-permute-start.14 = (bf16[8,32,2816]{2,1,0:T(8,128)(2,1)}, bf16[8,32,2816]{2,1,0:T(8,128)(2,1)}, u32[]{:S(2)}, u32[]{:S(2)}) collective-permute-start(bf16[8,32,2816]{2,1,0:T(8,128)(2,1)} %pad_maximum_fusion), channel_id=1, source_target_pairs={{0,2},{1,3},{2,0},{3,1},{4,6},{5,7},{6,4},{7,5},{8,10},{9,11},{10,... | collective-permute-start | bytes 4325384 | tf_op jit(solution)/shard_map/ppermute | solution.py:78
  182.2 36.7 %collective-permute-start.18 = (bf16[16,88,1024]{2,1,0:T(8,128)(2,1)}, bf16[16,88,1024]{2,1,0:T(8,128)(2,1)}, u32[]{:S(2)}, u32[]{:S(2)}) collective-permute-start(bf16[16,88,1024]{2,1,0:T(8,128)(2,1)} %constant_dynamic-update-slice_fusion.26.down_own_ref), channel_id=1, source_target_pairs={{0,4},{4,0},{8,12},{12,8},{16,20},{20,16},{24,28},{28,24},{1,5},{5... | collective-permute-start | bytes 8650760 | tf_op jit(solution)/shard_map/ppermute | solution.py:78
  184.8 34.0 %collective-permute-start.17 = (bf16[16,32,2816]{2,1,0:T(8,128)(2,1)}, bf16[16,32,2816]{2,1,0:T(8,128)(2,1)}, u32[]{:S(2)}, u32[]{:S(2)}) collective-permute-start(bf16[16,32,2816]{2,1,0:T(8,128)(2,1)} %constant_dynamic-update-slice_fusion.21.up_own_ref), channel_id=1, source_target_pairs={{0,4},{4,0},{8,12},{12,8},{16,20},{20,16},{24,28},{28,24},{1,5},{5... | collective-permute-start | bytes 8650760 | tf_op jit(solution)/shard_map/ppermute | solution.py:78
  270.4 29.5 %collective-permute-start.21 = (bf16[16,88,1024]{2,1,0:T(8,128)(2,1)}, bf16[16,88,1024]{2,1,0:T(8,128)(2,1)}, u32[]{:S(2)}, u32[]{:S(2)}) collective-permute-start(bf16[16,88,1024]{2,1,0:T(8,128)(2,1)} %get-tuple-element.152), channel_id=1, source_target_pairs={{0,4},{4,0},{8,12},{12,8},{16,20},{20,16},{24,28},{28,24},{1,5},{5... | collective-permute-start | bytes 8650760 | tf_op jit(solution)/shard_map/ppermute | solution.py:78
  270.5 29.4 %collective-permute-start.20 = (bf16[16,32,2816]{2,1,0:T(8,128)(2,1)}, bf16[16,32,2816]{2,1,0:T(8,128)(2,1)}, u32[]{:S(2)}, u32[]{:S(2)}) collective-permute-start(bf16[16,32,2816]{2,1,0:T(8,128)(2,1)} %get-tuple-element.151), channel_id=1, source_target_pairs={{0,4},{4,0},{8,12},{12,8},{16,20},{20,16},{24,28},{28,24},{1,5},{5... | collective-permute-start | bytes 8650760 | tf_op jit(solution)/shard_map/ppermute | solution.py:78
  271.0 28.9 %collective-permute-start.19 = (bf16[16,32,2816]{2,1,0:T(8,128)(2,1)}, bf16[16,32,2816]{2,1,0:T(8,128)(2,1)}, u32[]{:S(2)}, u32[]{:S(2)}) collective-permute-start(bf16[16,32,2816]{2,1,0:T(8,128)(2,1)} %get-tuple-element.150), channel_id=1, source_target_pairs={{0,4},{4,0},{8,12},{12,8},{16,20},{20,16},{24,28},{28,24},{1,5},{5... | collective-permute-start | bytes 8650760 | tf_op jit(solution)/shard_map/ppermute | solution.py:78
  294.9 36.8 %collective-permute-start.25 = (bf16[16,32,2048]{2,1,0:T(8,128)(2,1)}, bf16[16,32,2048]{2,1,0:T(8,128)(2,1)}, u32[]{:S(2)}, u32[]{:S(2)}) collective-permute-start(bf16[16,32,2048]{2,1,0:T(8,128)(2,1)} %get-tuple-element.167), channel_id=1, source_target_pairs={{0,4},{4,0},{8,12},{12,8},{16,20},{20,16},{24,28},{28,24},{1,5},{5... | collective-permute-start | bytes 6291464 | tf_op jit(solution)/shard_map/ppermute | solution.py:78
  303.1 33.9 %collective-permute-start.24 = (bf16[8,88,1024]{2,1,0:T(8,128)(2,1)}, bf16[8,88,1024]{2,1,0:T(8,128)(2,1)}, u32[]{:S(2)}, u32[]{:S(2)}) collective-permute-start(bf16[8,88,1024]{2,1,0:T(8,128)(2,1)} %add_convert_fusion), channel_id=1, source_target_pairs={{0,8},{4,12},{8,0},{12,4},{16,24},{20,28},{24,16},{28,20},{1,9},{5... | collective-permute-start | bytes 4325384 | tf_op jit(solution)/shard_map/ppermute | solution.py:78
  307.9 33.6 %collective-permute-start.23 = (bf16[8,32,2816]{2,1,0:T(8,128)(2,1)}, bf16[8,32,2816]{2,1,0:T(8,128)(2,1)}, u32[]{:S(2)}, u32[]{:S(2)}) collective-permute-start(bf16[8,32,2816]{2,1,0:T(8,128)(2,1)} %add_convert_fusion.1), channel_id=1, source_target_pairs={{0,2},{1,3},{2,0},{3,1},{4,6},{5,7},{6,4},{7,5},{8,10},{9,11},{10,... | collective-permute-start | bytes 4325384 | tf_op jit(solution)/shard_map/ppermute | solution.py:78
  311.2 35.6 %collective-permute-start.22 = (bf16[8,32,2816]{2,1,0:T(8,128)(2,1)S(1)}, bf16[8,32,2816]{2,1,0:T(8,128)(2,1)}, u32[]{:S(2)}, u32[]{:S(2)}) collective-permute-start(bf16[8,32,2816]{2,1,0:T(8,128)(2,1)S(1)} %add_convert_fusion.2), channel_id=1, source_target_pairs={{0,1},{1,0},{2,3},{3,2},{4,5},{5,4},{6,7},{7,6},{8,9},{9,8},{10,11... | collective-permute-start | bytes 4325384 | tf_op jit(solution)/shard_map/ppermute | solution.py:78
  331.8 43.9 %collective-permute-start.30 = (bf16[16,32,2048]{2,1,0:T(8,128)(2,1)}, bf16[16,32,2048]{2,1,0:T(8,128)(2,1)}, u32[]{:S(2)}, u32[]{:S(2)}) collective-permute-start(bf16[16,32,2048]{2,1,0:T(8,128)(2,1)} %get-tuple-element.179), channel_id=1, source_target_pairs={{0,4},{4,0},{8,12},{12,8},{16,20},{20,16},{24,28},{28,24},{1,5},{5... | collective-permute-start | bytes 6291464 | tf_op jit(solution)/shard_map/ppermute | solution.py:78
  334.8 37.9 %collective-permute-start.29 = (bf16[8,32,2048]{2,1,0:T(8,128)(2,1)}, bf16[8,32,2048]{2,1,0:T(8,128)(2,1)}, u32[]{:S(2)}, u32[]{:S(2)}) collective-permute-start(bf16[8,32,2048]{2,1,0:T(8,128)(2,1)} %add_convert_fusion.4), channel_id=1, source_target_pairs={{0,8},{4,12},{8,0},{12,4},{16,24},{20,28},{24,16},{28,20},{1,9},{5... | collective-permute-start | bytes 3145736 | tf_op jit(solution)/shard_map/ppermute | solution.py:78
  349.3 29.0 %collective-permute-start.28 = (bf16[4,88,1024]{2,1,0:T(8,128)(2,1)}, bf16[4,88,1024]{2,1,0:T(8,128)(2,1)}, u32[]{:S(2)}, u32[]{:S(2)}) collective-permute-start(bf16[4,88,1024]{2,1,0:T(8,128)(2,1)} %add_convert_fusion.5), channel_id=1, source_target_pairs={{0,1},{1,0},{2,3},{3,2},{4,5},{5,4},{6,7},{7,6},{8,9},{9,8},{10,11... | collective-permute-start | bytes 2162696 | tf_op jit(solution)/shard_map/ppermute | solution.py:78
  350.9 28.9 %collective-permute-start.26 = (bf16[4,32,2816]{2,1,0:T(8,128)(2,1)}, bf16[4,32,2816]{2,1,0:T(8,128)(2,1)S(1)}, u32[]{:S(2)}, u32[]{:S(2)}) collective-permute-start(bf16[4,32,2816]{2,1,0:T(8,128)(2,1)} %add_convert_fusion.7), channel_id=1, source_target_pairs={{0,2},{1,3},{2,0},{3,1},{4,6},{5,7},{6,4},{7,5},{8,10},{9,11},{10,... | collective-permute-start | bytes 2162696 | tf_op jit(solution)/shard_map/ppermute | solution.py:78
  351.3 32.7 %collective-permute-start.27 = (bf16[4,32,2816]{2,1,0:T(8,128)(2,1)}, bf16[4,32,2816]{2,1,0:T(8,128)(2,1)S(1)}, u32[]{:S(2)}, u32[]{:S(2)}) collective-permute-start(bf16[4,32,2816]{2,1,0:T(8,128)(2,1)} %add_convert_fusion.6), channel_id=1, source_target_pairs={{0,1},{1,0},{2,3},{3,2},{4,5},{5,4},{6,7},{7,6},{8,9},{9,8},{10,11... | collective-permute-start | bytes 2162696 | tf_op jit(solution)/shard_map/ppermute | solution.py:78
  375.2 32.9 %collective-permute-start.37 = (bf16[4,32,2048]{2,1,0:T(8,128)(2,1)}, bf16[4,32,2048]{2,1,0:T(8,128)(2,1)}, u32[]{:S(2)}, u32[]{:S(2)}) collective-permute-start(bf16[4,32,2048]{2,1,0:T(8,128)(2,1)} %add_convert_fusion.9), channel_id=1, source_target_pairs={{0,1},{1,0},{2,3},{3,2},{4,5},{5,4},{6,7},{7,6},{8,9},{9,8},{10,11... | collective-permute-start | bytes 1572872 | tf_op jit(solution)/shard_map/ppermute | solution.py:78
  402.6 9.5 %collective-permute-start.31 = (bf16[128,1024]{1,0:T(8,128)(2,1)}, bf16[128,1024]{1,0:T(8,128)(2,1)}, u32[]{:S(2)}, u32[]{:S(2)}) collective-permute-start(bf16[128,1024]{1,0:T(8,128)(2,1)} %get-tuple-element.217), channel_id=1, source_target_pairs={{0,4},{4,8},{8,12},{12,16},{16,20},{20,24},{24,28},{1,5},{5,9},{9,... | collective-permute-start | bytes 786440 | tf_op jit(solution)/shard_map/ppermute | solution.py:35
  404.9 23.5 %collective-permute-start.36 = (bf16[2,88,1024]{2,1,0:T(8,128)(2,1)S(1)}, bf16[2,88,1024]{2,1,0:T(8,128)(2,1)}, u32[]{:S(2)}, u32[]{:S(2)}) collective-permute-start(bf16[2,88,1024]{2,1,0:T(8,128)(2,1)S(1)} %add_convert_fusion.10), channel_id=1, source_target_pairs={{0,2},{1,3},{2,0},{3,1},{4,6},{5,7},{6,4},{7,5},{8,10},{9,11},{10,... | collective-permute-start | bytes 1081352 | tf_op jit(solution)/shard_map/ppermute | solution.py:78
  406.5 27.4 %collective-permute-start.35 = (bf16[2,32,5632]{2,1,0:T(8,128)(2,1)}, bf16[2,32,5632]{2,1,0:T(8,128)(2,1)}, u32[]{:S(2)}, u32[]{:S(2)}) collective-permute-start(bf16[2,32,5632]{2,1,0:T(8,128)(2,1)} %pad_maximum_fusion.5), channel_id=1, source_target_pairs={{0,8},{4,12},{8,0},{12,4},{16,24},{20,28},{24,16},{28,20},{1,9},{5... | collective-permute-start | bytes 2162696 | tf_op jit(solution)/shard_map/ppermute | solution.py:78
  408.2 7.4 %collective-permute-start.32 = (bf16[128,1024]{1,0:T(8,128)(2,1)}, bf16[128,1024]{1,0:T(8,128)(2,1)S(1)}, u32[]{:S(2)}, u32[]{:S(2)}) collective-permute-start(bf16[128,1024]{1,0:T(8,128)(2,1)} %get-tuple-element.220), channel_id=1, source_target_pairs={{4,0},{8,4},{12,8},{16,12},{20,16},{24,20},{28,24},{5,1},{9,5},{13... | collective-permute-start | bytes 786440 | tf_op jit(solution)/shard_map/ppermute | solution.py:36
  409.7 9.4 %collective-permute-start.33 = (bf16[128,1024]{1,0:T(8,128)(2,1)}, bf16[128,1024]{1,0:T(8,128)(2,1)S(1)}, u32[]{:S(2)}, u32[]{:S(2)}) collective-permute-start(bf16[128,1024]{1,0:T(8,128)(2,1)} %get-tuple-element.219), channel_id=1, source_target_pairs={{0,1},{1,2},{2,3},{4,5},{5,6},{6,7},{8,9},{9,10},{10,11},{12,13},{... | collective-permute-start | bytes 786440 | tf_op jit(solution)/shard_map/ppermute | solution.py:35
  412.1 14.3 %collective-permute-start.34 = (bf16[128,1024]{1,0:T(8,128)(2,1)}, bf16[128,1024]{1,0:T(8,128)(2,1)S(1)}, u32[]{:S(2)}, u32[]{:S(2)}) collective-permute-start(bf16[128,1024]{1,0:T(8,128)(2,1)} %get-tuple-element.218), channel_id=1, source_target_pairs={{1,0},{2,1},{3,2},{5,4},{6,5},{7,6},{9,8},{10,9},{11,10},{13,12},{... | collective-permute-start | bytes 786440 | tf_op jit(solution)/shard_map/ppermute | solution.py:36
  415.5 20.8 %collective-permute-start.38 = (bf16[8,32,2048]{2,1,0:T(8,128)(2,1)}, bf16[8,32,2048]{2,1,0:T(8,128)(2,1)S(1)}, u32[]{:S(2)}, u32[]{:S(2)}) collective-permute-start(bf16[8,32,2048]{2,1,0:T(8,128)(2,1)} %add_convert_fusion.3), channel_id=1, source_target_pairs={{0,2},{1,3},{2,0},{3,1},{4,6},{5,7},{6,4},{7,5},{8,10},{9,11},{10,... | collective-permute-start | bytes 3145736 | tf_op jit(solution)/shard_map/ppermute | solution.py:78
  419.1 35.3 %collective-permute-start.39 = (bf16[2,32,2048]{2,1,0:T(8,128)(2,1)}, bf16[2,32,2048]{2,1,0:T(8,128)(2,1)}, u32[]{:S(2)}, u32[]{:S(2)}) collective-permute-start(bf16[2,32,2048]{2,1,0:T(8,128)(2,1)} %add_convert_fusion.14), channel_id=1, source_target_pairs={{0,2},{1,3},{2,0},{3,1},{4,6},{5,7},{6,4},{7,5},{8,10},{9,11},{10,... | collective-permute-start | bytes 786440 | tf_op jit(solution)/shard_map/ppermute | solution.py:78
  430.6 25.1 %collective-permute-start.45 = (bf16[1,88,1024]{2,1,0:T(8,128)(2,1)}, bf16[1,88,1024]{2,1,0:T(8,128)(2,1)}, u32[]{:S(2)}, u32[]{:S(2)}) collective-permute-start(bf16[1,88,1024]{2,1,0:T(8,128)(2,1)} %add_convert_fusion.15), channel_id=1, source_target_pairs={{0,16},{4,20},{8,24},{12,28},{16,0},{20,4},{24,8},{28,12},{1,17},{... | collective-permute-start | bytes 540680 | tf_op jit(solution)/shard_map/ppermute | solution.py:78
  436.3 26.1 %collective-permute-start.44 = (bf16[1,32,5632]{2,1,0:T(8,128)(2,1)}, bf16[1,32,5632]{2,1,0:T(8,128)(2,1)}, u32[]{:S(2)}, u32[]{:S(2)}) collective-permute-start(bf16[1,32,5632]{2,1,0:T(8,128)(2,1)} %pad_maximum_fusion.8), channel_id=1, source_target_pairs={{0,16},{4,20},{8,24},{12,28},{16,0},{20,4},{24,8},{28,12},{1,17},{... | collective-permute-start | bytes 1081352 | tf_op jit(solution)/shard_map/ppermute | solution.py:78
  438.4 26.5 %collective-permute-start.41 = (bf16[4,32,2048]{2,1,0:T(8,128)(2,1)}, bf16[4,32,2048]{2,1,0:T(8,128)(2,1)S(1)}, u32[]{:S(2)}, u32[]{:S(2)}) collective-permute-start(bf16[4,32,2048]{2,1,0:T(8,128)(2,1)} %add_convert_fusion.8), channel_id=1, source_target_pairs={{0,1},{1,0},{2,3},{3,2},{4,5},{5,4},{6,7},{7,6},{8,9},{9,8},{10,11... | collective-permute-start | bytes 1572872 | tf_op jit(solution)/shard_map/ppermute | solution.py:78
  455.7 16.9 %collective-permute-start.40 = (bf16[1,32,2048]{2,1,0:T(8,128)(2,1)S(1)}, bf16[1,32,2048]{2,1,0:T(8,128)(2,1)S(1)}, u32[]{:S(2)}, u32[]{:S(2)}) collective-permute-start(bf16[1,32,2048]{2,1,0:T(8,128)(2,1)S(1)} %add_convert_fusion.19), channel_id=1, source_target_pairs={{0,16},{4,20},{8,24},{12,28},{16,0},{20,4},{24,8},{28,12},{1,17},{... | collective-permute-start | bytes 393224 | tf_op jit(solution)/shard_map/ppermute | solution.py:78
  466.0 13.1 %collective-permute-start.42 = (bf16[2,32,2048]{2,1,0:T(8,128)(2,1)S(1)}, bf16[2,32,2048]{2,1,0:T(8,128)(2,1)S(1)}, u32[]{:S(2)}, u32[]{:S(2)}) collective-permute-start(bf16[2,32,2048]{2,1,0:T(8,128)(2,1)S(1)} %add_convert_fusion.13), channel_id=1, source_target_pairs={{0,8},{4,12},{8,0},{12,4},{16,24},{20,28},{24,16},{28,20},{1,9},{5... | collective-permute-start | bytes 786440 | tf_op jit(solution)/shard_map/ppermute | solution.py:78
  480.1 9.4 %collective-permute-start.43 = (bf16[1,32,2048]{2,1,0:T(8,128)(2,1)S(1)}, bf16[1,32,2048]{2,1,0:T(8,128)(2,1)S(1)}, u32[]{:S(2)}, u32[]{:S(2)}) collective-permute-start(bf16[1,32,2048]{2,1,0:T(8,128)(2,1)S(1)} %add_convert_fusion.18), channel_id=1, source_target_pairs={{0,16},{4,20},{8,24},{12,28},{16,0},{20,4},{24,8},{28,12},{1,17},{... | collective-permute-start | bytes 393224 | tf_op jit(solution)/shard_map/ppermute | solution.py:78
  (37 other events, 482.2 us)
Sparse Core Ops, SparseCore 0:
  12.6 151.1 all-gather.2
  408.3 67.0 all-gather.4

commit v3 on v2

--- a/solution.py
+++ b/solution.py
@@ -104,18 +104,9 @@
 class Scatter:
     def __init__(self, sent, kept, kind):
         self.stages = stages_of(kind)
-        self.parts = [kept]
-        self.sent = sent
-
-    def land(self, flight):
-        self.parts.append(flight)
-        half = flight.shape[0] // 2
-        self.sent = None
-        if self.stages:
-            self.sent = sum(part[half : 2 * half].astype(F32) for part in self.parts).astype(BF)
-
-    def total(self):
-        return sum(part[0].astype(F32) for part in self.parts)
+        self.first = sent
+        self.parts = [(kept, 0)]
+        self.pieces, self.rows, self.width = sent.shape
 
 
 class Rounds:
@@ -124,36 +115,82 @@
         self.flights = []
 
     def land(self, *done):
+        landed = [flight for chains, flight in self.flights]
         for chains, flight in self.flights:
             if done:
                 flight = after(flight, *done)
-            at = 0
-            for chain in chains:
-                width = chain.sent.shape[-1]
-                chain.land(flight[..., at : at + width])
-                at += width
+            for number, chain in enumerate(chains):
+                chain.parts.append((flight, number * chain.width))
         self.flights = []
-        self.chains = [chain for chain in self.chains if chain.sent is not None]
+        self.chains = [chain for chain in self.chains if chain.stages]
+        return landed
 
     def send(self):
-        groups = {}
+        sums, firsts = {}, []
         for chain in self.chains:
-            alone = id(chain) if chain.sent.shape[0] > 4 else 0
-            alike = (chain.stages.pop(0), chain.sent.shape[:-1], alone)
-            groups.setdefault(alike, []).append(chain)
-        sent = []
-        for (stage, *_), chains in groups.items():
-            values = [chain.sent for chain in chains]
-            values = jnp.concatenate(values, -1) if len(values) > 1 else values[0]
-            self.flights.append((chains, exchange(values, stage)))
-            sent.append(values)
-        return sent
+            stage = chain.stages.pop(0)
+            if chain.first is not None:
+                firsts.append(([chain], stage, chain.first))
+                chain.first = None
+            else:
+                chain.pieces //= 2
+                alike = (stage, chain.pieces, chain.rows, chain.width)
+                sums.setdefault(alike, []).append(chain)
+        sent = firsts
+        if sums:
+            values = piece_sums(list(sums.values()), True, BF)
+            sent = sent + [
+                (chains, alike[0], value)
+                for (alike, chains), value in zip(sums.items(), values)
+            ]
+        for chains, stage, value in sent:
+            self.flights.append((chains, exchange(value, stage)))
+        return [value for chains, stage, value in sent]
 
     def turn(self, *done):
         self.land(*done)
         return self.send()
 
 
+def sum_kernel(*refs, shares):
+    refs = list(refs)
+    outputs = refs[len(refs) - len(shares) :]
+    for out_ref, (counts, width) in zip(outputs, shares):
+        for number, count in enumerate(counts):
+            total = refs.pop(0)[...].astype(F32)
+            for _ in range(count - 1):
+                total = total + refs.pop(0)[...].astype(F32)
+            out_ref[:, :, number * width : (number + 1) * width] = total.astype(out_ref.dtype)
+
+
+def piece_sums(groups, upper, dtype):
+    steps = min([4] + [chains[0].pieces for chains in groups]) if upper else 1
+    arrays, in_specs, out_specs, out_shape, shares = [], [], [], [], []
+    for chains in groups:
+        pieces, rows, width = chains[0].pieces, chains[0].rows, chains[0].width
+        block = pieces // steps if upper else 1
+        for chain in chains:
+            for array, column in chain.parts:
+                arrays.append(array)
+                place = lambda i, lane=column // width: (steps + i if upper else 0, 0, lane)
+                in_specs.append(pl.BlockSpec((block, rows, width), place))
+        total = len(chains) * width
+        out_specs.append(pl.BlockSpec((block, rows, total), lambda i: (i, 0, 0)))
+        out_shape.append(jax.ShapeDtypeStruct((block * steps, rows, total), dtype))
+        shares.append(([len(chain.parts) for chain in chains], width))
+    moved = sum(2 * spec.block_shape[0] * spec.block_shape[1] * spec.block_shape[2] * steps for spec in in_specs)
+    return pl.pallas_call(
+        functools.partial(sum_kernel, shares=shares),
+        grid=(steps,),
+        in_specs=in_specs,
+        out_specs=out_specs,
+        out_shape=out_shape,
+        compiler_params=pltpu.CompilerParams(vmem_limit_bytes=VMEM_LIMIT),
+        cost_estimate=pl.CostEstimate(flops=moved, bytes_accessed=2 * moved, transcendentals=0),
+        name="piece_sums",
+    )(*arrays)
+
+
 def dot_nn(left, right):
     return lax.dot_general(left, right, (((1,), (0,)), ((), ())), preferred_element_type=F32)
 
@@ -164,6 +201,33 @@
 
 def dot_tn(left, right):
     return lax.dot_general(left, right, (((0,), (0,)), ((), ())), preferred_element_type=F32)
+
+
+def pack_kernel(*refs):
+    *sources, down_ref, out_ref = refs
+    at = 0
+    for source_ref in sources:
+        width = source_ref.shape[1]
+        out_ref[:, at : at + width] = source_ref[...]
+        at += width
+    down = down_ref[...].astype(F32)
+    for b in range(down.shape[0] // 8):
+        blocks = [down[8 * b : 8 * b + 8, a * 256 : (a + 1) * 256] for a in range(D // 256)]
+        out_ref[:, at + b * 256 : at + (b + 1) * 256] = jnp.concatenate(blocks, 0).astype(BF)
+
+
+def pack_shards(sources, down):
+    rows = sources[0].shape[0]
+    widths = [source.shape[1] for source in sources]
+    total = sum(widths) + down.shape[0] * D // rows
+    if down.shape[0] % 8 != 0 or rows * 256 != 8 * D:
+        return jnp.concatenate(list(sources) + [down.reshape(rows, -1)], 1)
+    return pl.pallas_call(
+        pack_kernel,
+        out_shape=jax.ShapeDtypeStruct((rows, total), BF),
+        compiler_params=pltpu.CompilerParams(vmem_limit_bytes=VMEM_LIMIT),
+        name="pack_shards",
+    )(*sources, down)
 
 
 LANE_GATHER = lax.GatherDimensionNumbers(
@@ -470,11 +534,10 @@
     out_cot_ref,
     mid_ref,
     gain_ref,
+    keep_ref,
     gate_ref,
-    up_own_ref,
-    up_other_ref,
-    down_own_ref,
-    down_other_ref,
+    up_ref,
+    packed_ref,
     gate_sent_ref,
     gate_kept_ref,
     up_sent_ref,
@@ -485,16 +548,16 @@
     middle_grad_ref,
     attn_grad_ref,
     gain_grad_ref,
-    stat_ref,
     turned_ref,
     branch_ref,
     back_ref,
     down_all_ref,
-    pair_ref,
-    pair_grad_ref,
+    gate_grad_ref,
+    up_grad_ref,
     down_ref,
+    landed_ref,
+    landed_sem,
     *,
-    gather_order,
     scatter_order,
 ):
     step = pl.program_id(0)
@@ -503,19 +566,35 @@
 
     @pl.when(step == 0)
     def _():
+        if landed_ref.shape[0] == D:
+            at = packed_ref.shape[1] - landed_ref.shape[1]
+            source_ref = packed_ref.at[:, at:]
+        else:
+            source_ref = packed_ref
+        copy = pltpu.make_async_copy(source_ref, landed_ref, landed_sem)
+        copy.start()
         turned_ref[...] = normed_ref[...].T
-        join_pieces(down_own_ref, down_other_ref, down_all_ref, down_device, *gather_order[2])
-
-    pair_ref[:, :FF_TILE] = gate_ref[...].astype(pair_ref.dtype)
-    join_pieces(up_own_ref, up_other_ref, pair_ref, device, *gather_order[1], FF_TILE)
+        copy.wait()
+        if landed_ref.shape[0] != D:
+            down_all_ref[...] = landed_ref[...].astype(F32)
+        else:
+            height = landed_ref.shape[1] // 32
+            for d in range(D // 32):
+                for b in range(height // 8):
+                    block = landed_ref[d * 32 : (d + 1) * 32, b * 256 : (b + 1) * 256].astype(F32)
+                    rows = slice(d * height + 8 * b, d * height + 8 * b + 8)
+                    for a in range(D // 256):
+                        lanes = slice(a * 256, (a + 1) * 256)
+                        down_all_ref[rows, lanes] = block[8 * a : 8 * a + 8]
+        branch_ref[...] = jnp.zeros_like(branch_ref)
+        back_ref[...] = jnp.zeros_like(back_ref)
+
     here = pl.ds(pl.multiple_of(step * FF_TILE, FF_TILE), FF_TILE)
     down_ref[...] = down_all_ref[here, :].astype(BF)
 
     normed = normed_ref[...]
-    pair_weight = pair_ref[...].astype(BF)
-    both = dot_nn(normed, pair_weight)
-    gate = both[:, :FF_TILE]
-    up = both[:, FF_TILE:]
+    gate = dot_nn(normed, gate_ref[...])
+    up = dot_nn(normed, up_ref[...])
     grad_act = dot_nt(out_cot_ref[...], down_ref[...])
     scale = 0.7978845608028654
     square = gate * gate
@@ -526,23 +605,12 @@
     activated = (curved * up).astype(BF)
     grad_gate = (grad_act * up * slope).astype(BF)
     grad_up = (grad_act * curved).astype(BF)
-    grad_pair = jnp.concatenate([grad_gate, grad_up], 1)
-    branch = dot_nn(activated, down_ref[...])
-    back = dot_nt(grad_pair, pair_weight)
-
-    @pl.when(step == 0)
-    def _():
-        branch_ref[...] = branch
-        back_ref[...] = back
-
-    @pl.when(step > 0)
-    def _():
-        branch_ref[...] += branch
-        back_ref[...] += back
-
-    pair_grad_ref[...] = dot_nn(turned_ref[...], grad_pair).astype(pair_grad_ref.dtype)
-    part_pieces(pair_grad_ref, gate_sent_ref, gate_kept_ref, device, scatter_order[0])
-    part_pieces(pair_grad_ref, up_sent_ref, up_kept_ref, device, scatter_order[1], 0, FF_TILE)
+    branch_ref[...] += dot_nn(activated, down_ref[...])
+    back_ref[...] += dot_nt(grad_gate, gate_ref[...]) + dot_nt(grad_up, up_ref[...])
+    gate_grad_ref[...] = dot_nn(turned_ref[...], grad_gate).astype(gate_grad_ref.dtype)
+    part_pieces(gate_grad_ref, gate_sent_ref, gate_kept_ref, device, scatter_order[0])
+    up_grad_ref[...] = dot_nn(turned_ref[...], grad_up).astype(up_grad_ref.dtype)
+    part_pieces(up_grad_ref, up_sent_ref, up_kept_ref, device, scatter_order[1])
     down_all_ref[here, :] = dot_tn(activated, out_cot_ref[...])
 
     @pl.when(step == pl.num_programs(0) - 1)
@@ -562,7 +630,8 @@
             layer_ref[rows, :] = final.astype(BF)
             mid_sum = jnp.sum(middle * middle, -1, keepdims=True)
             final_sum = jnp.sum(final * final, -1, keepdims=True)
-            stat_ref[rows, :] = jnp.where(lane == 0, mid_sum, final_sum)
+            sums = jnp.where(lane == 1, mid_sum, jnp.where(lane == 2, final_sum, 1.0))
+            gain_grad_ref[1:2, :128] += jnp.sum(keep_ref[rows, :] * sums, 0, keepdims=True)
             inverse = lax.rsqrt(mid_sum * (1.0 / D) + EPS)
             unit = middle * inverse
             grad_normed = back_ref[rows, :]
@@ -574,18 +643,20 @@
             gain_grad_ref[0:1, :] += jnp.sum(grad_normed * unit, 0, keepdims=True)
 
 
-def feed_forward(scalars, normed_two, out_cot, middle, gain_two, weights, up, down):
+def feed_forward(scalars, normed_two, out_cot, middle, gain_two, keep, weights, down):
     tokens = normed_two.shape[0]
-    half, rows, ff = up[0].shape
+    ff = (weights.shape[1] - 4 * D) // 3
+    half = lax.axis_size("row") * lax.axis_size("col") // 2
+    down_rows = ff // (2 * half)
+    rows = D // (2 * half)
     gate_at = 4 * D // FF_TILE
-    down_rows = down[0].shape[1]
+    up_at = gate_at + ff // FF_TILE
     once = pl.Buffered(1)
     full = lambda shape: pl.BlockSpec(shape, lambda i, c: (0,) * len(shape), pipeline_mode=once)
     tile = pl.BlockSpec((half, rows, FF_TILE), lambda i, c: (0, 0, i))
     shape = jax.ShapeDtypeStruct
     kernel = functools.partial(
         ffn_kernel,
-        gather_order=[None, gather_masks(1), gather_masks(3)],
         scatter_order=[scatter_masks(kind) for kind in range(3)],
     )
     return pl.pallas_call(
@@ -598,11 +669,10 @@
                 full((tokens, D)),
                 full((tokens, D)),
                 full((8, D)),
+                full((tokens, 128)),
                 pl.BlockSpec((D, FF_TILE), lambda i, c: (0, gate_at + i)),
-                tile,
-                tile,
-                full((half, down_rows, D)),
-                full((half, down_rows, D)),
+                pl.BlockSpec((D, FF_TILE), lambda i, c: (0, up_at + i)),
+                pl.BlockSpec(memory_space=pl.ANY),
             ],
             out_specs=[
                 tile,
@@ -615,16 +685,17 @@
                 full((tokens, D)),
                 full((tokens, D)),
                 full((8, D)),
-                full((tokens, 128)),
             ],
             scratch_shapes=[
                 pltpu.VMEM((D, tokens), BF),
                 pltpu.VMEM((tokens, D), F32),
                 pltpu.VMEM((tokens, D), F32),
                 pltpu.VMEM((ff, D), F32),
-                pltpu.VMEM((D, 2 * FF_TILE), held_type(rows)),
-                pltpu.VMEM((D, 2 * FF_TILE), held_type(rows)),
+                pltpu.VMEM((D, FF_TILE), held_type(rows)),
+                pltpu.VMEM((D, FF_TILE), held_type(rows)),
                 pltpu.VMEM((FF_TILE, D), BF),
+                pltpu.VMEM((ff, D) if down is not None else (D, ff), BF),
+                pltpu.SemaphoreType.DMA(()),
             ],
         ),
         out_shape=[shape((half, rows, ff), BF)] * 4
@@ -634,14 +705,13 @@
             shape((tokens, D), F32),
             shape((tokens, D), BF),
             shape((8, D), F32),
-            shape((tokens, 128), F32),
         ],
         compiler_params=pltpu.CompilerParams(vmem_limit_bytes=VMEM_LIMIT),
         cost_estimate=pl.CostEstimate(
             flops=27_000_000_000, bytes_accessed=44_000_000, transcendentals=1_500_000
         ),
         name="feed_forward",
-    )(scalars, normed_two, out_cot, middle, gain_two, weights, *up, *down)
+    )(scalars, normed_two, out_cot, middle, gain_two, keep, weights, weights, weights if down is None else down)
 
 
 def add_histogram(split_ref, grad_ref, hist_ref, chosen_ref, keys):
@@ -683,8 +753,8 @@
     prob_ref,
     codes_ref,
     table_ref,
-    normed_turned_ref,
-    picked_turned_ref,
+    normed_ref,
+    picked_ref,
     mixed_ref,
     dq_ref,
     dk_ref,
@@ -781,15 +851,15 @@
         part_pieces(joined_ref, sent_ref, kept_ref, count_ref[1], scatter_order, at)
 
     def finish(keys):
-        leave(1, dot_nn(picked_turned_ref[:, 0:keys], dk_ref[0:keys, :]))
-        leave(2, dot_nn(picked_turned_ref[:, 0:keys], dv_ref[0:keys, :]))
+        leave(1, dot_tn(picked_ref[0:keys, :], dk_ref[0:keys, :]))
+        leave(2, dot_tn(picked_ref[0:keys, :], dv_ref[0:keys, :]))
 
     @pl.when(step == pl.num_programs(0) - 1)
     def _():
         dk_ref[...] = dk_sum_ref[...].astype(BF)
         dv_ref[...] = dv_sum_ref[...].astype(BF)
         dq_ref[...] = dq_turned_ref[...].T
-        leave(0, dot_nn(normed_turned_ref[...], dq_ref[...]))
+        leave(0, dot_tn(normed_ref[...], dq_ref[...]))
         first = first_head * HEAD_DIM
         leave(3, dot_nn(mixed_ref[...], attn_grad_ref[:, first : first + heads * HEAD_DIM]))
         take_histogram(hist_ref, hist_out_ref)
@@ -810,8 +880,8 @@
     probs,
     codes,
     table_lanes,
-    normed_turned,
-    picked_turned,
+    normed,
+    picked,
     mixed,
 ):
     tokens = queries.shape[0]
@@ -844,8 +914,8 @@
                 pl.BlockSpec((heads, FEW, COLS), lambda i, c: (half, 0, i)),
                 across(key_total),
                 full(table_lanes.shape),
-                full((D, tokens)),
-                full((D, key_total)),
+                full((tokens, D)),
+                full((key_total, D)),
                 full((D, tokens)),
             ],
             out_specs=[
@@ -896,8 +966,8 @@
         probs,
         codes,
         table_lanes,
-        normed_turned,
-        picked_turned,
+        normed,
+        picked,
         mixed,
     )
 
@@ -1109,8 +1179,9 @@
     region = row_index * col_count + col_index
     device_count = row_count * col_count
 
-    packed_weights = jnp.concatenate(
-        [query_weight, key_weight, value_weight, output_weight, gate_weight], 1
+    packed_weights = pack_shards(
+        (query_weight, key_weight, value_weight, output_weight, gate_weight, up_weight),
+        down_weight,
     )
     weights = lax.all_gather(packed_weights, ("row", "col"), axis=0, tiled=True)
     small = jnp.stack(
@@ -1118,17 +1189,15 @@
         + [jnp.pad(t, (0, rows - table_share)) for t in (relative_table, horiz_table, vert_table)],
         1,
     )
-    small = jnp.pad(small, ((0, 0), (0, 128 - small.shape[1])))
-    small, up_weight, down_weight = after((small, up_weight, down_weight), packed_weights)
+    small = after(jnp.pad(small, ((0, 0), (0, 128 - small.shape[1]))), packed_weights)
     small_gather = Gather(small, 0, True)
-    ffn_gathers = [Gather(up_weight, 1), Gather(down_weight, 3)]
 
     def turn(gathers, *done):
         for gather in gathers:
             gather.land(*done)
         return [gather.send() for gather in gathers]
 
-    sent = turn([small_gather] + ffn_gathers)
+    sent = turn([small_gather])
 
     halo_rows, key_keep, x_early = after((halo_rows, key_keep, hidden_in), sent)
     own_lists = lax.dynamic_index_in_dim(halo_rows, region, 0, keepdims=False)
@@ -1155,7 +1224,7 @@
     slots = jnp.arange(key_total, dtype=jnp.int32)
     pack = ((place[:, None] == slots) & (key_mask[:, None] > 0)).astype(BF)
 
-    sent = turn([small_gather] + ffn_gathers, pack)
+    sent = turn([small_gather], pack)
     packed_by, relative_bucket = after((pack, relative_bucket), sent)
     found = [
         lax.dot_general(
@@ -1173,7 +1242,6 @@
     turn([small_gather], picked_x)
     while small_gather.flight is not None:
         turn([small_gather])
-    sent = turn(ffn_gathers, small_gather.held)
     small_masks = [0]
     for stage in stages_of(0)[::-1]:
         small_masks = small_masks + [mask ^ mask_of(stage) for mask in small_masks]
@@ -1193,20 +1261,17 @@
     gain_one = gain_attn.astype(F32)
     gain_two = jnp.broadcast_to(gain_ffn.astype(F32), (8, D))
 
-    low_bias = layout_bias(after(codes, sent), table_lanes, 0)
-    sent = turn(ffn_gathers, low_bias)
-    high_bias = layout_bias(after(codes, sent, low_bias), table_lanes, HEADS // 2)
+    low_bias = layout_bias(codes, table_lanes, 0)
+    high_bias = layout_bias(after(codes, low_bias), table_lanes, HEADS // 2)
     x_input = hidden_in.astype(F32)
     normed_one = norm_rows(x_input, gain_one).astype(BF)
     picked = norm_rows(picked_x.astype(F32), gain_one).astype(BF)
-    normed_turned = normed_one.T
-    picked_turned = picked.T
-    turn(ffn_gathers, high_bias, picked_turned, normed_turned)
-    while any(gather.flight is not None for gather in ffn_gathers):
-        turn(ffn_gathers)
-    gathered = [gather.held for gather in ffn_gathers]
-    ffn_weights = [(held, exchange(held, ("row", 0))) for held in gathered]
-    normed_one = after(normed_one, gathered, normed_turned, picked_turned)
+    owner_lists = own_lists.reshape(-1)
+    owner = (jnp.arange(tokens, dtype=jnp.int32)[:, None] == owner_lists).astype(BF)
+    x_sum = jnp.sum(x_input * x_input, -1, keepdims=True)
+    lanes = jnp.arange(128, dtype=jnp.int32)
+    keep = own_keep.astype(F32)[:, None] * jnp.where(lanes == 0, x_sum, 1.0)
+    weights = after(weights, high_bias, normed_one, picked, owner, keep)
     queries, keys, values, mixed, lse, probs, x_middle, normed_two = attention_forward(
         scalars,
         normed_one,
@@ -1218,12 +1283,8 @@
         hidden_in,
         gain_two,
     )
-    ffn_weights = [(own, after(other, normed_two)) for own, other in ffn_weights]
-    uneven = down_weight.shape[0] % 8 != 0
-    if uneven:
-        order, core_mask = gather_masks(3)
-        order = order + tuple(mask ^ core_mask for mask in order)
-        ffn_weights[1] = reordered(*ffn_weights[1], order, region)
+    uneven = down_weight.shape[0] % 8 != 0 or rows * 256 != 8 * D
+    down = weights[:, weights.shape[1] - gate_weight.shape[1] :].reshape(-1, D) if uneven else None
     (
         gate_sent,
         gate_kept,
@@ -1234,12 +1295,11 @@
         layer_out,
         grad_middle,
         grad_attn,
-        ffn_gain_part,
-        row_stats,
+        ffn_small,
     ) = feed_forward(
-        scalars, normed_two, out_cotangent, x_middle, gain_two, weights, *ffn_weights
+        scalars, normed_two, out_cotangent, x_middle, gain_two, keep, weights, down
     )
-    if uneven:
+    if down_weight.shape[0] % 8 != 0:
         down_kept, down_sent = reordered(down_kept, down_sent, scatter_masks(2), region)
     ffn_chains = [
         Scatter(gate_sent, gate_kept, 0),
@@ -1263,8 +1323,8 @@
             probs,
             codes,
             table_lanes,
-            normed_turned,
-            picked_turned,
+            normed_one,
+            picked,
             mixed,
         )
 
@@ -1294,39 +1354,29 @@
     )
     hist = short_hist + jnp.concatenate([low_half[4], high_half[4]], 1)
     grad_table = jnp.sum(hist.reshape(TABLES * BUCKETS, HEADS, HIST_ROWS), -1)
-    keep_float = own_keep.astype(F32)
-    stat_part = jnp.stack(
-        [
-            jnp.sum(keep_float * jnp.sum(x_input * x_input, -1)),
-            jnp.sum(keep_float * row_stats[:, 0]),
-            jnp.sum(keep_float * row_stats[:, 1]),
-            jnp.sum(keep_float),
-        ]
-    )
     small_part = jnp.concatenate(
         [
-            jnp.pad(stat_part, (0, 124)),
-            ffn_gain_part[0],
+            ffn_small[1, :128],
+            ffn_small[0],
             attn_gain_part[0],
             grad_table.reshape(-1),
         ]
     ).reshape(-1, 128)
     small_rows = small_part.shape[0]
     small_part = jnp.pad(small_part, ((0, 128 - small_rows), (0, 0)))
-    small_parts = lax.all_gather(small_part, ("row", "col"), axis=0, tiled=True)
-    summed = jnp.sum(small_parts.reshape(device_count, 128, 128)[:, :small_rows], 0).reshape(-1)
-    rounds.land(lent)
-    lent = lent.reshape(4, -1, D)
+    landed = rounds.land(lent)
+    small_parts = lax.all_gather(after(small_part, landed), ("row", "col"), axis=0, tiled=True)
+    sent = rounds.send()
+    lent = after(lent, sent).reshape(4, -1, D)
     back_above, back_below = shifted(lent[0:2], "row")
     back_left, back_right = shifted(lent[2:4], "col")
+    returned = jnp.concatenate([back_above, back_below, back_left, back_right], 0)
+    landed = rounds.land()
     sent = rounds.send()
-    returned = jnp.concatenate([back_above, back_below, back_left, back_right], 0)
-    owner_lists = own_lists.reshape(-1)
-    owner = (jnp.arange(tokens, dtype=jnp.int32)[:, None] == owner_lists).astype(BF)
     input_grad = input_gradient(
         own_grads,
         owner,
-        after(returned, sent),
+        after(returned, landed, sent),
         hidden_in,
         jnp.broadcast_to(gain_one, (8, D)),
         grad_middle,
@@ -1334,6 +1384,7 @@
     rounds.turn(input_grad)
     while rounds.chains:
         rounds.turn()
+    summed = jnp.sum(small_parts.reshape(device_count, 128, 128)[:, :small_rows], 0).reshape(-1)
 
     residual_rms = jnp.sqrt(summed[:3] / (summed[3] * D))
     own_part = lambda at, size: lax.dynamic_slice_in_dim(summed, at + region * size, size)
@@ -1341,8 +1392,12 @@
     attn_gain_grad = own_part(128 + D, rows)
     table_at = 128 + 2 * D
     table_grads = [own_part(table_at + t * BUCKETS * HEADS, table_share) for t in range(TABLES)]
-    gate_grad, up_grad, down_grad = [chain.total() for chain in ffn_chains]
-    sides = [low_chain.total(), high_chain.total()]
+    gate_grad, up_grad, down_grad = [
+        total[0] for total in piece_sums([[chain] for chain in ffn_chains], False, F32)
+    ]
+    sides = [
+        total[0] for total in piece_sums([[low_chain], [high_chain]], False, F32)
+    ]
     width = D // 2
     query_grad, key_grad, value_grad, output_grad = [
         jnp.concatenate([side[:, i * width : (i + 1) * width] for side in sides], 1)

time: 510 us -> 484 us (0.949)
  other arithmetic: 77.5 us -> 16 us
  waiting for transfers between devices: 71.9 us -> 127 us
  starting transfers between devices: 84.7 us -> 53.2 us
  Pallas kernels: 193 us -> 220 us
  local copies, waits for them, and re-layouts: 52.7 us -> 36.5 us
    all_gather x1, waiting for transfers between devices: 0.01 us -> 70.4 us  [on_device(): weights = lax.all_gather(packed_weights, ('row', 'col'), axis=0, tiled=True)]
    convert_element_type x19 -> x2, other arithmetic: 39.6 us -> 1.99 us  [the longest x1 1.91 us: on_device(): picked = norm_rows(picked_x.astype(F32), gain_one).astype(BF)]
    pallas_call x0 -> x9, Pallas kernels: none -> 33.2 us  [the longest x8 31 us: piece_sums(): pl.pallas_call(functools.partial(sum_kernel, shares=shares), grid=(steps,...]
    ppermute x38 -> x28, starting transfers between devices: 69.8 us -> 38.1 us  [exchange(): return lax.ppermute(values, axis, pairs)]
    ppermute x38 -> x28, waiting for transfers between devices: 67.7 us -> 55 us  [exchange(): return lax.ppermute(values, axis, pairs)]
    concatenate x9 -> x3, other arithmetic: 8.34 us -> 0.02 us  [land(): self.held = jnp.concatenate([self.held, self.flight], 0)]
    add x4 -> x0, other arithmetic: 7.07 us -> none  [total(): return sum((part[0].astype(F32) for part in self.parts))]
    pallas_call x1, Pallas kernels: 51.5 us -> 45.9 us  [feed_forward(): pl.pallas_call(kernel, grid_spec=pltpu.PrefetchScalarGridSpec(num_scalar_...]
  transfers between devices with their start and end apart: 48 -> 38, of which waited for: 11 -> 12; matrix products, arithmetic and copies ran while one was open for 26% -> 10% of each run, Pallas kernels for 28% -> 29%
where the time goes in v3:
time: 484 us; the launch traced here: 477 us
  Pallas kernels  220 us (45%)
  waiting for transfers between devices  127 us (26%)
  starting transfers between devices  53.2 us (11%)
  local copies, waits for them, and re-layouts  36.5 us (8%)
  between operations  16.3 us (3%)
  other arithmetic  16 us (3%)
  matrix products  8.32 us (2%)
    all_gather x1, waiting for transfers between devices, on_device(): weights = lax.all_gather(packed_weights, ('row', 'col'), axis=0, tiled=True)  70.4 us
    ppermute x28, waiting for transfers between devices, exchange(): return lax.ppermute(values, axis, pairs)  55 us
    pallas_call x1, Pallas kernels, feed_forward(): pl.pallas_call(kernel, grid_spec=pltpu.PrefetchScalarGridSpec(num_scalar_...  45.9 us
    pallas_call x2, Pallas kernels, attention_backward(): pl.pallas_call(functools.partial(backward_kernel, first_head=half * heads...  39.1 us
    ppermute x28, starting transfers between devices, exchange(): return lax.ppermute(values, axis, pairs)  38.1 us
    pallas_call x2, Pallas kernels, layout_bias(): pl.pallas_call(functools.partial(bias_kernel, first_head=first_head), gri...  34.6 us
    pallas_call x8, Pallas kernels, piece_sums(): pl.pallas_call(functools.partial(sum_kernel, shares=shares), grid=(steps,...  31 us
    pallas_call x1, Pallas kernels, attention_forward(): pl.pallas_call(attend_kernel, grid_spec=pltpu.PrefetchScalarGridSpec(num_...  27.8 us
  transfers between devices with their start and end apart: 38, of which 12 were waited for; matrix products, arithmetic and copies ran while one was open for 10% of the time, Pallas kernels for 29%

profile of v3, /device:TPU:0, one launch (start us, length us, event | category | flops | bytes accessed | tf_op | source)
XLA Modules:
  0.0 477.3 jit_solution(13056713157036243835)
XLA Ops:
  7.3 2.2 pack_shards.1
  9.8 4.1 collective-permute-start
  20.8 2.1 gather_fusion
  23.0 1.6 collective-permute-start.1
  26.1 3.1 gather_fusion.2
  30.6 1.4 collective-permute-start.4
  33.3 3.4 collective-permute-start.6
  36.7 1.5 collective-permute-start.7
  41.3 3.6 collective-permute-start.2
  47.8 3.2 multiply_add_fusion.codes_ref
  51.6 1.4 collective-permute-start.3
  53.8 2.5 fusion
  60.4 1.6 gather_fusion.4
  66.4 17.3 %layout_bias.2.low_bias_ref = f32[8,384,512]{2,1,0:T(8,128)} custom-call(s32[1024,512]{1,0:T(8,128)} %multiply_add_fusion.codes_ref, f32[48,128]{1,0:T(8,128)} %bitcast.104), custom_call_target="tpu_custom_call" | custom-call | flops 16000000000 | bytes 7000000 | tf_op jit(solution)/shard_map/layout_bias/pallas_call | solution.py:335
  85.6 1.9 fusion.2.picked_ref
  87.5 17.3 %layout_bias.3.high_bias_ref = f32[8,384,512]{2,1,0:T(8,128)} custom-call(s32[1024,512]{1,0:T(8,128)} %multiply_add_fusion.codes_ref, f32[48,128]{1,0:T(8,128)} %bitcast.105), custom_call_target="tpu_custom_call" | custom-call | flops 16000000000 | bytes 7000000 | tf_op jit(solution)/shard_map/layout_bias/pallas_call | solution.py:335
  104.8 70.4 %all-gather.3.cloned.1.call-done.wq_ref.wk_ref.wv_ref.wo_ref.gate_ref.up_ref.packed_ref = bf16[1024,12544]{1,0:T(8,128)(2,1)} async-done(((bf16[32,12544]{1,0:T(8,128)(2,1)}), bf16[1024,12544]{1,0:T(8,128)(2,1)}) %all-gather.3.cloned.1.call-update) | async-done | bytes 25690128 | tf_op jit(solution)/shard_map/all_gather | solution.py:1186
  175.7 27.8 %attention_forward.1 = (bf16[512,1024]{1,0:T(8,128)(2,1)}, bf16[1024,1024]{1,0:T(8,128)(2,1)}, bf16[1024,1024]{1,0:T(8,128)(2,1)}, bf16[1024,512]{1,0:T(8,128)(2...) custom-call(s32[2]{0:T(128)} %pad_add_fusion.1.count_ref.scalar_ref, ...), custom_call_target="tpu_custom_call" | custom-call | flops 20000000000 | bytes 50000000 | tf_op jit(solution)/shard_map/attention_forward/pallas_call | solution.py:478
  203.5 45.9 %feed_forward.1 = (bf16[16,32,2816]{2,1,0:T(8,128)(2,1)}, bf16[16,32,2816]{2,1,0:T(8,128)(2,1)}, bf16[16,32,2816]{2,1,0:T(8,128)(2,1)}, bf16[16,32,2816]{2,1,0:T...) custom-call(s32[2]{0:T(128)} %pad_add_fusion.1.count_ref.scalar_ref,, ...), custom_call_target="tpu_custom_call" | custom-call | flops 27000000512 | bytes 44000000 | tf_op jit(solution)/shard_map/feed_forward/pallas_call | solution.py:662
  250.3 19.6 %attention_backward.2 = (bf16[512,512]{1,0:T(8,128)(2,1)}, bf16[1024,512]{1,0:T(8,128)(2,1)}, bf16[1024,512]{1,0:T(8,128)(2,1)}, bf16[8,384,512]{2,1,0:T(8,128)(...) custom-call(s32[2]{0:T(128)} %pad_add_fusion.1.count_ref.scalar_ref, ...), custom_call_target="tpu_custom_call" | custom-call | flops 15000000512 | bytes 30000000 | tf_op jit(solution)/shard_map/attention_backward/pallas_call | solution.py:898
  270.2 1.6 copy-done.2
  272.5 6.3 %piece_sums.8 = (bf16[8,32,2816]{2,1,0:T(8,128)(2,1)}, bf16[8,32,2816]{2,1,0:T(8,128)(2,1)}, bf16[8,88,1024]{2,1,0:T(8,128)(2,1)}) custom-call(bf16[16,32,2816]{2,1,0:T(8,128)(2,1)} %get-tuple-element.157.refs_0_, bf16[16,32,2816]{2,1,0:T(8,128)(2,1)} %collective-permute-done.9.refs_1_, ...), custom_call_target="tpu_custom_call" | custom-call | flops 8650752 | bytes 17301504 | tf_op jit(solution)/shard_map/piece_sums/pallas_call | solution.py:182
  278.9 1.5 collective-permute-start.13
  282.5 19.6 %attention_backward.3 = (bf16[512,512]{1,0:T(8,128)(2,1)}, bf16[1024,512]{1,0:T(8,128)(2,1)}, bf16[1024,512]{1,0:T(8,128)(2,1)}, bf16[8,384,512]{2,1,0:T(8,128)(...) custom-call(s32[2]{0:T(128)} %pad_add_fusion.1.count_ref.scalar_ref, ...), custom_call_target="tpu_custom_call" | custom-call | flops 15000000512 | bytes 30000000 | tf_op jit(solution)/shard_map/attention_backward/pallas_call | solution.py:898
  302.1 10.7 %collective-permute-done.14.refs_8_.refs_10_.refs_12_.refs_14_ = bf16[8,88,1024]{2,1,0:T(8,128)(2,1)S(1)} collective-permute-done((bf16[8,88,1024]{2,1,0:T(8,128)(2,1)}, bf16[8,88,1024]{2,1,0:T(8,128)(2,1)S(1)}, u32[]{:S(2)}, u32[]{:S(2)}) %collective-permute-start.14) | collective-permute-done | bytes 1441824 | tf_op jit(solution)/shard_map/ppermute | solution.py:78
  315.3 5.9 %piece_sums.9 = (bf16[4,32,2816]{2,1,0:T(8,128)(2,1)}, bf16[4,32,2816]{2,1,0:T(8,128)(2,1)}, bf16[4,88,1024]{2,1,0:T(8,128)(2,1)}, bf16[8,32,2048]{2,1,0:T(8,128)(2,1)}) custom-call(bf16[16,32,2816]{2,1,0:T(8,128)(2,1)} %get-tuple-element.157.refs_0_, bf16[16,32,2816]{2,1,0:T(8,128)(2,1)} %collective-permute-done.9.refs_1_, bf16[8,32,2816]{2,1,0:T(8,128)(2,1)} %copy-done.8, ...), custom_call_target="tpu_custom_call" | custom-call | flops 8585216 | bytes 17170432 | tf_op jit(solution)/shard_map/piece_sums/pallas_call | solution.py:182
  321.2 1.7 collective-permute-start.19
  325.7 19.9 %table_histogram.1 = f32[96,256]{1,0:T(8,128)} custom-call(s32[2]{0:T(128)} %pad_add_fusion.1.count_ref.scalar_ref, s32[1024,512]{1,0:T(8,128)} %multiply_add_fusion.codes_ref, bf16[8,384,512]{2,1,0:T(8,128)(2,1)} %get-tuple-element.183.low_ref, bf16[8,384,512]{2,1,0:T(8,128)(2,1)} %get-tuple-element.184.high_ref), custom_call_target="tpu_custom_call" | custom-call | flops 20000000000 | bytes 8000000 | tf_op jit(solution)/shard_map/table_histogram/pallas_call | solution.py:994
  346.7 8.6 %collective-permute-done.17.refs_7_.refs_8_.refs_9_ = bf16[4,32,2816]{2,1,0:T(8,128)(2,1)} collective-permute-done((bf16[4,32,2816]{2,1,0:T(8,128)(2,1)}, bf16[4,32,2816]{2,1,0:T(8,128)(2,1)}, u32[]{:S(2)}, u32[]{:S(2)}) %collective-permute-start.17) | collective-permute-done | bytes 720928 | tf_op jit(solution)/shard_map/ppermute | solution.py:78
  356.2 4.9 %piece_sums.10 = (bf16[2,32,5632]{2,1,0:T(8,128)(2,1)}, bf16[2,88,1024]{2,1,0:T(8,128)(2,1)}, bf16[4,32,2048]{2,1,0:T(8,128)(2,1)}, bf16[8,32,2048]{2,1,0:T(8,128)(2,1)}) custom-call(bf16[16,32,2816]{2,1,0:T(8,128)(2,1)} %get-tuple-element.157.refs_0_, bf16[16,32,2816]{2,1,0:T(8,128)(2,1)} %collective-permute-done.9.refs_1_, bf16[8,32,2816]{2,1,0:T(8,128)(2,1)} %copy-done.8, ...), custom_call_target="tpu_custom_call" | custom-call | flops 7995392 | bytes 15990784 | tf_op jit(solution)/shard_map/piece_sums/pallas_call | solution.py:182
  364.1 1.4 collective-permute-start.22
  365.6 13.8 %key_gradients.1 = (bf16[512,1024]{1,0:T(8,128)(2,1)}, f32[512,1024]{1,0:T(8,128)}, f32[8,1024]{1,0:T(8,128)}) custom-call(s32[2]{0:T(128)} %pad_add_fusion.1.count_ref.scalar_ref, bf16[512,512]{1,0:T(8,128)(2,1)} %get-tuple-element.155.dq_low_ref, bf16[512,512]{1,0:T(8,128)(2,1)} %get-tuple-element.167.dq_high_ref, ...), custom_call_target="tpu_custom_call" | custom-call | flops 8999999488 | bytes 18000000 | tf_op jit(solution)/shard_map/key_gradients/pallas_call | solution.py:1081
  380.7 11.0 %collective-permute-done.22.refs_14_.refs_16_ = bf16[2,88,1024]{2,1,0:T(8,128)(2,1)S(1)} collective-permute-done((bf16[2,88,1024]{2,1,0:T(8,128)(2,1)}, bf16[2,88,1024]{2,1,0:T(8,128)(2,1)S(1)}, u32[]{:S(2)}, u32[]{:S(2)}) %collective-permute-start.22) | collective-permute-done | bytes 360480 | tf_op jit(solution)/shard_map/ppermute | solution.py:78
  393.3 4.1 piece_sums.11
  397.4 1.5 collective-permute-start.32
  402.2 3.3 collective-permute-start.27
  405.7 1.5 collective-permute-start.28
  407.2 4.4 collective-permute-start.29
  412.4 2.4 piece_sums.12
  414.8 2.1 collective-permute-start.34
  416.9 1.7 collective-permute-done.28
  419.7 6.2 %collective-permute-start.33 = (bf16[1,32,2048]{2,1,0:T(8,128)(2,1)S(1)}, bf16[1,32,2048]{2,1,0:T(8,128)(2,1)S(1)}, u32[]{:S(2)}, u32[]{:S(2)}) collective-permute-start(bf16[1,32,2048]{2,1,0:T(8,128)(2,1)S(1)} %copy-done.41), channel_id=1, source_target_pairs={{0,16},{4,20},{8,24},{12,28},{16,0},{20,4},{24,8},{28,12},{1,17},{... | collective-permute-start | bytes 393224 | tf_op jit(solution)/shard_map/ppermute | solution.py:78
  425.9 16.2 %collective-permute-done.30.refs_17_ = bf16[1,88,1024]{2,1,0:T(8,128)(2,1)S(1)} collective-permute-done((bf16[1,88,1024]{2,1,0:T(8,128)(2,1)S(1)}, bf16[1,88,1024]{2,1,0:T(8,128)(2,1)S(1)}, u32[]{:S(2)}, u32[]{:S(2)}) %collective-permute-start.30) | collective-permute-done | bytes 180256 | tf_op jit(solution)/shard_map/ppermute | solution.py:78
  442.8 5.5 %input_gradient.1 = bf16[512,1024]{1,0:T(8,128)(2,1)} custom-call(f32[512,1024]{1,0:T(8,128)} %get-tuple-element.196.own_ref, bf16[512,512]{1,0:T(8,128)(2,1)} %fusion.13.owner_ref, bf16[512,1024]{1,0:T(8,128)(2,1)} %pad_maximum_fusion.returned_ref, bf16[512,1024]{1,0:T(8,128)(2,1)} %x_ref.5, f32[8,1024]{1,0:T(8,128)} %broadcast_in_dim.64.gain_ref, ...), custom_call_target="tpu_custom_call" | custom-call | flops 1000000000 | bytes 8000000 | tf_op jit(solution)/shard_map/input_gradient/pallas_call | solution.py:1130
  449.0 1.9 piece_sums.13
  450.9 3.1 piece_sums.15
  454.1 4.5 collective-permute-done.35.refs_11_
  459.3 2.3 piece_sums.14
  (233 shorter events, 61.3 us)
Async XLA Ops:
  7.2 9.6 %copy-start.1 = (bf16[512,1024]{1,0:T(8,128)(2,1)S(1)}, bf16[512,1024]{1,0:T(8,128)(2,1)}, u32[]{:S(2)}) copy-start(bf16[512,1024]{1,0:T(8,128)(2,1)} %x_ref.5) | copy-start | bytes 3145732
  7.3 167.9 %all-gather.3.cloned.1.call-start = ((), (), s32[]{:S(2)}) async-start(), calls=%async_computation | async-start | bytes 26492928 | tf_op jit(solution)/shard_map/all_gather | solution.py:1186
  9.6 456.6 %all-gather.5.cloned.1.call-start = ((), (), s32[]{:S(2)}) async-start(), calls=%async_computation.1 | async-start | bytes 2162688 | tf_op jit(solution)/shard_map/all_gather | solution.py:1368
  9.8 13.1 %collective-permute-start = (bf16[1,32,128]{1,2,0:T(8,128)(2,1)S(1)}, bf16[1,32,128]{1,2,0:T(8,128)(2,1)S(1)}, u32[]{:S(2)}, u32[]{:S(2)}) collective-permute-start(bf16[1,32,128]{1,2,0:T(8,128)(2,1)S(1)} %bitcast.101), channel_id=1, source_target_pairs={{0,16},{4,20},{8,24},{12,28},{16,0},{20,4},{24,8},{28,12},{1,17},{... | collective-permute-start | bytes 24584 | tf_op jit(solution)/shard_map/ppermute | solution.py:78
  23.0 18.3 %collective-permute-start.1 = (bf16[2,32,128]{2,1,0:T(8,128)(2,1)S(1)}, bf16[2,32,128]{2,1,0:T(8,128)(2,1)S(1)}, u32[]{:S(2)}, u32[]{:S(2)}) collective-permute-start(bf16[2,32,128]{2,1,0:T(8,128)(2,1)S(1)} %pad_maximum_fusion.7), channel_id=1, source_target_pairs={{0,8},{4,12},{8,0},{12,4},{16,24},{20,28},{24,16},{28,20},{1,9},{5... | collective-permute-start | bytes 49160 | tf_op jit(solution)/shard_map/ppermute | solution.py:78
  30.5 14.4 %copy-start.37 = (s32[512,1024]{1,0:T(8,128)S(1)}, s32[512,1024]{1,0:T(8,128)}, u32[]{:S(2)}) copy-start(s32[512,1024]{1,0:T(8,128)} %param.39) | copy-start | bytes 6291460
  30.6 23.1 %collective-permute-start.4 = (bf16[128,1024]{1,0:T(8,128)(2,1)S(1)}, bf16[128,1024]{1,0:T(8,128)(2,1)S(1)}, u32[]{:S(2)}, u32[]{:S(2)}) collective-permute-start(bf16[128,1024]{1,0:T(8,128)(2,1)S(1)} %get-tuple-element.234), channel_id=1, source_target_pairs={{0,4},{4,8},{8,12},{12,16},{16,20},{20,24},{24,28},{1,5},{5,9},{9,... | collective-permute-start | bytes 786440 | tf_op jit(solution)/shard_map/ppermute | solution.py:35
  32.0 21.7 %collective-permute-start.5 = (bf16[128,1024]{1,0:T(8,128)(2,1)S(1)}, bf16[128,1024]{1,0:T(8,128)(2,1)S(1)}, u32[]{:S(2)}, u32[]{:S(2)}) collective-permute-start(bf16[128,1024]{1,0:T(8,128)(2,1)S(1)} %get-tuple-element.233), channel_id=1, source_target_pairs={{4,0},{8,4},{12,8},{16,12},{20,16},{24,20},{28,24},{5,1},{9,5},{13... | collective-permute-start | bytes 786440 | tf_op jit(solution)/shard_map/ppermute | solution.py:36
  33.3 20.4 %collective-permute-start.6 = (bf16[128,1024]{1,0:T(8,128)(2,1)S(1)}, bf16[128,1024]{1,0:T(8,128)(2,1)S(1)}, u32[]{:S(2)}, u32[]{:S(2)}) collective-permute-start(bf16[128,1024]{1,0:T(8,128)(2,1)S(1)} %get-tuple-element.232), channel_id=1, source_target_pairs={{0,1},{1,2},{2,3},{4,5},{5,6},{6,7},{8,9},{9,10},{10,11},{12,13},{... | collective-permute-start | bytes 786440 | tf_op jit(solution)/shard_map/ppermute | solution.py:35
  36.7 17.0 %collective-permute-start.7 = (bf16[128,1024]{1,0:T(8,128)(2,1)S(1)}, bf16[128,1024]{1,0:T(8,128)(2,1)S(1)}, u32[]{:S(2)}, u32[]{:S(2)}) collective-permute-start(bf16[128,1024]{1,0:T(8,128)(2,1)S(1)} %get-tuple-element.231), channel_id=1, source_target_pairs={{1,0},{2,1},{3,2},{5,4},{6,5},{7,6},{9,8},{10,9},{11,10},{13,12},{... | collective-permute-start | bytes 786440 | tf_op jit(solution)/shard_map/ppermute | solution.py:36
  40.5 13.2 %copy-start.9 = (bf16[1024,1024]{1,0:T(8,128)(2,1)}, bf16[1024,1024]{1,0:T(8,128)(2,1)S(1)}, u32[]{:S(2)}) copy-start(bf16[1024,1024]{1,0:T(8,128)(2,1)S(1)} %fusion.4.pack_ref) | copy-start | bytes 6291460
  41.3 10.3 %collective-permute-start.2 = (bf16[4,32,128]{2,1,0:T(8,128)(2,1)S(1)}, bf16[4,32,128]{2,1,0:T(8,128)(2,1)S(1)}, u32[]{:S(2)}, u32[]{:S(2)}) collective-permute-start(bf16[4,32,128]{2,1,0:T(8,128)(2,1)S(1)} %pad_maximum_fusion.6), channel_id=1, source_target_pairs={{0,2},{1,3},{2,0},{3,1},{4,6},{5,7},{6,4},{7,5},{8,10},{9,11},{10,... | collective-permute-start | bytes 98312 | tf_op jit(solution)/shard_map/ppermute | solution.py:78
  51.6 6.1 %collective-permute-start.3 = (bf16[8,32,128]{2,1,0:T(8,128)(2,1)S(1)}, bf16[8,32,128]{2,1,0:T(8,128)(2,1)S(1)}, u32[]{:S(2)}, u32[]{:S(2)}) collective-permute-start(bf16[8,32,128]{2,1,0:T(8,128)(2,1)S(1)} %pad_maximum_fusion.5), channel_id=1, source_target_pairs={{0,1},{1,0},{2,3},{3,2},{4,5},{5,4},{6,7},{7,6},{8,9},{9,8},{10,11... | collective-permute-start | bytes 196616 | tf_op jit(solution)/shard_map/ppermute | solution.py:78
  56.3 29.3 %copy-start.13 = (bf16[1024,1024]{1,0:T(8,128)(2,1)}, bf16[1024,1024]{1,0:T(8,128)(2,1)S(1)}, u32[]{:S(2)}) copy-start(bf16[1024,1024]{1,0:T(8,128)(2,1)S(1)} %get-tuple-element.262.picked_ref) | copy-start | bytes 6291460
  58.4 1.3 collective-permute-start.8
  66.4 17.9 %copy-start.31 = (f32[512]{0:T(512)S(1)}, f32[512]{0:T(512)}, u32[]{:S(2)}) copy-start(f32[512]{0:T(512)} %add_rsqrt_fusion.1) | copy-start | bytes 6148
  249.4 20.7 %collective-permute-start.11 = (bf16[16,88,1024]{2,1,0:T(8,128)(2,1)}, bf16[16,88,1024]{2,1,0:T(8,128)(2,1)S(1)}, u32[]{:S(2)}, u32[]{:S(2)}) collective-permute-start(bf16[16,88,1024]{2,1,0:T(8,128)(2,1)} %get-tuple-element.147), channel_id=1, source_target_pairs={{0,4},{4,0},{8,12},{12,8},{16,20},{20,16},{24,28},{28,24},{1,5},{5... | collective-permute-start | bytes 8650760 | tf_op jit(solution)/shard_map/ppermute | solution.py:78
  249.7 20.4 %collective-permute-start.10 = (bf16[16,32,2816]{2,1,0:T(8,128)(2,1)}, bf16[16,32,2816]{2,1,0:T(8,128)(2,1)S(1)}, u32[]{:S(2)}, u32[]{:S(2)}) collective-permute-start(bf16[16,32,2816]{2,1,0:T(8,128)(2,1)} %get-tuple-element.146), channel_id=1, source_target_pairs={{0,4},{4,0},{8,12},{12,8},{16,20},{20,16},{24,28},{28,24},{1,5},{5... | collective-permute-start | bytes 8650760 | tf_op jit(solution)/shard_map/ppermute | solution.py:78
  250.0 20.2 %collective-permute-start.9 = (bf16[16,32,2816]{2,1,0:T(8,128)(2,1)}, bf16[16,32,2816]{2,1,0:T(8,128)(2,1)}, u32[]{:S(2)}, u32[]{:S(2)}) collective-permute-start(bf16[16,32,2816]{2,1,0:T(8,128)(2,1)} %get-tuple-element.145), channel_id=1, source_target_pairs={{0,4},{4,0},{8,12},{12,8},{16,20},{20,16},{24,28},{28,24},{1,5},{5... | collective-permute-start | bytes 8650760 | tf_op jit(solution)/shard_map/ppermute | solution.py:78
  269.8 32.2 %collective-permute-start.15 = (bf16[16,32,2048]{2,1,0:T(8,128)(2,1)}, bf16[16,32,2048]{2,1,0:T(8,128)(2,1)}, u32[]{:S(2)}, u32[]{:S(2)}) collective-permute-start(bf16[16,32,2048]{2,1,0:T(8,128)(2,1)} %get-tuple-element.156), channel_id=1, source_target_pairs={{0,4},{4,0},{8,12},{12,8},{16,20},{20,16},{24,28},{28,24},{1,5},{5... | collective-permute-start | bytes 6291464 | tf_op jit(solution)/shard_map/ppermute | solution.py:78
  278.9 34.0 %collective-permute-start.14 = (bf16[8,88,1024]{2,1,0:T(8,128)(2,1)}, bf16[8,88,1024]{2,1,0:T(8,128)(2,1)S(1)}, u32[]{:S(2)}, u32[]{:S(2)}) collective-permute-start(bf16[8,88,1024]{2,1,0:T(8,128)(2,1)} %get-tuple-element.165), channel_id=1, source_target_pairs={{0,8},{4,12},{8,0},{12,4},{16,24},{20,28},{24,16},{28,20},{1,9},{5... | collective-permute-start | bytes 4325384 | tf_op jit(solution)/shard_map/ppermute | solution.py:78
  278.9 34.0 %collective-permute-start.13 = (bf16[8,32,2816]{2,1,0:T(8,128)(2,1)}, bf16[8,32,2816]{2,1,0:T(8,128)(2,1)S(1)}, u32[]{:S(2)}, u32[]{:S(2)}) collective-permute-start(bf16[8,32,2816]{2,1,0:T(8,128)(2,1)} %get-tuple-element.164), channel_id=1, source_target_pairs={{0,2},{1,3},{2,0},{3,1},{4,6},{5,7},{6,4},{7,5},{8,10},{9,11},{10,... | collective-permute-start | bytes 4325384 | tf_op jit(solution)/shard_map/ppermute | solution.py:78
  280.5 33.7 %collective-permute-start.12 = (bf16[8,32,2816]{2,1,0:T(8,128)(2,1)}, bf16[8,32,2816]{2,1,0:T(8,128)(2,1)S(1)}, u32[]{:S(2)}, u32[]{:S(2)}) collective-permute-start(bf16[8,32,2816]{2,1,0:T(8,128)(2,1)} %get-tuple-element.163), channel_id=1, source_target_pairs={{0,1},{1,0},{2,3},{3,2},{4,5},{5,4},{6,7},{7,6},{8,9},{9,8},{10,11... | collective-permute-start | bytes 4325384 | tf_op jit(solution)/shard_map/ppermute | solution.py:78
  302.1 44.6 %collective-permute-start.20 = (bf16[16,32,2048]{2,1,0:T(8,128)(2,1)}, bf16[16,32,2048]{2,1,0:T(8,128)(2,1)S(1)}, u32[]{:S(2)}, u32[]{:S(2)}) collective-permute-start(bf16[16,32,2048]{2,1,0:T(8,128)(2,1)} %get-tuple-element.172), channel_id=1, source_target_pairs={{0,4},{4,0},{8,12},{12,8},{16,20},{20,16},{24,28},{28,24},{1,5},{5... | collective-permute-start | bytes 6291464 | tf_op jit(solution)/shard_map/ppermute | solution.py:78
  321.2 34.1 %collective-permute-start.19 = (bf16[8,32,2048]{2,1,0:T(8,128)(2,1)}, bf16[8,32,2048]{2,1,0:T(8,128)(2,1)S(1)}, u32[]{:S(2)}, u32[]{:S(2)}) collective-permute-start(bf16[8,32,2048]{2,1,0:T(8,128)(2,1)} %get-tuple-element.181), channel_id=1, source_target_pairs={{0,8},{4,12},{8,0},{12,4},{16,24},{20,28},{24,16},{28,20},{1,9},{5... | collective-permute-start | bytes 3145736 | tf_op jit(solution)/shard_map/ppermute | solution.py:78
  322.9 23.8 %collective-permute-start.18 = (bf16[4,88,1024]{2,1,0:T(8,128)(2,1)}, bf16[4,88,1024]{2,1,0:T(8,128)(2,1)}, u32[]{:S(2)}, u32[]{:S(2)}) collective-permute-start(bf16[4,88,1024]{2,1,0:T(8,128)(2,1)} %get-tuple-element.180), channel_id=1, source_target_pairs={{0,1},{1,0},{2,3},{3,2},{4,5},{5,4},{6,7},{7,6},{8,9},{9,8},{10,11... | collective-permute-start | bytes 2162696 | tf_op jit(solution)/shard_map/ppermute | solution.py:78
  323.7 31.6 %collective-permute-start.17 = (bf16[4,32,2816]{2,1,0:T(8,128)(2,1)}, bf16[4,32,2816]{2,1,0:T(8,128)(2,1)}, u32[]{:S(2)}, u32[]{:S(2)}) collective-permute-start(bf16[4,32,2816]{2,1,0:T(8,128)(2,1)} %get-tuple-element.179), channel_id=1, source_target_pairs={{0,1},{1,0},{2,3},{3,2},{4,5},{5,4},{6,7},{7,6},{8,9},{9,8},{10,11... | collective-permute-start | bytes 2162696 | tf_op jit(solution)/shard_map/ppermute | solution.py:78
  324.9 30.3 %collective-permute-start.16 = (bf16[4,32,2816]{2,1,0:T(8,128)(2,1)}, bf16[4,32,2816]{2,1,0:T(8,128)(2,1)}, u32[]{:S(2)}, u32[]{:S(2)}) collective-permute-start(bf16[4,32,2816]{2,1,0:T(8,128)(2,1)} %get-tuple-element.178), channel_id=1, source_target_pairs={{0,2},{1,3},{2,0},{3,1},{4,6},{5,7},{6,4},{7,5},{8,10},{9,11},{10,... | collective-permute-start | bytes 2162696 | tf_op jit(solution)/shard_map/ppermute | solution.py:78
  325.7 19.9 %copy-start.29 = (f32[96,128]{1,0:T(8,128)S(1)}, f32[96,128]{1,0:T(8,128)}, u32[]{:S(2)}) copy-start(f32[96,128]{1,0:T(8,128)} %get-tuple-element.217) | copy-start | bytes 147460
  325.7 19.9 %copy-start.30 = (f32[96,128]{1,0:T(8,128)S(1)}, f32[96,128]{1,0:T(8,128)}, u32[]{:S(2)}) copy-start(f32[96,128]{1,0:T(8,128)} %get-tuple-element.218) | copy-start | bytes 147460
  361.1 30.7 %collective-permute-start.24 = (bf16[8,32,2048]{2,1,0:T(8,128)(2,1)}, bf16[8,32,2048]{2,1,0:T(8,128)(2,1)S(1)}, u32[]{:S(2)}, u32[]{:S(2)}) collective-permute-start(bf16[8,32,2048]{2,1,0:T(8,128)(2,1)} %get-tuple-element.194), channel_id=1, source_target_pairs={{0,2},{1,3},{2,0},{3,1},{4,6},{5,7},{6,4},{7,5},{8,10},{9,11},{10,... | collective-permute-start | bytes 3145736 | tf_op jit(solution)/shard_map/ppermute | solution.py:78
  362.5 29.3 %collective-permute-start.21 = (bf16[2,32,5632]{2,1,0:T(8,128)(2,1)}, bf16[2,32,5632]{2,1,0:T(8,128)(2,1)S(1)}, u32[]{:S(2)}, u32[]{:S(2)}) collective-permute-start(bf16[2,32,5632]{2,1,0:T(8,128)(2,1)} %get-tuple-element.191), channel_id=1, source_target_pairs={{0,8},{4,12},{8,0},{12,4},{16,24},{20,28},{24,16},{28,20},{1,9},{5... | collective-permute-start | bytes 2162696 | tf_op jit(solution)/shard_map/ppermute | solution.py:78
  363.5 28.2 %collective-permute-start.23 = (bf16[4,32,2048]{2,1,0:T(8,128)(2,1)}, bf16[4,32,2048]{2,1,0:T(8,128)(2,1)S(1)}, u32[]{:S(2)}, u32[]{:S(2)}) collective-permute-start(bf16[4,32,2048]{2,1,0:T(8,128)(2,1)} %get-tuple-element.193), channel_id=1, source_target_pairs={{0,1},{1,0},{2,3},{3,2},{4,5},{5,4},{6,7},{7,6},{8,9},{9,8},{10,11... | collective-permute-start | bytes 1572872 | tf_op jit(solution)/shard_map/ppermute | solution.py:78
  364.1 27.6 %collective-permute-start.22 = (bf16[2,88,1024]{2,1,0:T(8,128)(2,1)}, bf16[2,88,1024]{2,1,0:T(8,128)(2,1)S(1)}, u32[]{:S(2)}, u32[]{:S(2)}) collective-permute-start(bf16[2,88,1024]{2,1,0:T(8,128)(2,1)} %get-tuple-element.192), channel_id=1, source_target_pairs={{0,2},{1,3},{2,0},{3,1},{4,6},{5,7},{6,4},{7,5},{8,10},{9,11},{10,... | collective-permute-start | bytes 1081352 | tf_op jit(solution)/shard_map/ppermute | solution.py:78
  397.4 9.8 %copy-start.39 = (bf16[1,32,5632]{2,1,0:T(8,128)(2,1)S(1)}, bf16[1,32,5632]{2,1,0:T(8,128)(2,1)}, u32[]{:S(2)}) copy-start(bf16[1,32,5632]{2,1,0:T(8,128)(2,1)} %get-tuple-element.202) | copy-start | bytes 1081348
  397.4 14.2 %copy-start.40 = (bf16[1,88,1024]{2,1,0:T(8,128)(2,1)S(1)}, bf16[1,88,1024]{2,1,0:T(8,128)(2,1)}, u32[]{:S(2)}) copy-start(bf16[1,88,1024]{2,1,0:T(8,128)(2,1)} %get-tuple-element.203) | copy-start | bytes 540676
  397.4 14.2 %collective-permute-start.32 = (bf16[4,32,2048]{2,1,0:T(8,128)(2,1)}, bf16[4,32,2048]{2,1,0:T(8,128)(2,1)S(1)}, u32[]{:S(2)}, u32[]{:S(2)}) collective-permute-start(bf16[4,32,2048]{2,1,0:T(8,128)(2,1)} %get-tuple-element.205), channel_id=1, source_target_pairs={{0,1},{1,0},{2,3},{3,2},{4,5},{5,4},{6,7},{7,6},{8,9},{9,8},{10,11... | collective-permute-start | bytes 1572872 | tf_op jit(solution)/shard_map/ppermute | solution.py:78
  398.9 6.8 %collective-permute-start.31 = (bf16[2,32,2048]{2,1,0:T(8,128)(2,1)}, bf16[2,32,2048]{2,1,0:T(8,128)(2,1)S(1)}, u32[]{:S(2)}, u32[]{:S(2)}) collective-permute-start(bf16[2,32,2048]{2,1,0:T(8,128)(2,1)} %get-tuple-element.204), channel_id=1, source_target_pairs={{0,2},{1,3},{2,0},{3,1},{4,6},{5,7},{6,4},{7,5},{8,10},{9,11},{10,... | collective-permute-start | bytes 786440 | tf_op jit(solution)/shard_map/ppermute | solution.py:78
  399.6 7.6 %collective-permute-start.25 = (bf16[128,1024]{1,0:T(8,128)(2,1)S(1)}, bf16[128,1024]{1,0:T(8,128)(2,1)S(1)}, u32[]{:S(2)}, u32[]{:S(2)}) collective-permute-start(bf16[128,1024]{1,0:T(8,128)(2,1)S(1)} %get-tuple-element.227), channel_id=1, source_target_pairs={{0,4},{4,8},{8,12},{12,16},{16,20},{20,24},{24,28},{1,5},{5,9},{9,... | collective-permute-start | bytes 786440 | tf_op jit(solution)/shard_map/ppermute | solution.py:35
  400.9 13.9 %collective-permute-start.26 = (bf16[128,1024]{1,0:T(8,128)(2,1)S(1)}, bf16[128,1024]{1,0:T(8,128)(2,1)S(1)}, u32[]{:S(2)}, u32[]{:S(2)}) collective-permute-start(bf16[128,1024]{1,0:T(8,128)(2,1)S(1)} %get-tuple-element.230), channel_id=1, source_target_pairs={{4,0},{8,4},{12,8},{16,12},{20,16},{24,20},{28,24},{5,1},{9,5},{13... | collective-permute-start | bytes 786440 | tf_op jit(solution)/shard_map/ppermute | solution.py:36
  402.2 14.7 %collective-permute-start.27 = (bf16[128,1024]{1,0:T(8,128)(2,1)S(1)}, bf16[128,1024]{1,0:T(8,128)(2,1)S(1)}, u32[]{:S(2)}, u32[]{:S(2)}) collective-permute-start(bf16[128,1024]{1,0:T(8,128)(2,1)S(1)} %get-tuple-element.229), channel_id=1, source_target_pairs={{0,1},{1,2},{2,3},{4,5},{5,6},{6,7},{8,9},{9,10},{10,11},{12,13},{... | collective-permute-start | bytes 786440 | tf_op jit(solution)/shard_map/ppermute | solution.py:35
  405.7 12.9 %collective-permute-start.28 = (bf16[128,1024]{1,0:T(8,128)(2,1)S(1)}, bf16[128,1024]{1,0:T(8,128)(2,1)S(1)}, u32[]{:S(2)}, u32[]{:S(2)}) collective-permute-start(bf16[128,1024]{1,0:T(8,128)(2,1)S(1)} %get-tuple-element.228), channel_id=1, source_target_pairs={{1,0},{2,1},{3,2},{5,4},{6,5},{7,6},{9,8},{10,9},{11,10},{13,12},{... | collective-permute-start | bytes 786440 | tf_op jit(solution)/shard_map/ppermute | solution.py:36
  407.2 34.9 %collective-permute-start.29 = (bf16[1,32,5632]{2,1,0:T(8,128)(2,1)S(1)}, bf16[1,32,5632]{2,1,0:T(8,128)(2,1)S(1)}, u32[]{:S(2)}, u32[]{:S(2)}) collective-permute-start(bf16[1,32,5632]{2,1,0:T(8,128)(2,1)S(1)} %copy-done.39), channel_id=1, source_target_pairs={{0,16},{4,20},{8,24},{12,28},{16,0},{20,4},{24,8},{28,12},{1,17},{... | collective-permute-start | bytes 1081352 | tf_op jit(solution)/shard_map/ppermute | solution.py:78
  411.6 30.4 %collective-permute-start.30 = (bf16[1,88,1024]{2,1,0:T(8,128)(2,1)S(1)}, bf16[1,88,1024]{2,1,0:T(8,128)(2,1)S(1)}, u32[]{:S(2)}, u32[]{:S(2)}) collective-permute-start(bf16[1,88,1024]{2,1,0:T(8,128)(2,1)S(1)} %copy-done.40), channel_id=1, source_target_pairs={{0,16},{4,20},{8,24},{12,28},{16,0},{20,4},{24,8},{28,12},{1,17},{... | collective-permute-start | bytes 540680 | tf_op jit(solution)/shard_map/ppermute | solution.py:78
  414.8 27.3 %copy-start.28 = (f32[1024]{0:T(1024)S(1)}, f32[1024]{0:T(1024)}, u32[]{:S(2)}) copy-start(f32[1024]{0:T(1024)} %copy-done.27) | copy-start | bytes 12292
  414.8 33.5 %collective-permute-start.34 = (bf16[2,32,2048]{2,1,0:T(8,128)(2,1)}, bf16[2,32,2048]{2,1,0:T(8,128)(2,1)S(1)}, u32[]{:S(2)}, u32[]{:S(2)}) collective-permute-start(bf16[2,32,2048]{2,1,0:T(8,128)(2,1)} %get-tuple-element.208), channel_id=1, source_target_pairs={{0,8},{4,12},{8,0},{12,4},{16,24},{20,28},{24,16},{28,20},{1,9},{5... | collective-permute-start | bytes 786440 | tf_op jit(solution)/shard_map/ppermute | solution.py:78
  419.7 34.4 %collective-permute-start.33 = (bf16[1,32,2048]{2,1,0:T(8,128)(2,1)S(1)}, bf16[1,32,2048]{2,1,0:T(8,128)(2,1)S(1)}, u32[]{:S(2)}, u32[]{:S(2)}) collective-permute-start(bf16[1,32,2048]{2,1,0:T(8,128)(2,1)S(1)} %copy-done.41), channel_id=1, source_target_pairs={{0,16},{4,20},{8,24},{12,28},{16,0},{20,4},{24,8},{28,12},{1,17},{... | collective-permute-start | bytes 393224 | tf_op jit(solution)/shard_map/ppermute | solution.py:78
  450.9 7.7 %collective-permute-start.35 = (bf16[1,32,2048]{2,1,0:T(8,128)(2,1)}, bf16[1,32,2048]{2,1,0:T(8,128)(2,1)S(1)}, u32[]{:S(2)}, u32[]{:S(2)}) collective-permute-start(bf16[1,32,2048]{2,1,0:T(8,128)(2,1)} %piece_sums.13), channel_id=1, source_target_pairs={{0,16},{4,20},{8,24},{12,28},{16,0},{20,4},{24,8},{28,12},{1,17},{... | collective-permute-start | bytes 393224 | tf_op jit(solution)/shard_map/ppermute | solution.py:78
  (33 other events, 111.0 us)
Sparse Core Ops, SparseCore 0:
  11.5 163.5 all-gather.2
  391.9 63.7 all-gather.4

commit v4 on v3

--- a/solution.py
+++ b/solution.py
@@ -49,7 +49,7 @@
     if kind == 1:
         return row_bits[:1] + col_bits[::-1] + row_bits[1:]
     if kind == 2:
-        return row_bits[:2] + col_bits + row_bits[2:]
+        return row_bits[:2] + col_bits[:1] + row_bits[2:] + col_bits[1:]
     return row_bits[:2] + col_bits[::-1] + row_bits[2:]
 
 
@@ -972,46 +972,84 @@
     )
 
 
-def histogram_kernel(
-    count_ref, codes_ref, low_ref, high_ref, out_ref, split_ref, both_ref, hist_ref, chosen_ref
-):
-    out_ref[...] = jnp.zeros_like(out_ref)
-
-    @pl.when(count_ref[0] <= FEW)
+def onehot_kernel(codes_ref, out_ref, split_ref):
+    code = codes_ref[...]
+    split_ref[0] = code & 31
+    split_ref[1] = (code >> 5) & 31
+    split_ref[2] = code >> 10
+    bucket = lax.broadcasted_iota(jnp.int32, (BUCKETS, code.shape[1]), 0)
+    for row in range(HIST_ROWS):
+        for t in range(TABLES):
+            at = (row * TABLES + t) * BUCKETS
+            match = split_ref[t, row : row + 1, :] == bucket
+            out_ref[at : at + BUCKETS, :] = match.astype(F32).astype(BF)
+
+
+def bucket_onehots(codes):
+    tokens = codes.shape[1]
+    height = HIST_ROWS * TABLES * BUCKETS
+    return pl.pallas_call(
+        onehot_kernel,
+        grid=(FEW // HIST_ROWS,),
+        in_specs=[pl.BlockSpec((HIST_ROWS, tokens), lambda i: (i, 0))],
+        out_specs=pl.BlockSpec((height, tokens), lambda i: (i, 0)),
+        out_shape=jax.ShapeDtypeStruct((FEW // HIST_ROWS * height, tokens), BF),
+        scratch_shapes=[pltpu.VMEM((TABLES, HIST_ROWS, tokens), jnp.int32)],
+        compiler_params=pltpu.CompilerParams(vmem_limit_bytes=VMEM_LIMIT),
+        cost_estimate=pl.CostEstimate(
+            flops=40_000_000, bytes_accessed=39_000_000, transcendentals=0
+        ),
+        name="bucket_onehots",
+    )(codes)
+
+
+def histogram_kernel(count_ref, chosen_ref, low_ref, high_ref, out_ref, hist_ref):
+    step = pl.program_id(0)
+    few = count_ref[0] <= FEW
+
+    @pl.when(step == 0)
     def _():
-        unpack_codes(codes_ref, split_ref, FEW)
-        both_ref[: HEADS // 2] = low_ref[...]
-        both_ref[HEADS // 2 :] = high_ref[...]
+        out_ref[...] = jnp.zeros_like(out_ref)
         hist_ref[...] = jnp.zeros_like(hist_ref)
-        add_histogram(split_ref, both_ref, hist_ref, chosen_ref, FEW)
+
+    @pl.when(few)
+    def _():
+        rows = pl.ds(pl.multiple_of(step * HIST_ROWS, HIST_ROWS), HIST_ROWS)
+        cols = low_ref.shape[2]
+        grads = [part[:, rows, :].reshape(-1, cols) for part in (low_ref, high_ref)]
+        hist_ref[...] += dot_nt(chosen_ref[...], jnp.concatenate(grads, 0))
+
+    @pl.when(jnp.logical_and(few, step == pl.num_programs(0) - 1))
+    def _():
         take_histogram(hist_ref, out_ref)
 
 
-def table_histogram(count, codes, low, high):
-    tokens = codes.shape[1]
+def table_histogram(count, onehots, low, high):
+    tokens = onehots.shape[1]
     hist_shape = (TABLES * BUCKETS, HEADS * HIST_ROWS)
-    whole = lambda shape: pl.BlockSpec(shape, lambda i, c: (0,) * len(shape))
+    height = HIST_ROWS * TABLES * BUCKETS
+    once = pl.Buffered(1)
+    whole = lambda shape: pl.BlockSpec(shape, lambda i, c: (0,) * len(shape), pipeline_mode=once)
     return pl.pallas_call(
         histogram_kernel,
         grid_spec=pltpu.PrefetchScalarGridSpec(
             num_scalar_prefetch=1,
-            grid=(1,),
-            in_specs=[whole((FEW, tokens)), whole(low.shape), whole(high.shape)],
+            grid=(FEW // HIST_ROWS,),
+            in_specs=[
+                pl.BlockSpec((height, tokens), lambda i, c: (i, 0)),
+                whole(low.shape),
+                whole(high.shape),
+            ],
             out_specs=whole(hist_shape),
-            scratch_shapes=[
-                pltpu.VMEM((TABLES, FEW, tokens), jnp.int32),
-                pltpu.VMEM((HEADS, FEW, tokens), BF),
-                pltpu.VMEM((HIST_ROWS * hist_shape[0], hist_shape[1]), F32),
-                pltpu.VMEM((HIST_ROWS * hist_shape[0], tokens), BF),
-            ],
+            scratch_shapes=[pltpu.VMEM((height, hist_shape[1]), F32)],
         ),
         out_shape=jax.ShapeDtypeStruct(hist_shape, F32),
         compiler_params=pltpu.CompilerParams(vmem_limit_bytes=VMEM_LIMIT),
         cost_estimate=pl.CostEstimate(
-            flops=20_000_000_000, bytes_accessed=8_000_000, transcendentals=0
+            flops=10_000_000_000, bytes_accessed=45_000_000, transcendentals=0
         ),
         name="table_histogram",
-    )(count, codes, low, high)
+    )(count, onehots, low, high)
 
 
 def key_gradients_kernel(
@@ -1271,7 +1309,8 @@
     x_sum = jnp.sum(x_input * x_input, -1, keepdims=True)
     lanes = jnp.arange(128, dtype=jnp.int32)
     keep = own_keep.astype(F32)[:, None] * jnp.where(lanes == 0, x_sum, 1.0)
-    weights = after(weights, high_bias, normed_one, picked, owner, keep)
+    onehots = bucket_onehots(after(codes, high_bias))
+    weights = after(weights, high_bias, normed_one, picked, owner, keep, onehots)
     queries, keys, values, mixed, lse, probs, x_middle, normed_two = attention_forward(
         scalars,
         normed_one,
@@ -1329,26 +1368,25 @@
         )
 
     sent = rounds.send()
-    low_half = backward(0, 2, after(grad_attn, sent))
-    low_chain = Scatter(low_half[5], low_half[6], 2)
+    low_half = backward(0, 3, after(grad_attn, sent))
+    low_chain = Scatter(low_half[5], low_half[6], 3)
     rounds.land(low_half[0])
     rounds.chains.append(low_chain)
     sent = rounds.send()
-    high_half = backward(1, 1, after(grad_attn, low_half[0], sent))
-    high_chain = Scatter(high_half[5], high_half[6], 1)
+    high_half = backward(1, 0, after(grad_attn, low_half[0], sent))
+    high_chain = Scatter(high_half[5], high_half[6], 0)
     rounds.land(high_half[0])
     rounds.chains.append(high_chain)
     sent = rounds.send()
     short_hist = table_histogram(
-        scalars, after(codes, high_half[0], sent), low_half[3], high_half[3]
+        scalars, after(onehots, high_half[0], sent), low_half[3], high_half[3]
     )
-    sent = rounds.turn(short_hist)
     lent, own_grads, attn_gain_part = key_gradients(
         scalars,
         low_half[:3],
         high_half[:3],
         weights,
-        after(pack, short_hist, sent),
+        after(pack, short_hist),
         hidden_in,
         picked_x,
     )
@@ -1364,7 +1402,7 @@
     ).reshape(-1, 128)
     small_rows = small_part.shape[0]
     small_part = jnp.pad(small_part, ((0, 128 - small_rows), (0, 0)))
-    landed = rounds.land(lent)
+    landed = rounds.land(lent, short_hist)
     small_parts = lax.all_gather(after(small_part, landed), ("row", "col"), axis=0, tiled=True)
     sent = rounds.send()
     lent = after(lent, sent).reshape(4, -1, D)

time: 484 us -> 504 us (1.041)
  Pallas kernels: 220 us -> 249 us
  starting transfers between devices: 53.2 us -> 45.2 us
    pallas_call x0 -> x1, Pallas kernels: none -> 19.2 us  [bucket_onehots(): pl.pallas_call(onehot_kernel, grid=(FEW // HIST_ROWS,), in_specs=[pl.Bloc...]
    all_gather x1, waiting for transfers between devices: 70.4 us -> 51.6 us  [on_device(): weights = lax.all_gather(packed_weights, ('row', 'col'), axis=0, tiled=True)]
    pallas_call x1, Pallas kernels: 19.9 us -> 29.9 us  [table_histogram(): pl.pallas_call(histogram_kernel, grid_spec=pltpu.PrefetchScalarGridSpec(n...]
    ppermute x28, starting transfers between devices: 38.1 us -> 31 us  [exchange(): return lax.ppermute(values, axis, pairs)]
    ppermute x4, waiting for transfers between devices: 1.68 us -> 7.79 us  [shifted(): lax.ppermute(block[0], axis, backward)]
    ppermute x4, waiting for transfers between devices: 0.01 us -> 5.68 us  [shifted(): lax.ppermute(block[1], axis, forward)]
    unnamed x94 -> x92, local copies, waits for them, and re-layouts: 12.5 us -> 15.4 us
  transfers between devices with their start and end apart: 38 -> 38, of which waited for: 12 -> 12; matrix products, arithmetic and copies ran while one was open for 10% -> 10% of each run, Pallas kernels for 29% -> 35%
where the time goes in v4:
time: 504 us; the launch traced here: 497 us
  Pallas kernels  249 us (49%)
  waiting for transfers between devices  123 us (24%)
  starting transfers between devices  45.2 us (9%)
  local copies, waits for them, and re-layouts  38.9 us (8%)
  between operations  16.3 us (3%)
  other arithmetic  15.9 us (3%)
  matrix products  8.36 us (2%)
    ppermute x28, waiting for transfers between devices, exchange(): return lax.ppermute(values, axis, pairs)  58 us
    all_gather x1, waiting for transfers between devices, on_device(): weights = lax.all_gather(packed_weights, ('row', 'col'), axis=0, tiled=True)  51.6 us
    pallas_call x1, Pallas kernels, feed_forward(): pl.pallas_call(kernel, grid_spec=pltpu.PrefetchScalarGridSpec(num_scalar_...  45.7 us
    pallas_call x2, Pallas kernels, attention_backward(): pl.pallas_call(functools.partial(backward_kernel, first_head=half * heads...  39.5 us
    pallas_call x2, Pallas kernels, layout_bias(): pl.pallas_call(functools.partial(bias_kernel, first_head=first_head), gri...  34.6 us
    ppermute x28, starting transfers between devices, exchange(): return lax.ppermute(values, axis, pairs)  31 us
    pallas_call x8, Pallas kernels, piece_sums(): pl.pallas_call(functools.partial(sum_kernel, shares=shares), grid=(steps,...  30.9 us
    pallas_call x1, Pallas kernels, table_histogram(): pl.pallas_call(histogram_kernel, grid_spec=pltpu.PrefetchScalarGridSpec(n...  29.9 us
  transfers between devices with their start and end apart: 38, of which 12 were waited for; matrix products, arithmetic and copies ran while one was open for 10% of the time, Pallas kernels for 35%

profile of v4, /device:TPU:0, one launch (start us, length us, event | category | flops | bytes accessed | tf_op | source)
XLA Modules:
  0.0 497.2 jit_solution(1958854008157256381)
XLA Ops:
  7.3 2.2 pack_shards.1
  9.8 4.1 collective-permute-start
  20.8 2.1 gather_fusion
  22.9 1.6 collective-permute-start.1
  24.6 1.4 gather_fusion.1
  26.1 3.1 gather_fusion.2
  30.5 1.4 collective-permute-start.4
  33.3 3.4 collective-permute-start.6
  36.7 1.5 collective-permute-start.7
  41.2 3.6 collective-permute-start.2
  47.8 3.2 multiply_add_fusion.codes_ref
  51.6 1.4 collective-permute-start.3
  53.8 2.5 fusion
  56.3 1.5 collective-permute-done.3
  60.4 1.6 gather_fusion.4
  66.0 17.3 %layout_bias.2.low_bias_ref = f32[8,384,512]{2,1,0:T(8,128)} custom-call(s32[1024,512]{1,0:T(8,128)} %multiply_add_fusion.codes_ref, f32[48,128]{1,0:T(8,128)} %bitcast.104), custom_call_target="tpu_custom_call" | custom-call | flops 16000000000 | bytes 7000000 | tf_op jit(solution)/shard_map/layout_bias/pallas_call | solution.py:335
  83.3 17.3 %layout_bias.3.high_bias_ref = f32[8,384,512]{2,1,0:T(8,128)} custom-call(s32[1024,512]{1,0:T(8,128)} %multiply_add_fusion.codes_ref, f32[48,128]{1,0:T(8,128)} %bitcast.105), custom_call_target="tpu_custom_call" | custom-call | flops 16000000000 | bytes 7000000 | tf_op jit(solution)/shard_map/layout_bias/pallas_call | solution.py:335
  101.2 19.2 %bucket_onehots.1.chosen_ref = bf16[36864,512]{1,0:T(8,128)(2,1)} custom-call(s32[1024,512]{1,0:T(8,128)} %multiply_add_fusion.codes_ref), custom_call_target="tpu_custom_call" | custom-call | flops 40000000 | bytes 39000000 | tf_op jit(solution)/shard_map/bucket_onehots/pallas_call | solution.py:991
  121.7 1.8 fusion.2.picked_ref
  123.6 51.6 %all-gather.3.cloned.1.call-done.wq_ref.wk_ref.wv_ref.wo_ref.gate_ref.up_ref.packed_ref = bf16[1024,12544]{1,0:T(8,128)(2,1)} async-done(((bf16[32,12544]{1,0:T(8,128)(2,1)}), bf16[1024,12544]{1,0:T(8,128)(2,1)}) %all-gather.3.cloned.1.call-update) | async-done | bytes 25690128 | tf_op jit(solution)/shard_map/all_gather | solution.py:1224
  175.8 28.2 %attention_forward.1 = (bf16[512,1024]{1,0:T(8,128)(2,1)}, bf16[1024,1024]{1,0:T(8,128)(2,1)}, bf16[1024,1024]{1,0:T(8,128)(2,1)}, bf16[1024,512]{1,0:T(8,128)(2...) custom-call(s32[2]{0:T(128)} %pad_add_fusion.1.count_ref.scalar_ref, ...), custom_call_target="tpu_custom_call" | custom-call | flops 20000000000 | bytes 50000000 | tf_op jit(solution)/shard_map/attention_forward/pallas_call | solution.py:478
  204.0 45.7 %feed_forward.1 = (bf16[16,32,2816]{2,1,0:T(8,128)(2,1)}, bf16[16,32,2816]{2,1,0:T(8,128)(2,1)}, bf16[16,32,2816]{2,1,0:T(8,128)(2,1)}, bf16[16,32,2816]{2,1,0:T...) custom-call(s32[2]{0:T(128)} %pad_add_fusion.1.count_ref.scalar_ref,, ...), custom_call_target="tpu_custom_call" | custom-call | flops 27000000512 | bytes 44000000 | tf_op jit(solution)/shard_map/feed_forward/pallas_call | solution.py:662
  250.5 19.8 %attention_backward.2 = (bf16[512,512]{1,0:T(8,128)(2,1)}, bf16[1024,512]{1,0:T(8,128)(2,1)}, bf16[1024,512]{1,0:T(8,128)(2,1)}, bf16[8,384,512]{2,1,0:T(8,128)(...) custom-call(s32[2]{0:T(128)} %pad_add_fusion.1.count_ref.scalar_ref, ...), custom_call_target="tpu_custom_call" | custom-call | flops 15000000512 | bytes 30000000 | tf_op jit(solution)/shard_map/attention_backward/pallas_call | solution.py:898
  270.6 1.7 copy-done.2
  273.1 6.3 %piece_sums.8 = (bf16[8,32,2816]{2,1,0:T(8,128)(2,1)}, bf16[8,32,2816]{2,1,0:T(8,128)(2,1)}, bf16[8,88,1024]{2,1,0:T(8,128)(2,1)}) custom-call(bf16[16,32,2816]{2,1,0:T(8,128)(2,1)} %get-tuple-element.157.refs_0_, bf16[16,32,2816]{2,1,0:T(8,128)(2,1)} %collective-permute-done.9.refs_1_, ...), custom_call_target="tpu_custom_call" | custom-call | flops 8650752 | bytes 17301504 | tf_op jit(solution)/shard_map/piece_sums/pallas_call | solution.py:182
  279.5 1.6 collective-permute-start.13
  283.1 19.7 %attention_backward.3 = (bf16[512,512]{1,0:T(8,128)(2,1)}, bf16[1024,512]{1,0:T(8,128)(2,1)}, bf16[1024,512]{1,0:T(8,128)(2,1)}, bf16[8,384,512]{2,1,0:T(8,128)(...) custom-call(s32[2]{0:T(128)} %pad_add_fusion.1.count_ref.scalar_ref, ...), custom_call_target="tpu_custom_call" | custom-call | flops 15000000512 | bytes 30000000 | tf_op jit(solution)/shard_map/attention_backward/pallas_call | solution.py:898
  302.9 10.6 %collective-permute-done.14.refs_8_.refs_10_.refs_12_.refs_14_ = bf16[8,88,1024]{2,1,0:T(8,128)(2,1)S(1)} collective-permute-done((bf16[8,88,1024]{2,1,0:T(8,128)(2,1)}, bf16[8,88,1024]{2,1,0:T(8,128)(2,1)S(1)}, u32[]{:S(2)}, u32[]{:S(2)}) %collective-permute-start.14) | collective-permute-done | bytes 1441824 | tf_op jit(solution)/shard_map/ppermute | solution.py:78
  315.8 5.9 %piece_sums.9 = (bf16[4,32,2816]{2,1,0:T(8,128)(2,1)}, bf16[4,32,2816]{2,1,0:T(8,128)(2,1)}, bf16[4,88,1024]{2,1,0:T(8,128)(2,1)}, bf16[8,32,2048]{2,1,0:T(8,128)(2,1)}) custom-call(bf16[16,32,2816]{2,1,0:T(8,128)(2,1)} %get-tuple-element.157.refs_0_, bf16[16,32,2816]{2,1,0:T(8,128)(2,1)} %collective-permute-done.9.refs_1_, bf16[8,32,2816]{2,1,0:T(8,128)(2,1)} %copy-done.8, ...), custom_call_target="tpu_custom_call" | custom-call | flops 8585216 | bytes 17170432 | tf_op jit(solution)/shard_map/piece_sums/pallas_call | solution.py:182
  321.8 1.7 collective-permute-start.19
  326.3 29.9 %table_histogram.1 = f32[96,256]{1,0:T(8,128)} custom-call(s32[2]{0:T(128)} %pad_add_fusion.1.count_ref.scalar_ref, bf16[36864,512]{1,0:T(8,128)(2,1)} %bucket_onehots.1.chosen_ref, bf16[8,384,512]{2,1,0:T(8,128)(2,1)} %get-tuple-element.183.low_ref, bf16[8,384,512]{2,1,0:T(8,128)(2,1)} %get-tuple-element.184.high_ref), custom_call_target="tpu_custom_call" | custom-call | flops 10000000000 | bytes 45000000 | tf_op jit(solution)/shard_map/table_histogram/pallas_call | solution.py:1033
  357.4 13.8 %key_gradients.1 = (bf16[512,1024]{1,0:T(8,128)(2,1)}, f32[512,1024]{1,0:T(8,128)}, f32[8,1024]{1,0:T(8,128)}) custom-call(s32[2]{0:T(128)} %pad_add_fusion.1.count_ref.scalar_ref, bf16[512,512]{1,0:T(8,128)(2,1)} %get-tuple-element.155.dq_low_ref, bf16[512,512]{1,0:T(8,128)(2,1)} %get-tuple-element.167.dq_high_ref, ...), custom_call_target="tpu_custom_call" | custom-call | flops 8999999488 | bytes 18000000 | tf_op jit(solution)/shard_map/key_gradients/pallas_call | solution.py:1119
  374.2 4.9 piece_sums.10
  381.9 1.5 collective-permute-start.26
  384.7 22.8 %collective-permute-done.26.refs_14_.refs_16_ = bf16[2,88,1024]{2,1,0:T(8,128)(2,1)S(1)} collective-permute-done((bf16[2,88,1024]{2,1,0:T(8,128)(2,1)}, bf16[2,88,1024]{2,1,0:T(8,128)(2,1)S(1)}, u32[]{:S(2)}, u32[]{:S(2)}) %collective-permute-start.26) | collective-permute-done | bytes 360480 | tf_op jit(solution)/shard_map/ppermute | solution.py:78
  409.7 4.1 piece_sums.11
  416.2 2.6 collective-permute-start.23
  420.1 2.7 collective-permute-start.29
  422.8 5.7 %collective-permute-done.23 = bf16[128,1024]{1,0:T(8,128)(2,1)S(1)} collective-permute-done((bf16[128,1024]{1,0:T(8,128)(2,1)S(1)}, bf16[128,1024]{1,0:T(8,128)(2,1)S(1)}, u32[]{:S(2)}, u32[]{:S(2)}) %collective-permute-start.23) | collective-permute-done | bytes 262176 | tf_op jit(solution)/shard_map/ppermute | solution.py:35
  428.5 7.8 %collective-permute-done.24 = bf16[128,1024]{1,0:T(8,128)(2,1)S(1)} collective-permute-done((bf16[128,1024]{1,0:T(8,128)(2,1)S(1)}, bf16[128,1024]{1,0:T(8,128)(2,1)S(1)}, u32[]{:S(2)}, u32[]{:S(2)}) %collective-permute-start.24) | collective-permute-done | bytes 262176 | tf_op jit(solution)/shard_map/ppermute | solution.py:36
  437.9 5.5 %input_gradient.1 = bf16[512,1024]{1,0:T(8,128)(2,1)} custom-call(f32[512,1024]{1,0:T(8,128)} %get-tuple-element.186.own_ref, bf16[512,512]{1,0:T(8,128)(2,1)} %fusion.13.owner_ref, bf16[512,1024]{1,0:T(8,128)(2,1)} %pad_maximum_fusion.returned_ref, bf16[512,1024]{1,0:T(8,128)(2,1)} %x_ref.5, f32[8,1024]{1,0:T(8,128)} %broadcast_in_dim.64.gain_ref, ...), custom_call_target="tpu_custom_call" | custom-call | flops 1000000000 | bytes 8000000 | tf_op jit(solution)/shard_map/input_gradient/pallas_call | solution.py:1168
  444.9 2.4 piece_sums.12
  447.7 3.5 collective-permute-start.34
  451.4 10.2 %collective-permute-done.32.refs_4_.refs_10_ = bf16[2,32,2048]{2,1,0:T(8,128)(2,1)S(1)} collective-permute-done((bf16[2,32,2048]{2,1,0:T(8,128)(2,1)}, bf16[2,32,2048]{2,1,0:T(8,128)(2,1)S(1)}, u32[]{:S(2)}, u32[]{:S(2)}) %collective-permute-start.32) | collective-permute-done | bytes 262176 | tf_op jit(solution)/shard_map/ppermute | solution.py:78
  462.3 1.9 piece_sums.13
  464.2 9.7 %collective-permute-done.34.refs_5_.refs_11_ = bf16[1,32,5632]{2,1,0:T(8,128)(2,1)S(1)} collective-permute-done((bf16[1,32,5632]{2,1,0:T(8,128)(2,1)S(1)}, bf16[1,32,5632]{2,1,0:T(8,128)(2,1)S(1)}, u32[]{:S(2)}, u32[]{:S(2)}) %collective-permute-start.34) | collective-permute-done | bytes 360480 | tf_op jit(solution)/shard_map/ppermute | solution.py:78
  474.6 3.1 piece_sums.15
  479.3 2.3 piece_sums.14
  (232 shorter events, 63.7 us)
Async XLA Ops:
  7.2 9.6 %copy-start.1 = (bf16[512,1024]{1,0:T(8,128)(2,1)S(1)}, bf16[512,1024]{1,0:T(8,128)(2,1)}, u32[]{:S(2)}) copy-start(bf16[512,1024]{1,0:T(8,128)(2,1)} %x_ref.5) | copy-start | bytes 3145732
  7.3 167.9 %all-gather.3.cloned.1.call-start = ((), (), s32[]{:S(2)}) async-start(), calls=%async_computation | async-start | bytes 26492928 | tf_op jit(solution)/shard_map/all_gather | solution.py:1224
  9.6 476.6 %all-gather.5.cloned.1.call-start = ((), (), s32[]{:S(2)}) async-start(), calls=%async_computation.1 | async-start | bytes 2162688 | tf_op jit(solution)/shard_map/all_gather | solution.py:1406
  9.8 13.1 %collective-permute-start = (bf16[1,32,128]{1,2,0:T(8,128)(2,1)S(1)}, bf16[1,32,128]{1,2,0:T(8,128)(2,1)S(1)}, u32[]{:S(2)}, u32[]{:S(2)}) collective-permute-start(bf16[1,32,128]{1,2,0:T(8,128)(2,1)S(1)} %bitcast.101), channel_id=1, source_target_pairs={{0,16},{4,20},{8,24},{12,28},{16,0},{20,4},{24,8},{28,12},{1,17},{... | collective-permute-start | bytes 24584 | tf_op jit(solution)/shard_map/ppermute | solution.py:78
  22.9 18.3 %collective-permute-start.1 = (bf16[2,32,128]{2,1,0:T(8,128)(2,1)S(1)}, bf16[2,32,128]{2,1,0:T(8,128)(2,1)S(1)}, u32[]{:S(2)}, u32[]{:S(2)}) collective-permute-start(bf16[2,32,128]{2,1,0:T(8,128)(2,1)S(1)} %pad_maximum_fusion.7), channel_id=1, source_target_pairs={{0,8},{4,12},{8,0},{12,4},{16,24},{20,28},{24,16},{28,20},{1,9},{5... | collective-permute-start | bytes 49160 | tf_op jit(solution)/shard_map/ppermute | solution.py:78
  30.5 14.4 %copy-start.37 = (s32[512,1024]{1,0:T(8,128)S(1)}, s32[512,1024]{1,0:T(8,128)}, u32[]{:S(2)}) copy-start(s32[512,1024]{1,0:T(8,128)} %param.39) | copy-start | bytes 6291460
  30.5 23.1 %collective-permute-start.4 = (bf16[128,1024]{1,0:T(8,128)(2,1)S(1)}, bf16[128,1024]{1,0:T(8,128)(2,1)S(1)}, u32[]{:S(2)}, u32[]{:S(2)}) collective-permute-start(bf16[128,1024]{1,0:T(8,128)(2,1)S(1)} %get-tuple-element.232), channel_id=1, source_target_pairs={{0,4},{4,8},{8,12},{12,16},{16,20},{20,24},{24,28},{1,5},{5,9},{9,... | collective-permute-start | bytes 786440 | tf_op jit(solution)/shard_map/ppermute | solution.py:35
  32.0 21.7 %collective-permute-start.5 = (bf16[128,1024]{1,0:T(8,128)(2,1)S(1)}, bf16[128,1024]{1,0:T(8,128)(2,1)S(1)}, u32[]{:S(2)}, u32[]{:S(2)}) collective-permute-start(bf16[128,1024]{1,0:T(8,128)(2,1)S(1)} %get-tuple-element.231), channel_id=1, source_target_pairs={{4,0},{8,4},{12,8},{16,12},{20,16},{24,20},{28,24},{5,1},{9,5},{13... | collective-permute-start | bytes 786440 | tf_op jit(solution)/shard_map/ppermute | solution.py:36
  33.3 20.4 %collective-permute-start.6 = (bf16[128,1024]{1,0:T(8,128)(2,1)S(1)}, bf16[128,1024]{1,0:T(8,128)(2,1)S(1)}, u32[]{:S(2)}, u32[]{:S(2)}) collective-permute-start(bf16[128,1024]{1,0:T(8,128)(2,1)S(1)} %get-tuple-element.230), channel_id=1, source_target_pairs={{0,1},{1,2},{2,3},{4,5},{5,6},{6,7},{8,9},{9,10},{10,11},{12,13},{... | collective-permute-start | bytes 786440 | tf_op jit(solution)/shard_map/ppermute | solution.py:35
  36.7 17.0 %collective-permute-start.7 = (bf16[128,1024]{1,0:T(8,128)(2,1)S(1)}, bf16[128,1024]{1,0:T(8,128)(2,1)S(1)}, u32[]{:S(2)}, u32[]{:S(2)}) collective-permute-start(bf16[128,1024]{1,0:T(8,128)(2,1)S(1)} %get-tuple-element.229), channel_id=1, source_target_pairs={{1,0},{2,1},{3,2},{5,4},{6,5},{7,6},{9,8},{10,9},{11,10},{13,12},{... | collective-permute-start | bytes 786440 | tf_op jit(solution)/shard_map/ppermute | solution.py:36
  40.5 13.3 %copy-start.9 = (bf16[1024,1024]{1,0:T(8,128)(2,1)}, bf16[1024,1024]{1,0:T(8,128)(2,1)S(1)}, u32[]{:S(2)}) copy-start(bf16[1024,1024]{1,0:T(8,128)(2,1)S(1)} %fusion.4.pack_ref) | copy-start | bytes 6291460
  41.2 10.4 %collective-permute-start.2 = (bf16[4,32,128]{2,1,0:T(8,128)(2,1)S(1)}, bf16[4,32,128]{2,1,0:T(8,128)(2,1)S(1)}, u32[]{:S(2)}, u32[]{:S(2)}) collective-permute-start(bf16[4,32,128]{2,1,0:T(8,128)(2,1)S(1)} %pad_maximum_fusion.6), channel_id=1, source_target_pairs={{0,2},{1,3},{2,0},{3,1},{4,6},{5,7},{6,4},{7,5},{8,10},{9,11},{10,... | collective-permute-start | bytes 98312 | tf_op jit(solution)/shard_map/ppermute | solution.py:78
  51.6 6.1 %collective-permute-start.3 = (bf16[8,32,128]{2,1,0:T(8,128)(2,1)S(1)}, bf16[8,32,128]{2,1,0:T(8,128)(2,1)S(1)}, u32[]{:S(2)}, u32[]{:S(2)}) collective-permute-start(bf16[8,32,128]{2,1,0:T(8,128)(2,1)S(1)} %pad_maximum_fusion.5), channel_id=1, source_target_pairs={{0,1},{1,0},{2,3},{3,2},{4,5},{5,4},{6,7},{7,6},{8,9},{9,8},{10,11... | collective-permute-start | bytes 196616 | tf_op jit(solution)/shard_map/ppermute | solution.py:78
  56.3 65.4 %copy-start.13 = (bf16[1024,1024]{1,0:T(8,128)(2,1)}, bf16[1024,1024]{1,0:T(8,128)(2,1)S(1)}, u32[]{:S(2)}) copy-start(bf16[1024,1024]{1,0:T(8,128)(2,1)S(1)} %get-tuple-element.260.picked_ref) | copy-start | bytes 6291460
  58.4 1.3 collective-permute-start.8
  101.2 20.6 %copy-start.27 = (f32[1024]{0:T(1024)}, f32[1024]{0:T(1024)S(1)}, u32[]{:S(2)}) copy-start(f32[1024]{0:T(1024)S(1)} %reshape.407) | copy-start | bytes 12292
  101.2 19.2 %copy-start.31 = (f32[512]{0:T(512)S(1)}, f32[512]{0:T(512)}, u32[]{:S(2)}) copy-start(f32[512]{0:T(512)} %add_rsqrt_fusion.1) | copy-start | bytes 6148
  249.7 20.9 %collective-permute-start.11 = (bf16[16,88,1024]{2,1,0:T(8,128)(2,1)}, bf16[16,88,1024]{2,1,0:T(8,128)(2,1)S(1)}, u32[]{:S(2)}, u32[]{:S(2)}) collective-permute-start(bf16[16,88,1024]{2,1,0:T(8,128)(2,1)} %get-tuple-element.147), channel_id=1, source_target_pairs={{0,4},{4,0},{8,12},{12,8},{16,20},{20,16},{24,28},{28,24},{1,5},{5... | collective-permute-start | bytes 8650760 | tf_op jit(solution)/shard_map/ppermute | solution.py:78
  250.0 20.6 %collective-permute-start.10 = (bf16[16,32,2816]{2,1,0:T(8,128)(2,1)}, bf16[16,32,2816]{2,1,0:T(8,128)(2,1)S(1)}, u32[]{:S(2)}, u32[]{:S(2)}) collective-permute-start(bf16[16,32,2816]{2,1,0:T(8,128)(2,1)} %get-tuple-element.146), channel_id=1, source_target_pairs={{0,4},{4,0},{8,12},{12,8},{16,20},{20,16},{24,28},{28,24},{1,5},{5... | collective-permute-start | bytes 8650760 | tf_op jit(solution)/shard_map/ppermute | solution.py:78
  250.2 20.4 %collective-permute-start.9 = (bf16[16,32,2816]{2,1,0:T(8,128)(2,1)}, bf16[16,32,2816]{2,1,0:T(8,128)(2,1)}, u32[]{:S(2)}, u32[]{:S(2)}) collective-permute-start(bf16[16,32,2816]{2,1,0:T(8,128)(2,1)} %get-tuple-element.145), channel_id=1, source_target_pairs={{0,4},{4,0},{8,12},{12,8},{16,20},{20,16},{24,28},{28,24},{1,5},{5... | collective-permute-start | bytes 8650760 | tf_op jit(solution)/shard_map/ppermute | solution.py:78
  270.3 32.5 %collective-permute-start.15 = (bf16[16,32,2048]{2,1,0:T(8,128)(2,1)}, bf16[16,32,2048]{2,1,0:T(8,128)(2,1)}, u32[]{:S(2)}, u32[]{:S(2)}) collective-permute-start(bf16[16,32,2048]{2,1,0:T(8,128)(2,1)} %get-tuple-element.156), channel_id=1, source_target_pairs={{0,4},{4,0},{8,12},{12,8},{16,20},{20,16},{24,28},{28,24},{1,5},{5... | collective-permute-start | bytes 6291464 | tf_op jit(solution)/shard_map/ppermute | solution.py:78
  279.4 34.0 %collective-permute-start.14 = (bf16[8,88,1024]{2,1,0:T(8,128)(2,1)}, bf16[8,88,1024]{2,1,0:T(8,128)(2,1)S(1)}, u32[]{:S(2)}, u32[]{:S(2)}) collective-permute-start(bf16[8,88,1024]{2,1,0:T(8,128)(2,1)} %get-tuple-element.165), channel_id=1, source_target_pairs={{0,8},{4,12},{8,0},{12,4},{16,24},{20,28},{24,16},{28,20},{1,9},{5... | collective-permute-start | bytes 4325384 | tf_op jit(solution)/shard_map/ppermute | solution.py:78
  279.5 34.0 %collective-permute-start.13 = (bf16[8,32,2816]{2,1,0:T(8,128)(2,1)}, bf16[8,32,2816]{2,1,0:T(8,128)(2,1)S(1)}, u32[]{:S(2)}, u32[]{:S(2)}) collective-permute-start(bf16[8,32,2816]{2,1,0:T(8,128)(2,1)} %get-tuple-element.164), channel_id=1, source_target_pairs={{0,2},{1,3},{2,0},{3,1},{4,6},{5,7},{6,4},{7,5},{8,10},{9,11},{10,... | collective-permute-start | bytes 4325384 | tf_op jit(solution)/shard_map/ppermute | solution.py:78
  281.1 33.7 %collective-permute-start.12 = (bf16[8,32,2816]{2,1,0:T(8,128)(2,1)}, bf16[8,32,2816]{2,1,0:T(8,128)(2,1)S(1)}, u32[]{:S(2)}, u32[]{:S(2)}) collective-permute-start(bf16[8,32,2816]{2,1,0:T(8,128)(2,1)} %get-tuple-element.163), channel_id=1, source_target_pairs={{0,1},{1,0},{2,3},{3,2},{4,5},{5,4},{6,7},{7,6},{8,9},{9,8},{10,11... | collective-permute-start | bytes 4325384 | tf_op jit(solution)/shard_map/ppermute | solution.py:78
  302.8 69.7 %collective-permute-start.20 = (bf16[16,32,2048]{2,1,0:T(8,128)(2,1)}, bf16[16,32,2048]{2,1,0:T(8,128)(2,1)S(1)}, u32[]{:S(2)}, u32[]{:S(2)}) collective-permute-start(bf16[16,32,2048]{2,1,0:T(8,128)(2,1)} %get-tuple-element.172), channel_id=1, source_target_pairs={{0,4},{4,0},{8,12},{12,8},{16,20},{20,16},{24,28},{28,24},{1,5},{5... | collective-permute-start | bytes 6291464 | tf_op jit(solution)/shard_map/ppermute | solution.py:78
  321.8 50.8 %collective-permute-start.19 = (bf16[8,32,2048]{2,1,0:T(8,128)(2,1)}, bf16[8,32,2048]{2,1,0:T(8,128)(2,1)S(1)}, u32[]{:S(2)}, u32[]{:S(2)}) collective-permute-start(bf16[8,32,2048]{2,1,0:T(8,128)(2,1)} %get-tuple-element.181), channel_id=1, source_target_pairs={{0,8},{4,12},{8,0},{12,4},{16,24},{20,28},{24,16},{28,20},{1,9},{5... | collective-permute-start | bytes 3145736 | tf_op jit(solution)/shard_map/ppermute | solution.py:78
  323.5 49.0 %collective-permute-start.16 = (bf16[4,32,2816]{2,1,0:T(8,128)(2,1)}, bf16[4,32,2816]{2,1,0:T(8,128)(2,1)}, u32[]{:S(2)}, u32[]{:S(2)}) collective-permute-start(bf16[4,32,2816]{2,1,0:T(8,128)(2,1)} %get-tuple-element.178), channel_id=1, source_target_pairs={{0,2},{1,3},{2,0},{3,1},{4,6},{5,7},{6,4},{7,5},{8,10},{9,11},{10,... | collective-permute-start | bytes 2162696 | tf_op jit(solution)/shard_map/ppermute | solution.py:78
  324.2 48.3 %collective-permute-start.17 = (bf16[4,32,2816]{2,1,0:T(8,128)(2,1)}, bf16[4,32,2816]{2,1,0:T(8,128)(2,1)}, u32[]{:S(2)}, u32[]{:S(2)}) collective-permute-start(bf16[4,32,2816]{2,1,0:T(8,128)(2,1)} %get-tuple-element.179), channel_id=1, source_target_pairs={{0,1},{1,0},{2,3},{3,2},{4,5},{5,4},{6,7},{7,6},{8,9},{9,8},{10,11... | collective-permute-start | bytes 2162696 | tf_op jit(solution)/shard_map/ppermute | solution.py:78
  325.5 47.1 %collective-permute-start.18 = (bf16[4,88,1024]{2,1,0:T(8,128)(2,1)}, bf16[4,88,1024]{2,1,0:T(8,128)(2,1)}, u32[]{:S(2)}, u32[]{:S(2)}) collective-permute-start(bf16[4,88,1024]{2,1,0:T(8,128)(2,1)} %get-tuple-element.180), channel_id=1, source_target_pairs={{0,1},{1,0},{2,3},{3,2},{4,5},{5,4},{6,7},{7,6},{8,9},{9,8},{10,11... | collective-permute-start | bytes 2162696 | tf_op jit(solution)/shard_map/ppermute | solution.py:78
  326.3 29.9 %copy-start.29 = (f32[96,128]{1,0:T(8,128)S(1)}, f32[96,128]{1,0:T(8,128)}, u32[]{:S(2)}) copy-start(f32[96,128]{1,0:T(8,128)} %get-tuple-element.213) | copy-start | bytes 147460
  326.3 29.9 %copy-start.30 = (f32[96,128]{1,0:T(8,128)S(1)}, f32[96,128]{1,0:T(8,128)}, u32[]{:S(2)}) copy-start(f32[96,128]{1,0:T(8,128)} %get-tuple-element.214) | copy-start | bytes 147460
  379.1 28.5 %collective-permute-start.28 = (bf16[8,32,2048]{2,1,0:T(8,128)(2,1)}, bf16[8,32,2048]{2,1,0:T(8,128)(2,1)S(1)}, u32[]{:S(2)}, u32[]{:S(2)}) collective-permute-start(bf16[8,32,2048]{2,1,0:T(8,128)(2,1)} %get-tuple-element.197), channel_id=1, source_target_pairs={{0,1},{1,0},{2,3},{3,2},{4,5},{5,4},{6,7},{7,6},{8,9},{9,8},{10,11... | collective-permute-start | bytes 3145736 | tf_op jit(solution)/shard_map/ppermute | solution.py:78
  380.4 27.1 %collective-permute-start.25 = (bf16[2,32,5632]{2,1,0:T(8,128)(2,1)}, bf16[2,32,5632]{2,1,0:T(8,128)(2,1)S(1)}, u32[]{:S(2)}, u32[]{:S(2)}) collective-permute-start(bf16[2,32,5632]{2,1,0:T(8,128)(2,1)} %get-tuple-element.194), channel_id=1, source_target_pairs={{0,8},{4,12},{8,0},{12,4},{16,24},{20,28},{24,16},{28,20},{1,9},{5... | collective-permute-start | bytes 2162696 | tf_op jit(solution)/shard_map/ppermute | solution.py:78
  380.8 26.8 %collective-permute-start.27 = (bf16[4,32,2048]{2,1,0:T(8,128)(2,1)}, bf16[4,32,2048]{2,1,0:T(8,128)(2,1)S(1)}, u32[]{:S(2)}, u32[]{:S(2)}) collective-permute-start(bf16[4,32,2048]{2,1,0:T(8,128)(2,1)} %get-tuple-element.196), channel_id=1, source_target_pairs={{0,2},{1,3},{2,0},{3,1},{4,6},{5,7},{6,4},{7,5},{8,10},{9,11},{10,... | collective-permute-start | bytes 1572872 | tf_op jit(solution)/shard_map/ppermute | solution.py:78
  381.9 25.7 %collective-permute-start.26 = (bf16[2,88,1024]{2,1,0:T(8,128)(2,1)}, bf16[2,88,1024]{2,1,0:T(8,128)(2,1)S(1)}, u32[]{:S(2)}, u32[]{:S(2)}) collective-permute-start(bf16[2,88,1024]{2,1,0:T(8,128)(2,1)} %get-tuple-element.195), channel_id=1, source_target_pairs={{0,16},{4,20},{8,24},{12,28},{16,0},{20,4},{24,8},{28,12},{1,17},{... | collective-permute-start | bytes 1081352 | tf_op jit(solution)/shard_map/ppermute | solution.py:78
  383.4 36.7 %collective-permute-start.21 = (bf16[128,1024]{1,0:T(8,128)(2,1)S(1)}, bf16[128,1024]{1,0:T(8,128)(2,1)S(1)}, u32[]{:S(2)}, u32[]{:S(2)}) collective-permute-start(bf16[128,1024]{1,0:T(8,128)(2,1)S(1)} %get-tuple-element.225), channel_id=1, source_target_pairs={{0,4},{4,8},{8,12},{12,16},{16,20},{20,24},{24,28},{1,5},{5,9},{9,... | collective-permute-start | bytes 786440 | tf_op jit(solution)/shard_map/ppermute | solution.py:35
  413.7 23.6 %copy-start.28 = (f32[1024]{0:T(1024)S(1)}, f32[1024]{0:T(1024)}, u32[]{:S(2)}) copy-start(f32[1024]{0:T(1024)} %copy-done.27) | copy-start | bytes 12292
  413.8 29.7 %collective-permute-start.30 = (bf16[4,32,2048]{2,1,0:T(8,128)(2,1)}, bf16[4,32,2048]{2,1,0:T(8,128)(2,1)S(1)}, u32[]{:S(2)}, u32[]{:S(2)}) collective-permute-start(bf16[4,32,2048]{2,1,0:T(8,128)(2,1)} %get-tuple-element.202), channel_id=1, source_target_pairs={{0,2},{1,3},{2,0},{3,1},{4,6},{5,7},{6,4},{7,5},{8,10},{9,11},{10,... | collective-permute-start | bytes 1572872 | tf_op jit(solution)/shard_map/ppermute | solution.py:78
  414.9 7.9 %collective-permute-start.22 = (bf16[128,1024]{1,0:T(8,128)(2,1)S(1)}, bf16[128,1024]{1,0:T(8,128)(2,1)S(1)}, u32[]{:S(2)}, u32[]{:S(2)}) collective-permute-start(bf16[128,1024]{1,0:T(8,128)(2,1)S(1)} %get-tuple-element.228), channel_id=1, source_target_pairs={{4,0},{8,4},{12,8},{16,12},{20,16},{24,20},{28,24},{5,1},{9,5},{13... | collective-permute-start | bytes 786440 | tf_op jit(solution)/shard_map/ppermute | solution.py:36
  416.2 12.3 %collective-permute-start.23 = (bf16[128,1024]{1,0:T(8,128)(2,1)S(1)}, bf16[128,1024]{1,0:T(8,128)(2,1)S(1)}, u32[]{:S(2)}, u32[]{:S(2)}) collective-permute-start(bf16[128,1024]{1,0:T(8,128)(2,1)S(1)} %get-tuple-element.227), channel_id=1, source_target_pairs={{0,1},{1,2},{2,3},{4,5},{5,6},{6,7},{8,9},{9,10},{10,11},{12,13},{... | collective-permute-start | bytes 786440 | tf_op jit(solution)/shard_map/ppermute | solution.py:35
  418.8 17.5 %collective-permute-start.24 = (bf16[128,1024]{1,0:T(8,128)(2,1)S(1)}, bf16[128,1024]{1,0:T(8,128)(2,1)S(1)}, u32[]{:S(2)}, u32[]{:S(2)}) collective-permute-start(bf16[128,1024]{1,0:T(8,128)(2,1)S(1)} %get-tuple-element.226), channel_id=1, source_target_pairs={{1,0},{2,1},{3,2},{5,4},{6,5},{7,6},{9,8},{10,9},{11,10},{13,12},{... | collective-permute-start | bytes 786440 | tf_op jit(solution)/shard_map/ppermute | solution.py:36
  420.1 23.3 %collective-permute-start.29 = (bf16[2,32,2048]{2,1,0:T(8,128)(2,1)}, bf16[2,32,2048]{2,1,0:T(8,128)(2,1)S(1)}, u32[]{:S(2)}, u32[]{:S(2)}) collective-permute-start(bf16[2,32,2048]{2,1,0:T(8,128)(2,1)} %get-tuple-element.201), channel_id=1, source_target_pairs={{0,1},{1,0},{2,3},{3,2},{4,5},{5,4},{6,7},{7,6},{8,9},{9,8},{10,11... | collective-permute-start | bytes 786440 | tf_op jit(solution)/shard_map/ppermute | solution.py:78
  447.3 14.3 %collective-permute-start.32 = (bf16[2,32,2048]{2,1,0:T(8,128)(2,1)}, bf16[2,32,2048]{2,1,0:T(8,128)(2,1)S(1)}, u32[]{:S(2)}, u32[]{:S(2)}) collective-permute-start(bf16[2,32,2048]{2,1,0:T(8,128)(2,1)} %get-tuple-element.208), channel_id=1, source_target_pairs={{0,8},{4,12},{8,0},{12,4},{16,24},{20,28},{24,16},{28,20},{1,9},{5... | collective-permute-start | bytes 786440 | tf_op jit(solution)/shard_map/ppermute | solution.py:78
  447.7 26.1 %collective-permute-start.34 = (bf16[1,32,5632]{2,1,0:T(8,128)(2,1)S(1)}, bf16[1,32,5632]{2,1,0:T(8,128)(2,1)S(1)}, u32[]{:S(2)}, u32[]{:S(2)}) collective-permute-start(bf16[1,32,5632]{2,1,0:T(8,128)(2,1)S(1)} %copy-done.39), channel_id=1, source_target_pairs={{0,16},{4,20},{8,24},{12,28},{16,0},{20,4},{24,8},{28,12},{1,17},{... | collective-permute-start | bytes 1081352 | tf_op jit(solution)/shard_map/ppermute | solution.py:78
  451.2 12.9 %collective-permute-start.35 = (bf16[1,88,1024]{2,1,0:T(8,128)(2,1)S(1)}, bf16[1,88,1024]{2,1,0:T(8,128)(2,1)S(1)}, u32[]{:S(2)}, u32[]{:S(2)}) collective-permute-start(bf16[1,88,1024]{2,1,0:T(8,128)(2,1)S(1)} %copy-done.40), channel_id=1, source_target_pairs={{0,2},{1,3},{2,0},{3,1},{4,6},{5,7},{6,4},{7,5},{8,10},{9,11},{10,... | collective-permute-start | bytes 540680 | tf_op jit(solution)/shard_map/ppermute | solution.py:78
  451.2 26.4 %collective-permute-start.31 = (bf16[1,32,2048]{2,1,0:T(8,128)(2,1)}, bf16[1,32,2048]{2,1,0:T(8,128)(2,1)S(1)}, u32[]{:S(2)}, u32[]{:S(2)}) collective-permute-start(bf16[1,32,2048]{2,1,0:T(8,128)(2,1)} %get-tuple-element.207), channel_id=1, source_target_pairs={{0,16},{4,20},{8,24},{12,28},{16,0},{20,4},{24,8},{28,12},{1,17},{... | collective-permute-start | bytes 393224 | tf_op jit(solution)/shard_map/ppermute | solution.py:78
  464.2 14.4 %collective-permute-start.33 = (bf16[1,32,2048]{2,1,0:T(8,128)(2,1)}, bf16[1,32,2048]{2,1,0:T(8,128)(2,1)S(1)}, u32[]{:S(2)}, u32[]{:S(2)}) collective-permute-start(bf16[1,32,2048]{2,1,0:T(8,128)(2,1)} %piece_sums.13), channel_id=1, source_target_pairs={{0,16},{4,20},{8,24},{12,28},{16,0},{20,4},{24,8},{28,12},{1,17},{... | collective-permute-start | bytes 393224 | tf_op jit(solution)/shard_map/ppermute | solution.py:78
  464.2 9.7 %copy-start.23 = (bf16[1,88,1024]{2,1,0:T(8,128)(2,1)}, bf16[1,88,1024]{2,1,0:T(8,128)(2,1)S(1)}, u32[]{:S(2)}) copy-start(bf16[1,88,1024]{2,1,0:T(8,128)(2,1)S(1)} %collective-permute-done.35.refs_17_) | copy-start | bytes 540676
  (32 other events, 90.2 us)
Sparse Core Ops, SparseCore 0:
  11.5 163.5 all-gather.2
  372.7 64.1 all-gather.4

commit v5 on v3

--- a/solution.py
+++ b/solution.py
@@ -49,7 +49,7 @@
     if kind == 1:
         return row_bits[:1] + col_bits[::-1] + row_bits[1:]
     if kind == 2:
-        return row_bits[:2] + col_bits + row_bits[2:]
+        return row_bits[:2] + col_bits[:1] + row_bits[2:] + col_bits[1:]
     return row_bits[:2] + col_bits[::-1] + row_bits[2:]
 
 
@@ -124,6 +124,14 @@
         self.flights = []
         self.chains = [chain for chain in self.chains if chain.stages]
         return landed
+
+    def land_with(self, values):
+        flights, values = lax.optimization_barrier(
+            ([flight for chains, flight in self.flights], values)
+        )
+        self.flights = [(chains, flight) for (chains, _), flight in zip(self.flights, flights)]
+        self.land()
+        return values
 
     def send(self):
         sums, firsts = {}, []
@@ -1329,13 +1337,13 @@
         )
 
     sent = rounds.send()
-    low_half = backward(0, 2, after(grad_attn, sent))
-    low_chain = Scatter(low_half[5], low_half[6], 2)
+    low_half = backward(0, 3, after(grad_attn, sent))
+    low_chain = Scatter(low_half[5], low_half[6], 3)
     rounds.land(low_half[0])
     rounds.chains.append(low_chain)
     sent = rounds.send()
-    high_half = backward(1, 1, after(grad_attn, low_half[0], sent))
-    high_chain = Scatter(high_half[5], high_half[6], 1)
+    high_half = backward(1, 0, after(grad_attn, low_half[0], sent))
+    high_chain = Scatter(high_half[5], high_half[6], 0)
     rounds.land(high_half[0])
     rounds.chains.append(high_chain)
     sent = rounds.send()
@@ -1371,12 +1379,12 @@
     back_above, back_below = shifted(lent[0:2], "row")
     back_left, back_right = shifted(lent[2:4], "col")
     returned = jnp.concatenate([back_above, back_below, back_left, back_right], 0)
-    landed = rounds.land()
+    returned = rounds.land_with(returned)
     sent = rounds.send()
     input_grad = input_gradient(
         own_grads,
         owner,
-        after(returned, landed, sent),
+        after(returned, sent),
         hidden_in,
         jnp.broadcast_to(gain_one, (8, D)),
         grad_middle,

time: 484 us -> 477 us (0.986)
    unnamed x94 -> x96, local copies, waits for them, and re-layouts: 12.5 us -> 12.4 us
  transfers between devices with their start and end apart: 38 -> 38, of which waited for: 12 -> 15; matrix products, arithmetic and copies ran while one was open for 10% -> 10% of each run, Pallas kernels for 29% -> 29%
where the time goes in v5:
time: 477 us; the launch traced here: 472 us
  Pallas kernels  220 us (46%)
  waiting for transfers between devices  125 us (26%)
  starting transfers between devices  50 us (10%)
  local copies, waits for them, and re-layouts  36.3 us (8%)
  between operations  16.3 us (3%)
  other arithmetic  16 us (3%)
  matrix products  8.33 us (2%)
    all_gather x1, waiting for transfers between devices, on_device(): weights = lax.all_gather(packed_weights, ('row', 'col'), axis=0, tiled=True)  70.4 us
    ppermute x28, waiting for transfers between devices, exchange(): return lax.ppermute(values, axis, pairs)  53 us
    pallas_call x1, Pallas kernels, feed_forward(): pl.pallas_call(kernel, grid_spec=pltpu.PrefetchScalarGridSpec(num_scalar_...  45.9 us
    pallas_call x2, Pallas kernels, attention_backward(): pl.pallas_call(functools.partial(backward_kernel, first_head=half * heads...  39.1 us
    ppermute x28, starting transfers between devices, exchange(): return lax.ppermute(values, axis, pairs)  34.6 us
    pallas_call x2, Pallas kernels, layout_bias(): pl.pallas_call(functools.partial(bias_kernel, first_head=first_head), gri...  34.6 us
    pallas_call x8, Pallas kernels, piece_sums(): pl.pallas_call(functools.partial(sum_kernel, shares=shares), grid=(steps,...  30.9 us
    pallas_call x1, Pallas kernels, attention_forward(): pl.pallas_call(attend_kernel, grid_spec=pltpu.PrefetchScalarGridSpec(num_...  27.8 us
  transfers between devices with their start and end apart: 38, of which 15 were waited for; matrix products, arithmetic and copies ran while one was open for 10% of the time, Pallas kernels for 29%

profile of v5, /device:TPU:0, one launch (start us, length us, event | category | flops | bytes accessed | tf_op | source)
XLA Modules:
  0.0 471.6 jit_solution(5461035114918796232)
XLA Ops:
  7.3 2.2 pack_shards.1
  9.8 4.1 collective-permute-start
  20.8 2.1 gather_fusion
  22.9 1.6 collective-permute-start.1
  26.1 3.1 gather_fusion.2
  33.3 3.4 collective-permute-start.6
  36.7 1.5 collective-permute-start.7
  41.2 3.6 collective-permute-start.2
  47.8 3.2 multiply_add_fusion.codes_ref
  53.8 2.5 fusion
  60.4 1.6 gather_fusion.4
  66.4 17.3 %layout_bias.2.low_bias_ref = f32[8,384,512]{2,1,0:T(8,128)} custom-call(s32[1024,512]{1,0:T(8,128)} %multiply_add_fusion.codes_ref, f32[48,128]{1,0:T(8,128)} %bitcast.104), custom_call_target="tpu_custom_call" | custom-call | flops 16000000000 | bytes 7000000 | tf_op jit(solution)/shard_map/layout_bias/pallas_call | solution.py:343
  85.6 1.9 fusion.2.picked_ref
  87.5 17.3 %layout_bias.3.high_bias_ref = f32[8,384,512]{2,1,0:T(8,128)} custom-call(s32[1024,512]{1,0:T(8,128)} %multiply_add_fusion.codes_ref, f32[48,128]{1,0:T(8,128)} %bitcast.105), custom_call_target="tpu_custom_call" | custom-call | flops 16000000000 | bytes 7000000 | tf_op jit(solution)/shard_map/layout_bias/pallas_call | solution.py:343
  104.8 70.4 %all-gather.3.cloned.1.call-done.wq_ref.wk_ref.wv_ref.wo_ref.gate_ref.up_ref.packed_ref = bf16[1024,12544]{1,0:T(8,128)(2,1)} async-done(((bf16[32,12544]{1,0:T(8,128)(2,1)}), bf16[1024,12544]{1,0:T(8,128)(2,1)}) %all-gather.3.cloned.1.call-update) | async-done | bytes 25690128 | tf_op jit(solution)/shard_map/all_gather | solution.py:1194
  175.7 27.8 %attention_forward.1 = (bf16[512,1024]{1,0:T(8,128)(2,1)}, bf16[1024,1024]{1,0:T(8,128)(2,1)}, bf16[1024,1024]{1,0:T(8,128)(2,1)}, bf16[1024,512]{1,0:T(8,128)(2...) custom-call(s32[2]{0:T(128)} %pad_add_fusion.1.count_ref.scalar_ref, ...), custom_call_target="tpu_custom_call" | custom-call | flops 20000000000 | bytes 50000000 | tf_op jit(solution)/shard_map/attention_forward/pallas_call | solution.py:486
  203.5 45.9 %feed_forward.1 = (bf16[16,32,2816]{2,1,0:T(8,128)(2,1)}, bf16[16,32,2816]{2,1,0:T(8,128)(2,1)}, bf16[16,32,2816]{2,1,0:T(8,128)(2,1)}, bf16[16,32,2816]{2,1,0:T...) custom-call(s32[2]{0:T(128)} %pad_add_fusion.1.count_ref.scalar_ref,, ...), custom_call_target="tpu_custom_call" | custom-call | flops 27000000512 | bytes 44000000 | tf_op jit(solution)/shard_map/feed_forward/pallas_call | solution.py:670
  250.2 19.6 %attention_backward.2 = (bf16[512,512]{1,0:T(8,128)(2,1)}, bf16[1024,512]{1,0:T(8,128)(2,1)}, bf16[1024,512]{1,0:T(8,128)(2,1)}, bf16[8,384,512]{2,1,0:T(8,128)(...) custom-call(s32[2]{0:T(128)} %pad_add_fusion.1.count_ref.scalar_ref, ...), custom_call_target="tpu_custom_call" | custom-call | flops 15000000512 | bytes 30000000 | tf_op jit(solution)/shard_map/attention_backward/pallas_call | solution.py:906
  270.1 1.6 copy-done.2
  272.5 6.3 %piece_sums.8 = (bf16[8,32,2816]{2,1,0:T(8,128)(2,1)}, bf16[8,32,2816]{2,1,0:T(8,128)(2,1)}, bf16[8,88,1024]{2,1,0:T(8,128)(2,1)}) custom-call(bf16[16,32,2816]{2,1,0:T(8,128)(2,1)} %get-tuple-element.162.refs_0_, bf16[16,32,2816]{2,1,0:T(8,128)(2,1)} %collective-permute-done.9.refs_1_, ...), custom_call_target="tpu_custom_call" | custom-call | flops 8650752 | bytes 17301504 | tf_op jit(solution)/shard_map/piece_sums/pallas_call | solution.py:190
  278.9 1.6 collective-permute-start.13
  282.5 19.6 %attention_backward.3 = (bf16[512,512]{1,0:T(8,128)(2,1)}, bf16[1024,512]{1,0:T(8,128)(2,1)}, bf16[1024,512]{1,0:T(8,128)(2,1)}, bf16[8,384,512]{2,1,0:T(8,128)(...) custom-call(s32[2]{0:T(128)} %pad_add_fusion.1.count_ref.scalar_ref, ...), custom_call_target="tpu_custom_call" | custom-call | flops 15000000512 | bytes 30000000 | tf_op jit(solution)/shard_map/attention_backward/pallas_call | solution.py:906
  302.1 10.8 %collective-permute-done.14.refs_8_.refs_10_.refs_12_.refs_14_ = bf16[8,88,1024]{2,1,0:T(8,128)(2,1)S(1)} collective-permute-done((bf16[8,88,1024]{2,1,0:T(8,128)(2,1)}, bf16[8,88,1024]{2,1,0:T(8,128)(2,1)S(1)}, u32[]{:S(2)}, u32[]{:S(2)}) %collective-permute-start.14) | collective-permute-done | bytes 1441824 | tf_op jit(solution)/shard_map/ppermute | solution.py:78
  315.3 5.9 %piece_sums.9 = (bf16[4,32,2816]{2,1,0:T(8,128)(2,1)}, bf16[4,32,2816]{2,1,0:T(8,128)(2,1)}, bf16[4,88,1024]{2,1,0:T(8,128)(2,1)}, bf16[8,32,2048]{2,1,0:T(8,128)(2,1)}) custom-call(bf16[16,32,2816]{2,1,0:T(8,128)(2,1)} %get-tuple-element.162.refs_0_, bf16[16,32,2816]{2,1,0:T(8,128)(2,1)} %collective-permute-done.9.refs_1_, bf16[8,32,2816]{2,1,0:T(8,128)(2,1)} %copy-done.8, ...), custom_call_target="tpu_custom_call" | custom-call | flops 8585216 | bytes 17170432 | tf_op jit(solution)/shard_map/piece_sums/pallas_call | solution.py:190
  321.2 1.7 collective-permute-start.19
  325.7 19.9 %table_histogram.1 = f32[96,256]{1,0:T(8,128)} custom-call(s32[2]{0:T(128)} %pad_add_fusion.1.count_ref.scalar_ref, s32[1024,512]{1,0:T(8,128)} %multiply_add_fusion.codes_ref, bf16[8,384,512]{2,1,0:T(8,128)(2,1)} %get-tuple-element.188.low_ref, bf16[8,384,512]{2,1,0:T(8,128)(2,1)} %get-tuple-element.189.high_ref), custom_call_target="tpu_custom_call" | custom-call | flops 20000000000 | bytes 8000000 | tf_op jit(solution)/shard_map/table_histogram/pallas_call | solution.py:1002
  346.7 8.6 %collective-permute-done.17.refs_7_.refs_8_.refs_9_ = bf16[4,32,2816]{2,1,0:T(8,128)(2,1)} collective-permute-done((bf16[4,32,2816]{2,1,0:T(8,128)(2,1)}, bf16[4,32,2816]{2,1,0:T(8,128)(2,1)}, u32[]{:S(2)}, u32[]{:S(2)}) %collective-permute-start.17) | collective-permute-done | bytes 720928 | tf_op jit(solution)/shard_map/ppermute | solution.py:78
  356.2 4.9 %piece_sums.10 = (bf16[2,32,5632]{2,1,0:T(8,128)(2,1)}, bf16[2,88,1024]{2,1,0:T(8,128)(2,1)}, bf16[4,32,2048]{2,1,0:T(8,128)(2,1)}, bf16[8,32,2048]{2,1,0:T(8,128)(2,1)}) custom-call(bf16[16,32,2816]{2,1,0:T(8,128)(2,1)} %get-tuple-element.162.refs_0_, bf16[16,32,2816]{2,1,0:T(8,128)(2,1)} %collective-permute-done.9.refs_1_, bf16[8,32,2816]{2,1,0:T(8,128)(2,1)} %copy-done.8, ...), custom_call_target="tpu_custom_call" | custom-call | flops 7995392 | bytes 15990784 | tf_op jit(solution)/shard_map/piece_sums/pallas_call | solution.py:190
  364.1 1.5 collective-permute-start.22
  365.6 13.8 %key_gradients.1 = (bf16[512,1024]{1,0:T(8,128)(2,1)}, f32[512,1024]{1,0:T(8,128)}, f32[8,1024]{1,0:T(8,128)}) custom-call(s32[2]{0:T(128)} %pad_add_fusion.1.count_ref.scalar_ref, bf16[512,512]{1,0:T(8,128)(2,1)} %get-tuple-element.160.dq_low_ref, bf16[512,512]{1,0:T(8,128)(2,1)} %get-tuple-element.172.dq_high_ref, ...), custom_call_target="tpu_custom_call" | custom-call | flops 8999999488 | bytes 18000000 | tf_op jit(solution)/shard_map/key_gradients/pallas_call | solution.py:1089
  380.8 4.2 collective-permute-done.22.refs_14_.refs_16_
  387.3 4.1 piece_sums.11
  395.0 3.4 collective-permute-start.31
  398.4 1.5 collective-permute-start.32
  399.9 5.6 %collective-permute-start.25 = (bf16[1,32,5632]{2,1,0:T(8,128)(2,1)S(1)}, bf16[1,32,5632]{2,1,0:T(8,128)(2,1)S(1)}, u32[]{:S(2)}, u32[]{:S(2)}) collective-permute-start(bf16[1,32,5632]{2,1,0:T(8,128)(2,1)S(1)} %copy-done.40), channel_id=1, source_target_pairs={{0,16},{4,20},{8,24},{12,28},{16,0},{20,4},{24,8},{28,12},{1,17},{... | collective-permute-start | bytes 1081352 | tf_op jit(solution)/shard_map/ppermute | solution.py:78
  405.5 2.6 collective-permute-start.27
  409.1 1.5 collective-permute-done.32
  411.7 4.2 collective-permute-done.26.refs_17_
  415.9 2.2 collective-permute-done.27.refs_4_
  418.1 6.2 %collective-permute-done.25.refs_5_.refs_11_ = bf16[1,32,5632]{2,1,0:T(8,128)(2,1)S(1)} collective-permute-done((bf16[1,32,5632]{2,1,0:T(8,128)(2,1)S(1)}, bf16[1,32,5632]{2,1,0:T(8,128)(2,1)S(1)}, u32[]{:S(2)}, u32[]{:S(2)}) %collective-permute-start.25) | collective-permute-done | bytes 360480 | tf_op jit(solution)/shard_map/ppermute | solution.py:78
  425.1 2.4 piece_sums.12
  427.5 1.6 collective-permute-start.33
  429.7 5.5 %input_gradient.1 = bf16[512,1024]{1,0:T(8,128)(2,1)} custom-call(f32[512,1024]{1,0:T(8,128)} %get-tuple-element.201.own_ref, bf16[512,512]{1,0:T(8,128)(2,1)} %fusion.13.owner_ref, bf16[512,1024]{1,0:T(8,128)(2,1)} %pad_maximum_fusion.returned_ref, bf16[512,1024]{1,0:T(8,128)(2,1)} %x_ref.5, f32[8,1024]{1,0:T(8,128)} %broadcast_in_dim.64.gain_ref, ...), custom_call_target="tpu_custom_call" | custom-call | flops 1000000000 | bytes 8000000 | tf_op jit(solution)/shard_map/input_gradient/pallas_call | solution.py:1138
  435.2 8.5 %collective-permute-done.34.refs_4_.refs_10_ = bf16[2,32,2048]{2,1,0:T(8,128)(2,1)S(1)} collective-permute-done((bf16[2,32,2048]{2,1,0:T(8,128)(2,1)}, bf16[2,32,2048]{2,1,0:T(8,128)(2,1)S(1)}, u32[]{:S(2)}, u32[]{:S(2)}) %collective-permute-start.34) | collective-permute-done | bytes 262176 | tf_op jit(solution)/shard_map/ppermute | solution.py:78
  444.3 1.9 piece_sums.13
  446.2 3.1 piece_sums.15
  449.3 3.5 collective-permute-done.35.refs_11_
  453.5 2.3 piece_sums.14
  (235 shorter events, 65.9 us)
Async XLA Ops:
  7.3 167.9 %all-gather.3.cloned.1.call-start = ((), (), s32[]{:S(2)}) async-start(), calls=%async_computation | async-start | bytes 26492928 | tf_op jit(solution)/shard_map/all_gather | solution.py:1194
  9.6 450.9 %all-gather.5.cloned.1.call-start = ((), (), s32[]{:S(2)}) async-start(), calls=%async_computation.1 | async-start | bytes 2162688 | tf_op jit(solution)/shard_map/all_gather | solution.py:1376
  9.8 13.1 %collective-permute-start = (bf16[1,32,128]{1,2,0:T(8,128)(2,1)S(1)}, bf16[1,32,128]{1,2,0:T(8,128)(2,1)S(1)}, u32[]{:S(2)}, u32[]{:S(2)}) collective-permute-start(bf16[1,32,128]{1,2,0:T(8,128)(2,1)S(1)} %bitcast.101), channel_id=1, source_target_pairs={{0,16},{4,20},{8,24},{12,28},{16,0},{20,4},{24,8},{28,12},{1,17},{... | collective-permute-start | bytes 24584 | tf_op jit(solution)/shard_map/ppermute | solution.py:78
  22.9 18.3 %collective-permute-start.1 = (bf16[2,32,128]{2,1,0:T(8,128)(2,1)S(1)}, bf16[2,32,128]{2,1,0:T(8,128)(2,1)S(1)}, u32[]{:S(2)}, u32[]{:S(2)}) collective-permute-start(bf16[2,32,128]{2,1,0:T(8,128)(2,1)S(1)} %pad_maximum_fusion.7), channel_id=1, source_target_pairs={{0,8},{4,12},{8,0},{12,4},{16,24},{20,28},{24,16},{28,20},{1,9},{5... | collective-permute-start | bytes 49160 | tf_op jit(solution)/shard_map/ppermute | solution.py:78
  30.5 14.4 %copy-start.37 = (s32[512,1024]{1,0:T(8,128)S(1)}, s32[512,1024]{1,0:T(8,128)}, u32[]{:S(2)}) copy-start(s32[512,1024]{1,0:T(8,128)} %param.39) | copy-start | bytes 6291460
  30.6 23.1 %collective-permute-start.4 = (bf16[128,1024]{1,0:T(8,128)(2,1)S(1)}, bf16[128,1024]{1,0:T(8,128)(2,1)S(1)}, u32[]{:S(2)}, u32[]{:S(2)}) collective-permute-start(bf16[128,1024]{1,0:T(8,128)(2,1)S(1)} %get-tuple-element.244), channel_id=1, source_target_pairs={{0,4},{4,8},{8,12},{12,16},{16,20},{20,24},{24,28},{1,5},{5,9},{9,... | collective-permute-start | bytes 786440 | tf_op jit(solution)/shard_map/ppermute | solution.py:35
  32.0 21.7 %collective-permute-start.5 = (bf16[128,1024]{1,0:T(8,128)(2,1)S(1)}, bf16[128,1024]{1,0:T(8,128)(2,1)S(1)}, u32[]{:S(2)}, u32[]{:S(2)}) collective-permute-start(bf16[128,1024]{1,0:T(8,128)(2,1)S(1)} %get-tuple-element.243), channel_id=1, source_target_pairs={{4,0},{8,4},{12,8},{16,12},{20,16},{24,20},{28,24},{5,1},{9,5},{13... | collective-permute-start | bytes 786440 | tf_op jit(solution)/shard_map/ppermute | solution.py:36
  33.3 20.4 %collective-permute-start.6 = (bf16[128,1024]{1,0:T(8,128)(2,1)S(1)}, bf16[128,1024]{1,0:T(8,128)(2,1)S(1)}, u32[]{:S(2)}, u32[]{:S(2)}) collective-permute-start(bf16[128,1024]{1,0:T(8,128)(2,1)S(1)} %get-tuple-element.242), channel_id=1, source_target_pairs={{0,1},{1,2},{2,3},{4,5},{5,6},{6,7},{8,9},{9,10},{10,11},{12,13},{... | collective-permute-start | bytes 786440 | tf_op jit(solution)/shard_map/ppermute | solution.py:35
  36.7 17.0 %collective-permute-start.7 = (bf16[128,1024]{1,0:T(8,128)(2,1)S(1)}, bf16[128,1024]{1,0:T(8,128)(2,1)S(1)}, u32[]{:S(2)}, u32[]{:S(2)}) collective-permute-start(bf16[128,1024]{1,0:T(8,128)(2,1)S(1)} %get-tuple-element.241), channel_id=1, source_target_pairs={{1,0},{2,1},{3,2},{5,4},{6,5},{7,6},{9,8},{10,9},{11,10},{13,12},{... | collective-permute-start | bytes 786440 | tf_op jit(solution)/shard_map/ppermute | solution.py:36
  40.5 13.3 %copy-start.9 = (bf16[1024,1024]{1,0:T(8,128)(2,1)}, bf16[1024,1024]{1,0:T(8,128)(2,1)S(1)}, u32[]{:S(2)}) copy-start(bf16[1024,1024]{1,0:T(8,128)(2,1)S(1)} %fusion.4.pack_ref) | copy-start | bytes 6291460
  41.2 10.4 %collective-permute-start.2 = (bf16[4,32,128]{2,1,0:T(8,128)(2,1)S(1)}, bf16[4,32,128]{2,1,0:T(8,128)(2,1)S(1)}, u32[]{:S(2)}, u32[]{:S(2)}) collective-permute-start(bf16[4,32,128]{2,1,0:T(8,128)(2,1)S(1)} %pad_maximum_fusion.6), channel_id=1, source_target_pairs={{0,2},{1,3},{2,0},{3,1},{4,6},{5,7},{6,4},{7,5},{8,10},{9,11},{10,... | collective-permute-start | bytes 98312 | tf_op jit(solution)/shard_map/ppermute | solution.py:78
  51.6 6.1 %collective-permute-start.3 = (bf16[8,32,128]{2,1,0:T(8,128)(2,1)S(1)}, bf16[8,32,128]{2,1,0:T(8,128)(2,1)S(1)}, u32[]{:S(2)}, u32[]{:S(2)}) collective-permute-start(bf16[8,32,128]{2,1,0:T(8,128)(2,1)S(1)} %pad_maximum_fusion.5), channel_id=1, source_target_pairs={{0,1},{1,0},{2,3},{3,2},{4,5},{5,4},{6,7},{7,6},{8,9},{9,8},{10,11... | collective-permute-start | bytes 196616 | tf_op jit(solution)/shard_map/ppermute | solution.py:78
  56.3 29.3 %copy-start.13 = (bf16[1024,1024]{1,0:T(8,128)(2,1)}, bf16[1024,1024]{1,0:T(8,128)(2,1)S(1)}, u32[]{:S(2)}) copy-start(bf16[1024,1024]{1,0:T(8,128)(2,1)S(1)} %get-tuple-element.272.picked_ref) | copy-start | bytes 6291460
  58.4 1.3 collective-permute-start.8
  66.4 17.9 %copy-start.31 = (f32[512]{0:T(512)S(1)}, f32[512]{0:T(512)}, u32[]{:S(2)}) copy-start(f32[512]{0:T(512)} %add_rsqrt_fusion.1) | copy-start | bytes 6148
  249.4 20.7 %collective-permute-start.11 = (bf16[16,88,1024]{2,1,0:T(8,128)(2,1)}, bf16[16,88,1024]{2,1,0:T(8,128)(2,1)S(1)}, u32[]{:S(2)}, u32[]{:S(2)}) collective-permute-start(bf16[16,88,1024]{2,1,0:T(8,128)(2,1)} %get-tuple-element.152), channel_id=1, source_target_pairs={{0,4},{4,0},{8,12},{12,8},{16,20},{20,16},{24,28},{28,24},{1,5},{5... | collective-permute-start | bytes 8650760 | tf_op jit(solution)/shard_map/ppermute | solution.py:78
  249.7 20.4 %collective-permute-start.10 = (bf16[16,32,2816]{2,1,0:T(8,128)(2,1)}, bf16[16,32,2816]{2,1,0:T(8,128)(2,1)S(1)}, u32[]{:S(2)}, u32[]{:S(2)}) collective-permute-start(bf16[16,32,2816]{2,1,0:T(8,128)(2,1)} %get-tuple-element.151), channel_id=1, source_target_pairs={{0,4},{4,0},{8,12},{12,8},{16,20},{20,16},{24,28},{28,24},{1,5},{5... | collective-permute-start | bytes 8650760 | tf_op jit(solution)/shard_map/ppermute | solution.py:78
  250.0 20.2 %collective-permute-start.9 = (bf16[16,32,2816]{2,1,0:T(8,128)(2,1)}, bf16[16,32,2816]{2,1,0:T(8,128)(2,1)}, u32[]{:S(2)}, u32[]{:S(2)}) collective-permute-start(bf16[16,32,2816]{2,1,0:T(8,128)(2,1)} %get-tuple-element.150), channel_id=1, source_target_pairs={{0,4},{4,0},{8,12},{12,8},{16,20},{20,16},{24,28},{28,24},{1,5},{5... | collective-permute-start | bytes 8650760 | tf_op jit(solution)/shard_map/ppermute | solution.py:78
  269.8 32.2 %collective-permute-start.15 = (bf16[16,32,2048]{2,1,0:T(8,128)(2,1)}, bf16[16,32,2048]{2,1,0:T(8,128)(2,1)}, u32[]{:S(2)}, u32[]{:S(2)}) collective-permute-start(bf16[16,32,2048]{2,1,0:T(8,128)(2,1)} %get-tuple-element.161), channel_id=1, source_target_pairs={{0,4},{4,0},{8,12},{12,8},{16,20},{20,16},{24,28},{28,24},{1,5},{5... | collective-permute-start | bytes 6291464 | tf_op jit(solution)/shard_map/ppermute | solution.py:78
  278.8 34.0 %collective-permute-start.14 = (bf16[8,88,1024]{2,1,0:T(8,128)(2,1)}, bf16[8,88,1024]{2,1,0:T(8,128)(2,1)S(1)}, u32[]{:S(2)}, u32[]{:S(2)}) collective-permute-start(bf16[8,88,1024]{2,1,0:T(8,128)(2,1)} %get-tuple-element.170), channel_id=1, source_target_pairs={{0,8},{4,12},{8,0},{12,4},{16,24},{20,28},{24,16},{28,20},{1,9},{5... | collective-permute-start | bytes 4325384 | tf_op jit(solution)/shard_map/ppermute | solution.py:78
  278.9 34.0 %collective-permute-start.13 = (bf16[8,32,2816]{2,1,0:T(8,128)(2,1)}, bf16[8,32,2816]{2,1,0:T(8,128)(2,1)S(1)}, u32[]{:S(2)}, u32[]{:S(2)}) collective-permute-start(bf16[8,32,2816]{2,1,0:T(8,128)(2,1)} %get-tuple-element.169), channel_id=1, source_target_pairs={{0,2},{1,3},{2,0},{3,1},{4,6},{5,7},{6,4},{7,5},{8,10},{9,11},{10,... | collective-permute-start | bytes 4325384 | tf_op jit(solution)/shard_map/ppermute | solution.py:78
  280.5 33.7 %collective-permute-start.12 = (bf16[8,32,2816]{2,1,0:T(8,128)(2,1)}, bf16[8,32,2816]{2,1,0:T(8,128)(2,1)S(1)}, u32[]{:S(2)}, u32[]{:S(2)}) collective-permute-start(bf16[8,32,2816]{2,1,0:T(8,128)(2,1)} %get-tuple-element.168), channel_id=1, source_target_pairs={{0,1},{1,0},{2,3},{3,2},{4,5},{5,4},{6,7},{7,6},{8,9},{9,8},{10,11... | collective-permute-start | bytes 4325384 | tf_op jit(solution)/shard_map/ppermute | solution.py:78
  302.0 44.6 %collective-permute-start.20 = (bf16[16,32,2048]{2,1,0:T(8,128)(2,1)}, bf16[16,32,2048]{2,1,0:T(8,128)(2,1)S(1)}, u32[]{:S(2)}, u32[]{:S(2)}) collective-permute-start(bf16[16,32,2048]{2,1,0:T(8,128)(2,1)} %get-tuple-element.177), channel_id=1, source_target_pairs={{0,4},{4,0},{8,12},{12,8},{16,20},{20,16},{24,28},{28,24},{1,5},{5... | collective-permute-start | bytes 6291464 | tf_op jit(solution)/shard_map/ppermute | solution.py:78
  321.2 34.1 %collective-permute-start.19 = (bf16[8,32,2048]{2,1,0:T(8,128)(2,1)}, bf16[8,32,2048]{2,1,0:T(8,128)(2,1)S(1)}, u32[]{:S(2)}, u32[]{:S(2)}) collective-permute-start(bf16[8,32,2048]{2,1,0:T(8,128)(2,1)} %get-tuple-element.186), channel_id=1, source_target_pairs={{0,8},{4,12},{8,0},{12,4},{16,24},{20,28},{24,16},{28,20},{1,9},{5... | collective-permute-start | bytes 3145736 | tf_op jit(solution)/shard_map/ppermute | solution.py:78
  322.9 23.8 %collective-permute-start.18 = (bf16[4,88,1024]{2,1,0:T(8,128)(2,1)}, bf16[4,88,1024]{2,1,0:T(8,128)(2,1)}, u32[]{:S(2)}, u32[]{:S(2)}) collective-permute-start(bf16[4,88,1024]{2,1,0:T(8,128)(2,1)} %get-tuple-element.185), channel_id=1, source_target_pairs={{0,1},{1,0},{2,3},{3,2},{4,5},{5,4},{6,7},{7,6},{8,9},{9,8},{10,11... | collective-permute-start | bytes 2162696 | tf_op jit(solution)/shard_map/ppermute | solution.py:78
  323.7 31.6 %collective-permute-start.17 = (bf16[4,32,2816]{2,1,0:T(8,128)(2,1)}, bf16[4,32,2816]{2,1,0:T(8,128)(2,1)}, u32[]{:S(2)}, u32[]{:S(2)}) collective-permute-start(bf16[4,32,2816]{2,1,0:T(8,128)(2,1)} %get-tuple-element.184), channel_id=1, source_target_pairs={{0,1},{1,0},{2,3},{3,2},{4,5},{5,4},{6,7},{7,6},{8,9},{9,8},{10,11... | collective-permute-start | bytes 2162696 | tf_op jit(solution)/shard_map/ppermute | solution.py:78
  324.9 30.3 %collective-permute-start.16 = (bf16[4,32,2816]{2,1,0:T(8,128)(2,1)}, bf16[4,32,2816]{2,1,0:T(8,128)(2,1)}, u32[]{:S(2)}, u32[]{:S(2)}) collective-permute-start(bf16[4,32,2816]{2,1,0:T(8,128)(2,1)} %get-tuple-element.183), channel_id=1, source_target_pairs={{0,2},{1,3},{2,0},{3,1},{4,6},{5,7},{6,4},{7,5},{8,10},{9,11},{10,... | collective-permute-start | bytes 2162696 | tf_op jit(solution)/shard_map/ppermute | solution.py:78
  325.7 19.9 %copy-start.29 = (f32[96,128]{1,0:T(8,128)S(1)}, f32[96,128]{1,0:T(8,128)}, u32[]{:S(2)}) copy-start(f32[96,128]{1,0:T(8,128)} %get-tuple-element.225) | copy-start | bytes 147460
  325.7 19.9 %copy-start.30 = (f32[96,128]{1,0:T(8,128)S(1)}, f32[96,128]{1,0:T(8,128)}, u32[]{:S(2)}) copy-start(f32[96,128]{1,0:T(8,128)} %get-tuple-element.226) | copy-start | bytes 147460
  361.1 25.0 %collective-permute-start.24 = (bf16[8,32,2048]{2,1,0:T(8,128)(2,1)}, bf16[8,32,2048]{2,1,0:T(8,128)(2,1)S(1)}, u32[]{:S(2)}, u32[]{:S(2)}) collective-permute-start(bf16[8,32,2048]{2,1,0:T(8,128)(2,1)} %get-tuple-element.199), channel_id=1, source_target_pairs={{0,1},{1,0},{2,3},{3,2},{4,5},{5,4},{6,7},{7,6},{8,9},{9,8},{10,11... | collective-permute-start | bytes 3145736 | tf_op jit(solution)/shard_map/ppermute | solution.py:78
  362.4 23.7 %collective-permute-start.21 = (bf16[2,32,5632]{2,1,0:T(8,128)(2,1)}, bf16[2,32,5632]{2,1,0:T(8,128)(2,1)S(1)}, u32[]{:S(2)}, u32[]{:S(2)}) collective-permute-start(bf16[2,32,5632]{2,1,0:T(8,128)(2,1)} %get-tuple-element.196), channel_id=1, source_target_pairs={{0,8},{4,12},{8,0},{12,4},{16,24},{20,28},{24,16},{28,20},{1,9},{5... | collective-permute-start | bytes 2162696 | tf_op jit(solution)/shard_map/ppermute | solution.py:78
  363.5 21.6 %collective-permute-start.23 = (bf16[4,32,2048]{2,1,0:T(8,128)(2,1)}, bf16[4,32,2048]{2,1,0:T(8,128)(2,1)S(1)}, u32[]{:S(2)}, u32[]{:S(2)}) collective-permute-start(bf16[4,32,2048]{2,1,0:T(8,128)(2,1)} %get-tuple-element.198), channel_id=1, source_target_pairs={{0,2},{1,3},{2,0},{3,1},{4,6},{5,7},{6,4},{7,5},{8,10},{9,11},{10,... | collective-permute-start | bytes 1572872 | tf_op jit(solution)/shard_map/ppermute | solution.py:78
  364.1 20.9 %collective-permute-start.22 = (bf16[2,88,1024]{2,1,0:T(8,128)(2,1)}, bf16[2,88,1024]{2,1,0:T(8,128)(2,1)S(1)}, u32[]{:S(2)}, u32[]{:S(2)}) collective-permute-start(bf16[2,88,1024]{2,1,0:T(8,128)(2,1)} %get-tuple-element.197), channel_id=1, source_target_pairs={{0,16},{4,20},{8,24},{12,28},{16,0},{20,4},{24,8},{28,12},{1,17},{... | collective-permute-start | bytes 1081352 | tf_op jit(solution)/shard_map/ppermute | solution.py:78
  391.4 14.1 %copy-start.41 = (bf16[2,32,2048]{2,1,0:T(8,128)(2,1)S(1)}, bf16[2,32,2048]{2,1,0:T(8,128)(2,1)}, u32[]{:S(2)}) copy-start(bf16[2,32,2048]{2,1,0:T(8,128)(2,1)} %get-tuple-element.209) | copy-start | bytes 786436
  391.5 16.7 %copy-start.42 = (bf16[1,88,1024]{2,1,0:T(8,128)(2,1)S(1)}, bf16[1,88,1024]{2,1,0:T(8,128)(2,1)}, u32[]{:S(2)}) copy-start(bf16[1,88,1024]{2,1,0:T(8,128)(2,1)} %get-tuple-element.208) | copy-start | bytes 540676
  391.6 8.3 %collective-permute-start.29 = (bf16[128,1024]{1,0:T(8,128)(2,1)S(1)}, bf16[128,1024]{1,0:T(8,128)(2,1)S(1)}, u32[]{:S(2)}, u32[]{:S(2)}) collective-permute-start(bf16[128,1024]{1,0:T(8,128)(2,1)S(1)} %get-tuple-element.237), channel_id=1, source_target_pairs={{0,4},{4,8},{8,12},{12,16},{16,20},{20,24},{24,28},{1,5},{5,9},{9,... | collective-permute-start | bytes 786440 | tf_op jit(solution)/shard_map/ppermute | solution.py:35
  393.0 12.5 %collective-permute-start.30 = (bf16[128,1024]{1,0:T(8,128)(2,1)S(1)}, bf16[128,1024]{1,0:T(8,128)(2,1)S(1)}, u32[]{:S(2)}, u32[]{:S(2)}) collective-permute-start(bf16[128,1024]{1,0:T(8,128)(2,1)S(1)} %get-tuple-element.240), channel_id=1, source_target_pairs={{4,0},{8,4},{12,8},{16,12},{20,16},{24,20},{28,24},{5,1},{9,5},{13... | collective-permute-start | bytes 786440 | tf_op jit(solution)/shard_map/ppermute | solution.py:36
  394.3 30.0 %collective-permute-start.28 = (bf16[4,32,2048]{2,1,0:T(8,128)(2,1)S(1)}, bf16[4,32,2048]{2,1,0:T(8,128)(2,1)S(1)}, u32[]{:S(2)}, u32[]{:S(2)}) collective-permute-start(bf16[4,32,2048]{2,1,0:T(8,128)(2,1)S(1)} %copy-done.39), channel_id=1, source_target_pairs={{0,2},{1,3},{2,0},{3,1},{4,6},{5,7},{6,4},{7,5},{8,10},{9,11},{10,... | collective-permute-start | bytes 1572872 | tf_op jit(solution)/shard_map/ppermute | solution.py:78
  395.0 13.2 %collective-permute-start.31 = (bf16[128,1024]{1,0:T(8,128)(2,1)S(1)}, bf16[128,1024]{1,0:T(8,128)(2,1)S(1)}, u32[]{:S(2)}, u32[]{:S(2)}) collective-permute-start(bf16[128,1024]{1,0:T(8,128)(2,1)S(1)} %get-tuple-element.239), channel_id=1, source_target_pairs={{0,1},{1,2},{2,3},{4,5},{5,6},{6,7},{8,9},{9,10},{10,11},{12,13},{... | collective-permute-start | bytes 786440 | tf_op jit(solution)/shard_map/ppermute | solution.py:35
  398.4 12.2 %collective-permute-start.32 = (bf16[128,1024]{1,0:T(8,128)(2,1)S(1)}, bf16[128,1024]{1,0:T(8,128)(2,1)S(1)}, u32[]{:S(2)}, u32[]{:S(2)}) collective-permute-start(bf16[128,1024]{1,0:T(8,128)(2,1)S(1)} %get-tuple-element.238), channel_id=1, source_target_pairs={{1,0},{2,1},{3,2},{5,4},{6,5},{7,6},{9,8},{10,9},{11,10},{13,12},{... | collective-permute-start | bytes 786440 | tf_op jit(solution)/shard_map/ppermute | solution.py:36
  399.9 24.4 %collective-permute-start.25 = (bf16[1,32,5632]{2,1,0:T(8,128)(2,1)S(1)}, bf16[1,32,5632]{2,1,0:T(8,128)(2,1)S(1)}, u32[]{:S(2)}, u32[]{:S(2)}) collective-permute-start(bf16[1,32,5632]{2,1,0:T(8,128)(2,1)S(1)} %copy-done.40), channel_id=1, source_target_pairs={{0,16},{4,20},{8,24},{12,28},{16,0},{20,4},{24,8},{28,12},{1,17},{... | collective-permute-start | bytes 1081352 | tf_op jit(solution)/shard_map/ppermute | solution.py:78
  405.5 12.6 %collective-permute-start.27 = (bf16[2,32,2048]{2,1,0:T(8,128)(2,1)S(1)}, bf16[2,32,2048]{2,1,0:T(8,128)(2,1)S(1)}, u32[]{:S(2)}, u32[]{:S(2)}) collective-permute-start(bf16[2,32,2048]{2,1,0:T(8,128)(2,1)S(1)} %copy-done.41), channel_id=1, source_target_pairs={{0,1},{1,0},{2,3},{3,2},{4,5},{5,4},{6,7},{7,6},{8,9},{9,8},{10,11... | collective-permute-start | bytes 786440 | tf_op jit(solution)/shard_map/ppermute | solution.py:78
  408.1 7.7 %collective-permute-start.26 = (bf16[1,88,1024]{2,1,0:T(8,128)(2,1)S(1)}, bf16[1,88,1024]{2,1,0:T(8,128)(2,1)S(1)}, u32[]{:S(2)}, u32[]{:S(2)}) collective-permute-start(bf16[1,88,1024]{2,1,0:T(8,128)(2,1)S(1)} %copy-done.42), channel_id=1, source_target_pairs={{0,2},{1,3},{2,0},{3,1},{4,6},{5,7},{6,4},{7,5},{8,10},{9,11},{10,... | collective-permute-start | bytes 540680 | tf_op jit(solution)/shard_map/ppermute | solution.py:78
  411.7 17.4 %copy-start.28 = (f32[1024]{0:T(1024)S(1)}, f32[1024]{0:T(1024)}, u32[]{:S(2)}) copy-start(f32[1024]{0:T(1024)} %copy-done.27) | copy-start | bytes 12292
  415.9 19.3 %copy-start.23 = (bf16[1,88,1024]{2,1,0:T(8,128)(2,1)}, bf16[1,88,1024]{2,1,0:T(8,128)(2,1)S(1)}, u32[]{:S(2)}) copy-start(bf16[1,88,1024]{2,1,0:T(8,128)(2,1)S(1)} %collective-permute-done.26.refs_17_) | copy-start | bytes 540676
  427.5 16.2 %collective-permute-start.34 = (bf16[2,32,2048]{2,1,0:T(8,128)(2,1)}, bf16[2,32,2048]{2,1,0:T(8,128)(2,1)S(1)}, u32[]{:S(2)}, u32[]{:S(2)}) collective-permute-start(bf16[2,32,2048]{2,1,0:T(8,128)(2,1)} %get-tuple-element.216), channel_id=1, source_target_pairs={{0,8},{4,12},{8,0},{12,4},{16,24},{20,28},{24,16},{28,20},{1,9},{5... | collective-permute-start | bytes 786440 | tf_op jit(solution)/shard_map/ppermute | solution.py:78
  427.5 21.9 %collective-permute-start.33 = (bf16[1,32,2048]{2,1,0:T(8,128)(2,1)}, bf16[1,32,2048]{2,1,0:T(8,128)(2,1)S(1)}, u32[]{:S(2)}, u32[]{:S(2)}) collective-permute-start(bf16[1,32,2048]{2,1,0:T(8,128)(2,1)} %get-tuple-element.215), channel_id=1, source_target_pairs={{0,16},{4,20},{8,24},{12,28},{16,0},{20,4},{24,8},{28,12},{1,17},{... | collective-permute-start | bytes 393224 | tf_op jit(solution)/shard_map/ppermute | solution.py:78
  446.2 6.6 %collective-permute-start.35 = (bf16[1,32,2048]{2,1,0:T(8,128)(2,1)}, bf16[1,32,2048]{2,1,0:T(8,128)(2,1)S(1)}, u32[]{:S(2)}, u32[]{:S(2)}) collective-permute-start(bf16[1,32,2048]{2,1,0:T(8,128)(2,1)} %piece_sums.13), channel_id=1, source_target_pairs={{0,16},{4,20},{8,24},{12,28},{16,0},{20,4},{24,8},{28,12},{1,17},{... | collective-permute-start | bytes 393224 | tf_op jit(solution)/shard_map/ppermute | solution.py:78
  (34 other events, 122.6 us)
Sparse Core Ops, SparseCore 0:
  11.5 163.5 all-gather.2
  386.2 58.8 all-gather.4

commit v6 on v5

--- a/solution.py
+++ b/solution.py
@@ -124,14 +124,6 @@
         self.flights = []
         self.chains = [chain for chain in self.chains if chain.stages]
         return landed
-
-    def land_with(self, values):
-        flights, values = lax.optimization_barrier(
-            ([flight for chains, flight in self.flights], values)
-        )
-        self.flights = [(chains, flight) for (chains, _), flight in zip(self.flights, flights)]
-        self.land()
-        return values
 
     def send(self):
         sums, firsts = {}, []
@@ -197,6 +189,35 @@
         cost_estimate=pl.CostEstimate(flops=moved, bytes_accessed=2 * moved, transcendentals=0),
         name="piece_sums",
     )(*arrays)
+
+
+def totals_kernel(*refs, low_count):
+    *parts, a_ref, b_ref, c_ref, d_ref = refs
+    width = a_ref.shape[1] // 2
+    for side, side_parts in enumerate((parts[:low_count], parts[low_count:])):
+        total = side_parts[0][0].astype(F32)
+        for part in side_parts[1:]:
+            total = total + part[0].astype(F32)
+        for number, out_ref in enumerate((a_ref, b_ref, c_ref, d_ref)):
+            taken = total[:, number * width : (number + 1) * width]
+            out_ref[:, side * width : (side + 1) * width] = taken
+
+
+def side_totals(low, high):
+    parts = low.parts + high.parts
+    specs = [
+        pl.BlockSpec((1, low.rows, low.width), lambda i, lane=column // low.width: (0, 0, lane))
+        for array, column in parts
+    ]
+    return pl.pallas_call(
+        functools.partial(totals_kernel, low_count=len(low.parts)),
+        grid=(1,),
+        in_specs=specs,
+        out_specs=[pl.BlockSpec((low.rows, D), lambda i: (0, 0))] * 4,
+        out_shape=[jax.ShapeDtypeStruct((low.rows, D), F32)] * 4,
+        compiler_params=pltpu.CompilerParams(vmem_limit_bytes=VMEM_LIMIT),
+        name="side_totals",
+    )(*[array for array, column in parts])
 
 
 def dot_nn(left, right):
@@ -1374,13 +1395,14 @@
     small_part = jnp.pad(small_part, ((0, 128 - small_rows), (0, 0)))
     landed = rounds.land(lent)
     small_parts = lax.all_gather(after(small_part, landed), ("row", "col"), axis=0, tiled=True)
+    rounds.send()
+    rounds.land()
     sent = rounds.send()
     lent = after(lent, sent).reshape(4, -1, D)
     back_above, back_below = shifted(lent[0:2], "row")
     back_left, back_right = shifted(lent[2:4], "col")
     returned = jnp.concatenate([back_above, back_below, back_left, back_right], 0)
-    returned = rounds.land_with(returned)
-    sent = rounds.send()
+    sent = rounds.turn()
     input_grad = input_gradient(
         own_grads,
         owner,
@@ -1403,14 +1425,7 @@
     gate_grad, up_grad, down_grad = [
         total[0] for total in piece_sums([[chain] for chain in ffn_chains], False, F32)
     ]
-    sides = [
-        total[0] for total in piece_sums([[low_chain], [high_chain]], False, F32)
-    ]
-    width = D // 2
-    query_grad, key_grad, value_grad, output_grad = [
-        jnp.concatenate([side[:, i * width : (i + 1) * width] for side in sides], 1)
-        for i in range(4)
-    ]
+    query_grad, key_grad, value_grad, output_grad = side_totals(low_chain, high_chain)
     return (
         layer_out,
         input_grad,

time: 477 us -> 467 us (0.979)
    ppermute x28, waiting for transfers between devices: 53 us -> 38 us  [exchange(): return lax.ppermute(values, axis, pairs)]
    all_gather x1, waiting for transfers between devices: 0.01 us -> 10.4 us  [on_device(): lax.all_gather(after(small_part, landed), ('row', 'col'), axis=0, tiled=T...]
    pallas_call x8 -> x7, Pallas kernels: 30.9 us -> 28.4 us  [piece_sums(): pl.pallas_call(functools.partial(sum_kernel, shares=shares), grid=(steps,...]
    unnamed x96 -> x90, local copies, waits for them, and re-layouts: 12.4 us -> 12.2 us
  transfers between devices with their start and end apart: 38 -> 38, of which waited for: 15 -> 14; matrix products, arithmetic and copies ran while one was open for 10% -> 9% of each run, Pallas kernels for 29% -> 30%
where the time goes in v6:
time: 467 us; the launch traced here: 462 us
  Pallas kernels  220 us (47%)
  waiting for transfers between devices  121 us (26%)
  starting transfers between devices  48.9 us (10%)
  local copies, waits for them, and re-layouts  34.2 us (7%)
  between operations  16.3 us (3%)
  other arithmetic  13.4 us (3%)
  matrix products  8.36 us (2%)
    all_gather x1, waiting for transfers between devices, on_device(): weights = lax.all_gather(packed_weights, ('row', 'col'), axis=0, tiled=True)  70.4 us
    pallas_call x1, Pallas kernels, feed_forward(): pl.pallas_call(kernel, grid_spec=pltpu.PrefetchScalarGridSpec(num_scalar_...  45.9 us
    pallas_call x2, Pallas kernels, attention_backward(): pl.pallas_call(functools.partial(backward_kernel, first_head=half * heads...  39.1 us
    ppermute x28, waiting for transfers between devices, exchange(): return lax.ppermute(values, axis, pairs)  38 us
    ppermute x28, starting transfers between devices, exchange(): return lax.ppermute(values, axis, pairs)  35.1 us
    pallas_call x2, Pallas kernels, layout_bias(): pl.pallas_call(functools.partial(bias_kernel, first_head=first_head), gri...  34.6 us
    pallas_call x7, Pallas kernels, piece_sums(): pl.pallas_call(functools.partial(sum_kernel, shares=shares), grid=(steps,...  28.4 us
    pallas_call x1, Pallas kernels, attention_forward(): pl.pallas_call(attend_kernel, grid_spec=pltpu.PrefetchScalarGridSpec(num_...  27.8 us
  transfers between devices with their start and end apart: 38, of which 14 were waited for; matrix products, arithmetic and copies ran while one was open for 9% of the time, Pallas kernels for 30%

profile of v6, /device:TPU:0, one launch (start us, length us, event | category | flops | bytes accessed | tf_op | source)
XLA Modules:
  0.0 462.1 jit_solution(7695681542090868957)
XLA Ops:
  7.3 2.2 pack_shards.1
  9.8 4.1 collective-permute-start
  20.8 2.1 gather_fusion
  22.9 1.6 collective-permute-start.1
  24.6 1.4 gather_fusion.1
  26.1 3.1 gather_fusion.2
  30.5 1.4 collective-permute-start.4
  33.3 3.4 collective-permute-start.6
  36.7 1.5 collective-permute-start.7
  41.2 3.6 collective-permute-start.2
  47.8 3.2 multiply_add_fusion.codes_ref
  53.8 2.5 fusion
  56.3 1.4 collective-permute-done.3
  60.4 1.6 gather_fusion.4
  66.4 17.3 %layout_bias.2.low_bias_ref = f32[8,384,512]{2,1,0:T(8,128)} custom-call(s32[1024,512]{1,0:T(8,128)} %multiply_add_fusion.codes_ref, f32[48,128]{1,0:T(8,128)} %bitcast.100), custom_call_target="tpu_custom_call" | custom-call | flops 16000000000 | bytes 7000000 | tf_op jit(solution)/shard_map/layout_bias/pallas_call | solution.py:364
  85.6 1.9 fusion.2.picked_ref
  87.5 17.3 %layout_bias.3.high_bias_ref = f32[8,384,512]{2,1,0:T(8,128)} custom-call(s32[1024,512]{1,0:T(8,128)} %multiply_add_fusion.codes_ref, f32[48,128]{1,0:T(8,128)} %bitcast.101), custom_call_target="tpu_custom_call" | custom-call | flops 16000000000 | bytes 7000000 | tf_op jit(solution)/shard_map/layout_bias/pallas_call | solution.py:364
  104.8 70.4 %all-gather.3.cloned.1.call-done.wq_ref.wk_ref.wv_ref.wo_ref.gate_ref.up_ref.packed_ref = bf16[1024,12544]{1,0:T(8,128)(2,1)} async-done(((bf16[32,12544]{1,0:T(8,128)(2,1)}), bf16[1024,12544]{1,0:T(8,128)(2,1)}) %all-gather.3.cloned.1.call-update) | async-done | bytes 25690128 | tf_op jit(solution)/shard_map/all_gather | solution.py:1215
  175.7 27.8 %attention_forward.1 = (bf16[512,1024]{1,0:T(8,128)(2,1)}, bf16[1024,1024]{1,0:T(8,128)(2,1)}, bf16[1024,1024]{1,0:T(8,128)(2,1)}, bf16[1024,512]{1,0:T(8,128)(2...) custom-call(s32[2]{0:T(128)} %pad_add_fusion.1.count_ref.scalar_ref, ...), custom_call_target="tpu_custom_call" | custom-call | flops 20000000000 | bytes 50000000 | tf_op jit(solution)/shard_map/attention_forward/pallas_call | solution.py:507
  203.5 45.9 %feed_forward.1 = (bf16[16,32,2816]{2,1,0:T(8,128)(2,1)}, bf16[16,32,2816]{2,1,0:T(8,128)(2,1)}, bf16[16,32,2816]{2,1,0:T(8,128)(2,1)}, bf16[16,32,2816]{2,1,0:T...) custom-call(s32[2]{0:T(128)} %pad_add_fusion.1.count_ref.scalar_ref,, ...), custom_call_target="tpu_custom_call" | custom-call | flops 27000000512 | bytes 44000000 | tf_op jit(solution)/shard_map/feed_forward/pallas_call | solution.py:691
  250.2 19.5 %attention_backward.2 = (bf16[512,512]{1,0:T(8,128)(2,1)}, bf16[1024,512]{1,0:T(8,128)(2,1)}, bf16[1024,512]{1,0:T(8,128)(2,1)}, bf16[8,384,512]{2,1,0:T(8,128)(...) custom-call(s32[2]{0:T(128)} %pad_add_fusion.1.count_ref.scalar_ref, ...), custom_call_target="tpu_custom_call" | custom-call | flops 15000000512 | bytes 30000000 | tf_op jit(solution)/shard_map/attention_backward/pallas_call | solution.py:927
  270.1 1.6 copy-done.2
  272.5 6.3 %piece_sums.7 = (bf16[8,32,2816]{2,1,0:T(8,128)(2,1)}, bf16[8,32,2816]{2,1,0:T(8,128)(2,1)}, bf16[8,88,1024]{2,1,0:T(8,128)(2,1)}) custom-call(bf16[16,32,2816]{2,1,0:T(8,128)(2,1)} %get-tuple-element.158.refs_0_, bf16[16,32,2816]{2,1,0:T(8,128)(2,1)} %collective-permute-done.9.refs_1_, ...), custom_call_target="tpu_custom_call" | custom-call | flops 8650752 | bytes 17301504 | tf_op jit(solution)/shard_map/piece_sums/pallas_call | solution.py:182
  278.9 1.5 collective-permute-start.13
  282.4 19.6 %attention_backward.3 = (bf16[512,512]{1,0:T(8,128)(2,1)}, bf16[1024,512]{1,0:T(8,128)(2,1)}, bf16[1024,512]{1,0:T(8,128)(2,1)}, bf16[8,384,512]{2,1,0:T(8,128)(...) custom-call(s32[2]{0:T(128)} %pad_add_fusion.1.count_ref.scalar_ref, ...), custom_call_target="tpu_custom_call" | custom-call | flops 15000000512 | bytes 30000000 | tf_op jit(solution)/shard_map/attention_backward/pallas_call | solution.py:927
  302.1 10.7 %collective-permute-done.14.refs_8_.refs_10_.refs_12_.refs_14_ = bf16[8,88,1024]{2,1,0:T(8,128)(2,1)S(1)} collective-permute-done((bf16[8,88,1024]{2,1,0:T(8,128)(2,1)}, bf16[8,88,1024]{2,1,0:T(8,128)(2,1)S(1)}, u32[]{:S(2)}, u32[]{:S(2)}) %collective-permute-start.14) | collective-permute-done | bytes 1441824 | tf_op jit(solution)/shard_map/ppermute | solution.py:78
  315.3 5.9 %piece_sums.8 = (bf16[4,32,2816]{2,1,0:T(8,128)(2,1)}, bf16[4,32,2816]{2,1,0:T(8,128)(2,1)}, bf16[4,88,1024]{2,1,0:T(8,128)(2,1)}, bf16[8,32,2048]{2,1,0:T(8,128)(2,1)}) custom-call(bf16[16,32,2816]{2,1,0:T(8,128)(2,1)} %get-tuple-element.158.refs_0_, bf16[16,32,2816]{2,1,0:T(8,128)(2,1)} %collective-permute-done.9.refs_1_, bf16[8,32,2816]{2,1,0:T(8,128)(2,1)} %copy-done.8, ...), custom_call_target="tpu_custom_call" | custom-call | flops 8585216 | bytes 17170432 | tf_op jit(solution)/shard_map/piece_sums/pallas_call | solution.py:182
  321.2 1.7 collective-permute-start.19
  325.7 19.9 %table_histogram.1 = f32[96,256]{1,0:T(8,128)} custom-call(s32[2]{0:T(128)} %pad_add_fusion.1.count_ref.scalar_ref, s32[1024,512]{1,0:T(8,128)} %multiply_add_fusion.codes_ref, bf16[8,384,512]{2,1,0:T(8,128)(2,1)} %get-tuple-element.184.low_ref, bf16[8,384,512]{2,1,0:T(8,128)(2,1)} %get-tuple-element.185.high_ref), custom_call_target="tpu_custom_call" | custom-call | flops 20000000000 | bytes 8000000 | tf_op jit(solution)/shard_map/table_histogram/pallas_call | solution.py:1023
  346.7 8.6 %collective-permute-done.17.refs_7_.refs_8_.refs_9_ = bf16[4,32,2816]{2,1,0:T(8,128)(2,1)} collective-permute-done((bf16[4,32,2816]{2,1,0:T(8,128)(2,1)}, bf16[4,32,2816]{2,1,0:T(8,128)(2,1)}, u32[]{:S(2)}, u32[]{:S(2)}) %collective-permute-start.17) | collective-permute-done | bytes 720928 | tf_op jit(solution)/shard_map/ppermute | solution.py:78
  356.2 4.8 %piece_sums.9 = (bf16[2,32,5632]{2,1,0:T(8,128)(2,1)}, bf16[2,88,1024]{2,1,0:T(8,128)(2,1)}, bf16[4,32,2048]{2,1,0:T(8,128)(2,1)}, bf16[8,32,2048]{2,1,0:T(8,128)(2,1)}) custom-call(bf16[16,32,2816]{2,1,0:T(8,128)(2,1)} %get-tuple-element.158.refs_0_, bf16[16,32,2816]{2,1,0:T(8,128)(2,1)} %collective-permute-done.9.refs_1_, bf16[8,32,2816]{2,1,0:T(8,128)(2,1)} %copy-done.8, ...), custom_call_target="tpu_custom_call" | custom-call | flops 7995392 | bytes 15990784 | tf_op jit(solution)/shard_map/piece_sums/pallas_call | solution.py:182
  364.1 1.5 collective-permute-start.23
  365.6 13.8 %key_gradients.1 = (bf16[512,1024]{1,0:T(8,128)(2,1)}, f32[512,1024]{1,0:T(8,128)}, f32[8,1024]{1,0:T(8,128)}) custom-call(s32[2]{0:T(128)} %pad_add_fusion.1.count_ref.scalar_ref, bf16[512,512]{1,0:T(8,128)(2,1)} %get-tuple-element.156.dq_low_ref, bf16[512,512]{1,0:T(8,128)(2,1)} %get-tuple-element.168.dq_high_ref, ...), custom_call_target="tpu_custom_call" | custom-call | flops 8999999488 | bytes 18000000 | tf_op jit(solution)/shard_map/key_gradients/pallas_call | solution.py:1110
  380.7 4.3 collective-permute-done.23.refs_14_.refs_16_
  387.2 4.0 piece_sums.10
  391.9 1.5 collective-permute-start.25
  393.4 2.5 collective-permute-start.34
  396.1 2.8 collective-permute-done.25.refs_4_
  399.0 6.6 %collective-permute-done.26.refs_8_.refs_3_.refs_9_ = bf16[4,32,2048]{2,1,0:T(8,128)(2,1)S(1)} collective-permute-done((bf16[4,32,2048]{2,1,0:T(8,128)(2,1)}, bf16[4,32,2048]{2,1,0:T(8,128)(2,1)S(1)}, u32[]{:S(2)}, u32[]{:S(2)}) %collective-permute-start.26) | collective-permute-done | bytes 524320 | tf_op jit(solution)/shard_map/ppermute | solution.py:78
  406.4 2.4 piece_sums.11
  412.1 2.2 collective-permute-start.29
  415.7 3.1 piece_sums.13
  418.8 5.8 %collective-permute-start.32 = (bf16[1,32,2048]{2,1,0:T(8,128)(2,1)S(1)}, bf16[1,32,2048]{2,1,0:T(8,128)(2,1)S(1)}, u32[]{:S(2)}, u32[]{:S(2)}) collective-permute-start(bf16[1,32,2048]{2,1,0:T(8,128)(2,1)S(1)} %copy-done.39), channel_id=1, source_target_pairs={{0,16},{4,20},{8,24},{12,28},{16,0},{20,4},{24,8},{28,12},{1,17},{... | collective-permute-start | bytes 393224 | tf_op jit(solution)/shard_map/ppermute | solution.py:78
  424.6 1.9 piece_sums.12
  427.1 2.6 collective-permute-done.30
  431.4 5.5 %input_gradient.1 = bf16[512,1024]{1,0:T(8,128)(2,1)} custom-call(f32[512,1024]{1,0:T(8,128)} %get-tuple-element.197.own_ref, bf16[512,512]{1,0:T(8,128)(2,1)} %fusion.13.owner_ref, bf16[512,1024]{1,0:T(8,128)(2,1)} %pad_maximum_fusion.returned_ref, bf16[512,1024]{1,0:T(8,128)(2,1)} %x_ref.5, f32[8,1024]{1,0:T(8,128)} %broadcast_in_dim.64.gain_ref, ...), custom_call_target="tpu_custom_call" | custom-call | flops 1000000000 | bytes 8000000 | tf_op jit(solution)/shard_map/input_gradient/pallas_call | solution.py:1159
  438.3 2.3 side_totals.1
  440.6 10.4 %all-gather.5.cloned.1.call-done = f32[4096,128]{1,0:T(8,128)} async-done(((f32[128,128]{1,0:T(8,128)}), f32[4096,128]{1,0:T(8,128)}) %all-gather.5.cloned.1.call-update) | async-done | bytes 2097168 | tf_op jit(solution)/shard_map/all_gather | solution.py:1397
  (223 shorter events, 58.7 us)
Async XLA Ops:
  7.2 9.6 %copy-start.1 = (bf16[512,1024]{1,0:T(8,128)(2,1)S(1)}, bf16[512,1024]{1,0:T(8,128)(2,1)}, u32[]{:S(2)}) copy-start(bf16[512,1024]{1,0:T(8,128)(2,1)} %x_ref.5) | copy-start | bytes 3145732
  7.3 8.9 %copy-start.4 = (s32[16384]{0:T(1024)S(1)}, s32[16384]{0:T(1024)}, u32[]{:S(2)}) copy-start(s32[16384]{0:T(1024)} %param.37) | copy-start | bytes 196612
  7.3 167.9 %all-gather.3.cloned.1.call-start = ((), (), s32[]{:S(2)}) async-start(), calls=%async_computation | async-start | bytes 26492928 | tf_op jit(solution)/shard_map/all_gather | solution.py:1215
  9.6 441.4 %all-gather.5.cloned.1.call-start = ((), (), s32[]{:S(2)}) async-start(), calls=%async_computation.1 | async-start | bytes 2162688 | tf_op jit(solution)/shard_map/all_gather | solution.py:1397
  9.8 13.1 %collective-permute-start = (bf16[1,32,128]{1,2,0:T(8,128)(2,1)S(1)}, bf16[1,32,128]{1,2,0:T(8,128)(2,1)S(1)}, u32[]{:S(2)}, u32[]{:S(2)}) collective-permute-start(bf16[1,32,128]{1,2,0:T(8,128)(2,1)S(1)} %bitcast.97), channel_id=1, source_target_pairs={{0,16},{4,20},{8,24},{12,28},{16,0},{20,4},{24,8},{28,12},{1,17},{... | collective-permute-start | bytes 24584 | tf_op jit(solution)/shard_map/ppermute | solution.py:78
  22.9 18.3 %collective-permute-start.1 = (bf16[2,32,128]{2,1,0:T(8,128)(2,1)S(1)}, bf16[2,32,128]{2,1,0:T(8,128)(2,1)S(1)}, u32[]{:S(2)}, u32[]{:S(2)}) collective-permute-start(bf16[2,32,128]{2,1,0:T(8,128)(2,1)S(1)} %pad_maximum_fusion.3), channel_id=1, source_target_pairs={{0,8},{4,12},{8,0},{12,4},{16,24},{20,28},{24,16},{28,20},{1,9},{5... | collective-permute-start | bytes 49160 | tf_op jit(solution)/shard_map/ppermute | solution.py:78
  30.4 14.4 %copy-start.37 = (s32[512,1024]{1,0:T(8,128)S(1)}, s32[512,1024]{1,0:T(8,128)}, u32[]{:S(2)}) copy-start(s32[512,1024]{1,0:T(8,128)} %param.39) | copy-start | bytes 6291460
  30.5 23.1 %collective-permute-start.4 = (bf16[128,1024]{1,0:T(8,128)(2,1)S(1)}, bf16[128,1024]{1,0:T(8,128)(2,1)S(1)}, u32[]{:S(2)}, u32[]{:S(2)}) collective-permute-start(bf16[128,1024]{1,0:T(8,128)(2,1)S(1)} %get-tuple-element.236), channel_id=1, source_target_pairs={{0,4},{4,8},{8,12},{12,16},{16,20},{20,24},{24,28},{1,5},{5,9},{9,... | collective-permute-start | bytes 786440 | tf_op jit(solution)/shard_map/ppermute | solution.py:35
  32.0 21.7 %collective-permute-start.5 = (bf16[128,1024]{1,0:T(8,128)(2,1)S(1)}, bf16[128,1024]{1,0:T(8,128)(2,1)S(1)}, u32[]{:S(2)}, u32[]{:S(2)}) collective-permute-start(bf16[128,1024]{1,0:T(8,128)(2,1)S(1)} %get-tuple-element.235), channel_id=1, source_target_pairs={{4,0},{8,4},{12,8},{16,12},{20,16},{24,20},{28,24},{5,1},{9,5},{13... | collective-permute-start | bytes 786440 | tf_op jit(solution)/shard_map/ppermute | solution.py:36
  33.3 20.4 %collective-permute-start.6 = (bf16[128,1024]{1,0:T(8,128)(2,1)S(1)}, bf16[128,1024]{1,0:T(8,128)(2,1)S(1)}, u32[]{:S(2)}, u32[]{:S(2)}) collective-permute-start(bf16[128,1024]{1,0:T(8,128)(2,1)S(1)} %get-tuple-element.234), channel_id=1, source_target_pairs={{0,1},{1,2},{2,3},{4,5},{5,6},{6,7},{8,9},{9,10},{10,11},{12,13},{... | collective-permute-start | bytes 786440 | tf_op jit(solution)/shard_map/ppermute | solution.py:35
  36.7 17.0 %collective-permute-start.7 = (bf16[128,1024]{1,0:T(8,128)(2,1)S(1)}, bf16[128,1024]{1,0:T(8,128)(2,1)S(1)}, u32[]{:S(2)}, u32[]{:S(2)}) collective-permute-start(bf16[128,1024]{1,0:T(8,128)(2,1)S(1)} %get-tuple-element.233), channel_id=1, source_target_pairs={{1,0},{2,1},{3,2},{5,4},{6,5},{7,6},{9,8},{10,9},{11,10},{13,12},{... | collective-permute-start | bytes 786440 | tf_op jit(solution)/shard_map/ppermute | solution.py:36
  40.5 13.3 %copy-start.9 = (bf16[1024,1024]{1,0:T(8,128)(2,1)}, bf16[1024,1024]{1,0:T(8,128)(2,1)S(1)}, u32[]{:S(2)}) copy-start(bf16[1024,1024]{1,0:T(8,128)(2,1)S(1)} %fusion.4.pack_ref) | copy-start | bytes 6291460
  41.2 10.4 %collective-permute-start.2 = (bf16[4,32,128]{2,1,0:T(8,128)(2,1)S(1)}, bf16[4,32,128]{2,1,0:T(8,128)(2,1)S(1)}, u32[]{:S(2)}, u32[]{:S(2)}) collective-permute-start(bf16[4,32,128]{2,1,0:T(8,128)(2,1)S(1)} %pad_maximum_fusion.2), channel_id=1, source_target_pairs={{0,2},{1,3},{2,0},{3,1},{4,6},{5,7},{6,4},{7,5},{8,10},{9,11},{10,... | collective-permute-start | bytes 98312 | tf_op jit(solution)/shard_map/ppermute | solution.py:78
  51.6 6.1 %collective-permute-start.3 = (bf16[8,32,128]{2,1,0:T(8,128)(2,1)S(1)}, bf16[8,32,128]{2,1,0:T(8,128)(2,1)S(1)}, u32[]{:S(2)}, u32[]{:S(2)}) collective-permute-start(bf16[8,32,128]{2,1,0:T(8,128)(2,1)S(1)} %pad_maximum_fusion.1), channel_id=1, source_target_pairs={{0,1},{1,0},{2,3},{3,2},{4,5},{5,4},{6,7},{7,6},{8,9},{9,8},{10,11... | collective-permute-start | bytes 196616 | tf_op jit(solution)/shard_map/ppermute | solution.py:78
  56.3 29.3 %copy-start.13 = (bf16[1024,1024]{1,0:T(8,128)(2,1)}, bf16[1024,1024]{1,0:T(8,128)(2,1)S(1)}, u32[]{:S(2)}) copy-start(bf16[1024,1024]{1,0:T(8,128)(2,1)S(1)} %get-tuple-element.256.picked_ref) | copy-start | bytes 6291460
  58.4 1.3 collective-permute-start.8
  66.4 17.9 %copy-start.31 = (f32[512]{0:T(512)S(1)}, f32[512]{0:T(512)}, u32[]{:S(2)}) copy-start(f32[512]{0:T(512)} %add_rsqrt_fusion.1) | copy-start | bytes 6148
  249.4 20.7 %collective-permute-start.11 = (bf16[16,88,1024]{2,1,0:T(8,128)(2,1)}, bf16[16,88,1024]{2,1,0:T(8,128)(2,1)S(1)}, u32[]{:S(2)}, u32[]{:S(2)}) collective-permute-start(bf16[16,88,1024]{2,1,0:T(8,128)(2,1)} %get-tuple-element.148), channel_id=1, source_target_pairs={{0,4},{4,0},{8,12},{12,8},{16,20},{20,16},{24,28},{28,24},{1,5},{5... | collective-permute-start | bytes 8650760 | tf_op jit(solution)/shard_map/ppermute | solution.py:78
  249.7 20.4 %collective-permute-start.10 = (bf16[16,32,2816]{2,1,0:T(8,128)(2,1)}, bf16[16,32,2816]{2,1,0:T(8,128)(2,1)S(1)}, u32[]{:S(2)}, u32[]{:S(2)}) collective-permute-start(bf16[16,32,2816]{2,1,0:T(8,128)(2,1)} %get-tuple-element.147), channel_id=1, source_target_pairs={{0,4},{4,0},{8,12},{12,8},{16,20},{20,16},{24,28},{28,24},{1,5},{5... | collective-permute-start | bytes 8650760 | tf_op jit(solution)/shard_map/ppermute | solution.py:78
  250.0 20.1 %collective-permute-start.9 = (bf16[16,32,2816]{2,1,0:T(8,128)(2,1)}, bf16[16,32,2816]{2,1,0:T(8,128)(2,1)}, u32[]{:S(2)}, u32[]{:S(2)}) collective-permute-start(bf16[16,32,2816]{2,1,0:T(8,128)(2,1)} %get-tuple-element.146), channel_id=1, source_target_pairs={{0,4},{4,0},{8,12},{12,8},{16,20},{20,16},{24,28},{28,24},{1,5},{5... | collective-permute-start | bytes 8650760 | tf_op jit(solution)/shard_map/ppermute | solution.py:78
  269.8 32.2 %collective-permute-start.15 = (bf16[16,32,2048]{2,1,0:T(8,128)(2,1)}, bf16[16,32,2048]{2,1,0:T(8,128)(2,1)}, u32[]{:S(2)}, u32[]{:S(2)}) collective-permute-start(bf16[16,32,2048]{2,1,0:T(8,128)(2,1)} %get-tuple-element.157), channel_id=1, source_target_pairs={{0,4},{4,0},{8,12},{12,8},{16,20},{20,16},{24,28},{28,24},{1,5},{5... | collective-permute-start | bytes 6291464 | tf_op jit(solution)/shard_map/ppermute | solution.py:78
  278.8 34.0 %collective-permute-start.14 = (bf16[8,88,1024]{2,1,0:T(8,128)(2,1)}, bf16[8,88,1024]{2,1,0:T(8,128)(2,1)S(1)}, u32[]{:S(2)}, u32[]{:S(2)}) collective-permute-start(bf16[8,88,1024]{2,1,0:T(8,128)(2,1)} %get-tuple-element.166), channel_id=1, source_target_pairs={{0,8},{4,12},{8,0},{12,4},{16,24},{20,28},{24,16},{28,20},{1,9},{5... | collective-permute-start | bytes 4325384 | tf_op jit(solution)/shard_map/ppermute | solution.py:78
  278.9 34.0 %collective-permute-start.13 = (bf16[8,32,2816]{2,1,0:T(8,128)(2,1)}, bf16[8,32,2816]{2,1,0:T(8,128)(2,1)S(1)}, u32[]{:S(2)}, u32[]{:S(2)}) collective-permute-start(bf16[8,32,2816]{2,1,0:T(8,128)(2,1)} %get-tuple-element.165), channel_id=1, source_target_pairs={{0,2},{1,3},{2,0},{3,1},{4,6},{5,7},{6,4},{7,5},{8,10},{9,11},{10,... | collective-permute-start | bytes 4325384 | tf_op jit(solution)/shard_map/ppermute | solution.py:78
  280.4 33.7 %collective-permute-start.12 = (bf16[8,32,2816]{2,1,0:T(8,128)(2,1)}, bf16[8,32,2816]{2,1,0:T(8,128)(2,1)S(1)}, u32[]{:S(2)}, u32[]{:S(2)}) collective-permute-start(bf16[8,32,2816]{2,1,0:T(8,128)(2,1)} %get-tuple-element.164), channel_id=1, source_target_pairs={{0,1},{1,0},{2,3},{3,2},{4,5},{5,4},{6,7},{7,6},{8,9},{9,8},{10,11... | collective-permute-start | bytes 4325384 | tf_op jit(solution)/shard_map/ppermute | solution.py:78
  302.1 44.6 %collective-permute-start.20 = (bf16[16,32,2048]{2,1,0:T(8,128)(2,1)}, bf16[16,32,2048]{2,1,0:T(8,128)(2,1)S(1)}, u32[]{:S(2)}, u32[]{:S(2)}) collective-permute-start(bf16[16,32,2048]{2,1,0:T(8,128)(2,1)} %get-tuple-element.173), channel_id=1, source_target_pairs={{0,4},{4,0},{8,12},{12,8},{16,20},{20,16},{24,28},{28,24},{1,5},{5... | collective-permute-start | bytes 6291464 | tf_op jit(solution)/shard_map/ppermute | solution.py:78
  321.2 34.1 %collective-permute-start.19 = (bf16[8,32,2048]{2,1,0:T(8,128)(2,1)}, bf16[8,32,2048]{2,1,0:T(8,128)(2,1)S(1)}, u32[]{:S(2)}, u32[]{:S(2)}) collective-permute-start(bf16[8,32,2048]{2,1,0:T(8,128)(2,1)} %get-tuple-element.182), channel_id=1, source_target_pairs={{0,8},{4,12},{8,0},{12,4},{16,24},{20,28},{24,16},{28,20},{1,9},{5... | collective-permute-start | bytes 3145736 | tf_op jit(solution)/shard_map/ppermute | solution.py:78
  322.9 23.7 %collective-permute-start.18 = (bf16[4,88,1024]{2,1,0:T(8,128)(2,1)}, bf16[4,88,1024]{2,1,0:T(8,128)(2,1)}, u32[]{:S(2)}, u32[]{:S(2)}) collective-permute-start(bf16[4,88,1024]{2,1,0:T(8,128)(2,1)} %get-tuple-element.181), channel_id=1, source_target_pairs={{0,1},{1,0},{2,3},{3,2},{4,5},{5,4},{6,7},{7,6},{8,9},{9,8},{10,11... | collective-permute-start | bytes 2162696 | tf_op jit(solution)/shard_map/ppermute | solution.py:78
  323.7 31.6 %collective-permute-start.17 = (bf16[4,32,2816]{2,1,0:T(8,128)(2,1)}, bf16[4,32,2816]{2,1,0:T(8,128)(2,1)}, u32[]{:S(2)}, u32[]{:S(2)}) collective-permute-start(bf16[4,32,2816]{2,1,0:T(8,128)(2,1)} %get-tuple-element.180), channel_id=1, source_target_pairs={{0,1},{1,0},{2,3},{3,2},{4,5},{5,4},{6,7},{7,6},{8,9},{9,8},{10,11... | collective-permute-start | bytes 2162696 | tf_op jit(solution)/shard_map/ppermute | solution.py:78
  324.9 30.3 %collective-permute-start.16 = (bf16[4,32,2816]{2,1,0:T(8,128)(2,1)}, bf16[4,32,2816]{2,1,0:T(8,128)(2,1)}, u32[]{:S(2)}, u32[]{:S(2)}) collective-permute-start(bf16[4,32,2816]{2,1,0:T(8,128)(2,1)} %get-tuple-element.179), channel_id=1, source_target_pairs={{0,2},{1,3},{2,0},{3,1},{4,6},{5,7},{6,4},{7,5},{8,10},{9,11},{10,... | collective-permute-start | bytes 2162696 | tf_op jit(solution)/shard_map/ppermute | solution.py:78
  325.7 19.9 %copy-start.29 = (f32[96,128]{1,0:T(8,128)S(1)}, f32[96,128]{1,0:T(8,128)}, u32[]{:S(2)}) copy-start(f32[96,128]{1,0:T(8,128)} %get-tuple-element.217) | copy-start | bytes 147460
  325.7 19.9 %copy-start.30 = (f32[96,128]{1,0:T(8,128)S(1)}, f32[96,128]{1,0:T(8,128)}, u32[]{:S(2)}) copy-start(f32[96,128]{1,0:T(8,128)} %get-tuple-element.218) | copy-start | bytes 147460
  346.6 8.6 %copy-start.5 = (bf16[16,32,2048]{2,1,0:T(8,128)(2,1)}, bf16[16,32,2048]{2,1,0:T(8,128)(2,1)S(1)}, u32[]{:S(2)}) copy-start(bf16[16,32,2048]{2,1,0:T(8,128)(2,1)S(1)} %collective-permute-done.20.refs_16_.refs_20_.refs_6_.refs_1_.refs_7_) | copy-start | bytes 6291460
  361.0 25.0 %collective-permute-start.24 = (bf16[8,32,2048]{2,1,0:T(8,128)(2,1)}, bf16[8,32,2048]{2,1,0:T(8,128)(2,1)S(1)}, u32[]{:S(2)}, u32[]{:S(2)}) collective-permute-start(bf16[8,32,2048]{2,1,0:T(8,128)(2,1)} %get-tuple-element.195), channel_id=1, source_target_pairs={{0,1},{1,0},{2,3},{3,2},{4,5},{5,4},{6,7},{7,6},{8,9},{9,8},{10,11... | collective-permute-start | bytes 3145736 | tf_op jit(solution)/shard_map/ppermute | solution.py:78
  362.4 23.7 %collective-permute-start.22 = (bf16[2,32,5632]{2,1,0:T(8,128)(2,1)}, bf16[2,32,5632]{2,1,0:T(8,128)(2,1)S(1)}, u32[]{:S(2)}, u32[]{:S(2)}) collective-permute-start(bf16[2,32,5632]{2,1,0:T(8,128)(2,1)} %get-tuple-element.192), channel_id=1, source_target_pairs={{0,8},{4,12},{8,0},{12,4},{16,24},{20,28},{24,16},{28,20},{1,9},{5... | collective-permute-start | bytes 2162696 | tf_op jit(solution)/shard_map/ppermute | solution.py:78
  363.4 21.6 %collective-permute-start.21 = (bf16[4,32,2048]{2,1,0:T(8,128)(2,1)}, bf16[4,32,2048]{2,1,0:T(8,128)(2,1)S(1)}, u32[]{:S(2)}, u32[]{:S(2)}) collective-permute-start(bf16[4,32,2048]{2,1,0:T(8,128)(2,1)} %get-tuple-element.194), channel_id=1, source_target_pairs={{0,2},{1,3},{2,0},{3,1},{4,6},{5,7},{6,4},{7,5},{8,10},{9,11},{10,... | collective-permute-start | bytes 1572872 | tf_op jit(solution)/shard_map/ppermute | solution.py:78
  364.1 20.9 %collective-permute-start.23 = (bf16[2,88,1024]{2,1,0:T(8,128)(2,1)}, bf16[2,88,1024]{2,1,0:T(8,128)(2,1)S(1)}, u32[]{:S(2)}, u32[]{:S(2)}) collective-permute-start(bf16[2,88,1024]{2,1,0:T(8,128)(2,1)} %get-tuple-element.193), channel_id=1, source_target_pairs={{0,16},{4,20},{8,24},{12,28},{16,0},{20,4},{24,8},{28,12},{1,17},{... | collective-permute-start | bytes 1081352 | tf_op jit(solution)/shard_map/ppermute | solution.py:78
  391.3 14.3 %collective-permute-start.26 = (bf16[4,32,2048]{2,1,0:T(8,128)(2,1)}, bf16[4,32,2048]{2,1,0:T(8,128)(2,1)S(1)}, u32[]{:S(2)}, u32[]{:S(2)}) collective-permute-start(bf16[4,32,2048]{2,1,0:T(8,128)(2,1)} %get-tuple-element.204), channel_id=1, source_target_pairs={{0,2},{1,3},{2,0},{3,1},{4,6},{5,7},{6,4},{7,5},{8,10},{9,11},{10,... | collective-permute-start | bytes 1572872 | tf_op jit(solution)/shard_map/ppermute | solution.py:78
  391.9 7.1 %collective-permute-start.25 = (bf16[2,32,2048]{2,1,0:T(8,128)(2,1)}, bf16[2,32,2048]{2,1,0:T(8,128)(2,1)S(1)}, u32[]{:S(2)}, u32[]{:S(2)}) collective-permute-start(bf16[2,32,2048]{2,1,0:T(8,128)(2,1)} %get-tuple-element.203), channel_id=1, source_target_pairs={{0,1},{1,0},{2,3},{3,2},{4,5},{5,4},{6,7},{7,6},{8,9},{9,8},{10,11... | collective-permute-start | bytes 786440 | tf_op jit(solution)/shard_map/ppermute | solution.py:78
  393.4 20.9 %collective-permute-start.34 = (bf16[1,32,5632]{2,1,0:T(8,128)(2,1)}, bf16[1,32,5632]{2,1,0:T(8,128)(2,1)S(1)}, u32[]{:S(2)}, u32[]{:S(2)}) collective-permute-start(bf16[1,32,5632]{2,1,0:T(8,128)(2,1)} %get-tuple-element.220), channel_id=1, source_target_pairs={{0,16},{4,20},{8,24},{12,28},{16,0},{20,4},{24,8},{28,12},{1,17},{... | collective-permute-start | bytes 1081352 | tf_op jit(solution)/shard_map/ppermute | solution.py:78
  395.9 13.5 %copy-start.21 = (bf16[512,1024]{1,0:T(8,128)(2,1)S(1)}, bf16[512,1024]{1,0:T(8,128)(2,1)}, u32[]{:S(2)}) copy-start(bf16[512,1024]{1,0:T(8,128)(2,1)} %get-tuple-element.207) | copy-start | bytes 3145732
  395.9 16.2 %collective-permute-start.35 = (bf16[1,88,1024]{2,1,0:T(8,128)(2,1)}, bf16[1,88,1024]{2,1,0:T(8,128)(2,1)S(1)}, u32[]{:S(2)}, u32[]{:S(2)}) collective-permute-start(bf16[1,88,1024]{2,1,0:T(8,128)(2,1)} %get-tuple-element.221), channel_id=1, source_target_pairs={{0,2},{1,3},{2,0},{3,1},{4,6},{5,7},{6,4},{7,5},{8,10},{9,11},{10,... | collective-permute-start | bytes 540680 | tf_op jit(solution)/shard_map/ppermute | solution.py:78
  408.8 10.0 %collective-permute-start.31 = (bf16[2,32,2048]{2,1,0:T(8,128)(2,1)}, bf16[2,32,2048]{2,1,0:T(8,128)(2,1)S(1)}, u32[]{:S(2)}, u32[]{:S(2)}) collective-permute-start(bf16[2,32,2048]{2,1,0:T(8,128)(2,1)} %get-tuple-element.206), channel_id=1, source_target_pairs={{0,8},{4,12},{8,0},{12,4},{16,24},{20,28},{24,16},{28,20},{1,9},{5... | collective-permute-start | bytes 786440 | tf_op jit(solution)/shard_map/ppermute | solution.py:78
  409.5 17.0 %collective-permute-start.27 = (bf16[128,1024]{1,0:T(8,128)(2,1)S(1)}, bf16[128,1024]{1,0:T(8,128)(2,1)S(1)}, u32[]{:S(2)}, u32[]{:S(2)}) collective-permute-start(bf16[128,1024]{1,0:T(8,128)(2,1)S(1)} %get-tuple-element.229), channel_id=1, source_target_pairs={{0,4},{4,8},{8,12},{12,16},{16,20},{20,24},{24,28},{1,5},{5,9},{9,... | collective-permute-start | bytes 786440 | tf_op jit(solution)/shard_map/ppermute | solution.py:35
  410.8 16.3 %collective-permute-start.28 = (bf16[128,1024]{1,0:T(8,128)(2,1)S(1)}, bf16[128,1024]{1,0:T(8,128)(2,1)S(1)}, u32[]{:S(2)}, u32[]{:S(2)}) collective-permute-start(bf16[128,1024]{1,0:T(8,128)(2,1)S(1)} %get-tuple-element.232), channel_id=1, source_target_pairs={{4,0},{8,4},{12,8},{16,12},{20,16},{24,20},{28,24},{5,1},{9,5},{13... | collective-permute-start | bytes 786440 | tf_op jit(solution)/shard_map/ppermute | solution.py:36
  412.1 15.0 %collective-permute-start.29 = (bf16[128,1024]{1,0:T(8,128)(2,1)S(1)}, bf16[128,1024]{1,0:T(8,128)(2,1)S(1)}, u32[]{:S(2)}, u32[]{:S(2)}) collective-permute-start(bf16[128,1024]{1,0:T(8,128)(2,1)S(1)} %get-tuple-element.231), channel_id=1, source_target_pairs={{0,1},{1,2},{2,3},{4,5},{5,6},{6,7},{8,9},{9,10},{10,11},{12,13},{... | collective-permute-start | bytes 786440 | tf_op jit(solution)/shard_map/ppermute | solution.py:35
  414.3 15.4 %collective-permute-start.30 = (bf16[128,1024]{1,0:T(8,128)(2,1)S(1)}, bf16[128,1024]{1,0:T(8,128)(2,1)S(1)}, u32[]{:S(2)}, u32[]{:S(2)}) collective-permute-start(bf16[128,1024]{1,0:T(8,128)(2,1)S(1)} %get-tuple-element.230), channel_id=1, source_target_pairs={{1,0},{2,1},{3,2},{5,4},{6,5},{7,6},{9,8},{10,9},{11,10},{13,12},{... | collective-permute-start | bytes 786440 | tf_op jit(solution)/shard_map/ppermute | solution.py:36
  418.8 18.2 %collective-permute-start.32 = (bf16[1,32,2048]{2,1,0:T(8,128)(2,1)S(1)}, bf16[1,32,2048]{2,1,0:T(8,128)(2,1)S(1)}, u32[]{:S(2)}, u32[]{:S(2)}) collective-permute-start(bf16[1,32,2048]{2,1,0:T(8,128)(2,1)S(1)} %copy-done.39), channel_id=1, source_target_pairs={{0,16},{4,20},{8,24},{12,28},{16,0},{20,4},{24,8},{28,12},{1,17},{... | collective-permute-start | bytes 393224 | tf_op jit(solution)/shard_map/ppermute | solution.py:78
  426.5 10.5 %collective-permute-start.33 = (bf16[1,32,2048]{2,1,0:T(8,128)(2,1)}, bf16[1,32,2048]{2,1,0:T(8,128)(2,1)S(1)}, u32[]{:S(2)}, u32[]{:S(2)}) collective-permute-start(bf16[1,32,2048]{2,1,0:T(8,128)(2,1)} %piece_sums.12), channel_id=1, source_target_pairs={{0,16},{4,20},{8,24},{12,28},{16,0},{20,4},{24,8},{28,12},{1,17},{... | collective-permute-start | bytes 393224 | tf_op jit(solution)/shard_map/ppermute | solution.py:78
  (31 other events, 83.9 us)
Sparse Core Ops, SparseCore 0:
  11.5 163.5 all-gather.2
  386.2 64.7 all-gather.4

commit v7 on v6

--- a/solution.py
+++ b/solution.py
@@ -814,17 +814,19 @@
     @pl.when(step == 0)
     def _():
         back_ref[...] = dot_nt(attn_grad_ref[...], wo_ref[...]).astype(BF)
+
+    @pl.when(jnp.logical_and(step == 0, few))
+    def _():
+        turned_ref[:, 0:FEW] = k_ref[0:FEW, :].T
+        dk_sum_ref[0:FEW, :] = jnp.zeros_like(dk_sum_ref[0:FEW, :])
+        dv_sum_ref[0:FEW, :] = jnp.zeros_like(dv_sum_ref[0:FEW, :])
+
+    @pl.when(jnp.logical_and(step == 0, jnp.logical_not(few)))
+    def _():
+        turned_ref[...] = k_ref[...].T
         dk_sum_ref[...] = jnp.zeros_like(dk_sum_ref)
         dv_sum_ref[...] = jnp.zeros_like(dv_sum_ref)
         hist_ref[...] = jnp.zeros_like(hist_ref)
-
-    @pl.when(jnp.logical_and(step == 0, few))
-    def _():
-        turned_ref[:, 0:FEW] = k_ref[0:FEW, :].T
-
-    @pl.when(jnp.logical_and(step == 0, jnp.logical_not(few)))
-    def _():
-        turned_ref[...] = k_ref[...].T
 
     here = pl.ds(pl.multiple_of(step * COLS, COLS), COLS)
     masks = head_masks()
@@ -880,18 +882,21 @@
         part_pieces(joined_ref, sent_ref, kept_ref, count_ref[1], scatter_order, at)
 
     def finish(keys):
+        dk_ref[0:keys, :] = dk_sum_ref[0:keys, :].astype(BF)
+        dv_ref[0:keys, :] = dv_sum_ref[0:keys, :].astype(BF)
+        if keys == total_keys:
+            take_histogram(hist_ref, hist_out_ref)
+        else:
+            hist_out_ref[...] = jnp.zeros_like(hist_out_ref)
         leave(1, dot_tn(picked_ref[0:keys, :], dk_ref[0:keys, :]))
         leave(2, dot_tn(picked_ref[0:keys, :], dv_ref[0:keys, :]))
 
     @pl.when(step == pl.num_programs(0) - 1)
     def _():
-        dk_ref[...] = dk_sum_ref[...].astype(BF)
-        dv_ref[...] = dv_sum_ref[...].astype(BF)
         dq_ref[...] = dq_turned_ref[...].T
         leave(0, dot_tn(normed_ref[...], dq_ref[...]))
         first = first_head * HEAD_DIM
         leave(3, dot_nn(mixed_ref[...], attn_grad_ref[:, first : first + heads * HEAD_DIM]))
-        take_histogram(hist_ref, hist_out_ref)
         pl.when(few)(lambda: finish(FEW))
         pl.when(jnp.logical_not(few))(lambda: finish(total_keys))
 
@@ -1394,7 +1399,7 @@
     small_rows = small_part.shape[0]
     small_part = jnp.pad(small_part, ((0, 128 - small_rows), (0, 0)))
     landed = rounds.land(lent)
-    small_parts = lax.all_gather(after(small_part, landed), ("row", "col"), axis=0, tiled=True)
+    small_parts = lax.all_gather(after(small_part, landed[:1]), ("row", "col"), axis=0, tiled=True)
     rounds.send()
     rounds.land()
     sent = rounds.send()

time: 467 us -> 470 us (level)
    ppermute x28, waiting for transfers between devices: 38 us -> 54 us  [exchange(): return lax.ppermute(values, axis, pairs)]
    all_gather x1, waiting for transfers between devices: 10.4 us -> 0.01 us  [on_device(): lax.all_gather(after(small_part, landed[:1]), ('row', 'col'), axis=0, til...]
    unnamed x90 -> x96, local copies, waits for them, and re-layouts: 12.2 us -> 12 us
  transfers between devices with their start and end apart: 38 -> 38, of which waited for: 14 -> 13; matrix products, arithmetic and copies ran while one was open for 9% -> 9% of each run, Pallas kernels for 30% -> 30%
where the time goes in v7:
time: 470 us; the launch traced here: 465 us
  Pallas kernels  219 us (47%)
  waiting for transfers between devices  124 us (26%)
  starting transfers between devices  49.3 us (10%)
  local copies, waits for them, and re-layouts  34 us (7%)
  between operations  16.3 us (3%)
  other arithmetic  13.3 us (3%)
  matrix products  8.36 us (2%)
    all_gather x1, waiting for transfers between devices, on_device(): weights = lax.all_gather(packed_weights, ('row', 'col'), axis=0, tiled=True)  70.4 us
    ppermute x28, waiting for transfers between devices, exchange(): return lax.ppermute(values, axis, pairs)  54 us
    pallas_call x1, Pallas kernels, feed_forward(): pl.pallas_call(kernel, grid_spec=pltpu.PrefetchScalarGridSpec(num_scalar_...  45.9 us
    pallas_call x2, Pallas kernels, attention_backward(): pl.pallas_call(functools.partial(backward_kernel, first_head=half * heads...  38.4 us
    pallas_call x2, Pallas kernels, layout_bias(): pl.pallas_call(functools.partial(bias_kernel, first_head=first_head), gri...  34.6 us
    ppermute x28, starting transfers between devices, exchange(): return lax.ppermute(values, axis, pairs)  34.3 us
    pallas_call x7, Pallas kernels, piece_sums(): pl.pallas_call(functools.partial(sum_kernel, shares=shares), grid=(steps,...  28.5 us
    pallas_call x1, Pallas kernels, attention_forward(): pl.pallas_call(attend_kernel, grid_spec=pltpu.PrefetchScalarGridSpec(num_...  27.8 us
  transfers between devices with their start and end apart: 38, of which 13 were waited for; matrix products, arithmetic and copies ran while one was open for 9% of the time, Pallas kernels for 30%

profile of v7, /device:TPU:0, one launch (start us, length us, event | category | flops | bytes accessed | tf_op | source)
XLA Modules:
  0.0 464.6 jit_solution(7422318642232397716)
XLA Ops:
  7.3 2.2 pack_shards.1
  9.8 4.1 collective-permute-start
  20.8 2.1 gather_fusion
  22.9 1.6 collective-permute-start.1
  26.1 3.1 gather_fusion.2
  30.5 1.4 collective-permute-start.4
  33.3 3.4 collective-permute-start.6
  36.7 1.5 collective-permute-start.7
  41.2 3.6 collective-permute-start.2
  47.8 3.2 multiply_add_fusion.codes_ref
  53.8 2.5 fusion
  60.4 1.6 gather_fusion.4
  66.4 17.3 %layout_bias.2.low_bias_ref = f32[8,384,512]{2,1,0:T(8,128)} custom-call(s32[1024,512]{1,0:T(8,128)} %multiply_add_fusion.codes_ref, f32[48,128]{1,0:T(8,128)} %bitcast.100), custom_call_target="tpu_custom_call" | custom-call | flops 16000000000 | bytes 7000000 | tf_op jit(solution)/shard_map/layout_bias/pallas_call | solution.py:364
  85.6 1.9 fusion.2.picked_ref
  87.5 17.3 %layout_bias.3.high_bias_ref = f32[8,384,512]{2,1,0:T(8,128)} custom-call(s32[1024,512]{1,0:T(8,128)} %multiply_add_fusion.codes_ref, f32[48,128]{1,0:T(8,128)} %bitcast.101), custom_call_target="tpu_custom_call" | custom-call | flops 16000000000 | bytes 7000000 | tf_op jit(solution)/shard_map/layout_bias/pallas_call | solution.py:364
  104.7 70.4 %all-gather.3.cloned.1.call-done.wq_ref.wk_ref.wv_ref.wo_ref.gate_ref.up_ref.packed_ref = bf16[1024,12544]{1,0:T(8,128)(2,1)} async-done(((bf16[32,12544]{1,0:T(8,128)(2,1)}), bf16[1024,12544]{1,0:T(8,128)(2,1)}) %all-gather.3.cloned.1.call-update) | async-done | bytes 25690128 | tf_op jit(solution)/shard_map/all_gather | solution.py:1220
  175.7 27.8 %attention_forward.1 = (bf16[512,1024]{1,0:T(8,128)(2,1)}, bf16[1024,1024]{1,0:T(8,128)(2,1)}, bf16[1024,1024]{1,0:T(8,128)(2,1)}, bf16[1024,512]{1,0:T(8,128)(2...) custom-call(s32[2]{0:T(128)} %pad_add_fusion.1.count_ref.scalar_ref, ...), custom_call_target="tpu_custom_call" | custom-call | flops 20000000000 | bytes 50000000 | tf_op jit(solution)/shard_map/attention_forward/pallas_call | solution.py:507
  203.5 45.9 %feed_forward.1 = (bf16[16,32,2816]{2,1,0:T(8,128)(2,1)}, bf16[16,32,2816]{2,1,0:T(8,128)(2,1)}, bf16[16,32,2816]{2,1,0:T(8,128)(2,1)}, bf16[16,32,2816]{2,1,0:T...) custom-call(s32[2]{0:T(128)} %pad_add_fusion.1.count_ref.scalar_ref,, ...), custom_call_target="tpu_custom_call" | custom-call | flops 27000000512 | bytes 44000000 | tf_op jit(solution)/shard_map/feed_forward/pallas_call | solution.py:691
  250.2 19.2 %attention_backward.2 = (bf16[512,512]{1,0:T(8,128)(2,1)}, bf16[1024,512]{1,0:T(8,128)(2,1)}, bf16[1024,512]{1,0:T(8,128)(2,1)}, bf16[8,384,512]{2,1,0:T(8,128)(...) custom-call(s32[2]{0:T(128)} %pad_add_fusion.1.count_ref.scalar_ref, ...), custom_call_target="tpu_custom_call" | custom-call | flops 15000000512 | bytes 30000000 | tf_op jit(solution)/shard_map/attention_backward/pallas_call | solution.py:932
  269.8 1.6 copy-done.2
  272.1 6.3 %piece_sums.7 = (bf16[8,32,2816]{2,1,0:T(8,128)(2,1)}, bf16[8,32,2816]{2,1,0:T(8,128)(2,1)}, bf16[8,88,1024]{2,1,0:T(8,128)(2,1)}) custom-call(bf16[16,32,2816]{2,1,0:T(8,128)(2,1)} %get-tuple-element.158.refs_0_, bf16[16,32,2816]{2,1,0:T(8,128)(2,1)} %collective-permute-done.9.refs_1_, ...), custom_call_target="tpu_custom_call" | custom-call | flops 8650752 | bytes 17301504 | tf_op jit(solution)/shard_map/piece_sums/pallas_call | solution.py:182
  278.5 1.5 collective-permute-start.13
  282.1 19.2 %attention_backward.3 = (bf16[512,512]{1,0:T(8,128)(2,1)}, bf16[1024,512]{1,0:T(8,128)(2,1)}, bf16[1024,512]{1,0:T(8,128)(2,1)}, bf16[8,384,512]{2,1,0:T(8,128)(...) custom-call(s32[2]{0:T(128)} %pad_add_fusion.1.count_ref.scalar_ref, ...), custom_call_target="tpu_custom_call" | custom-call | flops 15000000512 | bytes 30000000 | tf_op jit(solution)/shard_map/attention_backward/pallas_call | solution.py:932
  301.4 11.1 %collective-permute-done.14.refs_8_.refs_10_.refs_12_.refs_14_ = bf16[8,88,1024]{2,1,0:T(8,128)(2,1)S(1)} collective-permute-done((bf16[8,88,1024]{2,1,0:T(8,128)(2,1)}, bf16[8,88,1024]{2,1,0:T(8,128)(2,1)S(1)}, u32[]{:S(2)}, u32[]{:S(2)}) %collective-permute-start.14) | collective-permute-done | bytes 1441824 | tf_op jit(solution)/shard_map/ppermute | solution.py:78
  314.9 5.9 %piece_sums.8 = (bf16[4,32,2816]{2,1,0:T(8,128)(2,1)}, bf16[4,32,2816]{2,1,0:T(8,128)(2,1)}, bf16[4,88,1024]{2,1,0:T(8,128)(2,1)}, bf16[8,32,2048]{2,1,0:T(8,128)(2,1)}) custom-call(bf16[16,32,2816]{2,1,0:T(8,128)(2,1)} %get-tuple-element.158.refs_0_, bf16[16,32,2816]{2,1,0:T(8,128)(2,1)} %collective-permute-done.9.refs_1_, bf16[8,32,2816]{2,1,0:T(8,128)(2,1)} %copy-done.8, ...), custom_call_target="tpu_custom_call" | custom-call | flops 8585216 | bytes 17170432 | tf_op jit(solution)/shard_map/piece_sums/pallas_call | solution.py:182
  320.8 1.7 collective-permute-start.19
  325.3 19.9 %table_histogram.1 = f32[96,256]{1,0:T(8,128)} custom-call(s32[2]{0:T(128)} %pad_add_fusion.1.count_ref.scalar_ref, s32[1024,512]{1,0:T(8,128)} %multiply_add_fusion.codes_ref, bf16[8,384,512]{2,1,0:T(8,128)(2,1)} %get-tuple-element.184.low_ref, bf16[8,384,512]{2,1,0:T(8,128)(2,1)} %get-tuple-element.185.high_ref), custom_call_target="tpu_custom_call" | custom-call | flops 20000000000 | bytes 8000000 | tf_op jit(solution)/shard_map/table_histogram/pallas_call | solution.py:1028
  346.5 8.4 %collective-permute-done.17.refs_7_.refs_8_.refs_9_ = bf16[4,32,2816]{2,1,0:T(8,128)(2,1)} collective-permute-done((bf16[4,32,2816]{2,1,0:T(8,128)(2,1)}, bf16[4,32,2816]{2,1,0:T(8,128)(2,1)}, u32[]{:S(2)}, u32[]{:S(2)}) %collective-permute-start.17) | collective-permute-done | bytes 720928 | tf_op jit(solution)/shard_map/ppermute | solution.py:78
  355.8 4.8 %piece_sums.9 = (bf16[2,32,5632]{2,1,0:T(8,128)(2,1)}, bf16[2,88,1024]{2,1,0:T(8,128)(2,1)}, bf16[4,32,2048]{2,1,0:T(8,128)(2,1)}, bf16[8,32,2048]{2,1,0:T(8,128)(2,1)}) custom-call(bf16[16,32,2816]{2,1,0:T(8,128)(2,1)} %get-tuple-element.158.refs_0_, bf16[16,32,2816]{2,1,0:T(8,128)(2,1)} %collective-permute-done.9.refs_1_, bf16[8,32,2816]{2,1,0:T(8,128)(2,1)} %copy-done.8, ...), custom_call_target="tpu_custom_call" | custom-call | flops 7995392 | bytes 15990784 | tf_op jit(solution)/shard_map/piece_sums/pallas_call | solution.py:182
  361.4 13.9 %key_gradients.1 = (bf16[512,1024]{1,0:T(8,128)(2,1)}, f32[512,1024]{1,0:T(8,128)}, f32[8,1024]{1,0:T(8,128)}) custom-call(s32[2]{0:T(128)} %pad_add_fusion.1.count_ref.scalar_ref, bf16[512,512]{1,0:T(8,128)(2,1)} %get-tuple-element.156.dq_low_ref, bf16[512,512]{1,0:T(8,128)(2,1)} %get-tuple-element.168.dq_high_ref, ...), custom_call_target="tpu_custom_call" | custom-call | flops 8999999488 | bytes 18000000 | tf_op jit(solution)/shard_map/key_gradients/pallas_call | solution.py:1115
  376.7 1.5 collective-permute-start.24
  378.8 1.5 collective-permute-start.23
  380.3 16.0 %collective-permute-done.23.refs_14_.refs_16_ = bf16[2,88,1024]{2,1,0:T(8,128)(2,1)S(1)} collective-permute-done((bf16[2,88,1024]{2,1,0:T(8,128)(2,1)S(1)}, bf16[2,88,1024]{2,1,0:T(8,128)(2,1)S(1)}, u32[]{:S(2)}, u32[]{:S(2)}) %collective-permute-start.23) | collective-permute-done | bytes 360480 | tf_op jit(solution)/shard_map/ppermute | solution.py:78
  396.4 3.6 collective-permute-done.24.refs_21_.refs_7_.refs_2_.refs_8_
  401.0 4.0 piece_sums.10
  405.0 1.8 collective-permute-start.26
  407.2 1.4 collective-permute-start.34
  408.6 1.7 collective-permute-start.35
  410.3 3.1 collective-permute-done.25.refs_4_
  413.4 4.7 %collective-permute-done.26.refs_8_.refs_3_.refs_9_ = bf16[4,32,2048]{2,1,0:T(8,128)(2,1)S(1)} collective-permute-done((bf16[4,32,2048]{2,1,0:T(8,128)(2,1)}, bf16[4,32,2048]{2,1,0:T(8,128)(2,1)S(1)}, u32[]{:S(2)}, u32[]{:S(2)}) %collective-permute-start.26) | collective-permute-done | bytes 524320 | tf_op jit(solution)/shard_map/ppermute | solution.py:78
  418.9 2.3 piece_sums.11
  425.1 3.4 collective-permute-start.29
  429.8 3.1 piece_sums.13
  433.7 4.1 collective-permute-start.32
  437.8 1.9 piece_sums.12
  442.0 5.5 %input_gradient.1 = bf16[512,1024]{1,0:T(8,128)(2,1)} custom-call(f32[512,1024]{1,0:T(8,128)} %get-tuple-element.197.own_ref, bf16[512,512]{1,0:T(8,128)(2,1)} %fusion.13.owner_ref, bf16[512,1024]{1,0:T(8,128)(2,1)} %pad_maximum_fusion.returned_ref, bf16[512,1024]{1,0:T(8,128)(2,1)} %x_ref.5, f32[8,1024]{1,0:T(8,128)} %broadcast_in_dim.64.gain_ref, ...), custom_call_target="tpu_custom_call" | custom-call | flops 1000000000 | bytes 8000000 | tf_op jit(solution)/shard_map/input_gradient/pallas_call | solution.py:1164
  447.5 2.4 collective-permute-done.33.refs_11_
  451.2 2.3 side_totals.1
  (229 shorter events, 59.4 us)
Async XLA Ops:
  7.3 167.9 %all-gather.3.cloned.1.call-start = ((), (), s32[]{:S(2)}) async-start(), calls=%async_computation | async-start | bytes 26492928 | tf_op jit(solution)/shard_map/all_gather | solution.py:1220
  9.6 444.0 %all-gather.5.cloned.1.call-start = ((), (), s32[]{:S(2)}) async-start(), calls=%async_computation.1 | async-start | bytes 2162688 | tf_op jit(solution)/shard_map/all_gather | solution.py:1402
  9.8 13.1 %collective-permute-start = (bf16[1,32,128]{1,2,0:T(8,128)(2,1)S(1)}, bf16[1,32,128]{1,2,0:T(8,128)(2,1)S(1)}, u32[]{:S(2)}, u32[]{:S(2)}) collective-permute-start(bf16[1,32,128]{1,2,0:T(8,128)(2,1)S(1)} %bitcast.97), channel_id=1, source_target_pairs={{0,16},{4,20},{8,24},{12,28},{16,0},{20,4},{24,8},{28,12},{1,17},{... | collective-permute-start | bytes 24584 | tf_op jit(solution)/shard_map/ppermute | solution.py:78
  22.9 18.3 %collective-permute-start.1 = (bf16[2,32,128]{2,1,0:T(8,128)(2,1)S(1)}, bf16[2,32,128]{2,1,0:T(8,128)(2,1)S(1)}, u32[]{:S(2)}, u32[]{:S(2)}) collective-permute-start(bf16[2,32,128]{2,1,0:T(8,128)(2,1)S(1)} %pad_maximum_fusion.3), channel_id=1, source_target_pairs={{0,8},{4,12},{8,0},{12,4},{16,24},{20,28},{24,16},{28,20},{1,9},{5... | collective-permute-start | bytes 49160 | tf_op jit(solution)/shard_map/ppermute | solution.py:78
  30.5 14.4 %copy-start.37 = (s32[512,1024]{1,0:T(8,128)S(1)}, s32[512,1024]{1,0:T(8,128)}, u32[]{:S(2)}) copy-start(s32[512,1024]{1,0:T(8,128)} %param.39) | copy-start | bytes 6291460
  30.5 23.1 %collective-permute-start.4 = (bf16[128,1024]{1,0:T(8,128)(2,1)S(1)}, bf16[128,1024]{1,0:T(8,128)(2,1)S(1)}, u32[]{:S(2)}, u32[]{:S(2)}) collective-permute-start(bf16[128,1024]{1,0:T(8,128)(2,1)S(1)} %get-tuple-element.236), channel_id=1, source_target_pairs={{0,4},{4,8},{8,12},{12,16},{16,20},{20,24},{24,28},{1,5},{5,9},{9,... | collective-permute-start | bytes 786440 | tf_op jit(solution)/shard_map/ppermute | solution.py:35
  32.0 21.7 %collective-permute-start.5 = (bf16[128,1024]{1,0:T(8,128)(2,1)S(1)}, bf16[128,1024]{1,0:T(8,128)(2,1)S(1)}, u32[]{:S(2)}, u32[]{:S(2)}) collective-permute-start(bf16[128,1024]{1,0:T(8,128)(2,1)S(1)} %get-tuple-element.235), channel_id=1, source_target_pairs={{4,0},{8,4},{12,8},{16,12},{20,16},{24,20},{28,24},{5,1},{9,5},{13... | collective-permute-start | bytes 786440 | tf_op jit(solution)/shard_map/ppermute | solution.py:36
  33.3 20.4 %collective-permute-start.6 = (bf16[128,1024]{1,0:T(8,128)(2,1)S(1)}, bf16[128,1024]{1,0:T(8,128)(2,1)S(1)}, u32[]{:S(2)}, u32[]{:S(2)}) collective-permute-start(bf16[128,1024]{1,0:T(8,128)(2,1)S(1)} %get-tuple-element.234), channel_id=1, source_target_pairs={{0,1},{1,2},{2,3},{4,5},{5,6},{6,7},{8,9},{9,10},{10,11},{12,13},{... | collective-permute-start | bytes 786440 | tf_op jit(solution)/shard_map/ppermute | solution.py:35
  36.7 17.0 %collective-permute-start.7 = (bf16[128,1024]{1,0:T(8,128)(2,1)S(1)}, bf16[128,1024]{1,0:T(8,128)(2,1)S(1)}, u32[]{:S(2)}, u32[]{:S(2)}) collective-permute-start(bf16[128,1024]{1,0:T(8,128)(2,1)S(1)} %get-tuple-element.233), channel_id=1, source_target_pairs={{1,0},{2,1},{3,2},{5,4},{6,5},{7,6},{9,8},{10,9},{11,10},{13,12},{... | collective-permute-start | bytes 786440 | tf_op jit(solution)/shard_map/ppermute | solution.py:36
  41.2 10.4 %collective-permute-start.2 = (bf16[4,32,128]{2,1,0:T(8,128)(2,1)S(1)}, bf16[4,32,128]{2,1,0:T(8,128)(2,1)S(1)}, u32[]{:S(2)}, u32[]{:S(2)}) collective-permute-start(bf16[4,32,128]{2,1,0:T(8,128)(2,1)S(1)} %pad_maximum_fusion.2), channel_id=1, source_target_pairs={{0,2},{1,3},{2,0},{3,1},{4,6},{5,7},{6,4},{7,5},{8,10},{9,11},{10,... | collective-permute-start | bytes 98312 | tf_op jit(solution)/shard_map/ppermute | solution.py:78
  51.6 6.1 %collective-permute-start.3 = (bf16[8,32,128]{2,1,0:T(8,128)(2,1)S(1)}, bf16[8,32,128]{2,1,0:T(8,128)(2,1)S(1)}, u32[]{:S(2)}, u32[]{:S(2)}) collective-permute-start(bf16[8,32,128]{2,1,0:T(8,128)(2,1)S(1)} %pad_maximum_fusion.1), channel_id=1, source_target_pairs={{0,1},{1,0},{2,3},{3,2},{4,5},{5,4},{6,7},{7,6},{8,9},{9,8},{10,11... | collective-permute-start | bytes 196616 | tf_op jit(solution)/shard_map/ppermute | solution.py:78
  56.3 29.3 %copy-start.13 = (bf16[1024,1024]{1,0:T(8,128)(2,1)}, bf16[1024,1024]{1,0:T(8,128)(2,1)S(1)}, u32[]{:S(2)}) copy-start(bf16[1024,1024]{1,0:T(8,128)(2,1)S(1)} %get-tuple-element.256.picked_ref) | copy-start | bytes 6291460
  58.4 1.3 collective-permute-start.8
  66.4 17.9 %copy-start.31 = (f32[512]{0:T(512)S(1)}, f32[512]{0:T(512)}, u32[]{:S(2)}) copy-start(f32[512]{0:T(512)} %add_rsqrt_fusion.1) | copy-start | bytes 6148
  249.4 20.3 %collective-permute-start.11 = (bf16[16,88,1024]{2,1,0:T(8,128)(2,1)}, bf16[16,88,1024]{2,1,0:T(8,128)(2,1)S(1)}, u32[]{:S(2)}, u32[]{:S(2)}) collective-permute-start(bf16[16,88,1024]{2,1,0:T(8,128)(2,1)} %get-tuple-element.148), channel_id=1, source_target_pairs={{0,4},{4,0},{8,12},{12,8},{16,20},{20,16},{24,28},{28,24},{1,5},{5... | collective-permute-start | bytes 8650760 | tf_op jit(solution)/shard_map/ppermute | solution.py:78
  249.7 20.0 %collective-permute-start.10 = (bf16[16,32,2816]{2,1,0:T(8,128)(2,1)}, bf16[16,32,2816]{2,1,0:T(8,128)(2,1)S(1)}, u32[]{:S(2)}, u32[]{:S(2)}) collective-permute-start(bf16[16,32,2816]{2,1,0:T(8,128)(2,1)} %get-tuple-element.147), channel_id=1, source_target_pairs={{0,4},{4,0},{8,12},{12,8},{16,20},{20,16},{24,28},{28,24},{1,5},{5... | collective-permute-start | bytes 8650760 | tf_op jit(solution)/shard_map/ppermute | solution.py:78
  250.0 19.8 %collective-permute-start.9 = (bf16[16,32,2816]{2,1,0:T(8,128)(2,1)}, bf16[16,32,2816]{2,1,0:T(8,128)(2,1)}, u32[]{:S(2)}, u32[]{:S(2)}) collective-permute-start(bf16[16,32,2816]{2,1,0:T(8,128)(2,1)} %get-tuple-element.146), channel_id=1, source_target_pairs={{0,4},{4,0},{8,12},{12,8},{16,20},{20,16},{24,28},{28,24},{1,5},{5... | collective-permute-start | bytes 8650760 | tf_op jit(solution)/shard_map/ppermute | solution.py:78
  269.4 31.9 %collective-permute-start.15 = (bf16[16,32,2048]{2,1,0:T(8,128)(2,1)}, bf16[16,32,2048]{2,1,0:T(8,128)(2,1)}, u32[]{:S(2)}, u32[]{:S(2)}) collective-permute-start(bf16[16,32,2048]{2,1,0:T(8,128)(2,1)} %get-tuple-element.157), channel_id=1, source_target_pairs={{0,4},{4,0},{8,12},{12,8},{16,20},{20,16},{24,28},{28,24},{1,5},{5... | collective-permute-start | bytes 6291464 | tf_op jit(solution)/shard_map/ppermute | solution.py:78
  278.4 34.0 %collective-permute-start.14 = (bf16[8,88,1024]{2,1,0:T(8,128)(2,1)}, bf16[8,88,1024]{2,1,0:T(8,128)(2,1)S(1)}, u32[]{:S(2)}, u32[]{:S(2)}) collective-permute-start(bf16[8,88,1024]{2,1,0:T(8,128)(2,1)} %get-tuple-element.166), channel_id=1, source_target_pairs={{0,8},{4,12},{8,0},{12,4},{16,24},{20,28},{24,16},{28,20},{1,9},{5... | collective-permute-start | bytes 4325384 | tf_op jit(solution)/shard_map/ppermute | solution.py:78
  278.5 34.0 %collective-permute-start.13 = (bf16[8,32,2816]{2,1,0:T(8,128)(2,1)}, bf16[8,32,2816]{2,1,0:T(8,128)(2,1)S(1)}, u32[]{:S(2)}, u32[]{:S(2)}) collective-permute-start(bf16[8,32,2816]{2,1,0:T(8,128)(2,1)} %get-tuple-element.165), channel_id=1, source_target_pairs={{0,2},{1,3},{2,0},{3,1},{4,6},{5,7},{6,4},{7,5},{8,10},{9,11},{10,... | collective-permute-start | bytes 4325384 | tf_op jit(solution)/shard_map/ppermute | solution.py:78
  280.0 33.7 %collective-permute-start.12 = (bf16[8,32,2816]{2,1,0:T(8,128)(2,1)}, bf16[8,32,2816]{2,1,0:T(8,128)(2,1)S(1)}, u32[]{:S(2)}, u32[]{:S(2)}) collective-permute-start(bf16[8,32,2816]{2,1,0:T(8,128)(2,1)} %get-tuple-element.164), channel_id=1, source_target_pairs={{0,1},{1,0},{2,3},{3,2},{4,5},{5,4},{6,7},{7,6},{8,9},{9,8},{10,11... | collective-permute-start | bytes 4325384 | tf_op jit(solution)/shard_map/ppermute | solution.py:78
  301.3 45.2 %collective-permute-start.20 = (bf16[16,32,2048]{2,1,0:T(8,128)(2,1)}, bf16[16,32,2048]{2,1,0:T(8,128)(2,1)S(1)}, u32[]{:S(2)}, u32[]{:S(2)}) collective-permute-start(bf16[16,32,2048]{2,1,0:T(8,128)(2,1)} %get-tuple-element.173), channel_id=1, source_target_pairs={{0,4},{4,0},{8,12},{12,8},{16,20},{20,16},{24,28},{28,24},{1,5},{5... | collective-permute-start | bytes 6291464 | tf_op jit(solution)/shard_map/ppermute | solution.py:78
  320.8 34.1 %collective-permute-start.19 = (bf16[8,32,2048]{2,1,0:T(8,128)(2,1)}, bf16[8,32,2048]{2,1,0:T(8,128)(2,1)S(1)}, u32[]{:S(2)}, u32[]{:S(2)}) collective-permute-start(bf16[8,32,2048]{2,1,0:T(8,128)(2,1)} %get-tuple-element.182), channel_id=1, source_target_pairs={{0,8},{4,12},{8,0},{12,4},{16,24},{20,28},{24,16},{28,20},{1,9},{5... | collective-permute-start | bytes 3145736 | tf_op jit(solution)/shard_map/ppermute | solution.py:78
  322.5 24.0 %collective-permute-start.18 = (bf16[4,88,1024]{2,1,0:T(8,128)(2,1)}, bf16[4,88,1024]{2,1,0:T(8,128)(2,1)}, u32[]{:S(2)}, u32[]{:S(2)}) collective-permute-start(bf16[4,88,1024]{2,1,0:T(8,128)(2,1)} %get-tuple-element.181), channel_id=1, source_target_pairs={{0,1},{1,0},{2,3},{3,2},{4,5},{5,4},{6,7},{7,6},{8,9},{9,8},{10,11... | collective-permute-start | bytes 2162696 | tf_op jit(solution)/shard_map/ppermute | solution.py:78
  323.3 31.6 %collective-permute-start.17 = (bf16[4,32,2816]{2,1,0:T(8,128)(2,1)}, bf16[4,32,2816]{2,1,0:T(8,128)(2,1)}, u32[]{:S(2)}, u32[]{:S(2)}) collective-permute-start(bf16[4,32,2816]{2,1,0:T(8,128)(2,1)} %get-tuple-element.180), channel_id=1, source_target_pairs={{0,1},{1,0},{2,3},{3,2},{4,5},{5,4},{6,7},{7,6},{8,9},{9,8},{10,11... | collective-permute-start | bytes 2162696 | tf_op jit(solution)/shard_map/ppermute | solution.py:78
  324.5 30.3 %collective-permute-start.16 = (bf16[4,32,2816]{2,1,0:T(8,128)(2,1)}, bf16[4,32,2816]{2,1,0:T(8,128)(2,1)}, u32[]{:S(2)}, u32[]{:S(2)}) collective-permute-start(bf16[4,32,2816]{2,1,0:T(8,128)(2,1)} %get-tuple-element.179), channel_id=1, source_target_pairs={{0,2},{1,3},{2,0},{3,1},{4,6},{5,7},{6,4},{7,5},{8,10},{9,11},{10,... | collective-permute-start | bytes 2162696 | tf_op jit(solution)/shard_map/ppermute | solution.py:78
  325.3 19.9 %copy-start.29 = (f32[96,128]{1,0:T(8,128)S(1)}, f32[96,128]{1,0:T(8,128)}, u32[]{:S(2)}) copy-start(f32[96,128]{1,0:T(8,128)} %get-tuple-element.217) | copy-start | bytes 147460
  325.3 19.9 %copy-start.30 = (f32[96,128]{1,0:T(8,128)S(1)}, f32[96,128]{1,0:T(8,128)}, u32[]{:S(2)}) copy-start(f32[96,128]{1,0:T(8,128)} %get-tuple-element.218) | copy-start | bytes 147460
  360.6 16.1 %collective-permute-start.22 = (bf16[2,32,5632]{2,1,0:T(8,128)(2,1)}, bf16[2,32,5632]{2,1,0:T(8,128)(2,1)S(1)}, u32[]{:S(2)}, u32[]{:S(2)}) collective-permute-start(bf16[2,32,5632]{2,1,0:T(8,128)(2,1)} %get-tuple-element.192), channel_id=1, source_target_pairs={{0,8},{4,12},{8,0},{12,4},{16,24},{20,28},{24,16},{28,20},{1,9},{5... | collective-permute-start | bytes 2162696 | tf_op jit(solution)/shard_map/ppermute | solution.py:78
  361.4 15.3 %copy-start.39 = (bf16[8,32,2048]{2,1,0:T(8,128)(2,1)S(1)}, bf16[8,32,2048]{2,1,0:T(8,128)(2,1)}, u32[]{:S(2)}) copy-start(bf16[8,32,2048]{2,1,0:T(8,128)(2,1)} %get-tuple-element.195) | copy-start | bytes 3145732
  361.4 16.8 %copy-start.40 = (bf16[4,32,2048]{2,1,0:T(8,128)(2,1)S(1)}, bf16[4,32,2048]{2,1,0:T(8,128)(2,1)}, u32[]{:S(2)}) copy-start(bf16[4,32,2048]{2,1,0:T(8,128)(2,1)} %get-tuple-element.194) | copy-start | bytes 1572868
  361.4 17.4 %copy-start.41 = (bf16[2,88,1024]{2,1,0:T(8,128)(2,1)S(1)}, bf16[2,88,1024]{2,1,0:T(8,128)(2,1)}, u32[]{:S(2)}) copy-start(bf16[2,88,1024]{2,1,0:T(8,128)(2,1)} %get-tuple-element.193) | copy-start | bytes 1081348
  376.7 23.3 %copy-start.12 = (bf16[2,32,5632]{2,1,0:T(8,128)(2,1)}, bf16[2,32,5632]{2,1,0:T(8,128)(2,1)S(1)}, u32[]{:S(2)}) copy-start(bf16[2,32,5632]{2,1,0:T(8,128)(2,1)S(1)} %collective-permute-done.22.refs_4_.refs_9_.refs_10_) | copy-start | bytes 2162692
  376.7 23.3 %collective-permute-start.24 = (bf16[8,32,2048]{2,1,0:T(8,128)(2,1)S(1)}, bf16[8,32,2048]{2,1,0:T(8,128)(2,1)S(1)}, u32[]{:S(2)}, u32[]{:S(2)}) collective-permute-start(bf16[8,32,2048]{2,1,0:T(8,128)(2,1)S(1)} %copy-done.39), channel_id=1, source_target_pairs={{0,1},{1,0},{2,3},{3,2},{4,5},{5,4},{6,7},{7,6},{8,9},{9,8},{10,11... | collective-permute-start | bytes 3145736 | tf_op jit(solution)/shard_map/ppermute | solution.py:78
  378.2 18.2 %collective-permute-start.21 = (bf16[4,32,2048]{2,1,0:T(8,128)(2,1)S(1)}, bf16[4,32,2048]{2,1,0:T(8,128)(2,1)S(1)}, u32[]{:S(2)}, u32[]{:S(2)}) collective-permute-start(bf16[4,32,2048]{2,1,0:T(8,128)(2,1)S(1)} %copy-done.40), channel_id=1, source_target_pairs={{0,2},{1,3},{2,0},{3,1},{4,6},{5,7},{6,4},{7,5},{8,10},{9,11},{10,... | collective-permute-start | bytes 1572872 | tf_op jit(solution)/shard_map/ppermute | solution.py:78
  378.8 17.6 %collective-permute-start.23 = (bf16[2,88,1024]{2,1,0:T(8,128)(2,1)S(1)}, bf16[2,88,1024]{2,1,0:T(8,128)(2,1)S(1)}, u32[]{:S(2)}, u32[]{:S(2)}) collective-permute-start(bf16[2,88,1024]{2,1,0:T(8,128)(2,1)S(1)} %copy-done.41), channel_id=1, source_target_pairs={{0,16},{4,20},{8,24},{12,28},{16,0},{20,4},{24,8},{28,12},{1,17},{... | collective-permute-start | bytes 1081352 | tf_op jit(solution)/shard_map/ppermute | solution.py:78
  405.0 13.1 %collective-permute-start.26 = (bf16[4,32,2048]{2,1,0:T(8,128)(2,1)}, bf16[4,32,2048]{2,1,0:T(8,128)(2,1)S(1)}, u32[]{:S(2)}, u32[]{:S(2)}) collective-permute-start(bf16[4,32,2048]{2,1,0:T(8,128)(2,1)} %get-tuple-element.204), channel_id=1, source_target_pairs={{0,2},{1,3},{2,0},{3,1},{4,6},{5,7},{6,4},{7,5},{8,10},{9,11},{10,... | collective-permute-start | bytes 1572872 | tf_op jit(solution)/shard_map/ppermute | solution.py:78
  406.8 6.6 %collective-permute-start.25 = (bf16[2,32,2048]{2,1,0:T(8,128)(2,1)}, bf16[2,32,2048]{2,1,0:T(8,128)(2,1)S(1)}, u32[]{:S(2)}, u32[]{:S(2)}) collective-permute-start(bf16[2,32,2048]{2,1,0:T(8,128)(2,1)} %get-tuple-element.203), channel_id=1, source_target_pairs={{0,1},{1,0},{2,3},{3,2},{4,5},{5,4},{6,7},{7,6},{8,9},{9,8},{10,11... | collective-permute-start | bytes 786440 | tf_op jit(solution)/shard_map/ppermute | solution.py:78
  407.2 21.3 %collective-permute-start.34 = (bf16[1,32,5632]{2,1,0:T(8,128)(2,1)}, bf16[1,32,5632]{2,1,0:T(8,128)(2,1)S(1)}, u32[]{:S(2)}, u32[]{:S(2)}) collective-permute-start(bf16[1,32,5632]{2,1,0:T(8,128)(2,1)} %get-tuple-element.220), channel_id=1, source_target_pairs={{0,16},{4,20},{8,24},{12,28},{16,0},{20,4},{24,8},{28,12},{1,17},{... | collective-permute-start | bytes 1081352 | tf_op jit(solution)/shard_map/ppermute | solution.py:78
  408.6 13.8 %copy-start.21 = (bf16[512,1024]{1,0:T(8,128)(2,1)S(1)}, bf16[512,1024]{1,0:T(8,128)(2,1)}, u32[]{:S(2)}) copy-start(bf16[512,1024]{1,0:T(8,128)(2,1)} %get-tuple-element.207) | copy-start | bytes 3145732
  408.6 16.5 %collective-permute-start.35 = (bf16[1,88,1024]{2,1,0:T(8,128)(2,1)}, bf16[1,88,1024]{2,1,0:T(8,128)(2,1)S(1)}, u32[]{:S(2)}, u32[]{:S(2)}) collective-permute-start(bf16[1,88,1024]{2,1,0:T(8,128)(2,1)} %get-tuple-element.221), channel_id=1, source_target_pairs={{0,2},{1,3},{2,0},{3,1},{4,6},{5,7},{6,4},{7,5},{8,10},{9,11},{10,... | collective-permute-start | bytes 540680 | tf_op jit(solution)/shard_map/ppermute | solution.py:78
  421.3 12.4 %collective-permute-start.31 = (bf16[2,32,2048]{2,1,0:T(8,128)(2,1)}, bf16[2,32,2048]{2,1,0:T(8,128)(2,1)S(1)}, u32[]{:S(2)}, u32[]{:S(2)}) collective-permute-start(bf16[2,32,2048]{2,1,0:T(8,128)(2,1)} %get-tuple-element.206), channel_id=1, source_target_pairs={{0,8},{4,12},{8,0},{12,4},{16,24},{20,28},{24,16},{28,20},{1,9},{5... | collective-permute-start | bytes 786440 | tf_op jit(solution)/shard_map/ppermute | solution.py:78
  422.5 17.3 %collective-permute-start.27 = (bf16[128,1024]{1,0:T(8,128)(2,1)S(1)}, bf16[128,1024]{1,0:T(8,128)(2,1)S(1)}, u32[]{:S(2)}, u32[]{:S(2)}) collective-permute-start(bf16[128,1024]{1,0:T(8,128)(2,1)S(1)} %get-tuple-element.229), channel_id=1, source_target_pairs={{0,4},{4,8},{8,12},{12,16},{16,20},{20,24},{24,28},{1,5},{5,9},{9,... | collective-permute-start | bytes 786440 | tf_op jit(solution)/shard_map/ppermute | solution.py:35
  423.8 16.6 %collective-permute-start.28 = (bf16[128,1024]{1,0:T(8,128)(2,1)S(1)}, bf16[128,1024]{1,0:T(8,128)(2,1)S(1)}, u32[]{:S(2)}, u32[]{:S(2)}) collective-permute-start(bf16[128,1024]{1,0:T(8,128)(2,1)S(1)} %get-tuple-element.232), channel_id=1, source_target_pairs={{4,0},{8,4},{12,8},{16,12},{20,16},{24,20},{28,24},{5,1},{9,5},{13... | collective-permute-start | bytes 786440 | tf_op jit(solution)/shard_map/ppermute | solution.py:36
  425.1 15.3 %collective-permute-start.29 = (bf16[128,1024]{1,0:T(8,128)(2,1)S(1)}, bf16[128,1024]{1,0:T(8,128)(2,1)S(1)}, u32[]{:S(2)}, u32[]{:S(2)}) collective-permute-start(bf16[128,1024]{1,0:T(8,128)(2,1)S(1)} %get-tuple-element.231), channel_id=1, source_target_pairs={{0,1},{1,2},{2,3},{4,5},{5,6},{6,7},{8,9},{9,10},{10,11},{12,13},{... | collective-permute-start | bytes 786440 | tf_op jit(solution)/shard_map/ppermute | solution.py:35
  428.5 11.8 %collective-permute-start.30 = (bf16[128,1024]{1,0:T(8,128)(2,1)S(1)}, bf16[128,1024]{1,0:T(8,128)(2,1)S(1)}, u32[]{:S(2)}, u32[]{:S(2)}) collective-permute-start(bf16[128,1024]{1,0:T(8,128)(2,1)S(1)} %get-tuple-element.230), channel_id=1, source_target_pairs={{1,0},{2,1},{3,2},{5,4},{6,5},{7,6},{9,8},{10,9},{11,10},{13,12},{... | collective-permute-start | bytes 786440 | tf_op jit(solution)/shard_map/ppermute | solution.py:36
  433.7 16.2 %collective-permute-start.32 = (bf16[1,32,2048]{2,1,0:T(8,128)(2,1)S(1)}, bf16[1,32,2048]{2,1,0:T(8,128)(2,1)S(1)}, u32[]{:S(2)}, u32[]{:S(2)}) collective-permute-start(bf16[1,32,2048]{2,1,0:T(8,128)(2,1)S(1)} %copy-done.42), channel_id=1, source_target_pairs={{0,16},{4,20},{8,24},{12,28},{16,0},{20,4},{24,8},{28,12},{1,17},{... | collective-permute-start | bytes 393224 | tf_op jit(solution)/shard_map/ppermute | solution.py:78
  439.7 10.2 %collective-permute-start.33 = (bf16[1,32,2048]{2,1,0:T(8,128)(2,1)}, bf16[1,32,2048]{2,1,0:T(8,128)(2,1)S(1)}, u32[]{:S(2)}, u32[]{:S(2)}) collective-permute-start(bf16[1,32,2048]{2,1,0:T(8,128)(2,1)} %piece_sums.12), channel_id=1, source_target_pairs={{0,16},{4,20},{8,24},{12,28},{16,0},{20,4},{24,8},{28,12},{1,17},{... | collective-permute-start | bytes 393224 | tf_op jit(solution)/shard_map/ppermute | solution.py:78
  (34 other events, 123.8 us)
Sparse Core Ops, SparseCore 0:
  11.5 163.5 all-gather.2
  376.9 62.8 all-gather.4
